TPU v7x, 32 devices: a whole 2x2x4 slice. The times are simulated.
32 devices in a mesh: dp: 16 (over z, y, x), tensor: 2 (over core).
Axes of the slice: x: 2, y: 2, z: 4, core: 2. Of those that a mesh axis runs over, the one named last changes fastest.
Arguments:
- tokens: bfloat16 [16, 2048, 768], P('dp', 'tensor'), may hold values from -6 to 6
- segment_ids: int32 [16, 2048], P('dp', 'tensor'), may hold values from 0 to 7, never falling along the last dimension, each value on 1 to 1536 neighbouring positions
- routes: int32 [16, 2048, 2], P('dp', 'tensor'), may hold values from 0 to 11, all different within a row
- prev_logits: float32 [16, 2048, 12], P('dp', 'tensor'), may hold values from -6 to 6
- cotangent: bfloat16 [16, 2048, 768], P('dp', 'tensor'), may hold values from -6 to 6
- proj_weight: bfloat16 [3, 768, 768], P(None, 'dp', 'tensor'), may hold values from -0.21875 to 0.21875
- out_weight: bfloat16 [768, 768], P('dp', 'tensor'), may hold values from -0.875 to 0.875
- norm_gain: bfloat16 [2, 768], P(None, 'dp'), may hold values from 0.5 to 1.5
- expert_weight: bfloat16 [8, 3, 768, 2048], P(None, None, 'dp', 'tensor'), may hold values from -0.21875 to 0.21875
- router: bfloat16 [768, 16], P('dp'), may hold values from -0.109375 to 0.109375
- constant_vectors: bfloat16 [2, 768], P(None, 'dp'), may hold values from -6 to 6
- gate_mixing: float32 [12, 12], replicated, may hold values from -1.25 to 1.25
Outputs:
- mixed: bfloat16 [16, 2048, 768], P('dp', 'tensor')
- tokens_grad: float32 [16, 2048, 768], P('dp', 'tensor')
- prev_grad: float32 [16, 2048, 12], P('dp', 'tensor')
- proj_grad: float32 [3, 768, 768], P(None, 'dp', 'tensor')
- out_proj_grad: float32 [768, 768], P('dp', 'tensor')
- gain_grad: float32 [2, 768], P(None, 'dp')
- expert_grad: float32 [8, 3, 768, 2048], P(None, None, 'dp', 'tensor')
- router_grad: float32 [768, 16], P('dp')
- constant_grad: float32 [2, 768], P(None, 'dp')
- mixing_grad: float32 [12, 12], replicated
Inputs may be any that keep to these rules, and one draw needn't show every extreme that they name: `segment_ids`: within a sequence the ids never fall; each document holds at most 1536 tokens, and one holds exactly 1536. `routes`: the two experts of a token differ.
All inputs are finite; a program needn't handle non-finite values.
Results may differ from a plain program's by a relative error of at most 0.017.
Values may be sent and summed in bfloat16 or wider, within the bound.
A program may use at most 384 MiB of HBM per device.

v0:
```python
import jax
import jax.numpy as jnp
from jax import lax
from jax.sharding import PartitionSpec as P

HEAD_DIM = 64
EXPERTS_FF = 8
EXPERTS = 12
CAPACITY = 341


EPS = 1e-05
HIGH = lax.Precision.HIGHEST
NEG = -1e30


def rms_scale(rows):
    return lax.rsqrt(jnp.mean(rows * rows, axis=-1, keepdims=True) + EPS)


def softmax_last(values):
    peak = jnp.max(values, axis=-1, keepdims=True)
    expo = jnp.exp(values - peak)
    return expo / jnp.sum(expo, axis=-1, keepdims=True)


def slot_table(flat_routes):
    onehot = (flat_routes[:, None] == jnp.arange(EXPERTS_FF, dtype=jnp.int32)[None, :]).astype(
        jnp.int32
    )
    position = jnp.sum((jnp.cumsum(onehot, axis=0) - onehot) * onehot, axis=1)
    keep = (flat_routes < EXPERTS_FF) & (position < CAPACITY)
    target = jnp.where(keep, flat_routes, EXPERTS_FF)
    pairs = jnp.arange(flat_routes.shape[0], dtype=jnp.int32)
    empty = jnp.full((EXPERTS_FF, CAPACITY), flat_routes.shape[0], jnp.int32)
    return empty.at[target, position].set(pairs, mode="drop")


def block_scores(q_blk, key_rows, seg_rows, seg_keys, first):
    count = q_blk.shape[0]
    rows = first + jnp.arange(count, dtype=jnp.int32)
    cols = jnp.arange(key_rows.shape[0], dtype=jnp.int32)
    allowed = (cols[None, :] <= rows[:, None]) & (seg_keys[None, :] == seg_rows[:, None])
    scores = jnp.einsum(
        "qhd,khd->hqk", q_blk, key_rows, preferred_element_type=jnp.float32
    ) * HEAD_DIM ** (-0.5)
    return jnp.where(allowed[None], scores, NEG)


def expert_math(rows, out_grad, weights):
    single = jnp.float32
    half = jnp.bfloat16
    gate_pre = jnp.dot(rows, weights[0], preferred_element_type=single)
    up_pre = jnp.dot(rows, weights[1], preferred_element_type=single)
    sigma = jax.nn.sigmoid(gate_pre)
    active = gate_pre * sigma
    hidden = (active * up_pre).astype(half)
    expert_out = jnp.dot(hidden, weights[2].T, preferred_element_type=single)
    hidden_grad = jnp.dot(out_grad, weights[2], preferred_element_type=single)
    gate_pre_grad = (hidden_grad * up_pre * sigma * (1.0 + gate_pre * (1.0 - sigma))).astype(half)
    up_pre_grad = (hidden_grad * active).astype(half)
    weight_grads = jnp.stack(
        [
            jnp.dot(rows.T, gate_pre_grad, preferred_element_type=single),
            jnp.dot(rows.T, up_pre_grad, preferred_element_type=single),
            jnp.dot(out_grad.T, hidden, preferred_element_type=single),
        ]
    )
    in_grad = jnp.dot(gate_pre_grad, weights[0].T, preferred_element_type=single) + jnp.dot(
        up_pre_grad, weights[1].T, preferred_element_type=single
    )
    return (expert_out, in_grad, weight_grads)


def per_device(
    tokens,
    segment_ids,
    routes,
    prev_logits,
    cotangent,
    proj_weight,
    out_weight,
    norm_gain,
    expert_weight,
    router,
    constant_vectors,
    gate_mixing,
):
    single = jnp.float32
    half = jnp.bfloat16
    proj_full, outw_full, gain_full, expert_full, router_full, const_full = (
        lax.all_gather(proj_weight, "dp", axis=1, tiled=True),
        lax.all_gather(out_weight, "dp", axis=0, tiled=True),
        lax.all_gather(norm_gain, "dp", axis=1, tiled=True),
        lax.all_gather(expert_weight, "dp", axis=2, tiled=True),
        lax.all_gather(router, "dp", axis=0, tiled=True),
        lax.all_gather(constant_vectors, "dp", axis=1, tiled=True),
    )
    gains = gain_full.astype(single)
    x_rows = tokens[0].astype(single)
    local_rows = x_rows.shape[0]
    scale_one = rms_scale(x_rows)
    normed_one = (x_rows * scale_one * gains[0]).astype(half)
    full_one, seg_all = (
        lax.all_gather(normed_one[None], "tensor", axis=1, tiled=True),
        lax.all_gather(segment_ids.astype(half), "tensor", axis=1, tiled=True),
    )
    full_one = full_one[0]
    seg_keys = seg_all[0]
    seq = full_one.shape[0]
    width = full_one.shape[1]
    heads_local = proj_full.shape[2] // HEAD_DIM
    qkv = jnp.einsum("td,cdh->cth", full_one, proj_full, preferred_element_type=single).astype(half)
    queries = qkv[0].reshape(seq, heads_local, HEAD_DIM)
    keys_all = qkv[1].reshape(seq, heads_local, HEAD_DIM)
    values_all = qkv[2].reshape(seq, heads_local, HEAD_DIM)
    block = min(512, seq)
    outputs = []
    log_totals = []
    for first in range(0, seq, block):
        last = first + block
        scores = block_scores(
            queries[first:last], keys_all[:last], seg_keys[first:last], seg_keys[:last], first
        )
        peak = jnp.max(scores, axis=-1, keepdims=True)
        expo = jnp.exp(scores - peak)
        total = jnp.sum(expo, axis=-1, keepdims=True)
        probs_low = (expo / total).astype(half)
        outputs.append(
            jnp.einsum(
                "hqk,khd->qhd", probs_low, values_all[:last], preferred_element_type=single
            ).astype(half)
        )
        log_totals.append(peak + jnp.log(total))
    mixed_heads = jnp.concatenate(outputs, 0).reshape(seq, heads_local * HEAD_DIM)
    part = mixed_heads
    attn_out = lax.psum_scatter(
        jnp.einsum("th,dh->td", part, outw_full, preferred_element_type=single).astype(
            jnp.bfloat16
        ),
        "tensor",
        scatter_dimension=0,
        tiled=True,
    ).astype(jnp.float32)
    resid = x_rows + attn_out
    scale_two = rms_scale(resid)
    normed_two = (resid * scale_two * gains[1]).astype(half)
    two_rows = normed_two.astype(single)
    router_rows = jnp.dot(normed_two, router_full, preferred_element_type=single)
    prev_rows = prev_logits[0]
    logits = router_rows[:, :EXPERTS] + jnp.dot(prev_rows, gate_mixing, precision=HIGH)
    route_rows = routes[0]
    picks = (route_rows[:, :, None] == jnp.arange(EXPERTS, dtype=jnp.int32)[None, None, :]).astype(
        single
    )
    gates = softmax_last(jnp.sum(picks * logits[:, None, :], axis=-1))
    gate_low = gates.astype(half)
    grad_rows = cotangent[0].astype(single)
    full_two, gate_all, route_all, grad_all = (
        lax.all_gather(normed_two[None], "tensor", axis=1, tiled=True),
        lax.all_gather(gate_low[None], "tensor", axis=1, tiled=True),
        lax.all_gather(route_rows.astype(half)[None], "tensor", axis=1, tiled=True),
        lax.all_gather(cotangent, "tensor", axis=1, tiled=True),
    )
    full_two = full_two[0]
    grad_all = grad_all[0]
    gate_flat = gate_all[0].reshape(-1)
    groups = lax.axis_size("dp") // EXPERTS_FF
    per_dest = -(-CAPACITY // groups)
    wide = per_dest * groups
    table = slot_table(route_all[0].reshape(-1).astype(jnp.int32))
    table = jnp.concatenate([table, jnp.full((EXPERTS_FF, wide - CAPACITY), 2 * seq, jnp.int32)], 1)
    slot_tok = table // 2
    pad_two = jnp.concatenate([full_two, jnp.zeros((1, width), half)], 0)
    slot_rows = pad_two[slot_tok]
    slot_gate = jnp.concatenate([gate_flat, jnp.zeros((1,), half)], 0)[table].astype(single)
    pad_grad = jnp.concatenate([grad_all, jnp.zeros((1, width), half)], 0)
    slot_grad = pad_grad[slot_tok].astype(single)
    out_slot_grad = (slot_grad * slot_gate[:, :, None]).astype(half)
    expert_out, slot_in_grad, expert_grad = jax.vmap(expert_math)(
        slot_rows, out_slot_grad, expert_full
    )
    combined = (
        jnp.zeros((seq + 1, width), single)
        .at[slot_tok]
        .add(expert_out * slot_gate[:, :, None])[:seq]
    )
    gate_slot_grad = jnp.sum(slot_grad * expert_out, axis=-1)
    two_grad_all = jnp.zeros((seq + 1, width), single).at[slot_tok].add(slot_in_grad)[:seq]
    gate_grad_all = (
        jnp.zeros((2 * seq + 1,), single).at[table].add(gate_slot_grad)[: 2 * seq].reshape(seq, 2)
    )
    ffn_out, two_grad_ffn, gate_grad_ffn = (
        lax.psum_scatter(
            combined[None].astype(jnp.bfloat16), "tensor", scatter_dimension=1, tiled=True
        ).astype(jnp.float32),
        lax.psum_scatter(
            two_grad_all[None].astype(jnp.bfloat16), "tensor", scatter_dimension=1, tiled=True
        ).astype(jnp.float32),
        lax.psum_scatter(
            gate_grad_all[None].astype(jnp.bfloat16), "tensor", scatter_dimension=1, tiled=True
        ).astype(jnp.float32),
    )
    ffn_out = ffn_out[0]
    alphas = softmax_last(router_rows[:, EXPERTS:].reshape(local_rows, 2, 2))
    const_f = const_full.astype(single)
    copy_weight = jnp.sum(gates * picks[:, :, EXPERTS_FF + 1], axis=1)
    const_weight = jnp.sum(gates[:, :, None] * picks[:, :, EXPERTS_FF + 2 :], axis=1)
    own_weight = copy_weight + jnp.sum(const_weight * alphas[:, :, 0], axis=1)
    vec_weight = const_weight * alphas[:, :, 1]
    other_out = own_weight[:, None] * two_rows + jnp.dot(vec_weight, const_f, precision=HIGH)
    mixed = (resid + ffn_out + other_out).astype(half)[None]
    own_dot = jnp.sum(grad_rows * two_rows, axis=-1)
    vec_dot = jnp.dot(grad_rows, const_f.T, precision=HIGH)
    value_dot = jnp.stack(
        [
            jnp.zeros_like(own_dot),
            own_dot,
            alphas[:, 0, 0] * own_dot + alphas[:, 0, 1] * vec_dot[:, 0],
            alphas[:, 1, 0] * own_dot + alphas[:, 1, 1] * vec_dot[:, 1],
        ],
        -1,
    )
    gate_grad = gate_grad_ffn[0] + jnp.sum(
        picks[:, :, EXPERTS_FF:] * value_dot[:, None, :], axis=-1
    )
    alpha_grad = jnp.stack([const_weight * own_dot[:, None], const_weight * vec_dot], -1)
    mix_rows_grad = alphas * (alpha_grad - jnp.sum(alphas * alpha_grad, axis=-1, keepdims=True))
    const_vec_grad = jnp.dot(vec_weight.T, grad_rows, precision=HIGH)
    chosen_grad = gates * (gate_grad - jnp.sum(gates * gate_grad, axis=-1, keepdims=True))
    logit_grad = jnp.sum(picks * chosen_grad[:, :, None], axis=1)
    router_rows_grad = jnp.concatenate([logit_grad, mix_rows_grad.reshape(local_rows, 4)], -1)
    two_grad = (
        two_grad_ffn[0]
        + own_weight[:, None] * grad_rows
        + jnp.dot(router_rows_grad, router_full.astype(single).T, precision=HIGH)
    )
    router_grad = jnp.dot(two_rows.T, router_rows_grad, precision=HIGH)
    prev_grad = jnp.dot(logit_grad, gate_mixing.T, precision=HIGH)
    mixing_grad = jnp.dot(prev_rows.T, logit_grad, precision=HIGH)
    weighted_two = two_grad * gains[1]
    resid_grad = grad_rows + scale_two * (
        weighted_two
        - resid * scale_two * scale_two * jnp.mean(weighted_two * resid, axis=-1, keepdims=True)
    )
    gain_two_grad = jnp.sum(two_grad * resid * scale_two, axis=0)
    attn_grad_all = lax.all_gather(resid_grad.astype(half)[None], "tensor", axis=1, tiled=True)[0]
    heads_grad = jnp.dot(attn_grad_all, outw_full, preferred_element_type=single).astype(half)
    out_w_grad = jnp.einsum("td,th->dh", attn_grad_all, mixed_heads, preferred_element_type=single)
    heads_grad = heads_grad.reshape(seq, heads_local, HEAD_DIM)
    query_grads = []
    key_grad = jnp.zeros((seq, heads_local, HEAD_DIM), single)
    value_grad = jnp.zeros((seq, heads_local, HEAD_DIM), single)
    for index, first in enumerate(range(0, seq, block)):
        last = first + block
        q_blk = queries[first:last]
        scores = block_scores(q_blk, keys_all[:last], seg_keys[first:last], seg_keys[:last], first)
        probs = jnp.exp(scores - log_totals[index])
        prob_grad = jnp.einsum(
            "qhd,khd->hqk", heads_grad[first:last], values_all[:last], preferred_element_type=single
        )
        score_grad = (
            probs * (prob_grad - jnp.sum(probs * prob_grad, axis=-1, keepdims=True))
        ).astype(half)
        query_grads.append(
            jnp.einsum("hqk,khd->qhd", score_grad, keys_all[:last], preferred_element_type=single)
            * HEAD_DIM ** (-0.5)
        )
        key_grad = key_grad.at[:last].add(
            jnp.einsum("hqk,qhd->khd", score_grad, q_blk, preferred_element_type=single)
            * HEAD_DIM ** (-0.5)
        )
        value_grad = value_grad.at[:last].add(
            jnp.einsum(
                "hqk,qhd->khd",
                probs.astype(half),
                heads_grad[first:last],
                preferred_element_type=single,
            )
        )
    qkv_grad = (
        jnp.stack([jnp.concatenate(query_grads, 0), key_grad, value_grad])
        .reshape(3, seq, heads_local * HEAD_DIM)
        .astype(half)
    )
    proj_grad = jnp.einsum("td,cth->cdh", full_one, qkv_grad, preferred_element_type=single)
    part = qkv_grad
    one_grad = lax.psum_scatter(
        jnp.einsum("cth,cdh->td", part, proj_full, preferred_element_type=single).astype(
            jnp.bfloat16
        ),
        "tensor",
        scatter_dimension=0,
        tiled=True,
    ).astype(jnp.float32)
    weighted_one = one_grad * gains[0]
    tokens_grad = resid_grad + scale_one * (
        weighted_one
        - x_rows * scale_one * scale_one * jnp.mean(weighted_one * x_rows, axis=-1, keepdims=True)
    )
    gain_one_grad = jnp.sum(one_grad * x_rows * scale_one, axis=0)
    gain_total, router_total, const_total, mixing_total = lax.psum(
        (jnp.stack([gain_one_grad, gain_two_grad]), router_grad, const_vec_grad, mixing_grad),
        ("dp", "tensor"),
    )
    shard_rows = norm_gain.shape[1]
    offset = lax.axis_index("dp") * shard_rows
    gain_shard = lax.dynamic_slice_in_dim(gain_total, offset, shard_rows, 1)
    router_shard = lax.dynamic_slice_in_dim(router_total, offset, shard_rows, 0)
    const_shard = lax.dynamic_slice_in_dim(const_total, offset, shard_rows, 1)
    proj_shard, outw_shard, expert_shard = (
        lax.psum_scatter(proj_grad, "dp", scatter_dimension=1, tiled=True),
        lax.psum_scatter(out_w_grad, "dp", scatter_dimension=0, tiled=True),
        lax.psum_scatter(expert_grad, "dp", scatter_dimension=2, tiled=True),
    )
    return (
        mixed,
        tokens_grad[None],
        prev_grad[None],
        proj_shard,
        outw_shard,
        gain_shard,
        expert_shard,
        router_shard,
        const_shard,
        mixing_total,
    )


def solution(mesh):
    return jax.shard_map(
        per_device,
        mesh=mesh,
        in_specs=(
            P("dp", "tensor", None),
            P("dp", "tensor"),
            P("dp", "tensor", None),
            P("dp", "tensor", None),
            P("dp", "tensor", None),
            P(None, "dp", "tensor"),
            P("dp", "tensor"),
            P(None, "dp"),
            P(None, None, "dp", "tensor"),
            P("dp", None),
            P(None, "dp"),
            P(),
        ),
        out_specs=(
            P("dp", "tensor", None),
            P("dp", "tensor", None),
            P("dp", "tensor", None),
            P(None, "dp", "tensor"),
            P("dp", "tensor"),
            P(None, "dp"),
            P(None, None, "dp", "tensor"),
            P("dp", None),
            P(None, "dp"),
            P(),
        ),
        check_vma=False,
    )
```

profile of v0, /device:TPU:12, one launch (start us, length us, event | category | flops | bytes accessed | tf_op | source)
XLA Modules:
  0.0 2447.5 jit_solution(17126851824698093998)
XLA Ops:
  7.3 30.8 %all-gather.2 = bf16[16,48,2]{1,2,0:T(2,128)(2,1)S(1)} all-gather(bf16[1,48,2]{1,2,0:T(2,128)(2,1)} %bitcast.427), channel_id=1, replica_groups=mesh['dp'=16,'tensor'=2] {'dp'}, dimensions={0}, use_global_device_ids=true | all-gather | bytes 3264 | tf_op jit(solution)/shard_map/all_gather | solution.py:94
  48.6 41.9 %all_gather.46 = bf16[768,384]{1,0:T(8,128)(2,1)} all-gather(bf16[48,384]{1,0:T(8,128)(2,1)S(1)} %copy-done.95), channel_id=1, replica_groups=mesh['dp'=16,'tensor'=2] {'dp'}, dimensions={0}, use_global_device_ids=true | all-gather | bytes 626688 | tf_op jit(solution)/shard_map/all_gather | solution.py:93
  93.2 31.3 %all-gather.14.cloned.1.call-done = bf16[3,768,384]{2,1,0:T(8,128)(2,1)} async-done(((bf16[3,48,384]{2,1,0:T(8,128)(2,1)}), bf16[3,768,384]{2,1,0:T(8,128)(2,1)}) %all-gather.14.cloned.1.call-update) | async-done | bytes 1769488 | tf_op jit(solution)/shard_map/all_gather | solution.py:92
  124.5 6.3 convert_bitcast_fusion
  134.1 10.9 fusion.162
  144.9 10.4 fusion
  155.4 10.7 fusion.111
  166.1 8.2 fusion.163
  174.4 9.0 fusion.2
  183.4 8.8 fusion.112
  211.8 10.0 reduce-scatter.10.cloned.1.call-done
  233.6 31.0 %all-gather.3 = bf16[16,48,16]{1,2,0:T(8,128)(2,1)S(1)} all-gather(bf16[1,48,16]{1,2,0:T(8,128)(2,1)S(1)} %bitcast.426), channel_id=1, replica_groups=mesh['dp'=16,'tensor'=2] {'dp'}, dimensions={0}, use_global_device_ids=true | all-gather | bytes 26112 | tf_op jit(solution)/shard_map/all_gather | solution.py:96
  268.2 15.5 scatter_custom_fusion.3
  286.2 9.2 gather_fusion.2
  295.4 8.3 reshape.979
  307.4 16.5 gather_fusion.1
  326.2 9.2 gather_fusion
  335.4 4.1 reshape.909
  339.5 305.5 %all-gather.16.cloned.1.call-done = bf16[8,3,768,1024]{3,2,0,1:T(8,128)(2,1)} async-done(((bf16[8,3,48,1024]{3,2,0,1:T(8,128)(2,1)}), bf16[8,3,768,1024]{3,2,0,1:T(8,128)(2,1)}) %all-gather.16.cloned.1.call-update) | async-done | bytes 37748752 | tf_op jit(solution)/shard_map/all_gather | solution.py:95
  645.0 14.7 fusion.11
  659.8 11.9 fusion.13
  671.7 22.1 multiply_convert_fusion.3
  693.8 14.4 broadcast_multiply_fusion
  708.2 19.8 scatter_custom_fusion.2
  730.2 14.2 fusion.10
  744.4 14.4 fusion.82
  758.7 9.3 reshape.944
  768.1 24.1 scatter_custom_fusion.1
  792.1 4.9 fusion.58
  797.1 29.8 %all-gather.4 = bf16[16,48,2]{1,2,0:T(2,128)(2,1)S(1)} all-gather(bf16[1,48,2]{1,2,0:T(2,128)(2,1)S(1)} %bitcast.428), channel_id=1, replica_groups=mesh['dp'=16,'tensor'=2] {'dp'}, dimensions={0}, use_global_device_ids=true | all-gather | bytes 3264 | tf_op jit(solution)/shard_map/all_gather | solution.py:97
  832.0 5.2 multiply_reduce_fusion.5
  843.4 9.5 reshape.936
  852.9 24.3 scatter_custom_fusion
  877.1 4.8 fusion.57
  889.7 7.7 multiply_reduce_fusion.4
  898.5 7.1 multiply_reduce_fusion.2
  908.3 12.8 multiply_reduce_fusion.1
  921.1 8.1 fusion.78
  929.2 16.8 multiply_reduce_fusion
  946.0 12.0 fusion.59
  961.1 6.6 multiply_convert_fusion.7
  971.2 6.2 multiply_convert_fusion.2
  980.2 17.9 multiply_convert_fusion.1
  998.1 6.4 fusion.71
  1005.6 15.0 multiply_convert_fusion
  1020.7 7.1 fusion.60
  1032.1 4.9 fusion.110
  1037.1 6.8 fusion.109
  1043.8 8.5 fusion.108
  1054.1 7.4 fusion.83
  1067.4 8.0 bitcast_convert_fusion
  1075.5 16.4 convolution_bitcast_fusion.1
  1091.9 15.2 convolution_bitcast_fusion.2
  1107.1 15.4 convolution_bitcast_fusion
  1122.5 50.1 %maximum_bitcast_fusion = f32[8,3,768,1024]{3,2,0,1:T(8,128)} fusion(f32[1,8,768,1024]{3,2,1,0:T(8,128)} %convolution_bitcast_fusion, f32[1,8,768,1024]{3,2,1,0:T(8,128)} %convolution_bitcast_fusion.1, f32[1,8,768,1024]{3,2,1,0:T(8,128)} %convolution_bitcast_fusion.2), kind=kLoop, calls=%fused_computation.7 | loop fusion | flops 37748736 | bytes 150994944 | tf_op jit(solution)/shard_map/vmap()/transpose | solution.py:180
  1177.0 5.3 fusion.167
  1182.7 6.0 fusion.92
  1188.6 61.5 %all-reduce.9.cloned.1.call-done = f32[3,768,384]{2,0,1:T(4,128)} async-done(((f32[3,768,384]{2,0,1:T(4,128)}), f32[3,768,384]{2,0,1:T(4,128)}) %all-reduce.9.cloned.1.call-update) | async-done | bytes 3538960
  1251.8 12.1 reduce-scatter.16.cloned.1.call-done
  1266.7 45.5 %all-reduce.6 = (f32[2,768]{1,0:T(2,128)S(1)}, f32[768,16]{0,1:T(8,128)S(1)}, f32[2,768]{1,0:T(2,128)S(1)}, f32[12,12]{0,1:T(8,128)S(1)}) all-reduce(f32[2,768]{1,0:T(2,128)S(1)} %pad_maximum_fusion.11, f32[768,16]{0,1:T(8,128)S(1)} %fusion.125, f32[2,768]{1,0:T(2,128)S(1)} %fusion.88, ...), channel_id=1, replica_groups=mesh['dp'=16,'tensor'=2] {'dp','tensor'}, use_global_device_ids=true, to_apply=%region_46.47 | all-reduce | flops 15504 | bytes 124032 | tf_op jit(solution)/shard_map/psum | solution.py:302
  1314.3 5.6 fusion.40
  1319.9 992.1 %reduce-scatter.20.cloned.1.call-done = f32[8,3,48,1024]{3,2,0,1:T(8,128)} async-done(((f32[8,3,768,1024]{3,2,0,1:T(8,128)}), f32[8,3,48,1024]{3,2,0,1:T(8,128)}) %reduce-scatter.20.cloned.1.call-update) | async-done | bytes 4718608 | tf_op jit(solution)/shard_map/reduce_scatter | solution.py:314
  2312.0 5.2 copy.119
  2317.2 123.3 %reduce-scatter.18.cloned.1.call-done = f32[48,384]{1,0:T(8,128)} async-done(((f32[768,384]{1,0:T(8,128)}), f32[48,384]{1,0:T(8,128)}) %reduce-scatter.18.cloned.1.call-update) | async-done | bytes 73744 | tf_op jit(solution)/shard_map/reduce_scatter | solution.py:313
  (427 shorter events, 116.2 us)
Async XLA Ops:
  7.2 297.0 %copy-start = (f32[12,12]{1,0:T(8,128)S(1)}, f32[12,12]{1,0:T(8,128)}, u32[]{:S(2)}) copy-start(f32[12,12]{1,0:T(8,128)} %param.43) | copy-start | bytes 1732
  7.2 37.2 %copy-start.102 = (s32[1,1024]{1,0:T(1,128)S(1)}, s32[1,1024]{1,0:T(1,128)}, u32[]{:S(2)}) copy-start(s32[1,1024]{1,0:T(1,128)} %param.33) | copy-start | bytes 12292
  7.2 41.4 %copy-start.95 = (bf16[48,384]{1,0:T(8,128)(2,1)S(1)}, bf16[48,384]{1,0:T(8,128)(2,1)}, u32[]{:S(2)}) copy-start(bf16[48,384]{1,0:T(8,128)(2,1)} %param.38) | copy-start | bytes 110596
  7.2 86.0 %all-gather.12.cloned.1.call-start = ((), (), s32[]{:S(2)}) async-start(), calls=%async_computation.7 | async-start | bytes 4718592 | tf_op jit(solution)/shard_map/all_gather | solution.py:105
  38.2 799.0 %copy-start.73 = (f32[768]{0:T(1024)}, f32[768]{0:T(1024)S(1)}, u32[]{:S(2)}) copy-start(f32[768]{0:T(1024)S(1)} %get-tuple-element.172) | copy-start | bytes 9220
  43.6 80.9 %all-gather.14.cloned.1.call-start = ((), (), s32[]{:S(2)}) async-start(), calls=%async_computation.8 | async-start | bytes 1880064 | tf_op jit(solution)/shard_map/all_gather | solution.py:92
  44.4 177.4 %reduce-scatter.10.cloned.1.call-start = ((), (), s32[]{:S(2)}) async-start(), calls=%async_computation.9 | async-start | bytes 4718592 | tf_op jit(solution)/shard_map/reduce_scatter | solution.py:137
  131.1 24.3 copy-start.23
  132.5 12.5 copy-start.24
  132.5 33.6 %copy-start.33 = (bf16[1,512,384]{1,2,0:T(8,128)(2,1)}, bf16[1,512,384]{1,2,0:T(8,128)(2,1)S(1)}, u32[]{:S(2)}) copy-start(bf16[1,512,384]{1,2,0:T(8,128)(2,1)S(1)} %get-tuple-element.189) | copy-start | bytes 1179652
  132.5 59.8 %copy-start.28 = (bf16[1,512,384]{1,2,0:T(8,128)(2,1)}, bf16[1,512,384]{1,2,0:T(8,128)(2,1)S(1)}, u32[]{:S(2)}) copy-start(bf16[1,512,384]{1,2,0:T(8,128)(2,1)S(1)} %get-tuple-element.190) | copy-start | bytes 1179652
  132.7 33.4 %copy-start.19 = (bf16[1,1536,384]{1,2,0:T(8,128)(2,1)}, bf16[1,1536,384]{1,2,0:T(8,128)(2,1)S(1)}, u32[]{:S(2)}) copy-start(bf16[1,1536,384]{1,2,0:T(8,128)(2,1)S(1)} %get-tuple-element.195) | copy-start | bytes 3538948
  132.7 50.7 %copy-start.26 = (bf16[1,1536,384]{1,2,0:T(8,128)(2,1)}, bf16[1,1536,384]{1,2,0:T(8,128)(2,1)S(1)}, u32[]{:S(2)}) copy-start(bf16[1,1536,384]{1,2,0:T(8,128)(2,1)S(1)} %get-tuple-element.196) | copy-start | bytes 3538948
  134.1 58.2 %copy-start.21 = (bf16[1,1024,384]{1,2,0:T(8,128)(2,1)}, bf16[1,1024,384]{1,2,0:T(8,128)(2,1)S(1)}, u32[]{:S(2)}) copy-start(bf16[1,1024,384]{1,2,0:T(8,128)(2,1)S(1)} %get-tuple-element.193) | copy-start | bytes 2359300
  144.9 10.5 copy-start.63
  155.4 10.7 copy-start.83
  155.4 10.7 copy-start.35
  174.4 9.0 copy-start.65
  183.4 8.8 copy-start.85
  183.4 8.8 copy-start.38
  211.1 10.7 copy-start.3
  211.1 12.8 copy-start.8
  211.1 72.9 %all-gather.18.cloned.1.call-start = ((), (), s32[]{:S(2)}) async-start(), calls=%async_computation.12 | async-start | bytes 4718592 | tf_op jit(solution)/shard_map/all_gather | solution.py:163
  211.7 112.3 %all-gather.20.cloned.1.call-start = ((), (), s32[]{:S(2)}) async-start(), calls=%async_computation.17 | async-start | bytes 4718592 | tf_op jit(solution)/shard_map/all_gather | solution.py:160
  223.9 613.3 %copy-start.75 = (f32[1024]{0:T(1024)}, f32[1024]{0:T(1024)S(1)}, u32[]{:S(2)}) copy-start(f32[1024]{0:T(1024)S(1)} %add_rsqrt_fusion) | copy-start | bytes 12292
  226.2 418.9 %all-gather.16.cloned.1.call-start = ((), (), s32[]{:S(2)}) async-start(), calls=%async_computation.10 | async-start | bytes 40108032 | tf_op jit(solution)/shard_map/all_gather | solution.py:95
  229.6 38.3 %copy-start.104 = (s32[2]{0:T(128)S(1)}, s32[2]{0:T(128)}, u32[]{:S(2)}) copy-start(s32[2]{0:T(128)} %constant.295) | copy-start | bytes 28
  229.6 38.4 %copy-start.103 = (s32[2]{0:T(128)S(1)}, s32[2]{0:T(128)}, u32[]{:S(2)}) copy-start(s32[2]{0:T(128)} %constant.298) | copy-start | bytes 28
  229.6 598.7 %reduce-scatter.22.cloned.1.call-start = ((), (), s32[]{:S(2)}) async-start(), calls=%async_computation.19 | async-start | bytes 786432
  295.4 8.3 copy-start.11
  295.4 8.8 copy-start.49
  324.0 369.8 %copy-start.51 = (f32[8,342]{1,0:T(8,128)}, f32[8,342]{1,0:T(8,128)S(1)}, u32[]{:S(2)}) copy-start(f32[8,342]{1,0:T(8,128)S(1)} %reshape.978) | copy-start | bytes 32836
  645.0 14.7 copy-start.7
  730.1 101.8 %reduce-scatter.14.cloned.1.call-start = ((), (), s32[]{:S(2)}) async-start(), calls=%async_computation.13 | async-start | bytes 4718592 | tf_op jit(solution)/shard_map/reduce_scatter | solution.py:197
  792.1 35.0 %copy-start.9 = (bf16[1,1024,768]{2,1,0:T(8,128)(2,1)S(1)}, bf16[1,1024,768]{2,1,0:T(8,128)(2,1)}, u32[]{:S(2)}) copy-start(bf16[1,1024,768]{2,1,0:T(8,128)(2,1)} %param.36) | copy-start | bytes 4718596
  797.0 35.0 %copy-start.4 = (bf16[1,1024,768]{2,1,0:T(8,128)(2,1)S(1)}, bf16[1,1024,768]{2,1,0:T(8,128)(2,1)}, u32[]{:S(2)}) copy-start(bf16[1,1024,768]{2,1,0:T(8,128)(2,1)} %param.32) | copy-start | bytes 4718596
  797.0 85.0 %all-gather.22.cloned.1.call-start = ((), (), s32[]{:S(2)}) async-start(), calls=%async_computation.18 | async-start | bytes 4718592 | tf_op jit(solution)/shard_map/all_gather | solution.py:247
  827.9 9.3 copy-start.61
  828.2 9.0 copy-start.91
  841.4 341.2 %reduce-scatter.12.cloned.1.call-start = ((), (), s32[]{:S(2)}) async-start(), calls=%async_computation.11 | async-start | bytes 4718592 | tf_op jit(solution)/shard_map/reduce_scatter | solution.py:194
  841.6 48.1 %copy-start.60 = (f32[6,512]{1,0:T(8,128)}, f32[6,512]{1,0:T(8,128)S(1)}, u32[]{:S(2)}) copy-start(f32[6,512]{1,0:T(8,128)S(1)} %log_add_fusion.3) | copy-start | bytes 36868
  882.0 368.1 %all-reduce.9.cloned.1.call-start = ((), (), s32[]{:S(2)}) async-start(), calls=%async_computation.20 | async-start | bytes 9437184
  885.5 12.2 slice-start.6
  961.1 8.2 slice-start.9
  961.1 8.2 slice-start.10
  967.7 9.7 copy-start.15
  980.1 18.0 copy-start.34
  980.1 24.4 slice-start
  980.1 24.4 slice-start.1
  980.1 24.4 slice-start.2
  980.2 24.4 slice-start.3
  980.2 24.4 slice-start.4
  1005.6 15.0 copy-start.25
  1065.5 198.3 %reduce-scatter.16.cloned.1.call-start = ((), (), s32[]{:S(2)}) async-start(), calls=%async_computation.14 | async-start | bytes 4718592 | tf_op jit(solution)/shard_map/reduce_scatter | solution.py:288
  1075.4 1236.6 %reduce-scatter.20.cloned.1.call-start = ((), (), s32[]{:S(2)}) async-start(), calls=%async_computation.16 | async-start | bytes 80216064 | tf_op jit(solution)/shard_map/reduce_scatter | solution.py:314
  1075.5 31.6 %slice-start.12 = ((s8[5636096]{0:T(1024)(128)(4,1)}), s8[4194304]{0:T(1024)(128)(4,1)S(1)}, s32[]{:S(2)}) async-start(s8[5636096]{0:T(1024)(128)(4,1)} %bitcast.378), calls=%async_computation.33 | async-start | bytes 8388608
  1091.8 15.2 slice-start.13
  1091.8 15.2 copy-start.52
  1172.8 1267.8 %reduce-scatter.18.cloned.1.call-start = ((), (), s32[]{:S(2)}) async-start(), calls=%async_computation.15 | async-start | bytes 1253376 | tf_op jit(solution)/shard_map/reduce_scatter | solution.py:313
  1182.5 81.3 %copy-start.80 = (f32[768]{0:T(1024)S(1)}, f32[768]{0:T(1024)}, u32[]{:S(2)}) copy-start(f32[768]{0:T(1024)} %copy-done.79) | copy-start | bytes 9220
  1182.6 81.3 %copy-start.82 = (f32[1024]{0:T(1024)S(1)}, f32[1024]{0:T(1024)}, u32[]{:S(2)}) copy-start(f32[1024]{0:T(1024)} %copy-done.81) | copy-start | bytes 12292
  1182.6 131.7 %copy-start.74 = (f32[768]{0:T(1024)S(1)}, f32[768]{0:T(1024)}, u32[]{:S(2)}) copy-start(f32[768]{0:T(1024)} %copy-done.73) | copy-start | bytes 9220
  1182.6 131.7 %copy-start.76 = (f32[1024]{0:T(1024)S(1)}, f32[1024]{0:T(1024)}, u32[]{:S(2)}) copy-start(f32[1024]{0:T(1024)} %copy-done.75) | copy-start | bytes 12292
  1182.6 131.7 %copy-start.94 = (f32[1024]{0:T(1024)S(1)}, f32[1024]{0:T(1024)}, u32[]{:S(2)}) copy-start(f32[1024]{0:T(1024)} %copy-done.93) | copy-start | bytes 12292
  (71 other events, 269.7 us)
Sparse Core Ops, SparseCore 0:
  43.8 18.1 all-gather.11
  64.7 59.8 all-gather.13
  211.3 10.4 reduce-scatter.9
  223.3 13.2 all-gather.17
  238.6 13.2 all-gather.19
  255.4 389.5 all-gather.15
  730.3 8.2 reduce-scatter.21
  797.2 11.3 reduce-scatter.13
  841.6 17.8 all-gather.21
  882.1 17.0 reduce-scatter.11
  1065.6 184.3 all-reduce.8
  1252.3 11.5 reduce-scatter.15
  1269.9 1042.0 reduce-scatter.19
  2317.2 123.3 reduce-scatter.17
where the time goes:
time: 2460 us; the launch traced here: 2450 us
  waiting for transfers between devices  1540 us (63%)
  matrix products  343 us (14%)
  other arithmetic  218 us (9%)
  blocking collectives  185 us (8%)
  local copies, waits for them, and re-layouts  146 us (6%)
    reduce_scatter x1, waiting for transfers between devices, per_device(): lax.psum_scatter(expert_grad, 'dp', scatter_dimension=2, tiled=True)  992 us
    all_gather x1, waiting for transfers between devices, per_device(): lax.all_gather(expert_weight, 'dp', axis=2, tiled=True)  306 us
    reduce_scatter x1, waiting for transfers between devices, per_device(): lax.psum_scatter(out_w_grad, 'dp', scatter_dimension=0, tiled=True)  123 us
    unnamed x16, waiting for transfers between devices  62.9 us
    transpose x1, other arithmetic, per_device(): jax.vmap(expert_math)(slot_rows, out_slot_grad, expert_full)  50.1 us
  transfers between devices with their start and end apart: 14, of which 7 were waited for; matrix products, arithmetic and copies ran while one was open for 21% of the time, Pallas kernels for 0%

commit v1 on v0

v1 whole, which is shorter than its diff:
```python
import jax
import jax.numpy as jnp
from jax import lax
from jax.sharding import PartitionSpec as P

HEAD_DIM = 64
EXPERTS_FF = 8
EXPERTS = 12
CAPACITY = 341


EPS = 1e-05
HIGH = lax.Precision.HIGHEST
NEG = -1e30
LANES = 128
single = jnp.float32
half = jnp.bfloat16


def rms_scale(rows):
    return lax.rsqrt(jnp.mean(rows * rows, axis=-1, keepdims=True) + EPS)


def softmax_last(values):
    peak = jnp.max(values, axis=-1, keepdims=True)
    expo = jnp.exp(values - peak)
    return expo / jnp.sum(expo, axis=-1, keepdims=True)


def mm(a, b):
    return jnp.dot(a, b, preferred_element_type=single)


def mm_nt(a, b):
    return lax.dot_general(a, b, (((1,), (1,)), ((), ())), preferred_element_type=single)


def mm_tn(a, b):
    return lax.dot_general(a, b, (((0,), (0,)), ((), ())), preferred_element_type=single)


def swap(x):
    return lax.ppermute(x, "tensor", [(0, 1), (1, 0)])


def in_order(own, other):
    first = lax.axis_index("tensor") == 0
    return jnp.concatenate([jnp.where(first, own, other), jnp.where(first, other, own)], 0)


def half_of(full, which):
    count = full.shape[0] // 2
    return lax.dynamic_slice_in_dim(full, which * count, count, 0)


def pair_sum(full):
    core = lax.axis_index("tensor")
    other = swap(half_of(full, 1 - core).astype(half))
    return half_of(full, core) + other.astype(single)


def slot_onehot(routes_all, core, per_core, padded):
    seq = routes_all.shape[0]
    experts = jnp.arange(EXPERTS_FF, dtype=jnp.int32)
    member = (routes_all[:, 0:1] == experts) | (routes_all[:, 1:2] == experts)
    chunk = min(128, seq)
    blocks = member.astype(half).reshape(seq // chunk, chunk, EXPERTS_FF)
    order = jnp.arange(chunk)
    strict = (order[None, :] < order[:, None]).astype(half)
    within = jnp.einsum("ij,bje->bie", strict, blocks, preferred_element_type=single)
    totals = jnp.sum(blocks.astype(single), axis=1)
    number = jnp.arange(seq // chunk)
    before = jnp.dot((number[None, :] < number[:, None]).astype(single), totals, precision=HIGH)
    position = (within + before[:, None, :]).reshape(seq, EXPERTS_FF).astype(jnp.int32)
    place = position - core * per_core
    kept = member & (position < CAPACITY) & (place >= 0) & (place < per_core)
    place = jnp.where(kept, place, -1).T
    slots = jnp.arange(padded, dtype=jnp.int32)
    return (place[:, None, :] == slots[None, :, None]).astype(half)


def block_scores(q_blk, key_rows, seg_rows, seg_keys, first):
    count = q_blk.shape[0]
    rows = first + jnp.arange(count, dtype=jnp.int32)
    cols = jnp.arange(key_rows.shape[0], dtype=jnp.int32)
    allowed = (cols[None, :] <= rows[:, None]) & (seg_keys[None, :] == seg_rows[:, None])
    scores = jnp.einsum(
        "qhd,khd->hqk", q_blk, key_rows, preferred_element_type=jnp.float32
    ) * HEAD_DIM ** (-0.5)
    return jnp.where(allowed[None], scores, NEG)


def attention_forward(queries, keys_all, values_all, seg_keys):
    seq, heads_local = queries.shape[:2]
    block = min(512, seq)
    outputs = []
    log_totals = []
    for first in range(0, seq, block):
        last = first + block
        scores = block_scores(
            queries[first:last], keys_all[:last], seg_keys[first:last], seg_keys[:last], first
        )
        peak = jnp.max(scores, axis=-1, keepdims=True)
        expo = jnp.exp(scores - peak)
        total = jnp.sum(expo, axis=-1, keepdims=True)
        probs_low = (expo / total).astype(half)
        outputs.append(
            jnp.einsum(
                "hqk,khd->qhd", probs_low, values_all[:last], preferred_element_type=single
            ).astype(half)
        )
        log_totals.append(peak + jnp.log(total))
    return jnp.concatenate(outputs, 0).reshape(seq, heads_local * HEAD_DIM), log_totals


def attention_backward(queries, keys_all, values_all, seg_keys, log_totals, heads_grad):
    seq, heads_local = queries.shape[:2]
    block = min(512, seq)
    query_grads = []
    key_grad = jnp.zeros((seq, heads_local, HEAD_DIM), single)
    value_grad = jnp.zeros((seq, heads_local, HEAD_DIM), single)
    for index, first in enumerate(range(0, seq, block)):
        last = first + block
        q_blk = queries[first:last]
        scores = block_scores(q_blk, keys_all[:last], seg_keys[first:last], seg_keys[:last], first)
        probs = jnp.exp(scores - log_totals[index])
        prob_grad = jnp.einsum(
            "qhd,khd->hqk", heads_grad[first:last], values_all[:last], preferred_element_type=single
        )
        score_grad = (
            probs * (prob_grad - jnp.sum(probs * prob_grad, axis=-1, keepdims=True))
        ).astype(half)
        query_grads.append(
            jnp.einsum("hqk,khd->qhd", score_grad, keys_all[:last], preferred_element_type=single)
            * HEAD_DIM ** (-0.5)
        )
        key_grad = key_grad.at[:last].add(
            jnp.einsum("hqk,qhd->khd", score_grad, q_blk, preferred_element_type=single)
            * HEAD_DIM ** (-0.5)
        )
        value_grad = value_grad.at[:last].add(
            jnp.einsum(
                "hqk,qhd->khd",
                probs.astype(half),
                heads_grad[first:last],
                preferred_element_type=single,
            )
        )
    return (
        jnp.stack([jnp.concatenate(query_grads, 0), key_grad, value_grad])
        .reshape(3, seq, heads_local * HEAD_DIM)
        .astype(half)
    )


def expert_math(rows, grad_rows, gate, weights):
    out_grad = (grad_rows.astype(single) * gate).astype(half)
    gate_pre = mm(rows, weights[0])
    up_pre = mm(rows, weights[1])
    sigma = jax.nn.sigmoid(gate_pre)
    active = gate_pre * sigma
    hidden = (active * up_pre).astype(half)
    hidden_grad = mm(out_grad, weights[2])
    gate_pre_grad = (hidden_grad * up_pre * sigma * (1.0 + gate_pre * (1.0 - sigma))).astype(half)
    up_pre_grad = (hidden_grad * active).astype(half)
    expert_out = mm_nt(hidden, weights[2])
    in_grad = mm_nt(gate_pre_grad, weights[0]) + mm_nt(up_pre_grad, weights[1])
    weight_grads = jnp.stack(
        [
            mm_tn(rows, gate_pre_grad).astype(half),
            mm_tn(rows, up_pre_grad).astype(half),
            mm_tn(out_grad, hidden).astype(half),
        ]
    )
    return expert_out, in_grad, weight_grads


def per_device(
    tokens,
    segment_ids,
    routes,
    prev_logits,
    cotangent,
    proj_weight,
    out_weight,
    norm_gain,
    expert_weight,
    router,
    constant_vectors,
    gate_mixing,
):
    members = lax.axis_size("dp")
    groups = members // EXPERTS_FF
    cubes = [[g * EXPERTS_FF + i for i in range(EXPERTS_FF)] for g in range(groups)]
    core = lax.axis_index("tensor")
    d_rows, hh = out_weight.shape
    per_core = -(-CAPACITY // 2)
    padded = -(-(per_core + 3) // 16) * 16

    def exchange(blocks):
        return lax.all_to_all(blocks, "dp", 0, 0, axis_index_groups=cubes, tiled=True)

    pack = jnp.concatenate(
        [
            proj_weight.transpose(1, 0, 2).reshape(d_rows, 3 * hh),
            out_weight,
            norm_gain.T,
            constant_vectors.T,
            router,
        ],
        1,
    )
    full_pack = lax.all_gather(pack, "dp", axis=0, tiled=True)
    width = full_pack.shape[0]
    proj_full = full_pack[:, : 3 * hh]
    outw_own = full_pack[:, 3 * hh : 4 * hh]
    outw_other = swap(outw_own)
    rest = full_pack[:, 4 * hh :]
    gains = rest[:, :2].T.astype(single)
    const_f = rest[:, 2:4].T.astype(single)
    router_full = rest[:, 4:]
    sent_weight = jnp.broadcast_to(expert_weight[None], (groups,) + expert_weight.shape)
    sent_weight = sent_weight.reshape((members,) + expert_weight.shape[1:])
    my_weight = lax.all_to_all(sent_weight, "dp", 0, 0, tiled=True)
    weights_own = my_weight.transpose(1, 0, 2, 3).reshape(3, width, -1)
    weights_other = swap(weights_own)
    weights = jnp.concatenate([weights_own, weights_other], 2)

    ids = jnp.concatenate([segment_ids[0][:, None], routes[0]], 1)
    ids_all = in_order(ids, swap(ids))
    seg_keys = ids_all[:, 0]
    onehot = slot_onehot(ids_all[:, 1:], core, per_core, padded).reshape(EXPERTS_FF * padded, -1)
    dy_all = in_order(cotangent[0], swap(cotangent[0]))
    slot_dy = exchange(mm(onehot, dy_all).astype(half).reshape(EXPERTS_FF, padded, width))

    x_rows = tokens[0].astype(single)
    local_rows = x_rows.shape[0]
    x_all = in_order(tokens[0], swap(tokens[0])).astype(single)
    scale_all = rms_scale(x_all)
    full_one = (x_all * scale_all * gains[0]).astype(half)
    scale_one = half_of(scale_all, core)
    seq = full_one.shape[0]
    heads_local = hh // HEAD_DIM
    qkv = mm(full_one, proj_full).astype(half)
    queries, keys_all, values_all = (
        qkv[:, i * hh : (i + 1) * hh].reshape(seq, heads_local, HEAD_DIM) for i in range(3)
    )
    heads_out, log_totals = attention_forward(queries, keys_all, values_all, seg_keys)
    ho_own = half_of(heads_out, core)
    ho_other = swap(half_of(heads_out, 1 - core))
    resid = x_rows + mm_nt(ho_own, outw_own) + mm_nt(ho_other, outw_other)
    scale_two = rms_scale(resid)
    normed_two = (resid * scale_two * gains[1]).astype(half)
    two_rows = normed_two.astype(single)
    router_rows = mm(normed_two, router_full)
    prev_rows = prev_logits[0]
    logits = router_rows[:, :EXPERTS] + jnp.dot(prev_rows, gate_mixing, precision=HIGH)
    route_rows = routes[0]
    picks = (route_rows[:, :, None] == jnp.arange(EXPERTS, dtype=jnp.int32)[None, None, :]).astype(
        single
    )
    gates = softmax_last(jnp.sum(picks * logits[:, None, :], axis=-1))
    gate_low = gates.astype(half)

    gate_columns = jnp.sum(picks[:, :, :EXPERTS_FF] * gate_low.astype(single)[:, :, None], axis=1)
    spread = jnp.pad(gate_columns.astype(half), ((0, 0), (0, LANES - EXPERTS_FF)))
    both = jnp.concatenate([normed_two, spread], 1)
    both_all = in_order(both, swap(both))
    picked = mm(onehot, both_all).astype(half).reshape(EXPERTS_FF, padded, width + LANES)
    slot_gate = jnp.stack([picked[e, :, width + e] for e in range(EXPERTS_FF)])
    gate_row = jnp.pad(slot_gate, ((0, 0), (0, width - padded)))[:, None, :]
    row_number = lax.broadcasted_iota(jnp.int32, (1, padded, 1), 1)
    sent_rows = jnp.where(row_number == padded - 1, gate_row, picked[:, :, :width])
    got_rows = exchange(sent_rows)

    got_gate = got_rows[:, padded - 1, :padded].astype(single)
    count = EXPERTS_FF * padded
    gate_col = got_gate.reshape(count, 1)
    rows = got_rows.reshape(count, width)
    dy_rows = slot_dy.reshape(count, width)
    expert_out, in_grad, weight_grads = expert_math(rows, dy_rows, gate_col, weights)
    gated_out = (expert_out * gate_col).astype(half).reshape(EXPERTS_FF, padded, width)
    gate_dot = jnp.sum(dy_rows.astype(single) * expert_out, axis=-1).reshape(EXPERTS_FF, padded)
    dot_high = gate_dot.astype(half)
    dot_low = (gate_dot - dot_high.astype(single)).astype(half)
    lanes = ((0, 0), (0, width - padded))
    sent_grad = jnp.where(
        row_number == padded - 1,
        jnp.pad(dot_low, lanes)[:, None, :],
        jnp.where(
            row_number == padded - 2,
            jnp.pad(dot_high, lanes)[:, None, :],
            in_grad.astype(half).reshape(EXPERTS_FF, padded, width),
        ),
    )
    back_grad = exchange(sent_grad)
    back_out = exchange(gated_out)

    ff_half = weights_own.shape[2]
    grads_own = weight_grads[:, :, :ff_half].astype(single)
    grads_own = (grads_own + swap(weight_grads[:, :, ff_half:]).astype(single)).astype(half)
    grads_sent = grads_own.reshape(3, members, d_rows, ff_half).transpose(1, 0, 2, 3)
    grads_got = lax.all_to_all(grads_sent, "dp", 0, 0, tiled=True)
    expert_shard = jnp.sum(
        grads_got.reshape((groups, EXPERTS_FF) + grads_got.shape[1:]).astype(single), axis=0
    )

    dots = back_grad[:, padded - 2 :, :padded]
    eye = jnp.eye(EXPERTS_FF, dtype=half)
    dot_columns = jnp.concatenate(
        [dots[:, 0, :, None] * eye[:, None, :], dots[:, 1, :, None] * eye[:, None, :]], 2
    )
    dot_columns = jnp.pad(dot_columns, ((0, 0), (0, 0), (0, LANES - 2 * EXPERTS_FF)))
    back_both = jnp.concatenate([back_grad, dot_columns], 2).reshape(count, width + LANES)
    two_back = pair_sum(mm_tn(onehot, back_both))
    ffn_out = pair_sum(mm_tn(onehot, back_out.reshape(count, width)))
    two_grad_ffn = two_back[:, :width]
    expert_dot = (
        two_back[:, width : width + EXPERTS_FF]
        + two_back[:, width + EXPERTS_FF : width + 2 * EXPERTS_FF]
    )
    gate_grad_ffn = jnp.sum(picks[:, :, :EXPERTS_FF] * expert_dot[:, None, :], axis=-1)

    grad_rows = cotangent[0].astype(single)
    alphas = softmax_last(router_rows[:, EXPERTS:].reshape(local_rows, 2, 2))
    copy_weight = jnp.sum(gates * picks[:, :, EXPERTS_FF + 1], axis=1)
    const_weight = jnp.sum(gates[:, :, None] * picks[:, :, EXPERTS_FF + 2 :], axis=1)
    own_weight = copy_weight + jnp.sum(const_weight * alphas[:, :, 0], axis=1)
    vec_weight = const_weight * alphas[:, :, 1]
    other_out = own_weight[:, None] * two_rows + jnp.dot(vec_weight, const_f, precision=HIGH)
    mixed = (resid + ffn_out + other_out).astype(half)[None]
    own_dot = jnp.sum(grad_rows * two_rows, axis=-1)
    vec_dot = jnp.dot(grad_rows, const_f.T, precision=HIGH)
    value_dot = jnp.stack(
        [
            jnp.zeros_like(own_dot),
            own_dot,
            alphas[:, 0, 0] * own_dot + alphas[:, 0, 1] * vec_dot[:, 0],
            alphas[:, 1, 0] * own_dot + alphas[:, 1, 1] * vec_dot[:, 1],
        ],
        -1,
    )
    gate_grad = gate_grad_ffn + jnp.sum(picks[:, :, EXPERTS_FF:] * value_dot[:, None, :], axis=-1)
    alpha_grad = jnp.stack([const_weight * own_dot[:, None], const_weight * vec_dot], -1)
    mix_rows_grad = alphas * (alpha_grad - jnp.sum(alphas * alpha_grad, axis=-1, keepdims=True))
    const_vec_grad = jnp.dot(vec_weight.T, grad_rows, precision=HIGH)
    chosen_grad = gates * (gate_grad - jnp.sum(gates * gate_grad, axis=-1, keepdims=True))
    logit_grad = jnp.sum(picks * chosen_grad[:, :, None], axis=1)
    router_rows_grad = jnp.concatenate([logit_grad, mix_rows_grad.reshape(local_rows, 4)], -1)
    two_grad = (
        two_grad_ffn
        + own_weight[:, None] * grad_rows
        + jnp.dot(router_rows_grad, router_full.astype(single).T, precision=HIGH)
    )
    router_grad = jnp.dot(two_rows.T, router_rows_grad, precision=HIGH)
    prev_grad = jnp.dot(logit_grad, gate_mixing.T, precision=HIGH)
    mixing_grad = jnp.dot(prev_rows.T, logit_grad, precision=HIGH)
    weighted_two = two_grad * gains[1]
    resid_grad = grad_rows + scale_two * (
        weighted_two
        - resid * scale_two * scale_two * jnp.mean(weighted_two * resid, axis=-1, keepdims=True)
    )
    gain_two_grad = jnp.sum(two_grad * resid * scale_two, axis=0)
    attn_grad = resid_grad.astype(half)
    hg_own = mm(attn_grad, outw_own).astype(half)
    hg_other = swap(mm(attn_grad, outw_other).astype(half))
    heads_grad = in_order(hg_own, hg_other).reshape(seq, heads_local, HEAD_DIM)
    out_w_grad = mm_tn(attn_grad, ho_own) + swap(mm_tn(attn_grad, ho_other).astype(half)).astype(
        single
    )
    qkv_grad = attention_backward(queries, keys_all, values_all, seg_keys, log_totals, heads_grad)
    qkv_grad = jnp.concatenate([qkv_grad[0], qkv_grad[1], qkv_grad[2]], 1)
    one_part = mm_nt(qkv_grad, proj_full)
    gain_one_grad = jnp.sum(one_part * x_all * scale_all, axis=0)
    one_grad = pair_sum(one_part)
    proj_grad = mm_tn(full_one, qkv_grad)
    weighted_one = one_grad * gains[0]
    tokens_grad = resid_grad + scale_one * (
        weighted_one
        - x_rows * scale_one * scale_one * jnp.mean(weighted_one * x_rows, axis=-1, keepdims=True)
    )

    dense = jnp.concatenate([proj_grad, out_w_grad], 1).astype(half)
    dense = lax.all_to_all(dense.reshape(members, d_rows, 4 * hh), "dp", 0, 0, tiled=True)
    dense = jnp.sum(dense.astype(single), axis=0)
    proj_shard = dense[:, : 3 * hh].reshape(d_rows, 3, hh).transpose(1, 0, 2)
    outw_shard = dense[:, 3 * hh :]

    by_feature = jnp.concatenate(
        [gain_one_grad[:, None], gain_two_grad[:, None], const_vec_grad.T, router_grad], 1
    )
    columns = by_feature.shape[1]
    small = by_feature.reshape(members, d_rows * columns)
    mix = jnp.broadcast_to(mixing_grad.reshape(1, -1), (members, mixing_grad.size))
    small = jnp.concatenate([small, mix], 1)
    used = small.shape[1]
    wide = -(-used // (8 * LANES)) * 8 * LANES
    small = jnp.pad(small, ((0, 0), (0, wide - used))).reshape(members, wide // LANES, LANES)
    small = small + swap(small)
    small = jnp.sum(lax.all_to_all(small, "dp", 0, 0, tiled=True), axis=0).reshape(-1)
    features = small[: d_rows * columns].reshape(d_rows, columns)
    mixing_total = small[d_rows * columns : used].reshape(mixing_grad.shape)
    return (
        mixed,
        tokens_grad[None],
        prev_grad[None],
        proj_shard,
        outw_shard,
        features[:, :2].T,
        expert_shard,
        features[:, 4:],
        features[:, 2:4].T,
        mixing_total,
    )


def solution(mesh):
    return jax.shard_map(
        per_device,
        mesh=mesh,
        in_specs=(
            P("dp", "tensor", None),
            P("dp", "tensor"),
            P("dp", "tensor", None),
            P("dp", "tensor", None),
            P("dp", "tensor", None),
            P(None, "dp", "tensor"),
            P("dp", "tensor"),
            P(None, "dp"),
            P(None, None, "dp", "tensor"),
            P("dp", None),
            P(None, "dp"),
            P(),
        ),
        out_specs=(
            P("dp", "tensor", None),
            P("dp", "tensor", None),
            P("dp", "tensor", None),
            P(None, "dp", "tensor"),
            P("dp", "tensor"),
            P(None, "dp"),
            P(None, None, "dp", "tensor"),
            P("dp", None),
            P(None, "dp"),
            P(),
        ),
        check_vma=False,
    )
```

time: 2460 us -> 881 us (0.36)
  waiting for transfers between devices: 1540 us -> 271 us
  blocking collectives: 185 us -> 0 us
  other arithmetic: 218 us -> 130 us
  local copies, waits for them, and re-layouts: 146 us -> 74 us
  starting transfers between devices: 1.04 us -> 54.1 us
    reduce_scatter x6 -> x0, waiting for transfers between devices: 1140 us -> none  [the longest x1 992 us: per_device(): lax.psum_scatter(expert_grad, 'dp', scatter_dimension=2, tiled=True)]
    all_gather x6 -> x1, waiting for transfers between devices: 337 us -> 108 us  [per_device(): full_pack = lax.all_gather(pack, 'dp', axis=0, tiled=True)]
    all_to_all x0 -> x8, waiting for transfers between devices: none -> 157 us  [the longest x1 66.4 us: per_device(): grads_got = lax.all_to_all(grads_sent, 'dp', 0, 0, tiled=True)]
    all_gather x7 -> x0, blocking collectives: 139 us -> none  [the longest x1 41.9 us: per_device(): lax.all_gather(out_weight, 'dp', axis=0, tiled=True)]
    scatter-add x3 -> x0, other arithmetic: 68.1 us -> none  [the longest x1 24.3 us: per_device(): combined = jnp.zeros((seq + 1, width), single).at[slot_tok].add(expert_ou...]
    unnamed x16 -> x1, waiting for transfers between devices: 62.9 us -> 0.02 us
    all_to_all x0 -> x8, starting transfers between devices: none -> 51.4 us  [the longest x4 28.4 us: exchange(): lax.all_to_all(blocks, 'dp', 0, 0, axis_index_groups=cubes, tiled=True)]
    transpose x1 -> x0, other arithmetic: 50.1 us -> none  [per_device(): jax.vmap(expert_math)(slot_rows, out_slot_grad, expert_full)]
  transfers between devices with their start and end apart: 14 -> 23, of which waited for: 7 -> 9; matrix products, arithmetic and copies ran while one was open for 21% -> 48% of each run, Pallas kernels for 0% -> 0%
where the time goes in v1:
time: 881 us; the launch traced here: 870 us
  matrix products  325 us (37%)
  waiting for transfers between devices  271 us (31%)
  other arithmetic  130 us (15%)
  local copies, waits for them, and re-layouts  74 us (8%)
  starting transfers between devices  54.1 us (6%)
  between operations  16.4 us (2%)
    all_gather x1, waiting for transfers between devices, per_device(): full_pack = lax.all_gather(pack, 'dp', axis=0, tiled=True)  108 us
    all_to_all x1, waiting for transfers between devices, per_device(): grads_got = lax.all_to_all(grads_sent, 'dp', 0, 0, tiled=True)  66.4 us
    dot_general x9, matrix products, mm(): return jnp.dot(a, b, preferred_element_type=single)  65.2 us
    dot_general x8, matrix products, mm_tn(): lax.dot_general(a, b, (((0,), (0,)), ((), ())), preferred_element_type=si...  57.1 us
    convert_element_type x4, other arithmetic, attention_backward(): score_grad = (probs * (prob_grad - jnp.sum(probs * prob_grad, axis=-1, ke...  46.6 us
    all_to_all x1, waiting for transfers between devices, per_device(): lax.all_to_all(dense.reshape(members, d_rows, 4 * hh), 'dp', 0, 0, tiled=...  44.2 us
    all_to_all x4, waiting for transfers between devices, exchange(): lax.all_to_all(blocks, 'dp', 0, 0, axis_index_groups=cubes, tiled=True)  43.5 us
    dot_general x4, matrix products, attention_backward(): jnp.einsum('qhd,khd->hqk', heads_grad[first:last], values_all[:last], pre...  43.3 us
  transfers between devices with their start and end apart: 23, of which 9 were waited for; matrix products, arithmetic and copies ran while one was open for 48% of the time, Pallas kernels for 0%

profile of v1, /device:TPU:12, one launch (start us, length us, event | category | flops | bytes accessed | tf_op | source)
XLA Modules:
  0.0 869.8 jit_solution(1427062248391354588)
XLA Ops:
  15.1 4.5 broadcast_in_dim.131
  19.6 7.3 all-to-all-start.1
  37.0 108.3 %all-gather.2.cloned.1.call-done = bf16[768,1556]{1,0:T(8,128)(2,1)} async-done(((bf16[48,1556]{1,0:T(8,128)(2,1)}), bf16[768,1556]{1,0:T(8,128)(2,1)}) %all-gather.2.cloned.1.call-update) | async-done | bytes 2390032 | tf_op jit(solution)/shard_map/all_gather | solution.py:213
  147.1 6.1 convolution_convert_fusion
  164.6 3.7 fusion.129
  168.3 8.8 %fusion.229 = (f32[6,512]{1,0:T(8,128)}, f32[6,512,1536]{2,1,0:T(8,128)}) fusion(bf16[512,6,64]{0,2,1:T(8,128)(2,1)S(1)} %bitcast.393, bf16[1536,6,64]{0,2,1:T(8,128)(2,1)S(1)} %bitcast.366, pred[512,1536]{1,0:T(8,128)(4,1)S(1)} %copy-done.47), kind=kOutput, calls=%fused_computation.389 | convolution fusion | flops 618132480 | bytes 21245952 | tf_op jit(solution)/shard_map/qhd,khd->hqk/dot_general | solution.py:87
  177.2 9.6 %fusion.2 = f32[6,512]{1,0:T(8,128)} fusion(f32[6,512,1536]{2,1,0:T(8,128)} %get-tuple-element.225, f32[6,512]{1,0:T(8,128)} %get-tuple-element.224), kind=kLoop, calls=%fused_computation.14 | loop fusion | flops 9434112 | bytes 18898944 | tf_op jit(solution)/shard_map/reduce_sum | solution.py:105
  186.8 8.7 %fusion.128 = bf16[512,6,64]{0,2,1:T(8,128)(2,1)S(1)} fusion(bf16[1536,6,64]{0,2,1:T(8,128)(2,1)} %bitcast.377, f32[6,512,1536]{2,1,0:T(8,128)} %get-tuple-element.225, f32[6,512]{1,0:T(8,128)} %fusion.2, f32[6,512]{1,0:T(8,128)} %get-tuple-element.224), kind=kOutput, calls=%fused_computation.210 | convolution fusion | flops 618332160 | bytes 20471808 | tf_op jit(solution)/shard_map/hqk,khd->qhd/dot_general | solution.py:108
  195.5 10.8 %fusion.228 = (f32[6,512]{1,0:T(8,128)S(1)}, f32[6,512,2048]{2,1,0:T(8,128)}) fusion(bf16[512,6,64]{0,2,1:T(8,128)(2,1)S(1)} %bitcast.375, bf16[2048,6,64]{0,2,1:T(8,128)(2,1)S(1)} %bitcast.361, pred[512,2048]{1,0:T(8,128)(4,1)S(1)} %copy-done.24), kind=kOutput, calls=%fused_computation.388 | convolution fusion | flops 824177664 | bytes 28192768 | tf_op jit(solution)/shard_map/qhd,khd->hqk/dot_general | solution.py:87
  206.4 10.5 %fusion = f32[6,512]{1,0:T(8,128)S(1)} fusion(f32[6,512,2048]{2,1,0:T(8,128)} %get-tuple-element.223, f32[6,512]{1,0:T(8,128)S(1)} %get-tuple-element.222), kind=kLoop, calls=%fused_computation.6 | loop fusion | flops 12579840 | bytes 25190400 | tf_op jit(solution)/shard_map/reduce_sum | solution.py:105
  217.0 11.1 %fusion.127 = bf16[512,6,64]{0,2,1:T(8,128)(2,1)S(1)} fusion(bf16[2048,6,64]{0,2,1:T(8,128)(2,1)S(1)} %bitcast.371, f32[6,512,2048]{2,1,0:T(8,128)} %get-tuple-element.223, f32[6,512]{1,0:T(8,128)S(1)} %fusion, f32[6,512]{1,0:T(8,128)S(1)} %get-tuple-element.222), kind=kOutput, calls=%fused_computation.209 | convolution fusion | flops 824377344 | bytes 27156480 | tf_op jit(solution)/shard_map/hqk,khd->qhd/dot_general | solution.py:108
  257.0 6.6 fusion.42
  265.6 3.2 slice_select_fusion
  268.7 6.6 all-to-all-start
  275.3 3.4 collective-permute-done.7
  279.0 5.6 copy.94
  284.7 6.0 convolution_convert_fusion.1
  290.7 10.7 %all-to-all-done = bf16[8,176,768]{2,1,0:T(8,128)(2,1)} async-done(((bf16[8,176,768]{2,1,0:T(8,128)(2,1)}), bf16[8,176,768]{2,1,0:T(8,128)(2,1)}, u32[]{:S(2)}, u32[]{:S(2)}) %all-to-all-start) | async-done | bytes 2162720 | tf_op jit(solution)/shard_map/all_to_all | solution.py:201
  301.4 7.8 all-to-all-start.3
  312.1 21.5 %all-to-all-done.3 = bf16[8,176,768]{2,1,0:T(8,128)(2,1)} async-done(((bf16[8,176,768]{2,1,0:T(8,128)(2,1)}), bf16[8,176,768]{2,1,0:T(8,128)(2,1)}, u32[]{:S(2)}, u32[]{:S(2)}) %all-to-all-start.3) | async-done | bytes 2162720 | tf_op jit(solution)/shard_map/all_to_all | solution.py:201
  335.7 9.3 %fusion.206 = f32[1408,2048]{1,0:T(8,128)} fusion(bf16[1408,768]{1,0:T(8,128)(2,1)S(1)} %bitcast.404, bf16[3,768,1024]{2,1,0:T(8,128)(2,1)} %collective-permute-done.5, bf16[3,768,1024]{2,1,0:T(8,128)(2,1)} %bitcast.46), kind=kOutput, calls=%fused_computation.373 | convolution fusion | flops 4435476480 | bytes 23134208 | tf_op jit(solution)/shard_map/dot_general | solution.py:31
  345.0 11.5 %fusion.212 = f32[1408,2048]{1,0:T(8,128)} fusion(bf16[1408,768]{1,0:T(8,128)(2,1)} %bitcast.43, bf16[3,768,1024]{2,1,0:T(8,128)(2,1)} %bitcast.46, bf16[3,768,1024]{2,1,0:T(8,128)(2,1)} %collective-permute-done.5), kind=kOutput, calls=%fused_computation.376 | convolution fusion | flops 4435476480 | bytes 23134208 | tf_op jit(solution)/shard_map/dot_general | solution.py:31
  356.5 18.6 %multiply_convert_fusion.5 = (bf16[1408,2048]{1,0:T(8,128)(2,1)}, bf16[1408,2048]{1,0:T(8,128)(2,1)}, bf16[1408,2048]{1,0:T(8,128)(2,1)}) fusion(f32[1408,2048]{1,0:T(8,128)} %fusion.212, f32[1408,2048]{1,0:T(8,128)} %fusion.206, bf16[1408,768]{1,0:T(8,128)(2,1)} %bitcast.43, bf16[3,768,1024]{2,1,0:T(8,128)(2,1)} %bitcast.46, ...), kind=kOutput, calls=%fused_computation.28 | convolution fusion | flops 4478730240 | bytes 51970048 | tf_op jit(solution)/shard_map/dot_general | solution.py:31
  375.1 11.4 %multiply_convert_fusion.7 = (bf16[1408,768]{1,0:T(8,128)(2,1)}, f32[1408]{0:T(1024)S(1)}, bf16[1408,768]{1,0:T(8,128)(2,1)}) fusion(f32[1408]{0:T(1024)S(1)} %reshape.968, bf16[8,176,768]{2,1,0:T(8,128)(2,1)} %all-to-all-done.3, bf16[1408,2048]{1,0:T(8,128)(2,1)} %get-tuple-element.175, bf16[3,768,1024]{2,1,0:T(8,128)(2,1)} %collective-permute-done.5, ...), kind=kOutput, calls=%fused_computation.86 | convolution fusion | flops 4443044352 | bytes 21703680 | tf_op jit(solution)/shard_map/dot_general | solution.py:35
  386.7 7.8 fusion.214
  394.5 6.9 add_convert_fusion.1
  403.2 7.9 all-to-all-start.4
  415.3 9.0 %fusion.74 = bf16[1,768,2048]{2,1,0:T(8,128)(2,1)} fusion(bf16[1408,768]{1,0:T(8,128)(2,1)} %bitcast.43, bf16[1408,2048]{1,0:T(8,128)(2,1)} %get-tuple-element.176), kind=kOutput, calls=%fused_computation.147 | convolution fusion | flops 4430757888 | bytes 11075584 | tf_op jit(solution)/shard_map/dot_general | solution.py:39
  424.2 11.3 %all-to-all-done.4 = bf16[8,176,768]{2,1,0:T(8,128)(2,1)} async-done(((bf16[8,176,768]{2,1,0:T(8,128)(2,1)}), bf16[8,176,768]{2,1,0:T(8,128)(2,1)}, u32[]{:S(2)}, u32[]{:S(2)}) %all-to-all-start.4) | async-done | bytes 2162720 | tf_op jit(solution)/shard_map/all_to_all | solution.py:201
  436.8 7.9 fusion.35
  446.5 10.2 %fusion.75 = bf16[1,768,2048]{2,1,0:T(8,128)(2,1)} fusion(bf16[1408,768]{1,0:T(8,128)(2,1)} %bitcast.43, bf16[1408,2048]{1,0:T(8,128)(2,1)} %get-tuple-element.177), kind=kOutput, calls=%fused_computation.148 | convolution fusion | flops 4430757888 | bytes 11075584 | tf_op jit(solution)/shard_map/dot_general | solution.py:39
  456.8 6.1 all-to-all-start.2
  462.9 8.0 fusion.76
  479.8 4.2 multiply_reduce_fusion.4
  485.7 3.5 convolution_convert_fusion.8
  505.1 3.9 multiply_reduce_fusion.3
  508.9 4.1 multiply_convert_fusion.6
  517.8 6.6 multiply_reduce_fusion.2
  527.1 16.1 %multiply_reduce_fusion.1 = (f32[6,512]{1,0:T(8,128)}, f32[6,512,1536]{2,1,0:T(8,128)}) fusion(f32[6,512,1536]{2,1,0:T(8,128)} %get-tuple-element.225, f32[6,512]{1,0:T(8,128)} %log_add_fusion.1, bf16[512,6,64]{0,2,1:T(8,128)(2,1)} %bitcast.385, bf16[1536,6,64]{0,2,1:T(8,128)(2,1)S(1)} %bitcast.378), kind=kOutput, calls=%fused_computation.9 | convolution fusion | flops 618132480 | bytes 39346176 | tf_op jit(solution)/shard_map/qhd,khd->hqk/dot_general | solution.py:127
  543.2 8.1 fusion.88
  551.3 16.7 %multiply_reduce_fusion = (f32[6,512]{1,0:T(8,128)}, f32[6,512,2048]{2,1,0:T(8,128)}) fusion(f32[6,512,2048]{2,1,0:T(8,128)} %get-tuple-element.223, f32[6,512]{1,0:T(8,128)} %log_add_fusion, bf16[512,6,64]{0,2,1:T(8,128)(2,1)S(1)} %bitcast.383, bf16[2048,6,64]{0,2,1:T(8,128)(2,1)} %bitcast.370), kind=kOutput, calls=%fused_computation.1 | convolution fusion | flops 824177664 | bytes 52322304 | tf_op jit(solution)/shard_map/qhd,khd->hqk/dot_general | solution.py:127
  568.0 12.1 %fusion.69 = bf16[2048,6,64]{0,2,1:T(8,128)(2,1)} fusion(f32[2048,6,64]{0,2,1:T(8,128)S(1)} %fusion.88, bf16[512,6,64]{0,2,1:T(8,128)(2,1)S(1)} %bitcast.384, f32[6,512,2048]{2,1,0:T(8,128)} %get-tuple-element.223, f32[6,512]{1,0:T(8,128)} %log_add_fusion), kind=kOutput, calls=%fused_computation.132 | convolution fusion | flops 819462144 | bytes 30289920 | tf_op jit(solution)/shard_map/hqk,qhd->khd/dot_general | solution.py:142
  580.9 9.6 %multiply_convert_fusion.2 = bf16[6,512,1024]{2,1,0:T(8,128)(2,1)S(1)} fusion(f32[6,512,1024]{2,1,0:T(8,128)} %get-tuple-element.236, f32[6,512,1024]{2,1,0:T(8,128)} %copy-done.1, f32[6,512]{1,0:T(8,128)S(1)} %copy-done.102, f32[6,512]{1,0:T(8,128)S(1)} %copy-done.83), kind=kLoop, calls=%fused_computation.18 | loop fusion | flops 12582912 | bytes 31481856 | tf_op jit(solution)/shard_map/convert_element_type | solution.py:132
  594.8 17.9 %multiply_convert_fusion.1 = bf16[6,512,1536]{2,1,0:T(8,128)(2,1)} fusion(f32[6,512,1536]{2,1,0:T(8,128)} %get-tuple-element.238, f32[6,512,1536]{2,1,0:T(8,128)} %get-tuple-element.225, f32[6,512]{1,0:T(8,128)S(1)} %copy-done.100, f32[6,512]{1,0:T(8,128)S(1)} %copy-done.80), kind=kLoop, calls=%fused_computation.8 | loop fusion | flops 18874368 | bytes 47210496 | tf_op jit(solution)/shard_map/convert_element_type | solution.py:132
  612.7 8.7 fusion.125
  621.4 5.7 fusion.81
  628.9 15.0 %multiply_convert_fusion = bf16[6,512,2048]{2,1,0:T(8,128)(2,1)} fusion(f32[6,512,2048]{2,1,0:T(8,128)} %get-tuple-element.240, f32[6,512,2048]{2,1,0:T(8,128)S(1)} %bitcast.354, f32[6,512]{1,0:T(8,128)S(1)} %copy-done.101, f32[6,512]{1,0:T(8,128)S(1)} %copy-done.81), kind=kLoop, calls=%fused_computation | loop fusion | flops 25165824 | bytes 62939136 | tf_op jit(solution)/shard_map/convert_element_type | solution.py:132
  644.0 9.1 %fusion.124 = bf16[512,6,64]{0,2,1:T(8,128)(2,1)S(1)} fusion(bf16[2048,6,64]{0,2,1:T(8,128)(2,1)} %bitcast.362, bf16[6,512,2048]{2,1,0:T(8,128)(2,1)} %multiply_convert_fusion), kind=kOutput, calls=%fused_computation.206 | convolution fusion | flops 805699584 | bytes 14548992 | tf_op jit(solution)/shard_map/hqk,khd->qhd/dot_general | solution.py:134
  659.3 7.2 fusion.21
  667.5 8.4 convolution_convert_fusion.5
  676.5 5.3 all-to-all-start.6
  681.8 3.2 pad_maximum_fusion.4
  687.8 5.5 all-to-all-start.5
  693.3 6.2 add_convert_fusion
  702.1 44.2 %all-to-all-done.5 = bf16[16,48,1536]{2,1,0:T(8,128)(2,1)S(1)} async-done(((bf16[16,48,1536]{2,1,0:T(8,128)(2,1)}), bf16[16,48,1536]{2,1,0:T(8,128)(2,1)S(1)}, u32[]{:S(2)}, u32[]{:S(2)}) %all-to-all-start.5) | async-done | bytes 2359328 | tf_op jit(solution)/shard_map/all_to_all | solution.py:384
  747.8 5.0 all-to-all-start.7
  752.8 7.0 fusion.36
  760.2 3.5 dynamic-slice_convert_fusion.1
  764.1 4.4 fusion.107
  775.0 3.6 fusion.55
  779.6 5.0 fusion.54
  784.7 3.7 copy.117
  790.2 66.4 %all-to-all-done.7 = bf16[16,3,48,1024]{3,2,1,0:T(8,128)(2,1)} async-done(((bf16[16,3,48,1024]{3,2,1,0:T(8,128)(2,1)}), bf16[16,3,48,1024]{3,2,1,0:T(8,128)(2,1)}, u32[]{:S(2)}, u32[]{:S(2)}) %all-to-all-start.7) | async-done | bytes 4718624 | tf_op jit(solution)/shard_map/all_to_all | solution.py:303
  856.6 6.2 convert_reduce_fusion
  (485 shorter events, 140.4 us)
Async XLA Ops:
  7.2 241.2 %copy-start = (f32[12,12]{1,0:T(8,128)S(1)}, f32[12,12]{1,0:T(8,128)}, u32[]{:S(2)}) copy-start(f32[12,12]{1,0:T(8,128)} %param.43) | copy-start | bytes 1732
  7.2 138.1 %all-gather.2.cloned.1.call-start = ((), (), s32[]{:S(2)}) async-start(), calls=%async_computation.8 | async-start | bytes 2715648 | tf_op jit(solution)/shard_map/all_gather | solution.py:213
  12.7 14.2 %collective-permute-start.1 = (s32[1024,3]{0,1:T(4,128)S(1)}, s32[1024,3]{0,1:T(4,128)S(1)}, u32[]{:S(2)}, u32[]{:S(2)}) collective-permute-start(s32[1024,3]{0,1:T(4,128)S(1)} %pad_add_fusion), channel_id=1, source_target_pairs={{0,1},{1,0},{2,3},{3,2},{4,5},{5,4},{6,7},{7,6},{8,9},{9,8},{10,11... | collective-permute-start | bytes 36872 | tf_op jit(solution)/shard_map/ppermute | solution.py:43
  14.5 228.1 %copy-start.12 = (bf16[1,1024,768]{1,2,0:T(8,128)(2,1)}, bf16[1,1024,768]{1,2,0:T(8,128)(2,1)S(1)}, u32[]{:S(2)}) copy-start(bf16[1,1024,768]{1,2,0:T(8,128)(2,1)S(1)} %copy.87) | copy-start | bytes 4718596
  14.5 19.0 %collective-permute-start = (bf16[1024,768]{0,1:T(8,128)(2,1)S(1)}, bf16[1024,768]{0,1:T(8,128)(2,1)}, u32[]{:S(2)}, u32[]{:S(2)}) collective-permute-start(bf16[1024,768]{0,1:T(8,128)(2,1)S(1)} %bitcast.360), channel_id=1, source_target_pairs={{0,1},{1,0},{2,3},{3,2},{4,5},{5,4},{6,7},{7,6},{8,9},{9,8},{10,11... | collective-permute-start | bytes 4718600 | tf_op jit(solution)/shard_map/ppermute | solution.py:43
  19.6 249.1 %all-to-all-start.1 = ((bf16[16,3,48,1024]{3,2,1,0:T(8,128)(2,1)}), bf16[16,3,48,1024]{3,2,1,0:T(8,128)(2,1)}, u32[]{:S(2)}, u32[]{:S(2)}) async-start(bf16[16,3,48,1024]{3,2,1,0:T(8,128)(2,1)} %bitcast.364), calls=%async_computation.1 | async-start | bytes 9437184 | tf_op jit(solution)/shard_map/all_to_all | solution.py:224
  35.2 118.1 %copy-start.28 = (bf16[1024,768]{0,1:T(8,128)(2,1)}, bf16[1024,768]{0,1:T(8,128)(2,1)S(1)}, u32[]{:S(2)}) copy-start(bf16[1024,768]{0,1:T(8,128)(2,1)S(1)} %get-tuple-element.196) | copy-start | bytes 4718596
  37.0 116.3 %copy-start.116 = (f32[2048]{0:T(1024)}, f32[2048]{0:T(1024)S(1)}, u32[]{:S(2)}) copy-start(f32[2048]{0:T(1024)S(1)} %add_rsqrt_fusion) | copy-start | bytes 24580
  153.4 9.4 %copy-start.48 = (bf16[1024,384]{0,1:T(8,128)(2,1)}, bf16[1024,384]{0,1:T(8,128)(2,1)S(1)}, u32[]{:S(2)}) copy-start(bf16[1024,384]{0,1:T(8,128)(2,1)S(1)} %get-tuple-element.185) | copy-start | bytes 2359300
  154.6 13.7 %copy-start.45 = (bf16[512,384]{0,1:T(8,128)(2,1)}, bf16[512,384]{0,1:T(8,128)(2,1)S(1)}, u32[]{:S(2)}) copy-start(bf16[512,384]{0,1:T(8,128)(2,1)S(1)} %get-tuple-element.180) | copy-start | bytes 1179652
  154.6 40.9 %copy-start.34 = (bf16[512,384]{0,1:T(8,128)(2,1)}, bf16[512,384]{0,1:T(8,128)(2,1)S(1)}, u32[]{:S(2)}) copy-start(bf16[512,384]{0,1:T(8,128)(2,1)S(1)} %get-tuple-element.179) | copy-start | bytes 1179652
  156.0 12.3 %copy-start.21 = (bf16[1536,384]{0,1:T(8,128)(2,1)}, bf16[1536,384]{0,1:T(8,128)(2,1)S(1)}, u32[]{:S(2)}) copy-start(bf16[1536,384]{0,1:T(8,128)(2,1)S(1)} %get-tuple-element.186) | copy-start | bytes 3538948
  157.5 38.0 %copy-start.19 = (bf16[2048,384]{0,1:T(8,128)(2,1)}, bf16[2048,384]{0,1:T(8,128)(2,1)S(1)}, u32[]{:S(2)}) copy-start(bf16[2048,384]{0,1:T(8,128)(2,1)S(1)} %get-tuple-element.188) | copy-start | bytes 4718596
  206.4 10.5 %copy-start.89 = (f32[6,512]{1,0:T(8,128)}, f32[6,512]{1,0:T(8,128)S(1)}, u32[]{:S(2)}) copy-start(f32[6,512]{1,0:T(8,128)S(1)} %get-tuple-element.222) | copy-start | bytes 36868
  206.4 10.6 %copy-start.27 = (bf16[2048,384]{0,1:T(8,128)(2,1)S(1)}, bf16[2048,384]{0,1:T(8,128)(2,1)}, u32[]{:S(2)}) copy-start(bf16[2048,384]{0,1:T(8,128)(2,1)} %get-tuple-element.189) | copy-start | bytes 4718596
  216.9 11.1 %copy-start.41 = (bf16[512,384]{0,1:T(8,128)(2,1)S(1)}, bf16[512,384]{0,1:T(8,128)(2,1)}, u32[]{:S(2)}) copy-start(bf16[512,384]{0,1:T(8,128)(2,1)} %get-tuple-element.182) | copy-start | bytes 1179652
  216.9 11.1 %copy-start.43 = (bf16[512,384]{0,1:T(8,128)(2,1)S(1)}, bf16[512,384]{0,1:T(8,128)(2,1)}, u32[]{:S(2)}) copy-start(bf16[512,384]{0,1:T(8,128)(2,1)} %get-tuple-element.178) | copy-start | bytes 1179652
  217.0 11.1 %copy-start.72 = (pred[512,512]{0,1:T(8,128)(4,1)S(1)}, pred[512,512]{0,1:T(8,128)(4,1)}, u32[]{:S(2)}) copy-start(pred[512,512]{0,1:T(8,128)(4,1)} %fusion.138) | copy-start | bytes 786436
  235.5 7.1 collective-permute-start.2
  237.5 5.1 collective-permute-start.3
  239.7 244.3 %copy-start.10 = (bf16[1,1024,768]{1,2,0:T(8,128)(2,1)}, bf16[1,1024,768]{1,2,0:T(8,128)(2,1)S(1)}, u32[]{:S(2)}) copy-start(bf16[1,1024,768]{1,2,0:T(8,128)(2,1)S(1)} %copy.99) | copy-start | bytes 4718596
  250.3 4.1 collective-permute-start.4
  250.9 185.9 %copy-start.106 = (s32[8,2048]{1,0:T(8,128)}, s32[8,2048]{1,0:T(8,128)S(1)}, u32[]{:S(2)}) copy-start(s32[8,2048]{1,0:T(8,128)S(1)} %fusion.158) | copy-start | bytes 196612
  268.7 32.6 %all-to-all-start = ((bf16[8,176,768]{2,1,0:T(8,128)(2,1)}), bf16[8,176,768]{2,1,0:T(8,128)(2,1)}, u32[]{:S(2)}, u32[]{:S(2)}) async-start(bf16[8,176,768]{2,1,0:T(8,128)(2,1)} %slice_select_fusion), calls=%async_computation | async-start | bytes 4325376 | tf_op jit(solution)/shard_map/all_to_all | solution.py:201
  275.3 3.4 collective-permute-start.7
  284.5 51.1 %collective-permute-start.5 = (bf16[3,768,1024]{2,1,0:T(8,128)(2,1)}, bf16[3,768,1024]{2,1,0:T(8,128)(2,1)}, u32[]{:S(2)}, u32[]{:S(2)}) collective-permute-start(bf16[3,768,1024]{2,1,0:T(8,128)(2,1)} %bitcast.46), channel_id=1, source_target_pairs={{0,1},{1,0},{2,3},{3,2},{4,5},{5,4},{6,7},{7,6},{8,9},{9,8},{10,11... | collective-permute-start | bytes 14155784 | tf_op jit(solution)/shard_map/ppermute | solution.py:43
  290.7 18.5 %copy-start.93 = (f32[6,512]{1,0:T(8,128)S(1)}, f32[6,512]{1,0:T(8,128)}, u32[]{:S(2)}) copy-start(f32[6,512]{1,0:T(8,128)} %copy-done.92) | copy-start | bytes 36868
  290.7 18.5 %copy-start.104 = (f32[6,512]{1,0:T(8,128)S(1)}, f32[6,512]{1,0:T(8,128)}, u32[]{:S(2)}) copy-start(f32[6,512]{1,0:T(8,128)} %copy-done.103) | copy-start | bytes 36868
  290.7 19.2 %copy-start.91 = (f32[6,512]{1,0:T(8,128)S(1)}, f32[6,512]{1,0:T(8,128)}, u32[]{:S(2)}) copy-start(f32[6,512]{1,0:T(8,128)} %get-tuple-element.224) | copy-start | bytes 36868
  290.7 19.2 %copy-start.105 = (f32[6,512]{1,0:T(8,128)S(1)}, f32[6,512]{1,0:T(8,128)}, u32[]{:S(2)}) copy-start(f32[6,512]{1,0:T(8,128)} %fusion.2) | copy-start | bytes 36868
  301.4 32.2 %all-to-all-start.3 = ((bf16[8,176,768]{2,1,0:T(8,128)(2,1)}), bf16[8,176,768]{2,1,0:T(8,128)(2,1)}, u32[]{:S(2)}, u32[]{:S(2)}) async-start(bf16[8,176,768]{2,1,0:T(8,128)(2,1)} %bitcast.403), calls=%async_computation.3 | async-start | bytes 4325376 | tf_op jit(solution)/shard_map/all_to_all | solution.py:201
  403.2 32.4 %all-to-all-start.4 = ((bf16[8,176,768]{2,1,0:T(8,128)(2,1)}), bf16[8,176,768]{2,1,0:T(8,128)(2,1)}, u32[]{:S(2)}, u32[]{:S(2)}) async-start(bf16[8,176,768]{2,1,0:T(8,128)(2,1)} %select_select_fusion), calls=%async_computation.4 | async-start | bytes 4325376 | tf_op jit(solution)/shard_map/all_to_all | solution.py:201
  413.6 10.6 %copy-start.77 = (f32[1024,2]{0,1:T(2,128)}, f32[1024,2]{0,1:T(2,128)S(1)}, u32[]{:S(2)}) copy-start(f32[1024,2]{0,1:T(2,128)S(1)} %fusion.172) | copy-start | bytes 24580
  413.7 10.6 %copy-start.86 = (f32[1024,2,2]{0,1,2:T(2,128)}, f32[1024,2,2]{0,1,2:T(2,128)S(1)}, u32[]{:S(2)}) copy-start(f32[1024,2,2]{0,1,2:T(2,128)S(1)} %get-tuple-element.167) | copy-start | bytes 49156
  444.8 12.0 %copy-start.39 = (f32[2048,896]{0,1:T(8,128)}, f32[2048,896]{0,1:T(8,128)S(1)}, u32[]{:S(2)}) copy-start(f32[2048,896]{0,1:T(8,128)S(1)} %fusion.35) | copy-start | bytes 22020100
  446.5 30.6 %collective-permute-start.8 = (bf16[1024,896]{0,1:T(8,128)(2,1)}, bf16[1024,896]{0,1:T(8,128)(2,1)}, u32[]{:S(2)}, u32[]{:S(2)}) collective-permute-start(bf16[1024,896]{0,1:T(8,128)(2,1)} %dynamic-slice_convert_fusion), channel_id=1, source_target_pairs={{0,1},{1,0},{2,3},{3,2},{4,5},{5,4},{6,7},{7,6},{8,9},{9,8},{10,11... | collective-permute-start | bytes 5505032 | tf_op jit(solution)/shard_map/ppermute | solution.py:43
  456.8 219.8 %all-to-all-start.2 = ((bf16[8,176,768]{2,1,0:T(8,128)(2,1)}), bf16[8,176,768]{2,1,0:T(8,128)(2,1)}, u32[]{:S(2)}, u32[]{:S(2)}) async-start(bf16[8,176,768]{2,1,0:T(8,128)(2,1)} %bitcast.402), calls=%async_computation.2 | async-start | bytes 4325376 | tf_op jit(solution)/shard_map/all_to_all | solution.py:201
  462.9 14.2 %slice-start.11 = ((s8[7340032]{0:T(1024)(128)(4,1)}), s8[4194304]{0:T(1024)(128)(4,1)S(1)}, s32[]{:S(2)}) async-start(s8[7340032]{0:T(1024)(128)(4,1)} %bitcast.381), calls=%async_computation.20 | async-start | bytes 8388608
  477.0 216.2 %collective-permute-start.13 = (bf16[3,768,1024]{2,1,0:T(8,128)(2,1)}, bf16[3,768,1024]{2,1,0:T(8,128)(2,1)}, u32[]{:S(2)}, u32[]{:S(2)}) collective-permute-start(bf16[3,768,1024]{2,1,0:T(8,128)(2,1)} %slice.672), channel_id=1, source_target_pairs={{0,1},{1,0},{2,3},{3,2},{4,5},{5,4},{6,7},{7,6},{8,9},{9,8},{10,11... | collective-permute-start | bytes 14155784 | tf_op jit(solution)/shard_map/ppermute | solution.py:43
  479.7 13.9 %copy-start.60 = (f32[1024,12]{0,1:T(8,128)}, f32[1024,12]{0,1:T(8,128)S(1)}, u32[]{:S(2)}) copy-start(f32[1024,12]{0,1:T(8,128)S(1)} %select_reduce_fusion) | copy-start | bytes 147460
  489.2 8.9 %collective-permute-start.11 = (bf16[768,384]{1,0:T(8,128)(2,1)}, bf16[768,384]{1,0:T(8,128)(2,1)}, u32[]{:S(2)}, u32[]{:S(2)}) collective-permute-start(bf16[768,384]{1,0:T(8,128)(2,1)} %convolution_convert_fusion.8), channel_id=1, source_target_pairs={{0,1},{1,0},{2,3},{3,2},{4,5},{5,4},{6,7},{7,6},{8,9},{9,8},{10,11... | collective-permute-start | bytes 1769480 | tf_op jit(solution)/shard_map/ppermute | solution.py:43
  493.5 7.7 collective-permute-start.9
  527.0 16.1 %copy-start.40 = (bf16[512,384]{0,1:T(8,128)(2,1)S(1)}, bf16[512,384]{0,1:T(8,128)(2,1)}, u32[]{:S(2)}) copy-start(bf16[512,384]{0,1:T(8,128)(2,1)} %get-tuple-element.204) | copy-start | bytes 1179652
  527.1 16.1 %copy-start.79 = (f32[6,512]{1,0:T(8,128)S(1)}, f32[6,512]{1,0:T(8,128)}, u32[]{:S(2)}) copy-start(f32[6,512]{1,0:T(8,128)} %log_add_fusion.1) | copy-start | bytes 36868
  568.0 12.1 %copy-start.54 = (f32[512,6,64]{0,2,1:T(8,128)S(1)}, f32[512,6,64]{0,2,1:T(8,128)}, u32[]{:S(2)}) copy-start(f32[512,6,64]{0,2,1:T(8,128)} %fusion.113) | copy-start | bytes 2359300
  580.9 9.6 %copy-start.26 = (bf16[1024,384]{0,1:T(8,128)(2,1)S(1)}, bf16[1024,384]{0,1:T(8,128)(2,1)}, u32[]{:S(2)}) copy-start(bf16[1024,384]{0,1:T(8,128)(2,1)} %copy-done.25) | copy-start | bytes 2359300
  594.8 34.1 %slice-start = ((s8[25165824]{0:T(1024)(128)(4,1)}), s8[4194304]{0:T(1024)(128)(4,1)S(1)}, s32[]{:S(2)}) async-start(s8[25165824]{0:T(1024)(128)(4,1)} %bitcast.353), calls=%async_computation.9 | async-start | bytes 8388608
  594.8 34.1 %slice-start.1 = ((s8[25165824]{0:T(1024)(128)(4,1)}), s8[4194304]{0:T(1024)(128)(4,1)S(1)}, s32[]{:S(2)}) async-start(s8[25165824]{0:T(1024)(128)(4,1)} %bitcast.353), calls=%async_computation.10 | async-start | bytes 8388608
  594.8 34.1 %slice-start.2 = ((s8[25165824]{0:T(1024)(128)(4,1)}), s8[4194304]{0:T(1024)(128)(4,1)S(1)}, s32[]{:S(2)}) async-start(s8[25165824]{0:T(1024)(128)(4,1)} %bitcast.353), calls=%async_computation.11 | async-start | bytes 8388608
  594.8 34.1 %slice-start.3 = ((s8[25165824]{0:T(1024)(128)(4,1)}), s8[4194304]{0:T(1024)(128)(4,1)S(1)}, s32[]{:S(2)}) async-start(s8[25165824]{0:T(1024)(128)(4,1)} %bitcast.353), calls=%async_computation.12 | async-start | bytes 8388608
  612.7 16.2 %slice-start.4 = ((s8[25165824]{0:T(1024)(128)(4,1)}), s8[4194304]{0:T(1024)(128)(4,1)S(1)}, s32[]{:S(2)}) async-start(s8[25165824]{0:T(1024)(128)(4,1)} %bitcast.353), calls=%async_computation.13 | async-start | bytes 8388608
  644.0 9.2 %copy-start.65 = (bf16[512,6,64]{0,2,1:T(8,128)(2,1)S(1)}, bf16[512,6,64]{0,2,1:T(8,128)(2,1)}, u32[]{:S(2)}) copy-start(bf16[512,6,64]{0,2,1:T(8,128)(2,1)} %fusion.126) | copy-start | bytes 1179652
  644.0 9.2 %copy-start.66 = (bf16[512,6,64]{0,2,1:T(8,128)(2,1)S(1)}, bf16[512,6,64]{0,2,1:T(8,128)(2,1)}, u32[]{:S(2)}) copy-start(bf16[512,6,64]{0,2,1:T(8,128)(2,1)} %fusion.125) | copy-start | bytes 1179652
  644.0 9.2 %copy-start.71 = (bf16[512,6,64]{0,2,1:T(8,128)(2,1)S(1)}, bf16[512,6,64]{0,2,1:T(8,128)(2,1)}, u32[]{:S(2)}) copy-start(bf16[512,6,64]{0,2,1:T(8,128)(2,1)} %fusion.123) | copy-start | bytes 1179652
  644.0 9.4 %copy-start.3 = (bf16[6,512,2048]{2,1,0:T(8,128)(2,1)S(1)}, bf16[6,512,2048]{2,1,0:T(8,128)(2,1)}, u32[]{:S(2)}) copy-start(bf16[6,512,2048]{2,1,0:T(8,128)(2,1)} %multiply_convert_fusion) | copy-start | bytes 37748740
  644.0 9.4 %copy-start.35 = (bf16[512,384]{0,1:T(8,128)(2,1)S(1)}, bf16[512,384]{0,1:T(8,128)(2,1)}, u32[]{:S(2)}) copy-start(bf16[512,384]{0,1:T(8,128)(2,1)} %copy-done.34) | copy-start | bytes 1179652
  657.5 9.0 %copy-start.67 = (bf16[2048,6,64]{0,2,1:T(8,128)(2,1)}, bf16[2048,6,64]{0,2,1:T(8,128)(2,1)S(1)}, u32[]{:S(2)}) copy-start(bf16[2048,6,64]{0,2,1:T(8,128)(2,1)S(1)} %fusion.70) | copy-start | bytes 4718596
  667.0 14.8 %copy-start.73 = (bf16[768,384]{1,0:T(8,128)(2,1)S(1)}, bf16[768,384]{1,0:T(8,128)(2,1)}, u32[]{:S(2)}) copy-start(bf16[768,384]{1,0:T(8,128)(2,1)} %add_convert_fusion.2) | copy-start | bytes 1769476
  667.0 8.8 %collective-permute-start.12 = (f32[16,16,128]{2,1,0:T(8,128)S(1)}, f32[16,16,128]{2,1,0:T(8,128)S(1)}, u32[]{:S(2)}, u32[]{:S(2)}) collective-permute-start(f32[16,16,128]{2,1,0:T(8,128)S(1)} %bitcast.416), channel_id=1, source_target_pairs={{0,1},{1,0},{2,3},{3,2},{4,5},{5,4},{6,7},{7,6},{8,9},{9,8},{10,11... | collective-permute-start | bytes 393224 | tf_op jit(solution)/shard_map/ppermute | solution.py:43
  676.5 11.3 %all-to-all-start.6 = ((f32[16,16,128]{2,1,0:T(8,128)}), f32[16,16,128]{2,1,0:T(8,128)S(1)}, u32[]{:S(2)}, u32[]{:S(2)}) async-start(f32[16,16,128]{2,1,0:T(8,128)} %bitcast_add_fusion.4), calls=%async_computation.6 | async-start | bytes 262144 | tf_op jit(solution)/shard_map/all_to_all | solution.py:400
  687.8 58.6 %all-to-all-start.5 = ((bf16[16,48,1536]{2,1,0:T(8,128)(2,1)}), bf16[16,48,1536]{2,1,0:T(8,128)(2,1)S(1)}, u32[]{:S(2)}, u32[]{:S(2)}) async-start(bf16[16,48,1536]{2,1,0:T(8,128)(2,1)} %pad_maximum_fusion.4), calls=%async_computation.5 | async-start | bytes 4718592 | tf_op jit(solution)/shard_map/all_to_all | solution.py:384
  747.8 108.8 %all-to-all-start.7 = ((bf16[16,3,48,1024]{3,2,1,0:T(8,128)(2,1)}), bf16[16,3,48,1024]{3,2,1,0:T(8,128)(2,1)}, u32[]{:S(2)}, u32[]{:S(2)}) async-start(bf16[16,3,48,1024]{3,2,1,0:T(8,128)(2,1)} %bitcast.365), calls=%async_computation.7 | async-start | bytes 9437184 | tf_op jit(solution)/shard_map/all_to_all | solution.py:303
  760.1 3.9 collective-permute-start.6
  763.7 11.2 %collective-permute-start.10 = (bf16[1024,768]{0,1:T(8,128)(2,1)}, bf16[1024,768]{0,1:T(8,128)(2,1)}, u32[]{:S(2)}, u32[]{:S(2)}) collective-permute-start(bf16[1024,768]{0,1:T(8,128)(2,1)} %dynamic-slice_convert_fusion.1), channel_id=1, source_target_pairs={{0,1},{1,0},{2,3},{3,2},{4,5},{5,4},{6,7},{7,6},{8,9},{9,8},{10,11... | collective-permute-start | bytes 4718600 | tf_op jit(solution)/shard_map/ppermute | solution.py:43
  (95 other events, 398.5 us)
Sparse Core Ops, SparseCore 0:
  12.1 133.1 all-gather.1

commit v2 on v1

--- a/solution.py
+++ b/solution.py
@@ -1,6 +1,10 @@
+import functools
+
 import jax
 import jax.numpy as jnp
 from jax import lax
+from jax.experimental import pallas as pl
+from jax.experimental.pallas import tpu as pltpu
 from jax.sharding import PartitionSpec as P
 
 HEAD_DIM = 64
@@ -13,6 +17,9 @@
 HIGH = lax.Precision.HIGHEST
 NEG = -1e30
 LANES = 128
+DOCS = 8
+LOG2E = 1.4426950408889634
+MESH = pl.DeviceIdType.MESH
 single = jnp.float32
 half = jnp.bfloat16
 
@@ -79,100 +86,471 @@
     return (place[:, None, :] == slots[None, :, None]).astype(half)
 
 
-def block_scores(q_blk, key_rows, seg_rows, seg_keys, first):
-    count = q_blk.shape[0]
-    rows = first + jnp.arange(count, dtype=jnp.int32)
-    cols = jnp.arange(key_rows.shape[0], dtype=jnp.int32)
-    allowed = (cols[None, :] <= rows[:, None]) & (seg_keys[None, :] == seg_rows[:, None])
-    scores = jnp.einsum(
-        "qhd,khd->hqk", q_blk, key_rows, preferred_element_type=jnp.float32
-    ) * HEAD_DIM ** (-0.5)
-    return jnp.where(allowed[None], scores, NEG)
-
-
-def attention_forward(queries, keys_all, values_all, seg_keys):
-    seq, heads_local = queries.shape[:2]
-    block = min(512, seq)
-    outputs = []
-    log_totals = []
-    for first in range(0, seq, block):
-        last = first + block
-        scores = block_scores(
-            queries[first:last], keys_all[:last], seg_keys[first:last], seg_keys[:last], first
+def fit(seq, want):
+    return want if seq % want == 0 else seq
+
+def block_bounds(seg, size):
+    seq = seg.shape[0]
+    member = (seg[:, None] == jnp.arange(DOCS, dtype=jnp.int32)).astype(jnp.int32)
+    sizes = jnp.sum(member, axis=0)
+    ends = jnp.cumsum(sizes)
+    start = jnp.sum(member * (ends - sizes), axis=1)
+    end = jnp.sum(member * ends, axis=1) - 1
+    edges = start.reshape(-1, size)
+    number = jnp.arange(seq // size, dtype=jnp.int32)
+    low = edges[:, 0] // size
+    plain = jnp.clip((edges[:, -1] + size - 1) // size, low, number)
+    high = end.reshape(-1, size)[:, -1] // size
+    clear = jnp.sum((edges[None, :, -1] <= number[:, None] * size).astype(jnp.int32), axis=1)
+    clear = jnp.clip(clear, number + 1, high + 1)
+    return jnp.stack([low, plain, high, clear]), start
+
+def head_lanes(h, rows):
+    lane = lax.broadcasted_iota(jnp.int32, (rows, LANES), 1)
+    return (lane < HEAD_DIM) if h % 2 == 0 else (lane >= HEAD_DIM)
+
+def fwd_kernel(heads, bounds, q_ref, k_ref, v_ref, start_ref, o_ref, lse_ref, s_ref, m_ref, l_ref, acc_ref, qm_ref):
+    size = q_ref.shape[0]
+    i = pl.program_id(0)
+    low, plain = bounds[0, i], bounds[1, i]
+    factor = LOG2E * HEAD_DIM ** -0.5
+    for h in range(heads):
+        pair = pl.ds(h // 2 * LANES, LANES)
+        qm_ref[h] = jnp.where(head_lanes(h, size), q_ref[:, pair], 0).astype(half)
+    m_ref[...] = jnp.full(m_ref.shape, NEG, single)
+    l_ref[...] = jnp.zeros(l_ref.shape, single)
+    acc_ref[...] = jnp.zeros(acc_ref.shape, single)
+
+    def score(j, masked):
+        rows = pl.ds(pl.multiple_of(j * size, size), size)
+        if masked:
+            row = i * size + lax.broadcasted_iota(jnp.int32, (size, size), 0)
+            col = j * size + lax.broadcasted_iota(jnp.int32, (size, size), 1)
+            allowed = (col <= row) & (col >= start_ref[...])
+        for h in range(heads):
+            s = mm_nt(qm_ref[h], k_ref[rows, pl.ds(h // 2 * LANES, LANES)])
+            if masked:
+                s = jnp.where(allowed, s, NEG)
+            s_ref[h, j] = s
+            m = m_ref[h]
+            for c in range(size // LANES):
+                m = jnp.maximum(m, s[:, c * LANES : (c + 1) * LANES])
+            m_ref[h] = m
+
+    pl.loop(low, plain)(lambda j: score(j, True))
+    pl.loop(plain, i)(lambda j: score(j, False))
+    score(i, True)
+    for h in range(heads):
+        m_ref[h] = jnp.broadcast_to(jnp.max(m_ref[h], axis=1, keepdims=True) * factor, (size, LANES))
+
+    def gather(j):
+        rows = pl.ds(pl.multiple_of(j * size, size), size)
+        for h in range(heads):
+            s = s_ref[h, j]
+            m = m_ref[h]
+            l = l_ref[h]
+            parts = []
+            for c in range(size // LANES):
+                p = jnp.exp2(s[:, c * LANES : (c + 1) * LANES] * factor - m)
+                l = l + p
+                parts.append(p.astype(half))
+            l_ref[h] = l
+            acc_ref[h] += jnp.dot(jnp.concatenate(parts, 1), v_ref[rows, pl.ds(h // 2 * LANES, LANES)], preferred_element_type=single)
+
+    pl.loop(low, i + 1)(gather)
+    lane = lax.broadcasted_iota(jnp.int32, (size, LANES), 1)
+    lse = jnp.zeros((size, LANES), single)
+    for h in range(0, heads, 2):
+        outs = []
+        for k in (h, h + 1):
+            l = jnp.sum(l_ref[k], axis=1, keepdims=True)
+            outs.append(acc_ref[k] / l)
+            lse = jnp.where(lane == k, m_ref[k] + jnp.log2(l), lse)
+        o_ref[:, pl.ds(h // 2 * LANES, LANES)] = jnp.where(lane < HEAD_DIM, outs[0], outs[1])
+    lse_ref[...] = lse
+
+def attention_forward(qkv, seg_bounds, starts, size):
+    seq = qkv.shape[0]
+    hh = qkv.shape[1] // 3
+    heads = hh // HEAD_DIM
+    return pl.pallas_call(
+        functools.partial(fwd_kernel, heads),
+        grid_spec=pltpu.PrefetchScalarGridSpec(
+            num_scalar_prefetch=1,
+            grid=(seq // size,),
+            in_specs=[
+                pl.BlockSpec((size, hh), lambda i, b: (i, 0)),
+                pl.BlockSpec((seq, hh), lambda i, b: (0, 1)),
+                pl.BlockSpec((seq, hh), lambda i, b: (0, 2)),
+                pl.BlockSpec((size, 1), lambda i, b: (i, 0)),
+            ],
+            out_specs=[
+                pl.BlockSpec((size, hh), lambda i, b: (i, 0)),
+                pl.BlockSpec((size, LANES), lambda i, b: (i, 0)),
+            ],
+            scratch_shapes=[
+                pltpu.VMEM((heads, seq // size, size, size), single),
+                pltpu.VMEM((heads, size, LANES), single),
+                pltpu.VMEM((heads, size, LANES), single),
+                pltpu.VMEM((heads, size, LANES), single),
+                pltpu.VMEM((heads, size, LANES), half),
+            ],
+        ),
+        out_shape=[
+            jax.ShapeDtypeStruct((seq, hh), single),
+            jax.ShapeDtypeStruct((seq, LANES), single),
+        ],
+        compiler_params=pltpu.CompilerParams(vmem_limit_bytes=48 << 20),
+        cost_estimate=pl.CostEstimate(flops=4 * seq * seq * LANES * heads, bytes_accessed=16 * seq * hh, transcendentals=0),
+    )(seg_bounds, qkv, qkv, qkv, starts[:, None])
+
+def bwd_kernel(
+    heads, bounds, q_ref, k_ref, v_ref, do_ref, o_ref, lse_ref, start_ref, out_ref, dq_ref, dk_ref, dv_ref, stat_ref
+):
+    size = k_ref.shape[0]
+    j = pl.program_id(0)
+    high, clear = bounds[2, j], bounds[3, j]
+    factor = LOG2E * HEAD_DIM ** -0.5
+    hh = k_ref.shape[1]
+
+    @pl.when(j == 0)
+    def _():
+        dq_ref[...] = jnp.zeros(dq_ref.shape, single)
+        feature = lax.broadcasted_iota(jnp.int32, (hh, LANES), 0)
+        lane = lax.broadcasted_iota(jnp.int32, (hh, LANES), 1)
+        pick = (feature // HEAD_DIM + 8 == lane).astype(half)
+
+        @pl.loop(0, q_ref.shape[0] // size)
+        def _(i):
+            rows = pl.ds(pl.multiple_of(i * size, size), size)
+            product = o_ref[rows, :] * do_ref[rows, :].astype(single)
+            top = product.astype(half)
+            low = (product - top.astype(single)).astype(half)
+            both = mm(top, pick) + mm(low, pick) + lse_ref[rows, :]
+            stat_ref[:, rows] = both.T[:16, :]
+
+    dk_ref[...] = jnp.zeros(dk_ref.shape, single)
+    dv_ref[...] = jnp.zeros(dv_ref.shape, single)
+
+    def step(i, masked):
+        rows = pl.ds(pl.multiple_of(i * size, size), size)
+        if masked:
+            key = j * size + lax.broadcasted_iota(jnp.int32, (size, size), 0)
+            query = i * size + lax.broadcasted_iota(jnp.int32, (size, size), 1)
+            allowed = (key <= query) & (key >= start_ref[:, rows])
+        for pair in range(heads // 2):
+            lanes = pl.ds(pair * LANES, LANES)
+            k, v = k_ref[:, lanes], v_ref[:, lanes]
+            q, do = q_ref[rows, lanes], do_ref[rows, lanes]
+            ps, dss, qs, dos, ks = [], [], [], [], []
+            for h in (2 * pair, 2 * pair + 1):
+                mine = head_lanes(h, size)
+                qm = jnp.where(mine, q, 0).astype(half)
+                dom = jnp.where(mine, do, 0).astype(half)
+                s = mm_nt(k, qm) * factor - stat_ref[pl.ds(h, 1), rows]
+                if masked:
+                    s = jnp.where(allowed, s, NEG)
+                p = jnp.exp2(s)
+                ds = p * (mm_nt(v, dom) - stat_ref[pl.ds(8 + h, 1), rows])
+                ps.append(p.astype(half))
+                dss.append(ds.astype(half))
+                qs.append(qm)
+                dos.append(dom)
+                ks.append(jnp.where(mine, k, 0).astype(half))
+            dv_ref[:, lanes] += jnp.dot(jnp.concatenate(ps, 1), jnp.concatenate(dos, 0), preferred_element_type=single)
+            dk_ref[:, lanes] += jnp.dot(jnp.concatenate(dss, 1), jnp.concatenate(qs, 0), preferred_element_type=single)
+            dq_ref[rows, lanes] += mm_tn(jnp.concatenate(dss, 0), jnp.concatenate(ks, 0))
+
+    step(j, True)
+    pl.loop(j + 1, clear)(lambda i: step(i, False))
+    pl.loop(clear, high + 1)(lambda i: step(i, True))
+    mine = pl.ds(pl.multiple_of(j * size, size), size)
+    out_ref[mine, pl.ds(hh, hh)] = (dk_ref[...] * HEAD_DIM ** -0.5).astype(half)
+    out_ref[mine, pl.ds(2 * hh, hh)] = dv_ref[...].astype(half)
+    out_ref[mine, pl.ds(0, hh)] = (dq_ref[mine, :] * HEAD_DIM ** -0.5).astype(half)
+
+def attention_backward(qkv, do, heads_out, lse, seg_bounds, starts, size):
+    seq = qkv.shape[0]
+    hh = qkv.shape[1] // 3
+    heads = hh // HEAD_DIM
+    return pl.pallas_call(
+        functools.partial(bwd_kernel, heads),
+        grid_spec=pltpu.PrefetchScalarGridSpec(
+            num_scalar_prefetch=1,
+            grid=(seq // size,),
+            in_specs=[
+                pl.BlockSpec((seq, hh), lambda j, b: (0, 0)),
+                pl.BlockSpec((size, hh), lambda j, b: (j, 1)),
+                pl.BlockSpec((size, hh), lambda j, b: (j, 2)),
+                pl.BlockSpec((seq, hh), lambda j, b: (0, 0)),
+                pl.BlockSpec((seq, hh), lambda j, b: (0, 0)),
+                pl.BlockSpec((seq, LANES), lambda j, b: (0, 0)),
+                pl.BlockSpec((1, seq), lambda j, b: (0, 0)),
+            ],
+            out_specs=pl.BlockSpec((seq, 3 * hh), lambda j, b: (0, 0)),
+            scratch_shapes=[
+                pltpu.VMEM((seq, hh), single),
+                pltpu.VMEM((size, hh), single),
+                pltpu.VMEM((size, hh), single),
+                pltpu.VMEM((16, seq), single),
+            ],
+        ),
+        out_shape=jax.ShapeDtypeStruct((seq, 3 * hh), half),
+        compiler_params=pltpu.CompilerParams(vmem_limit_bytes=48 << 20),
+        cost_estimate=pl.CostEstimate(flops=10 * seq * seq * LANES * heads, bytes_accessed=20 * seq * hh, transcendentals=0),
+    )(seg_bounds, qkv, qkv, qkv, do, heads_out, lse, starts[None, :])
+
+
+def gather_kernel(members, low, x_ref, o_ref, send_sem, recv_sem, own_sem):
+    me = lax.axis_index("dp")
+    high = members // low
+    mine, row = lax.rem(me, low), me // low
+
+    def beside(k):
+        return row * low + lax.rem(mine + k, low)
+
+    def across(k):
+        return lax.rem(row + k, high) * low + mine
+
+    peers = [beside(k) for k in range(1, low)] + [across(k) for k in range(1, high)]
+    barrier = pltpu.get_barrier_semaphore()
+    for peer in peers:
+        pl.semaphore_signal(barrier, inc=1, device_id={"dp": peer}, device_id_type=MESH)
+    pl.semaphore_wait(barrier, len(peers))
+
+    def push(source, block, target, slot):
+        copy = pltpu.make_async_remote_copy(
+            src_ref=source,
+            dst_ref=o_ref.at[block],
+            send_sem=send_sem.at[slot],
+            recv_sem=recv_sem.at[block],
+            device_id={"dp": target},
+            device_id_type=MESH,
         )
-        peak = jnp.max(scores, axis=-1, keepdims=True)
-        expo = jnp.exp(scores - peak)
-        total = jnp.sum(expo, axis=-1, keepdims=True)
-        probs_low = (expo / total).astype(half)
-        outputs.append(
-            jnp.einsum(
-                "hqk,khd->qhd", probs_low, values_all[:last], preferred_element_type=single
-            ).astype(half)
-        )
-        log_totals.append(peak + jnp.log(total))
-    return jnp.concatenate(outputs, 0).reshape(seq, heads_local * HEAD_DIM), log_totals
-
-
-def attention_backward(queries, keys_all, values_all, seg_keys, log_totals, heads_grad):
-    seq, heads_local = queries.shape[:2]
-    block = min(512, seq)
-    query_grads = []
-    key_grad = jnp.zeros((seq, heads_local, HEAD_DIM), single)
-    value_grad = jnp.zeros((seq, heads_local, HEAD_DIM), single)
-    for index, first in enumerate(range(0, seq, block)):
-        last = first + block
-        q_blk = queries[first:last]
-        scores = block_scores(q_blk, keys_all[:last], seg_keys[first:last], seg_keys[:last], first)
-        probs = jnp.exp(scores - log_totals[index])
-        prob_grad = jnp.einsum(
-            "qhd,khd->hqk", heads_grad[first:last], values_all[:last], preferred_element_type=single
-        )
-        score_grad = (
-            probs * (prob_grad - jnp.sum(probs * prob_grad, axis=-1, keepdims=True))
-        ).astype(half)
-        query_grads.append(
-            jnp.einsum("hqk,khd->qhd", score_grad, keys_all[:last], preferred_element_type=single)
-            * HEAD_DIM ** (-0.5)
-        )
-        key_grad = key_grad.at[:last].add(
-            jnp.einsum("hqk,qhd->khd", score_grad, q_blk, preferred_element_type=single)
-            * HEAD_DIM ** (-0.5)
-        )
-        value_grad = value_grad.at[:last].add(
-            jnp.einsum(
-                "hqk,qhd->khd",
-                probs.astype(half),
-                heads_grad[first:last],
-                preferred_element_type=single,
+        copy.start()
+        return copy
+
+    def arrived(block):
+        pltpu.make_async_remote_copy(
+            src_ref=x_ref,
+            dst_ref=o_ref.at[block],
+            send_sem=send_sem.at[0],
+            recv_sem=recv_sem.at[block],
+            device_id={"dp": peers[0]},
+            device_id_type=MESH,
+        ).wait_recv()
+
+    own = pltpu.make_async_copy(x_ref, o_ref.at[me], own_sem)
+    own.start()
+    sent = [push(x_ref, me, across(k), k) for k in range(1, high)]
+    sent += [push(x_ref, me, beside(k), high + k) for k in range(1, low)]
+    for k in range(1, high):
+        block = across(high - k)
+        arrived(block)
+        for step in range(1, low):
+            sent.append(push(o_ref.at[block], block, beside(step), high + k * low + step))
+    for k in range(1, low):
+        block = beside(low - k)
+        arrived(block)
+        for step in range(1, high):
+            arrived(lax.rem(block + step * low, members))
+    for copy in sent:
+        copy.wait_send()
+    own.wait()
+
+
+def gather_all(x, members):
+    low = 4 if members % 4 == 0 else 1
+    high = members // low
+    return pl.pallas_call(
+        functools.partial(gather_kernel, members, low),
+        out_shape=jax.ShapeDtypeStruct((members,) + x.shape, x.dtype),
+        in_specs=[pl.BlockSpec(memory_space=pl.ANY)],
+        out_specs=pl.BlockSpec(memory_space=pl.ANY),
+        scratch_shapes=[
+            pltpu.SemaphoreType.DMA((high * (low + 1),)),
+            pltpu.SemaphoreType.DMA((members,)),
+            pltpu.SemaphoreType.DMA,
+        ],
+        compiler_params=pltpu.CompilerParams(collective_id=0, has_side_effects=True),
+        name="gather_all",
+    )(x)
+
+
+def exchange_kernel(count, *refs):
+    size = EXPERTS_FF
+    xs, os = refs[:count], refs[count : 2 * count]
+    send_sem, recv_sem, own_sem = refs[2 * count :]
+    me = lax.axis_index("dp")
+    mine = lax.rem(me, size)
+    base = me - mine
+    barrier = pltpu.get_barrier_semaphore()
+    for k in range(1, size):
+        peer = base + lax.rem(mine + k, size)
+        pl.semaphore_signal(barrier, inc=1, device_id={"dp": peer}, device_id_type=MESH)
+    pl.semaphore_wait(barrier, size - 1)
+    copies = []
+    for a in range(count):
+        for k in range(1, size):
+            to = lax.rem(mine + k, size)
+            copies.append(
+                pltpu.make_async_remote_copy(
+                    src_ref=xs[a].at[to],
+                    dst_ref=os[a].at[mine],
+                    send_sem=send_sem.at[a, k],
+                    recv_sem=recv_sem.at[a, k],
+                    device_id={"dp": base + to},
+                    device_id_type=MESH,
+                )
             )
-        )
-    return (
-        jnp.stack([jnp.concatenate(query_grads, 0), key_grad, value_grad])
-        .reshape(3, seq, heads_local * HEAD_DIM)
-        .astype(half)
-    )
-
-
-def expert_math(rows, grad_rows, gate, weights):
-    out_grad = (grad_rows.astype(single) * gate).astype(half)
-    gate_pre = mm(rows, weights[0])
-    up_pre = mm(rows, weights[1])
-    sigma = jax.nn.sigmoid(gate_pre)
-    active = gate_pre * sigma
-    hidden = (active * up_pre).astype(half)
-    hidden_grad = mm(out_grad, weights[2])
-    gate_pre_grad = (hidden_grad * up_pre * sigma * (1.0 + gate_pre * (1.0 - sigma))).astype(half)
-    up_pre_grad = (hidden_grad * active).astype(half)
-    expert_out = mm_nt(hidden, weights[2])
-    in_grad = mm_nt(gate_pre_grad, weights[0]) + mm_nt(up_pre_grad, weights[1])
-    weight_grads = jnp.stack(
-        [
-            mm_tn(rows, gate_pre_grad).astype(half),
-            mm_tn(rows, up_pre_grad).astype(half),
-            mm_tn(out_grad, hidden).astype(half),
-        ]
-    )
-    return expert_out, in_grad, weight_grads
+        copies.append(pltpu.make_async_copy(xs[a].at[mine], os[a].at[mine], own_sem.at[a]))
+    for copy in copies:
+        copy.start()
+    for copy in copies:
+        copy.wait()
+
+
+def exchange(number, *arrays):
+    count = len(arrays)
+    return pl.pallas_call(
+        functools.partial(exchange_kernel, count),
+        out_shape=[jax.ShapeDtypeStruct(x.shape, x.dtype) for x in arrays],
+        in_specs=[pl.BlockSpec(memory_space=pl.ANY)] * count,
+        out_specs=[pl.BlockSpec(memory_space=pl.ANY)] * count,
+        scratch_shapes=[
+            pltpu.SemaphoreType.DMA((count, EXPERTS_FF)),
+            pltpu.SemaphoreType.DMA((count, EXPERTS_FF)),
+            pltpu.SemaphoreType.DMA((count,)),
+        ],
+        compiler_params=pltpu.CompilerParams(collective_id=number, has_side_effects=True),
+        name=f"exchange_{number}",
+    )(*arrays)
+
+
+def expert_kernel(
+    padded,
+    x_ref,
+    dy_ref,
+    own_ref,
+    other_ref,
+    out_ref,
+    grad_ref,
+    own_grad_ref,
+    other_grad_ref,
+    gate_ref,
+    og_ref,
+    xt_ref,
+    ogt_ref,
+    eo_ref,
+    ig_ref,
+    hid_ref,
+    pg_ref,
+    pu_ref,
+    dot_ref,
+):
+    f = pl.program_id(0)
+    sources = x_ref.shape[0]
+    count, width = og_ref.shape
+    chunk = count // 4
+    x_all = x_ref.reshape(count, width)
+
+    @pl.when(f == 0)
+    def _():
+        for s in range(sources):
+            rows = pl.ds(s * padded, padded)
+            gates = x_ref[s, padded - 16 :, : 2 * LANES].astype(single).T
+            gate = jnp.broadcast_to(gates[:padded, 15:16], (padded, LANES))
+            gate_ref[rows, :] = gate
+            og_ref[rows, :] = (dy_ref[s].astype(single) * gate[:, :1]).astype(half)
+        xt_ref[...] = x_all[...].T
+        ogt_ref[...] = og_ref[...].T
+        eo_ref[...] = jnp.zeros(eo_ref.shape, single)
+        ig_ref[...] = jnp.zeros(ig_ref.shape, single)
+
+    for w_ref, wg_ref in ((own_ref, own_grad_ref), (other_ref, other_grad_ref)):
+        shape = wg_ref.shape[0], wg_ref.shape[2], wg_ref.shape[3]
+        gate_w, up_w, down_w = (w_ref[:, k].reshape(width, shape[2]) for k in range(3))
+        for r in range(4):
+            rows = pl.ds(r * chunk, chunk)
+            x = x_all[rows, :]
+            og = og_ref[rows, :]
+            pre = mm(x, gate_w)
+            up = mm(x, up_w)
+            hg = mm(og, down_w)
+            sigma = jax.nn.sigmoid(pre)
+            active = pre * sigma
+            hidden = (active * up).astype(half)
+            pg = (hg * up * (sigma * (1.0 + pre * (1.0 - sigma)))).astype(half)
+            pu = (hg * active).astype(half)
+            hid_ref[rows, :] = hidden
+            pg_ref[rows, :] = pg
+            pu_ref[rows, :] = pu
+            eo_ref[rows, :] += mm_nt(hidden, down_w)
+            ig_ref[rows, :] += mm_nt(pg, gate_w) + mm_nt(pu, up_w)
+        wg_ref[:, 0] = mm(xt_ref[...], pg_ref[...]).astype(half).reshape(shape)
+        wg_ref[:, 1] = mm(xt_ref[...], pu_ref[...]).astype(half).reshape(shape)
+        wg_ref[:, 2] = mm(ogt_ref[...], hid_ref[...]).astype(half).reshape(shape)
+
+    @pl.when(f == pl.num_programs(0) - 1)
+    def _():
+        dot_ref[...] = jnp.zeros(dot_ref.shape, single)
+        ones = jnp.ones((16, width), half)
+        for s in range(sources):
+            rows = pl.ds(s * padded, padded)
+            eo = eo_ref[rows, :]
+            out_ref[s] = (eo * gate_ref[rows, :1]).astype(half)
+            grad_ref[s] = ig_ref[rows, :].astype(half)
+            product = eo * dy_ref[s].astype(single)
+            top = product.astype(half)
+            low = (product - top.astype(single)).astype(half)
+            dot_ref[:, :padded] = mm_nt(ones, top) + mm_nt(ones, low)
+            dots = dot_ref[...]
+            high = dots.astype(half)
+            rest = (dots - high.astype(single)).astype(half)
+            row = lax.broadcasted_iota(jnp.int32, dots.shape, 0)
+            tail = ig_ref[pl.ds((s + 1) * padded - 16, 16), : 2 * LANES].astype(half)
+            tail = jnp.where(row == 14, high.astype(single), jnp.where(row == 15, rest.astype(single), tail.astype(single)))
+            grad_ref[s, padded - 16 :, : 2 * LANES] = tail.astype(half)
+
+
+def expert_step(x, dy, own, other, padded):
+    sources, _, width = x.shape
+    count = sources * padded
+    m, _, r, ff = own.shape
+    block = fit(ff, 256)
+    whole = pl.BlockSpec((sources, padded, width), lambda f: (0, 0, 0))
+    part = pl.BlockSpec((m, 3, r, block), lambda f: (0, 0, 0, f))
+    return pl.pallas_call(
+        functools.partial(expert_kernel, padded),
+        grid=(ff // block,),
+        in_specs=[whole, whole, part, part],
+        out_specs=[whole, whole, part, part],
+        out_shape=[
+            jax.ShapeDtypeStruct(x.shape, half),
+            jax.ShapeDtypeStruct(x.shape, half),
+            jax.ShapeDtypeStruct(own.shape, half),
+            jax.ShapeDtypeStruct(own.shape, half),
+        ],
+        scratch_shapes=[
+            pltpu.VMEM((count, LANES), single),
+            pltpu.VMEM((count, width), half),
+            pltpu.VMEM((width, count), half),
+            pltpu.VMEM((width, count), half),
+            pltpu.VMEM((count, width), single),
+            pltpu.VMEM((count, width), single),
+            pltpu.VMEM((count, block), half),
+            pltpu.VMEM((count, block), half),
+            pltpu.VMEM((count, block), half),
+            pltpu.VMEM((16, 2 * LANES), single),
+        ],
+        compiler_params=pltpu.CompilerParams(vmem_limit_bytes=60 << 20),
+        cost_estimate=pl.CostEstimate(
+            flops=18 * count * width * 2 * ff,
+            bytes_accessed=4 * 6 * width * ff + 8 * count * width,
+            transcendentals=0,
+        ),
+        name="expert_step",
+    )(x, dy, own, other)
 
 
 def per_device(
@@ -191,14 +569,10 @@
 ):
     members = lax.axis_size("dp")
     groups = members // EXPERTS_FF
-    cubes = [[g * EXPERTS_FF + i for i in range(EXPERTS_FF)] for g in range(groups)]
     core = lax.axis_index("tensor")
     d_rows, hh = out_weight.shape
     per_core = -(-CAPACITY // 2)
     padded = -(-(per_core + 3) // 16) * 16
-
-    def exchange(blocks):
-        return lax.all_to_all(blocks, "dp", 0, 0, axis_index_groups=cubes, tiled=True)
 
     pack = jnp.concatenate(
         [
@@ -210,8 +584,11 @@
         ],
         1,
     )
-    full_pack = lax.all_gather(pack, "dp", axis=0, tiled=True)
-    width = full_pack.shape[0]
+    columns = pack.shape[1]
+    pack = jnp.pad(pack, ((0, 0), (0, -columns % LANES)))
+    full_pack, expert_weight = lax.optimization_barrier((gather_all(pack, members), expert_weight))
+    full_pack = full_pack.reshape(members * d_rows, -1)[:, :columns]
+    width = members * d_rows
     proj_full = full_pack[:, : 3 * hh]
     outw_own = full_pack[:, 3 * hh : 4 * hh]
     outw_other = swap(outw_own)
@@ -222,16 +599,16 @@
     sent_weight = jnp.broadcast_to(expert_weight[None], (groups,) + expert_weight.shape)
     sent_weight = sent_weight.reshape((members,) + expert_weight.shape[1:])
     my_weight = lax.all_to_all(sent_weight, "dp", 0, 0, tiled=True)
-    weights_own = my_weight.transpose(1, 0, 2, 3).reshape(3, width, -1)
-    weights_other = swap(weights_own)
-    weights = jnp.concatenate([weights_own, weights_other], 2)
+    if d_rows % 16:
+        my_weight = my_weight.transpose(1, 0, 2, 3).reshape(1, 3, width, -1)
+    other_weight = swap(my_weight)
 
     ids = jnp.concatenate([segment_ids[0][:, None], routes[0]], 1)
     ids_all = in_order(ids, swap(ids))
     seg_keys = ids_all[:, 0]
     onehot = slot_onehot(ids_all[:, 1:], core, per_core, padded).reshape(EXPERTS_FF * padded, -1)
     dy_all = in_order(cotangent[0], swap(cotangent[0]))
-    slot_dy = exchange(mm(onehot, dy_all).astype(half).reshape(EXPERTS_FF, padded, width))
+    sent_dy = mm(onehot, dy_all).astype(half).reshape(EXPERTS_FF, padded, width)
 
     x_rows = tokens[0].astype(single)
     local_rows = x_rows.shape[0]
@@ -240,12 +617,11 @@
     full_one = (x_all * scale_all * gains[0]).astype(half)
     scale_one = half_of(scale_all, core)
     seq = full_one.shape[0]
-    heads_local = hh // HEAD_DIM
     qkv = mm(full_one, proj_full).astype(half)
-    queries, keys_all, values_all = (
-        qkv[:, i * hh : (i + 1) * hh].reshape(seq, heads_local, HEAD_DIM) for i in range(3)
-    )
-    heads_out, log_totals = attention_forward(queries, keys_all, values_all, seg_keys)
+    size = fit(seq, 256)
+    bounds, starts = block_bounds(seg_keys, size)
+    heads_full, lse = attention_forward(qkv, bounds, starts, size)
+    heads_out = heads_full.astype(half)
     ho_own = half_of(heads_out, core)
     ho_other = swap(half_of(heads_out, 1 - core))
     resid = x_rows + mm_nt(ho_own, outw_own) + mm_nt(ho_other, outw_other)
@@ -271,40 +647,19 @@
     gate_row = jnp.pad(slot_gate, ((0, 0), (0, width - padded)))[:, None, :]
     row_number = lax.broadcasted_iota(jnp.int32, (1, padded, 1), 1)
     sent_rows = jnp.where(row_number == padded - 1, gate_row, picked[:, :, :width])
-    got_rows = exchange(sent_rows)
-
-    got_gate = got_rows[:, padded - 1, :padded].astype(single)
+    got_rows, got_dy = exchange(1, sent_rows, sent_dy)
+
     count = EXPERTS_FF * padded
-    gate_col = got_gate.reshape(count, 1)
-    rows = got_rows.reshape(count, width)
-    dy_rows = slot_dy.reshape(count, width)
-    expert_out, in_grad, weight_grads = expert_math(rows, dy_rows, gate_col, weights)
-    gated_out = (expert_out * gate_col).astype(half).reshape(EXPERTS_FF, padded, width)
-    gate_dot = jnp.sum(dy_rows.astype(single) * expert_out, axis=-1).reshape(EXPERTS_FF, padded)
-    dot_high = gate_dot.astype(half)
-    dot_low = (gate_dot - dot_high.astype(single)).astype(half)
-    lanes = ((0, 0), (0, width - padded))
-    sent_grad = jnp.where(
-        row_number == padded - 1,
-        jnp.pad(dot_low, lanes)[:, None, :],
-        jnp.where(
-            row_number == padded - 2,
-            jnp.pad(dot_high, lanes)[:, None, :],
-            in_grad.astype(half).reshape(EXPERTS_FF, padded, width),
-        ),
-    )
-    back_grad = exchange(sent_grad)
-    back_out = exchange(gated_out)
-
-    ff_half = weights_own.shape[2]
-    grads_own = weight_grads[:, :, :ff_half].astype(single)
-    grads_own = (grads_own + swap(weight_grads[:, :, ff_half:]).astype(single)).astype(half)
-    grads_sent = grads_own.reshape(3, members, d_rows, ff_half).transpose(1, 0, 2, 3)
+    gated_out, in_grad, grads_own, grads_other = expert_step(
+        got_rows, got_dy, my_weight, other_weight, padded
+    )
+    back_grad, back_out = exchange(2, in_grad, gated_out)
+    back_grad, grads_own = lax.optimization_barrier((back_grad, grads_own))
+
+    grads_sent = (grads_own.astype(single) + swap(grads_other).astype(single)).astype(half)
+    if d_rows % 16:
+        grads_sent = grads_sent.reshape(3, members, d_rows, -1).transpose(1, 0, 2, 3)
     grads_got = lax.all_to_all(grads_sent, "dp", 0, 0, tiled=True)
-    expert_shard = jnp.sum(
-        grads_got.reshape((groups, EXPERTS_FF) + grads_got.shape[1:]).astype(single), axis=0
-    )
-
     dots = back_grad[:, padded - 2 :, :padded]
     eye = jnp.eye(EXPERTS_FF, dtype=half)
     dot_columns = jnp.concatenate(
@@ -364,12 +719,11 @@
     attn_grad = resid_grad.astype(half)
     hg_own = mm(attn_grad, outw_own).astype(half)
     hg_other = swap(mm(attn_grad, outw_other).astype(half))
-    heads_grad = in_order(hg_own, hg_other).reshape(seq, heads_local, HEAD_DIM)
+    heads_grad = in_order(hg_own, hg_other)
     out_w_grad = mm_tn(attn_grad, ho_own) + swap(mm_tn(attn_grad, ho_other).astype(half)).astype(
         single
     )
-    qkv_grad = attention_backward(queries, keys_all, values_all, seg_keys, log_totals, heads_grad)
-    qkv_grad = jnp.concatenate([qkv_grad[0], qkv_grad[1], qkv_grad[2]], 1)
+    qkv_grad = attention_backward(qkv, heads_grad, heads_full, lse, bounds, starts, size)
     one_part = mm_nt(qkv_grad, proj_full)
     gain_one_grad = jnp.sum(one_part * x_all * scale_all, axis=0)
     one_grad = pair_sum(one_part)
@@ -381,10 +735,15 @@
     )
 
     dense = jnp.concatenate([proj_grad, out_w_grad], 1).astype(half)
+    dense, grads_got = lax.optimization_barrier((dense, grads_got))
     dense = lax.all_to_all(dense.reshape(members, d_rows, 4 * hh), "dp", 0, 0, tiled=True)
     dense = jnp.sum(dense.astype(single), axis=0)
     proj_shard = dense[:, : 3 * hh].reshape(d_rows, 3, hh).transpose(1, 0, 2)
     outw_shard = dense[:, 3 * hh :]
+
+    expert_shard = jnp.sum(
+        grads_got.reshape((groups, EXPERTS_FF) + grads_got.shape[1:]).astype(single), axis=0
+    )
 
     by_feature = jnp.concatenate(
         [gain_one_grad[:, None], gain_two_grad[:, None], const_vec_grad.T, router_grad], 1

time: 881 us -> 590 us (0.67)
  Pallas kernels: 0 us -> 295 us
  matrix products: 325 us -> 86 us
  waiting for transfers between devices: 271 us -> 62 us
  other arithmetic: 130 us -> 52 us
  starting transfers between devices: 54.1 us -> 32.3 us
  local copies, waits for them, and re-layouts: 74 us -> 52.5 us
  between operations: 16.4 us -> 2.06 us
    pallas_call x0 -> x6, Pallas kernels: none -> 295 us  [the longest x2 123 us: exchange(): pl.pallas_call(functools.partial(exchange_kernel, count), out_shape=[jax....]
    dot_general x24 -> x0, matrix products: 150 us -> none  [the longest x4 43.3 us: attention_backward(): jnp.einsum('qhd,khd->hqk', heads_grad[first:last], values_all[:last], pre...]
    all_gather x1 -> x0, waiting for transfers between devices: 108 us -> none  [per_device(): full_pack = lax.all_gather(pack, 'dp', axis=0, tiled=True)]
    all_to_all x1, waiting for transfers between devices: 66.4 us -> 14.1 us  [per_device(): grads_got = lax.all_to_all(grads_sent, 'dp', 0, 0, tiled=True)]
    convert_element_type x9 -> x2, other arithmetic: 56.4 us -> 6.39 us  [the longest x1 6.22 us: per_device(): (grads_own.astype(single) + swap(grads_other).astype(single)).astype(half)]
    all_to_all x4 -> x0, waiting for transfers between devices: 43.5 us -> none  [exchange(): lax.all_to_all(blocks, 'dp', 0, 0, axis_index_groups=cubes, tiled=True)]
    dot_general x9 -> x6, matrix products: 65.2 us -> 26 us  [mm(): return jnp.dot(a, b, preferred_element_type=single)]
    all_to_all x1, waiting for transfers between devices: 44.2 us -> 12.5 us  [per_device(): lax.all_to_all(dense.reshape(members, d_rows, 4 * hh), 'dp', 0, 0, tiled=...]
  transfers between devices with their start and end apart: 23 -> 18, of which waited for: 9 -> 5; matrix products, arithmetic and copies ran while one was open for 48% -> 27% of each run, Pallas kernels for 0% -> 25%
where the time goes in v2:
time: 590 us; the launch traced here: 582 us
  Pallas kernels  295 us (50%)
  matrix products  86 us (15%)
  waiting for transfers between devices  62 us (11%)
  local copies, waits for them, and re-layouts  52.5 us (9%)
  other arithmetic  52 us (9%)
  starting transfers between devices  32.3 us (5%)
    pallas_call x2, Pallas kernels, exchange(): pl.pallas_call(functools.partial(exchange_kernel, count), out_shape=[jax....  123 us
    pallas_call x1, Pallas kernels, expert_step(): pl.pallas_call(functools.partial(expert_kernel, padded), grid=(ff // bloc...  58.1 us
    pallas_call x1, Pallas kernels, attention_backward(): pl.pallas_call(functools.partial(bwd_kernel, heads), grid_spec=pltpu.Pref...  48.8 us
    pallas_call x1, Pallas kernels, gather_all(): pl.pallas_call(functools.partial(gather_kernel, members, low), out_shape=...  32.8 us
    pallas_call x1, Pallas kernels, attention_forward(): pl.pallas_call(functools.partial(fwd_kernel, heads), grid_spec=pltpu.Pref...  32.5 us
    all_to_all x1, waiting for transfers between devices, per_device(): my_weight = lax.all_to_all(sent_weight, 'dp', 0, 0, tiled=True)  31.5 us
    unnamed x121, local copies, waits for them, and re-layouts  30 us
    dot_general x5, matrix products, mm_tn(): lax.dot_general(a, b, (((0,), (0,)), ((), ())), preferred_element_type=si...  27.8 us
  transfers between devices with their start and end apart: 18, of which 5 were waited for; matrix products, arithmetic and copies ran while one was open for 27% of the time, Pallas kernels for 25%

profile of v2, /device:TPU:12, one launch (start us, length us, event | category | flops | bytes accessed | tf_op | source)
XLA Modules:
  0.0 582.3 jit_solution(17294345199927451257)
XLA Ops:
  5.6 32.8 %gather_all.1 = bf16[16,48,1664]{2,1,0:T(8,128)(2,1)} custom-call(bf16[48,1664]{1,0:T(8,128)(2,1)} %pad.20.x_ref), custom_call_target="tpu_custom_call" | custom-call | tf_op jit(solution)/shard_map/gather_all/pallas_call | solution.py:365
  38.4 2.9 broadcast_in_dim.44
  41.4 6.6 %all-to-all-start = ((bf16[16,3,48,1024]{3,2,1,0:T(8,128)(2,1)}), bf16[16,3,48,1024]{3,2,1,0:T(8,128)(2,1)}, u32[]{:S(2)}, u32[]{:S(2)}) async-start(bf16[16,3,48,1024]{3,2,1,0:T(8,128)(2,1)} %bitcast.229), calls=%async_computation | async-start | bytes 9437184 | tf_op jit(solution)/shard_map/all_to_all | solution.py:601
  49.4 1.7 copy.151
  51.7 1.9 slice.216
  54.1 1.7 slice_convert_fusion
  55.8 1.1 copy.190
  57.6 1.3 copy.149.start_ref
  59.6 4.2 broadcast_select_fusion.3
  64.5 2.2 copy-done.19
  66.6 6.6 %convolution_convert_fusion.q_ref.k_ref.v_ref = bf16[2048,1152]{1,0:T(8,128)(2,1)} fusion(bf16[768,1664]{1,0:T(8,128)(2,1)S(1)} %bitcast.238, f32[768]{0:T(1024)S(1)} %get-tuple-element.110, f32[2048]{0:T(1024)S(1)} %add_rsqrt_fusion, bf16[1024,768]{0,1:T(8,128)(2,1)S(1)} %get-tuple-element.150, bf16[1024,768]{0,1:T(8,128)(2,1)S(1)} %get-tuple-element.151), kind=kOutput, calls=%fused_computation.9 | convolution fusion | flops 3637248000 | bytes 9646080 | tf_op jit(solution)/shard_map/dot_general | solution.py:38
  73.3 32.5 %shard_map.195 = (f32[2048,384]{1,0:T(8,128)S(1)}, f32[2048,128]{1,0:T(8,128)S(1)}) custom-call(s32[4,8]{1,0:T(4,128)S(1)} %pad_add_fusion.4.bounds, bf16[2048,1152]{1,0:T(8,128)(2,1)} %convolution_convert_fusion.q_ref.k_ref.v_ref, bf16[2048,1152]{1,0:T(8,128)(2,1)} %convolution_convert_fusion.q_ref.k_ref.v_ref, ...), custom_call_target="tpu_custom_call" | custom-call | flops 12884901888 | bytes 12582912 | tf_op jit(solution)/shard_map/pallas_call | solution.py:176
  105.9 1.2 constant_dynamic-slice_fusion
  107.6 2.4 fusion.53
  110.0 2.3 fusion.61
  112.3 2.5 multiply_reduce_fusion.2
  115.5 1.0 copy-done.4
  116.5 1.2 copy-done.7
  117.7 1.3 fusion.69
  119.4 31.5 %all-to-all-done.own_ref = bf16[16,3,48,1024]{3,2,1,0:T(8,128)(2,1)} async-done(((bf16[16,3,48,1024]{3,2,1,0:T(8,128)(2,1)}), bf16[16,3,48,1024]{3,2,1,0:T(8,128)(2,1)}, u32[]{:S(2)}, u32[]{:S(2)}) %all-to-all-start) | async-done | bytes 4718624 | tf_op jit(solution)/shard_map/all_to_all | solution.py:601
  151.1 2.9 fusion.42
  155.7 1.7 bitcast_compare_fusion
  157.4 6.0 %convolution_convert_fusion.1 = bf16[1408,768]{1,0:T(8,128)(2,1)} fusion(pred[1408,2048]{1,0:T(32,128)(4,1)S(1)} %bitcast_compare_fusion, bf16[1024,768]{0,1:T(8,128)(2,1)S(1)} %copy-done.35, bf16[1024,768]{0,1:T(8,128)(2,1)S(1)} %copy-done.34), kind=kOutput, calls=%fused_computation.38 | convolution fusion | flops 4436557824 | bytes 8192000 | tf_op jit(solution)/shard_map/dot_general | solution.py:38
  164.3 3.1 broadcast_select_fusion.1
  167.4 6.4 %fusion.17 = bf16[1408,896]{1,0:T(8,128)(2,1)S(1)} fusion(pred[1408,2048]{1,0:T(32,128)(4,1)S(1)} %copy-done.31, bf16[1024,896]{0,1:T(8,128)(2,1)S(1)} %get-tuple-element.119, bf16[1024,896]{0,1:T(8,128)(2,1)S(1)} %get-tuple-element.118), kind=kOutput, calls=%fused_computation.37 | convolution fusion | flops 5175984128 | bytes 9076736 | tf_op jit(solution)/shard_map/dot_general | solution.py:38
  173.8 1.6 copy-done.32
  175.9 3.2 slice_select_fusion.refs_0_
  179.1 63.2 %exchange_1.1 = (bf16[8,176,768]{2,1,0:T(8,128)(2,1)}, bf16[8,176,768]{2,1,0:T(8,128)(2,1)}) custom-call(bf16[8,176,768]{2,1,0:T(8,128)(2,1)} %slice_select_fusion.refs_0_, bf16[8,176,768]{2,1,0:T(8,128)(2,1)} %bitcast.244), custom_call_target="tpu_custom_call" | custom-call | tf_op jit(solution)/shard_map/exchange_1/pallas_call | solution.py:415
  242.3 58.1 %expert_step.1 = (bf16[8,176,768]{2,1,0:T(8,128)(2,1)}, bf16[8,176,768]{2,1,0:T(8,128)(2,1)}, bf16[16,3,48,1024]{3,2,1,0:T(8,128)(2,1)}, bf16[16,3,48,1024]{3,2,1,0:T(8,128)(2,1)}) custom-call(bf16[8,176,768]{2,1,0:T(8,128)(2,1)} %get-tuple-element.28.x_ref, bf16[8,176,768]{2,1,0:T(8,128)(2,1)} %get-tuple-element.29.dy_ref, ...), custom_call_target="tpu_custom_call" | custom-call | flops 39862665216 | bytes 27525120 | tf_op jit(solution)/shard_map/expert_step/pallas_call | solution.py:523
  300.4 60.1 %exchange_2.1 = (bf16[8,176,768]{2,1,0:T(8,128)(2,1)}, bf16[8,176,768]{2,1,0:T(8,128)(2,1)}) custom-call(bf16[8,176,768]{2,1,0:T(8,128)(2,1)} %get-tuple-element.31.refs_0_, bf16[8,176,768]{2,1,0:T(8,128)(2,1)} %get-tuple-element.32.refs_1_), custom_call_target="tpu_custom_call" | custom-call | tf_op jit(solution)/shard_map/exchange_2/pallas_call | solution.py:415
  362.4 8.1 %fusion.10 = f32[2048,896]{0,1:T(8,128)S(1)} fusion(s32[8,2048]{1,0:T(8,128)} %copy-done.41, bf16[8,176,16]{2,1,0:T(8,128)(2,1)} %copy.156, bf16[8,176,768]{2,1,0:T(8,128)(2,1)} %get-tuple-element.36), kind=kOutput, calls=%fused_computation.26 | convolution fusion | flops 5177835520 | bytes 9613312 | tf_op jit(solution)/shard_map/dot_general | solution.py:46
  370.5 2.9 copy-done.29
  373.4 1.6 dynamic-slice_convert_fusion
  375.8 2.3 fusion.56
  378.1 1.2 collective-permute-done.8
  379.2 3.5 convert_add_fusion.2
  382.7 1.8 copy-done.18
  384.8 6.2 %add_convert_fusion = bf16[16,3,48,1024]{3,2,1,0:T(8,128)(2,1)} fusion(bf16[16,3,48,1024]{3,2,1,0:T(8,128)(2,1)} %collective-permute-done.12, bf16[16,3,48,1024]{3,2,1,0:T(8,128)(2,1)S(1)} %bitcast.241), kind=kLoop, calls=%fused_computation.8 | loop fusion | flops 9437184 | bytes 14155776 | tf_op jit(solution)/shard_map/convert_element_type | solution.py:659
  391.0 8.7 %all-to-all-start.1 = ((bf16[16,3,48,1024]{3,2,1,0:T(8,128)(2,1)}), bf16[16,3,48,1024]{3,2,1,0:T(8,128)(2,1)}, u32[]{:S(2)}, u32[]{:S(2)}) async-start(bf16[16,3,48,1024]{3,2,1,0:T(8,128)(2,1)} %add_convert_fusion), calls=%async_computation.1 | async-start | bytes 9437184 | tf_op jit(solution)/shard_map/all_to_all | solution.py:662
  399.8 5.9 %multiply_reduce_fusion = (f32[768]{0:T(1024)S(1)}, f32[1024]{0:T(1024)S(1)}, f32[1024,768]{0,1:T(8,128)S(1)}) fusion(f32[1024,768]{0,1:T(8,128)} %copy-done.4, f32[1024]{0:T(1024)S(1)} %add_rsqrt_fusion.1, f32[768]{0:T(1024)S(1)} %get-tuple-element.109, bf16[768,1664]{1,0:T(8,128)(2,1)} %bitcast.235, f32[1024,4]{0,1:T(4,128)S(1)} %divide_multiply_fusion, ...), kind=kOutput, calls=%fused_computation.58 | convolution fusion | flops 158873856 | bytes 11290624 | tf_op jit(solution)/shard_map/dot_general | solution.py:708
  407.4 3.5 convolution_convert_fusion.5
  411.0 3.0 convolution_convert_fusion.3
  414.9 2.7 fusion.88
  417.6 2.7 convolution_convert_fusion.4
  420.4 2.9 add_convert_fusion.1
  424.5 48.8 %shard_map.196 = bf16[2048,1152]{1,0:T(8,128)(2,1)} custom-call(s32[4,8]{1,0:T(4,128)S(1)} %pad_add_fusion.4.bounds, bf16[2048,1152]{1,0:T(8,128)(2,1)} %convolution_convert_fusion.q_ref.k_ref.v_ref, bf16[2048,1152]{1,0:T(8,128)(2,1)} %convolution_convert_fusion.q_ref.k_ref.v_ref, bf16[2048,1152]{1,0:T(8,128)(2,1)} %convolution_convert_fusion.q_ref.k_ref.v_ref, ...), custom_call_target="tpu_custom_call" | custom-call | flops 32212254720 | bytes 15728640 | tf_op jit(solution)/shard_map/pallas_call | solution.py:276
  473.4 8.8 %fusion.6 = (f32[768]{0:T(1024)S(1)}, f32[2048,768]{0,1:T(8,128)}) fusion(f32[2048]{0:T(1024)S(1)} %copy-done.47, bf16[1024,768]{0,1:T(8,128)(2,1)S(1)} %copy-done.22, bf16[1024,768]{0,1:T(8,128)(2,1)S(1)} %copy-done.25, bf16[2048,1152]{1,0:T(8,128)(2,1)} %shard_map.196, bf16[768,1664]{1,0:T(8,128)(2,1)S(1)} %bitcast.239), kind=kOutput, calls=%fused_computation.14 | convolution fusion | flops 3634887936 | bytes 15936512 | tf_op jit(solution)/shard_map/dot_general | solution.py:42
  483.1 1.2 reshape.662
  484.5 7.9 %convolution_convert_fusion.2 = bf16[768,1152]{1,0:T(8,128)(2,1)} fusion(bf16[2048,1152]{1,0:T(8,128)(2,1)} %shard_map.196, f32[768]{0:T(1024)S(1)} %copy-done.45, f32[2048]{0:T(1024)S(1)} %copy-done.47, bf16[1024,768]{0,1:T(8,128)(2,1)S(1)} %copy-done.23, bf16[1024,768]{0,1:T(8,128)(2,1)S(1)} %copy-done.26), kind=kOutput, calls=%fused_computation.39 | convolution fusion | flops 3635773440 | bytes 9645056 | tf_op jit(solution)/shard_map/dot_general | solution.py:46
  493.1 14.1 %all-to-all-done.1 = bf16[16,3,48,1024]{3,2,1,0:T(8,128)(2,1)} async-done(((bf16[16,3,48,1024]{3,2,1,0:T(8,128)(2,1)}), bf16[16,3,48,1024]{3,2,1,0:T(8,128)(2,1)}, u32[]{:S(2)}, u32[]{:S(2)}) %all-to-all-start.1) | async-done | bytes 4718624 | tf_op jit(solution)/shard_map/all_to_all | solution.py:662
  507.2 6.6 %all-to-all-start.3 = ((f32[16,16,128]{2,1,0:T(8,128)}), f32[16,16,128]{2,1,0:T(8,128)S(1)}, u32[]{:S(2)}, u32[]{:S(2)}) async-start(f32[16,16,128]{2,1,0:T(8,128)} %bitcast_add_fusion), calls=%async_computation.3 | async-start | bytes 262144 | tf_op jit(solution)/shard_map/all_to_all | solution.py:759
  513.9 3.2 pad_maximum_fusion.1
  517.1 2.7 all-to-all-done.3
  519.7 6.5 %all-to-all-start.2 = ((bf16[16,48,1536]{2,1,0:T(8,128)(2,1)}), bf16[16,48,1536]{2,1,0:T(8,128)(2,1)}, u32[]{:S(2)}, u32[]{:S(2)}) async-start(bf16[16,48,1536]{2,1,0:T(8,128)(2,1)} %bitcast.48), calls=%async_computation.2 | async-start | bytes 4718592 | tf_op jit(solution)/shard_map/all_to_all | solution.py:739
  526.3 5.4 fusion.11
  532.1 3.5 dynamic-slice_convert_fusion.1
  535.9 4.4 fusion.50
  540.2 2.6 copy.167
  546.7 3.6 fusion.30
  551.4 5.0 fusion.29
  556.4 3.5 copy.168
  559.9 6.2 %convert_reduce_fusion = f32[8,3,48,1024]{3,2,1,0:T(8,128)} fusion(bf16[2,8,3,48,1024]{4,3,2,1,0:T(8,128)(2,1)} %bitcast.58), kind=kLoop, calls=%fused_computation.7 | loop fusion | flops 3538944 | bytes 9437184 | tf_op jit(solution)/shard_map/reduce_sum | solution.py:744
  566.2 12.5 %all-to-all-done.2 = bf16[16,48,1536]{2,1,0:T(8,128)(2,1)} async-done(((bf16[16,48,1536]{2,1,0:T(8,128)(2,1)}), bf16[16,48,1536]{2,1,0:T(8,128)(2,1)}, u32[]{:S(2)}, u32[]{:S(2)}) %all-to-all-start.2) | async-done | bytes 2359328 | tf_op jit(solution)/shard_map/all_to_all | solution.py:739
  578.7 2.0 convert_reduce_fusion.1
  (249 shorter events, 29.5 us)
Async XLA Ops:
  0.6 118.4 %copy-start = (f32[12,12]{1,0:T(8,128)S(1)}, f32[12,12]{1,0:T(8,128)}, u32[]{:S(2)}) copy-start(f32[12,12]{1,0:T(8,128)} %param.23) | copy-start | bytes 1732
  0.7 37.8 %copy-start.33 = (bf16[8,3,48,1024]{3,2,1,0:T(8,128)(2,1)S(1)}, bf16[8,3,48,1024]{3,2,1,0:T(8,128)(2,1)}, u32[]{:S(2)}) copy-start(bf16[8,3,48,1024]{3,2,1,0:T(8,128)(2,1)} %param.20) | copy-start | bytes 7077892
  41.3 6.6 %copy-start.40 = (s32[1,1024,2]{1,2,0:T(2,128)S(1)}, s32[1,1024,2]{1,2,0:T(2,128)}, u32[]{:S(2)}) copy-start(s32[1,1024,2]{1,2,0:T(2,128)} %param.14) | copy-start | bytes 24580
  41.4 6.6 %copy-start.48 = (s32[1,1024]{1,0:T(1,128)S(1)}, s32[1,1024]{1,0:T(1,128)}, u32[]{:S(2)}) copy-start(s32[1,1024]{1,0:T(1,128)} %param.13) | copy-start | bytes 12292
  41.4 6.7 %copy-start.38 = (bf16[1,1024,768]{2,1,0:T(8,128)(2,1)S(1)}, bf16[1,1024,768]{2,1,0:T(8,128)(2,1)}, u32[]{:S(2)}) copy-start(bf16[1,1024,768]{2,1,0:T(8,128)(2,1)} %param.12) | copy-start | bytes 4718596
  41.4 109.6 %all-to-all-start = ((bf16[16,3,48,1024]{3,2,1,0:T(8,128)(2,1)}), bf16[16,3,48,1024]{3,2,1,0:T(8,128)(2,1)}, u32[]{:S(2)}, u32[]{:S(2)}) async-start(bf16[16,3,48,1024]{3,2,1,0:T(8,128)(2,1)} %bitcast.229), calls=%async_computation | async-start | bytes 9437184 | tf_op jit(solution)/shard_map/all_to_all | solution.py:601
  48.0 9.0 %collective-permute-start = (s32[1024,3]{0,1:T(4,128)S(1)}, s32[1024,3]{0,1:T(4,128)S(1)}, u32[]{:S(2)}, u32[]{:S(2)}) collective-permute-start(s32[1024,3]{0,1:T(4,128)S(1)} %pad_add_fusion), channel_id=1, source_target_pairs={{0,1},{1,0},{2,3},{3,2},{4,5},{5,4},{6,7},{7,6},{8,9},{9,8},{10,11... | collective-permute-start | bytes 36872 | tf_op jit(solution)/shard_map/ppermute | solution.py:50
  48.8 10.7 %copy-start.13 = (bf16[1,1024,768]{1,2,0:T(8,128)(2,1)}, bf16[1,1024,768]{1,2,0:T(8,128)(2,1)S(1)}, u32[]{:S(2)}) copy-start(bf16[1,1024,768]{1,2,0:T(8,128)(2,1)S(1)} %copy.143) | copy-start | bytes 4718596
  48.9 10.7 %collective-permute-start.1 = (bf16[1024,768]{0,1:T(8,128)(2,1)S(1)}, bf16[1024,768]{0,1:T(8,128)(2,1)}, u32[]{:S(2)}, u32[]{:S(2)}) collective-permute-start(bf16[1024,768]{0,1:T(8,128)(2,1)S(1)} %bitcast.228), channel_id=1, source_target_pairs={{0,1},{1,0},{2,3},{3,2},{4,5},{5,4},{6,7},{7,6},{8,9},{9,8},{10,11... | collective-permute-start | bytes 4718600 | tf_op jit(solution)/shard_map/ppermute | solution.py:50
  51.1 12.7 %copy-start.9 = (bf16[1,1024,768]{1,2,0:T(8,128)(2,1)}, bf16[1,1024,768]{1,2,0:T(8,128)(2,1)S(1)}, u32[]{:S(2)}) copy-start(bf16[1,1024,768]{1,2,0:T(8,128)(2,1)S(1)} %copy.151) | copy-start | bytes 4718596
  51.1 8.4 %collective-permute-start.5 = (bf16[1024,768]{0,1:T(8,128)(2,1)S(1)}, bf16[1024,768]{0,1:T(8,128)(2,1)}, u32[]{:S(2)}, u32[]{:S(2)}) collective-permute-start(bf16[1024,768]{0,1:T(8,128)(2,1)S(1)} %bitcast.227), channel_id=1, source_target_pairs={{0,1},{1,0},{2,3},{3,2},{4,5},{5,4},{6,7},{7,6},{8,9},{9,8},{10,11... | collective-permute-start | bytes 4718600 | tf_op jit(solution)/shard_map/ppermute | solution.py:50
  53.6 58.7 %collective-permute-start.3 = (bf16[768,384]{1,0:T(8,128)(2,1)}, bf16[768,384]{1,0:T(8,128)(2,1)}, u32[]{:S(2)}, u32[]{:S(2)}) collective-permute-start(bf16[768,384]{1,0:T(8,128)(2,1)} %slice.216), channel_id=1, source_target_pairs={{0,1},{1,0},{2,3},{3,2},{4,5},{5,4},{6,7},{7,6},{8,9},{9,8},{10,11... | collective-permute-start | bytes 1769480 | tf_op jit(solution)/shard_map/ppermute | solution.py:50
  57.0 7.5 %copy-start.44 = (f32[768]{0:T(1024)}, f32[768]{0:T(1024)S(1)}, u32[]{:S(2)}) copy-start(f32[768]{0:T(1024)S(1)} %get-tuple-element.110) | copy-start | bytes 9220
  63.8 9.5 %copy-start.21 = (bf16[1024,768]{0,1:T(8,128)(2,1)}, bf16[1024,768]{0,1:T(8,128)(2,1)S(1)}, u32[]{:S(2)}) copy-start(bf16[1024,768]{0,1:T(8,128)(2,1)S(1)} %get-tuple-element.150) | copy-start | bytes 4718596
  63.8 9.5 %copy-start.24 = (bf16[1024,768]{0,1:T(8,128)(2,1)}, bf16[1024,768]{0,1:T(8,128)(2,1)S(1)}, u32[]{:S(2)}) copy-start(bf16[1024,768]{0,1:T(8,128)(2,1)S(1)} %get-tuple-element.151) | copy-start | bytes 4718596
  63.8 2.9 copy-start.19
  64.5 8.8 %copy-start.46 = (f32[2048]{0:T(1024)}, f32[2048]{0:T(1024)S(1)}, u32[]{:S(2)}) copy-start(f32[2048]{0:T(1024)S(1)} %add_rsqrt_fusion) | copy-start | bytes 24580
  66.6 6.6 %copy-start.1 = (s32[2048,1]{1,0:T(8,128)S(1)}, s32[2048,1]{1,0:T(8,128)}, u32[]{:S(2)}) copy-start(s32[2048,1]{1,0:T(8,128)} %copy.149.start_ref) | copy-start | bytes 24580
  107.1 5.2 collective-permute-start.2
  107.6 4.7 copy-start.14
  112.3 2.5 copy-start.10
  114.8 4.2 copy-start.39
  150.9 91.4 %collective-permute-start.6 = (bf16[16,3,48,1024]{3,2,1,0:T(8,128)(2,1)}, bf16[16,3,48,1024]{3,2,1,0:T(8,128)(2,1)}, u32[]{:S(2)}, u32[]{:S(2)}) collective-permute-start(bf16[16,3,48,1024]{3,2,1,0:T(8,128)(2,1)} %all-to-all-done.own_ref), channel_id=1, source_target_pairs={{0,1},{1,0},{2,3},{3,2},{4,5},{5,4},{6,7},{7,6},{8,9},{9,8},{10,11... | collective-permute-start | bytes 14155784 | tf_op jit(solution)/shard_map/ppermute | solution.py:50
  154.0 10.3 %collective-permute-start.4 = (bf16[1024,896]{0,1:T(8,128)(2,1)}, bf16[1024,896]{0,1:T(8,128)(2,1)}, u32[]{:S(2)}, u32[]{:S(2)}) collective-permute-start(bf16[1024,896]{0,1:T(8,128)(2,1)} %fusion.42), channel_id=1, source_target_pairs={{0,1},{1,0},{2,3},{3,2},{4,5},{5,4},{6,7},{7,6},{8,9},{9,8},{10,11... | collective-permute-start | bytes 5505032 | tf_op jit(solution)/shard_map/ppermute | solution.py:50
  154.6 2.8 copy-start.34
  154.6 2.8 copy-start.35
  157.4 6.1 %copy-start.30 = (pred[1408,2048]{1,0:T(32,128)(4,1)}, pred[1408,2048]{1,0:T(32,128)(4,1)S(1)}, u32[]{:S(2)}) copy-start(pred[1408,2048]{1,0:T(32,128)(4,1)S(1)} %bitcast_compare_fusion) | copy-start | bytes 8650756
  164.3 3.1 copy-start.31
  362.4 22.4 %collective-permute-start.12 = (bf16[16,3,48,1024]{3,2,1,0:T(8,128)(2,1)}, bf16[16,3,48,1024]{3,2,1,0:T(8,128)(2,1)}, u32[]{:S(2)}, u32[]{:S(2)}) collective-permute-start(bf16[16,3,48,1024]{3,2,1,0:T(8,128)(2,1)} %get-tuple-element.39), channel_id=1, source_target_pairs={{0,1},{1,0},{2,3},{3,2},{4,5},{5,4},{6,7},{7,6},{8,9},{9,8},{10,11... | collective-permute-start | bytes 14155784 | tf_op jit(solution)/shard_map/ppermute | solution.py:50
  370.4 2.9 copy-start.29
  373.4 2.4 copy-start.43
  374.9 4.3 collective-permute-start.8
  375.8 9.0 %slice-start = ((s8[4718592]{0:T(1024)(128)(4,1)}), s8[4194304]{0:T(1024)(128)(4,1)S(1)}, s32[]{:S(2)}) async-start(s8[4718592]{0:T(1024)(128)(4,1)} %bitcast.240), calls=%async_computation.4 | async-start | bytes 8388608
  378.0 6.7 %slice-start.1 = ((s8[4718592]{0:T(1024)(128)(4,1)}), s8[524288]{0:T(1024)(128)(4,1)S(1)}, s32[]{:S(2)}) async-start(s8[4718592]{0:T(1024)(128)(4,1)} %bitcast.240), calls=%async_computation.5 | async-start | bytes 1048576
  382.7 1.8 copy-start.18
  391.0 116.2 %all-to-all-start.1 = ((bf16[16,3,48,1024]{3,2,1,0:T(8,128)(2,1)}), bf16[16,3,48,1024]{3,2,1,0:T(8,128)(2,1)}, u32[]{:S(2)}, u32[]{:S(2)}) async-start(bf16[16,3,48,1024]{3,2,1,0:T(8,128)(2,1)} %add_convert_fusion), calls=%async_computation.1 | async-start | bytes 9437184 | tf_op jit(solution)/shard_map/all_to_all | solution.py:662
  399.8 6.0 %copy-start.5 = (f32[1024,768]{0,1:T(8,128)S(1)}, f32[1024,768]{0,1:T(8,128)}, u32[]{:S(2)}) copy-start(f32[1024,768]{0,1:T(8,128)} %copy-done.4) | copy-start | bytes 9437188
  399.8 6.0 %copy-start.11 = (bf16[1,1024,768]{1,2,0:T(8,128)(2,1)S(1)}, bf16[1,1024,768]{1,2,0:T(8,128)(2,1)}, u32[]{:S(2)}) copy-start(bf16[1,1024,768]{1,2,0:T(8,128)(2,1)} %copy-done.9) | copy-start | bytes 4718596
  405.7 1.7 copy-start.16
  407.4 3.6 copy-start.36
  410.9 9.4 %collective-permute-start.11 = (bf16[768,384]{1,0:T(8,128)(2,1)}, bf16[768,384]{1,0:T(8,128)(2,1)}, u32[]{:S(2)}, u32[]{:S(2)}) collective-permute-start(bf16[768,384]{1,0:T(8,128)(2,1)} %convolution_convert_fusion.5), channel_id=1, source_target_pairs={{0,1},{1,0},{2,3},{3,2},{4,5},{5,4},{6,7},{7,6},{8,9},{9,8},{10,11... | collective-permute-start | bytes 1769480 | tf_op jit(solution)/shard_map/ppermute | solution.py:50
  414.4 8.8 %collective-permute-start.9 = (bf16[1024,384]{1,0:T(8,128)(2,1)}, bf16[1024,384]{1,0:T(8,128)(2,1)S(1)}, u32[]{:S(2)}, u32[]{:S(2)}) collective-permute-start(bf16[1024,384]{1,0:T(8,128)(2,1)} %convolution_convert_fusion.3), channel_id=1, source_target_pairs={{0,1},{1,0},{2,3},{3,2},{4,5},{5,4},{6,7},{7,6},{8,9},{9,8},{10,11... | collective-permute-start | bytes 2359304 | tf_op jit(solution)/shard_map/ppermute | solution.py:50
  417.6 2.7 copy-start.28
  417.6 2.8 copy-start.37
  424.5 48.8 %copy-start.20 = (bf16[16,48,1664]{2,1,0:T(8,128)(2,1)S(1)}, bf16[16,48,1664]{2,1,0:T(8,128)(2,1)}, u32[]{:S(2)}) copy-start(bf16[16,48,1664]{2,1,0:T(8,128)(2,1)} %gather_all.1) | copy-start | bytes 7667716
  424.5 48.8 %copy-start.22 = (bf16[1024,768]{0,1:T(8,128)(2,1)S(1)}, bf16[1024,768]{0,1:T(8,128)(2,1)}, u32[]{:S(2)}) copy-start(bf16[1024,768]{0,1:T(8,128)(2,1)} %copy-done.21) | copy-start | bytes 4718596
  424.5 48.9 %copy-start.25 = (bf16[1024,768]{0,1:T(8,128)(2,1)S(1)}, bf16[1024,768]{0,1:T(8,128)(2,1)}, u32[]{:S(2)}) copy-start(bf16[1024,768]{0,1:T(8,128)(2,1)} %copy-done.24) | copy-start | bytes 4718596
  424.5 48.9 %copy-start.47 = (f32[2048]{0:T(1024)S(1)}, f32[2048]{0:T(1024)}, u32[]{:S(2)}) copy-start(f32[2048]{0:T(1024)} %copy-done.46) | copy-start | bytes 24580
  473.3 11.2 %copy-start.23 = (bf16[1024,768]{0,1:T(8,128)(2,1)S(1)}, bf16[1024,768]{0,1:T(8,128)(2,1)}, u32[]{:S(2)}) copy-start(bf16[1024,768]{0,1:T(8,128)(2,1)} %copy-done.21) | copy-start | bytes 4718596
  473.3 11.2 %copy-start.26 = (bf16[1024,768]{0,1:T(8,128)(2,1)S(1)}, bf16[1024,768]{0,1:T(8,128)(2,1)}, u32[]{:S(2)}) copy-start(bf16[1024,768]{0,1:T(8,128)(2,1)} %copy-done.24) | copy-start | bytes 4718596
  473.4 11.2 %copy-start.45 = (f32[768]{0:T(1024)S(1)}, f32[768]{0:T(1024)}, u32[]{:S(2)}) copy-start(f32[768]{0:T(1024)} %copy-done.44) | copy-start | bytes 9220
  484.4 8.1 %collective-permute-start.13 = (f32[16,16,128]{2,1,0:T(8,128)S(1)}, f32[16,16,128]{2,1,0:T(8,128)S(1)}, u32[]{:S(2)}, u32[]{:S(2)}) collective-permute-start(f32[16,16,128]{2,1,0:T(8,128)S(1)} %bitcast.246), channel_id=1, source_target_pairs={{0,1},{1,0},{2,3},{3,2},{4,5},{5,4},{6,7},{7,6},{8,9},{9,8},{10,11... | collective-permute-start | bytes 393224 | tf_op jit(solution)/shard_map/ppermute | solution.py:50
  507.2 12.5 %all-to-all-start.3 = ((f32[16,16,128]{2,1,0:T(8,128)}), f32[16,16,128]{2,1,0:T(8,128)S(1)}, u32[]{:S(2)}, u32[]{:S(2)}) async-start(f32[16,16,128]{2,1,0:T(8,128)} %bitcast_add_fusion), calls=%async_computation.3 | async-start | bytes 262144 | tf_op jit(solution)/shard_map/all_to_all | solution.py:759
  517.1 9.2 %copy-start.42 = (s32[8,2048]{1,0:T(8,128)S(1)}, s32[8,2048]{1,0:T(8,128)}, u32[]{:S(2)}) copy-start(s32[8,2048]{1,0:T(8,128)} %copy-done.41) | copy-start | bytes 196612
  517.1 9.2 %copy-start.49 = (bf16[8,176,768]{2,1,0:T(8,128)(2,1)S(1)}, bf16[8,176,768]{2,1,0:T(8,128)(2,1)}, u32[]{:S(2)}) copy-start(bf16[8,176,768]{2,1,0:T(8,128)(2,1)} %get-tuple-element.33) | copy-start | bytes 6488068
  519.7 58.9 %all-to-all-start.2 = ((bf16[16,48,1536]{2,1,0:T(8,128)(2,1)}), bf16[16,48,1536]{2,1,0:T(8,128)(2,1)}, u32[]{:S(2)}, u32[]{:S(2)}) async-start(bf16[16,48,1536]{2,1,0:T(8,128)(2,1)} %bitcast.48), calls=%async_computation.2 | async-start | bytes 4718592 | tf_op jit(solution)/shard_map/all_to_all | solution.py:739
  531.7 4.1 copy-start.6
  531.7 4.1 copy-start.8
  532.0 3.9 collective-permute-start.7
  535.5 11.1 %collective-permute-start.10 = (bf16[1024,768]{0,1:T(8,128)(2,1)}, bf16[1024,768]{0,1:T(8,128)(2,1)}, u32[]{:S(2)}, u32[]{:S(2)}) collective-permute-start(bf16[1024,768]{0,1:T(8,128)(2,1)} %dynamic-slice_convert_fusion.1), channel_id=1, source_target_pairs={{0,1},{1,0},{2,3},{3,2},{4,5},{5,4},{6,7},{7,6},{8,9},{9,8},{10,11... | collective-permute-start | bytes 4718600 | tf_op jit(solution)/shard_map/ppermute | solution.py:50
  546.7 3.7 copy-start.12
  546.7 3.8 copy-start.15
  546.7 4.7 copy-start.17
  546.7 4.7 dynamic-slice-start
  (7 other events, 9.3 us)

commit v3 on v2

v3 whole, which is shorter than its diff:
```python
import functools

import jax
import jax.numpy as jnp
from jax import lax
from jax.experimental import pallas as pl
from jax.experimental.pallas import tpu as pltpu
from jax.sharding import PartitionSpec as P

HEAD_DIM = 64
EXPERTS_FF = 8
EXPERTS = 12
CAPACITY = 341


EPS = 1e-05
HIGH = lax.Precision.HIGHEST
NEG = -1e30
LANES = 128
DOCS = 8
LOG2E = 1.4426950408889634
MESH = pl.DeviceIdType.MESH
single = jnp.float32
half = jnp.bfloat16


def rms_scale(rows):
    return lax.rsqrt(jnp.mean(rows * rows, axis=-1, keepdims=True) + EPS)


def softmax_last(values):
    peak = jnp.max(values, axis=-1, keepdims=True)
    expo = jnp.exp(values - peak)
    return expo / jnp.sum(expo, axis=-1, keepdims=True)


def mm(a, b):
    return jnp.dot(a, b, preferred_element_type=single)


def mm_nt(a, b):
    return lax.dot_general(a, b, (((1,), (1,)), ((), ())), preferred_element_type=single)


def mm_tn(a, b):
    return lax.dot_general(a, b, (((0,), (0,)), ((), ())), preferred_element_type=single)


def swap(x):
    return lax.ppermute(x, "tensor", [(0, 1), (1, 0)])


def in_order(own, other):
    first = lax.axis_index("tensor") == 0
    return jnp.concatenate([jnp.where(first, own, other), jnp.where(first, other, own)], 0)


def half_of(full, which):
    count = full.shape[0] // 2
    return lax.dynamic_slice_in_dim(full, which * count, count, 0)


def pair_sum(full):
    core = lax.axis_index("tensor")
    other = swap(half_of(full, 1 - core).astype(half))
    return half_of(full, core) + other.astype(single)


def fit(seq, want):
    return want if seq % want == 0 else seq

def block_bounds(start, end, size):
    edges = start.reshape(-1, size)
    number = jnp.arange(edges.shape[0], dtype=jnp.int32)
    low = edges[:, 0] // size
    plain = jnp.clip((edges[:, -1] + size - 1) // size, low, number)
    high = end.reshape(-1, size)[:, -1] // size
    clear = jnp.sum((edges[None, :, -1] <= number[:, None] * size).astype(jnp.int32), axis=1)
    clear = jnp.clip(clear, number + 1, high + 1)
    return jnp.stack([low, plain, high, clear])


def head_lanes(h, rows):
    lane = lax.broadcasted_iota(jnp.int32, (rows, LANES), 1)
    return (lane < HEAD_DIM) if h % 2 == 0 else (lane >= HEAD_DIM)

def fwd_kernel(heads, bounds, q_ref, k_ref, v_ref, start_ref, o_ref, low_ref, lse_ref, s_ref, m_ref, l_ref, acc_ref, qm_ref):
    size = q_ref.shape[0]
    i = pl.program_id(0)
    low, plain = bounds[0, i], bounds[1, i]
    factor = LOG2E * HEAD_DIM ** -0.5
    for h in range(heads):
        pair = pl.ds(h // 2 * LANES, LANES)
        qm_ref[h] = jnp.where(head_lanes(h, size), q_ref[:, pair], 0).astype(half)
    m_ref[...] = jnp.full(m_ref.shape, NEG, single)
    l_ref[...] = jnp.zeros(l_ref.shape, single)
    acc_ref[...] = jnp.zeros(acc_ref.shape, single)

    def score(j, masked):
        rows = pl.ds(pl.multiple_of(j * size, size), size)
        if masked:
            row = i * size + lax.broadcasted_iota(jnp.int32, (size, size), 0)
            col = j * size + lax.broadcasted_iota(jnp.int32, (size, size), 1)
            allowed = (col <= row) & (col >= start_ref[...])
        for h in range(heads):
            s = mm_nt(qm_ref[h], k_ref[rows, pl.ds(h // 2 * LANES, LANES)])
            if masked:
                s = jnp.where(allowed, s, NEG)
            s_ref[h, j] = s
            m = m_ref[h]
            for c in range(size // LANES):
                m = jnp.maximum(m, s[:, c * LANES : (c + 1) * LANES])
            m_ref[h] = m

    pl.loop(low, plain)(lambda j: score(j, True))
    pl.loop(plain, i)(lambda j: score(j, False))
    score(i, True)
    for h in range(heads):
        m_ref[h] = jnp.broadcast_to(jnp.max(m_ref[h], axis=1, keepdims=True) * factor, (size, LANES))

    def gather(j):
        rows = pl.ds(pl.multiple_of(j * size, size), size)
        for h in range(heads):
            s = s_ref[h, j]
            m = m_ref[h]
            l = l_ref[h]
            parts = []
            for c in range(size // LANES):
                p = jnp.exp2(s[:, c * LANES : (c + 1) * LANES] * factor - m)
                l = l + p
                parts.append(p.astype(half))
            l_ref[h] = l
            acc_ref[h] += jnp.dot(jnp.concatenate(parts, 1), v_ref[rows, pl.ds(h // 2 * LANES, LANES)], preferred_element_type=single)

    pl.loop(low, i + 1)(gather)
    lane = lax.broadcasted_iota(jnp.int32, (size, LANES), 1)
    lse = jnp.zeros((size, LANES), single)
    for h in range(0, heads, 2):
        outs = []
        for k in (h, h + 1):
            l = jnp.sum(l_ref[k], axis=1, keepdims=True)
            outs.append(acc_ref[k] / l)
            lse = jnp.where(lane == k, m_ref[k] + jnp.log2(l), lse)
        out = jnp.where(lane < HEAD_DIM, outs[0], outs[1])
        o_ref[:, pl.ds(h // 2 * LANES, LANES)] = out
        low_ref[:, pl.ds(h // 2 * LANES, LANES)] = out.astype(half)
    lse_ref[...] = lse

def attention_forward(qkv, seg_bounds, starts, size):
    seq = qkv.shape[0]
    hh = qkv.shape[1] // 3
    heads = hh // HEAD_DIM
    return pl.pallas_call(
        functools.partial(fwd_kernel, heads),
        grid_spec=pltpu.PrefetchScalarGridSpec(
            num_scalar_prefetch=1,
            grid=(seq // size,),
            in_specs=[
                pl.BlockSpec((size, hh), lambda i, b: (i, 0)),
                pl.BlockSpec((seq, hh), lambda i, b: (0, 1)),
                pl.BlockSpec((seq, hh), lambda i, b: (0, 2)),
                pl.BlockSpec((size, 1), lambda i, b: (i, 0)),
            ],
            out_specs=[
                pl.BlockSpec((size, hh), lambda i, b: (i, 0)),
                pl.BlockSpec((size, hh), lambda i, b: (i, 0)),
                pl.BlockSpec((size, LANES), lambda i, b: (i, 0)),
            ],
            scratch_shapes=[
                pltpu.VMEM((heads, seq // size, size, size), single),
                pltpu.VMEM((heads, size, LANES), single),
                pltpu.VMEM((heads, size, LANES), single),
                pltpu.VMEM((heads, size, LANES), single),
                pltpu.VMEM((heads, size, LANES), half),
            ],
        ),
        out_shape=[
            jax.ShapeDtypeStruct((seq, hh), single),
            jax.ShapeDtypeStruct((seq, hh), half),
            jax.ShapeDtypeStruct((seq, LANES), single),
        ],
        compiler_params=pltpu.CompilerParams(vmem_limit_bytes=48 << 20),
        cost_estimate=pl.CostEstimate(flops=4 * seq * seq * LANES * heads, bytes_accessed=16 * seq * hh, transcendentals=0),
    )(seg_bounds, qkv, qkv, qkv, starts[:, None])

def bwd_kernel(
    heads, bounds, q_ref, k_ref, v_ref, do_ref, o_ref, lse_ref, start_ref, out_ref, dq_ref, dk_ref, dv_ref, stat_ref
):
    size = k_ref.shape[0]
    j = pl.program_id(0)
    high, clear = bounds[2, j], bounds[3, j]
    factor = LOG2E * HEAD_DIM ** -0.5
    hh = k_ref.shape[1]

    @pl.when(j == 0)
    def _():
        dq_ref[...] = jnp.zeros(dq_ref.shape, single)
        feature = lax.broadcasted_iota(jnp.int32, (hh, LANES), 0)
        lane = lax.broadcasted_iota(jnp.int32, (hh, LANES), 1)
        pick = (feature // HEAD_DIM + 8 == lane).astype(half)

        @pl.loop(0, q_ref.shape[0] // size)
        def _(i):
            rows = pl.ds(pl.multiple_of(i * size, size), size)
            product = o_ref[rows, :] * do_ref[rows, :].astype(single)
            top = product.astype(half)
            low = (product - top.astype(single)).astype(half)
            both = mm(top, pick) + mm(low, pick) + lse_ref[rows, :]
            stat_ref[:, rows] = both.T[:16, :]

    dk_ref[...] = jnp.zeros(dk_ref.shape, single)
    dv_ref[...] = jnp.zeros(dv_ref.shape, single)

    def step(i, masked):
        rows = pl.ds(pl.multiple_of(i * size, size), size)
        if masked:
            key = j * size + lax.broadcasted_iota(jnp.int32, (size, size), 0)
            query = i * size + lax.broadcasted_iota(jnp.int32, (size, size), 1)
            allowed = (key <= query) & (key >= start_ref[:, rows])
        for pair in range(heads // 2):
            lanes = pl.ds(pair * LANES, LANES)
            k, v = k_ref[:, lanes], v_ref[:, lanes]
            q, do = q_ref[rows, lanes], do_ref[rows, lanes]
            ps, dss, qs, dos, ks = [], [], [], [], []
            for h in (2 * pair, 2 * pair + 1):
                mine = head_lanes(h, size)
                qm = jnp.where(mine, q, 0).astype(half)
                dom = jnp.where(mine, do, 0).astype(half)
                s = mm_nt(k, qm) * factor - stat_ref[pl.ds(h, 1), rows]
                if masked:
                    s = jnp.where(allowed, s, NEG)
                p = jnp.exp2(s)
                ds = p * (mm_nt(v, dom) - stat_ref[pl.ds(8 + h, 1), rows])
                ps.append(p.astype(half))
                dss.append(ds.astype(half))
                qs.append(qm)
                dos.append(dom)
                ks.append(jnp.where(mine, k, 0).astype(half))
            dv_ref[:, lanes] += jnp.dot(jnp.concatenate(ps, 1), jnp.concatenate(dos, 0), preferred_element_type=single)
            dk_ref[:, lanes] += jnp.dot(jnp.concatenate(dss, 1), jnp.concatenate(qs, 0), preferred_element_type=single)
            dq_ref[rows, lanes] += mm_tn(jnp.concatenate(dss, 0), jnp.concatenate(ks, 0))

    step(j, True)
    pl.loop(j + 1, clear)(lambda i: step(i, False))
    pl.loop(clear, high + 1)(lambda i: step(i, True))
    mine = pl.ds(pl.multiple_of(j * size, size), size)
    out_ref[mine, pl.ds(hh, hh)] = (dk_ref[...] * HEAD_DIM ** -0.5).astype(half)
    out_ref[mine, pl.ds(2 * hh, hh)] = dv_ref[...].astype(half)
    out_ref[mine, pl.ds(0, hh)] = (dq_ref[mine, :] * HEAD_DIM ** -0.5).astype(half)

def attention_backward(qkv, do, heads_out, lse, seg_bounds, starts, size):
    seq = qkv.shape[0]
    hh = qkv.shape[1] // 3
    heads = hh // HEAD_DIM
    return pl.pallas_call(
        functools.partial(bwd_kernel, heads),
        grid_spec=pltpu.PrefetchScalarGridSpec(
            num_scalar_prefetch=1,
            grid=(seq // size,),
            in_specs=[
                pl.BlockSpec((seq, hh), lambda j, b: (0, 0)),
                pl.BlockSpec((size, hh), lambda j, b: (j, 1)),
                pl.BlockSpec((size, hh), lambda j, b: (j, 2)),
                pl.BlockSpec((seq, hh), lambda j, b: (0, 0)),
                pl.BlockSpec((seq, hh), lambda j, b: (0, 0)),
                pl.BlockSpec((seq, LANES), lambda j, b: (0, 0)),
                pl.BlockSpec((1, seq), lambda j, b: (0, 0)),
            ],
            out_specs=pl.BlockSpec((seq, 3 * hh), lambda j, b: (0, 0)),
            scratch_shapes=[
                pltpu.VMEM((seq, hh), single),
                pltpu.VMEM((size, hh), single),
                pltpu.VMEM((size, hh), single),
                pltpu.VMEM((16, seq), single),
            ],
        ),
        out_shape=jax.ShapeDtypeStruct((seq, 3 * hh), half),
        compiler_params=pltpu.CompilerParams(vmem_limit_bytes=48 << 20),
        cost_estimate=pl.CostEstimate(flops=10 * seq * seq * LANES * heads, bytes_accessed=20 * seq * hh, transcendentals=0),
    )(seg_bounds, qkv, qkv, qkv, do, heads_out, lse, starts[None, :])


def start_kernel(
    members,
    low,
    per_core,
    padded,
    pack_ref,
    tok_ref,
    dy_ref,
    ids_ref,
    full_ref,
    all_ref,
    got_ref,
    hot_ref,
    info_ref,
    ids_all_ref,
    dy_all_ref,
    stage_ref,
    place_ref,
    send_sem,
    recv_sem,
    own_sem,
    swap_send,
    swap_recv,
    dy_send,
    dy_recv,
):
    size = EXPERTS_FF
    me = lax.axis_index("dp")
    core = lax.axis_index("tensor")
    high = members // low
    inside, row = lax.rem(me, low), me // low
    mine = lax.rem(me, size)
    base = me - mine
    local = tok_ref.shape[0]
    seq = 2 * local
    partner = {"tensor": 1 - core}

    def beside(k):
        return row * low + lax.rem(inside + k, low)

    def across(k):
        return lax.rem(row + k, high) * low + inside

    peers = [beside(k) for k in range(1, low)] + [across(k) for k in range(1, high)]
    peers += [base + lax.rem(mine + k, size) for k in range(1, size)]
    barrier = pltpu.get_barrier_semaphore()
    for peer in peers:
        pl.semaphore_signal(barrier, inc=1, device_id={"dp": peer}, device_id_type=MESH)
    pl.semaphore_signal(barrier, inc=1, device_id=partner, device_id_type=MESH)
    pl.semaphore_wait(barrier, len(peers) + 1)

    def remote(src, dst, send, recv, device):
        return pltpu.make_async_remote_copy(
            src_ref=src,
            dst_ref=dst,
            send_sem=send,
            recv_sem=recv,
            device_id=device,
            device_id_type=MESH,
        )

    def push(source, block, target, slot):
        copy = remote(
            source, full_ref.at[block], send_sem.at[slot], recv_sem.at[block], {"dp": target}
        )
        copy.start()
        return copy

    def arrived(block):
        remote(
            pack_ref, full_ref.at[block], send_sem.at[0], recv_sem.at[block], {"dp": peers[0]}
        ).wait_recv()

    sent = [push(pack_ref, me, across(k), k) for k in range(1, high)]
    sent += [push(pack_ref, me, beside(k), high + k) for k in range(1, low)]
    own_rows = pl.ds(pl.multiple_of(core * local, local), local)
    swaps = [
        remote(ids_ref, ids_all_ref.at[core], swap_send.at[0], swap_recv.at[0], partner),
        remote(dy_ref, dy_all_ref.at[own_rows], swap_send.at[1], swap_recv.at[1], partner),
        remote(tok_ref, all_ref.at[own_rows], swap_send.at[2], swap_recv.at[2], partner),
    ]
    owns = [
        pltpu.make_async_copy(ids_ref, ids_all_ref.at[core], own_sem.at[0]),
        pltpu.make_async_copy(dy_ref, dy_all_ref.at[own_rows], own_sem.at[1]),
        pltpu.make_async_copy(tok_ref, all_ref.at[own_rows], own_sem.at[2]),
        pltpu.make_async_copy(pack_ref, full_ref.at[me], own_sem.at[3]),
    ]
    for copy in swaps + owns:
        copy.start()

    swaps[0].wait()
    owns[0].wait()
    ids = jnp.concatenate([ids_all_ref[0], ids_all_ref[1]], 1)
    seg = ids[:1]
    number = lax.broadcasted_iota(jnp.int32, (8, seq), 0)
    starts = jnp.zeros((1, seq), jnp.int32)
    ends = jnp.zeros((1, seq), jnp.int32)
    total = jnp.zeros((1, 1), jnp.int32)
    for d in range(DOCS):
        here = seg == d
        starts = jnp.where(here, total, starts)
        total = total + jnp.sum(here.astype(jnp.int32), axis=1, keepdims=True)
        ends = jnp.where(here, total - 1, ends)
    row16 = lax.broadcasted_iota(jnp.int32, (16, LANES), 0)
    first = lax.broadcasted_iota(jnp.int32, (LANES, LANES), 0)
    second = lax.broadcasted_iota(jnp.int32, (LANES, LANES), 1)
    upper = (first < second).astype(half)
    before = jnp.zeros((16, 1), single)
    for c in range(seq // LANES):
        lanes = slice(c * LANES, (c + 1) * LANES)
        member = (ids[1:2, lanes] == row16) | (ids[2:3, lanes] == row16)
        member = jnp.where(member & (row16 < size), 1.0, 0.0)
        position = mm(member.astype(half), upper) + before
        before = before + jnp.sum(member, axis=1, keepdims=True)
        place = position - (core * per_core).astype(single)
        kept = (member > 0.5) & (position < CAPACITY) & (place >= 0) & (place < per_core)
        place_ref[:, lanes] = jnp.where(kept, place, -1.0).astype(jnp.int32)
    slot = lax.broadcasted_iota(jnp.int32, (padded, seq), 0)
    for e in range(size):
        hot_ref[e * padded : (e + 1) * padded, :] = jnp.where(
            place_ref[e : e + 1, :] == slot, 1.0, 0.0
        ).astype(half)

    info = jnp.where(number == 0, starts, jnp.where(number == 1, ends, -1))
    for k in range(2):
        chosen = jnp.full((1, seq), -1, jnp.int32)
        for e in range(size):
            place = place_ref[e : e + 1, :]
            chosen = jnp.where(
                (ids[k + 1 : k + 2] == e) & (place >= 0), place + e * padded, chosen
            )
        info = jnp.where(number == k + 2, chosen, info)
    info_ref[...] = info

    for k in range(1, high):
        block = across(high - k)
        arrived(block)
        for step in range(1, low):
            sent.append(push(full_ref.at[block], block, beside(step), high + k * low + step))

    swaps[1].wait()
    owns[1].wait()
    for pair in [(1, 2), (3, 4), (5, 6), (7, 0)]:
        slots = [
            pl.ds(pl.multiple_of(lax.rem(mine + k, size) * padded, 16), padded) for k in pair
        ]
        rows = mm(jnp.concatenate([hot_ref[s, :] for s in slots], 0), dy_all_ref[...])
        for place, k in enumerate(pair):
            to = lax.rem(mine + k, size)
            stage_ref[to] = rows[place * padded : (place + 1) * padded].astype(half)
            if k:
                copy = remote(
                    stage_ref.at[to], got_ref.at[mine], dy_send.at[k], dy_recv.at[k], {"dp": base + to}
                )
            else:
                copy = pltpu.make_async_copy(stage_ref.at[to], got_ref.at[mine], own_sem.at[4])
            copy.start()
            owns.append(copy)
    for k in range(1, low):
        block = beside(low - k)
        arrived(block)
        for step in range(1, high):
            arrived(lax.rem(block + step * low, members))
    for copy in sent:
        copy.wait_send()
    for copy in owns[2:]:
        copy.wait()
    swaps[2].wait()


def start(pack, tokens, dy, ids, members, per_core, padded):
    low = 4 if members % 4 == 0 else 1
    high = members // low
    local, width = tokens.shape
    count = EXPERTS_FF * padded
    any_spec = pl.BlockSpec(memory_space=pl.ANY)
    vmem = pl.BlockSpec(memory_space=pltpu.VMEM)
    dma = pltpu.SemaphoreType.DMA
    return pl.pallas_call(
        functools.partial(start_kernel, members, low, per_core, padded),
        out_shape=[
            jax.ShapeDtypeStruct((members,) + pack.shape, half),
            jax.ShapeDtypeStruct((2 * local, width), half),
            jax.ShapeDtypeStruct((EXPERTS_FF, padded, width), half),
            jax.ShapeDtypeStruct((count, 2 * local), half),
            jax.ShapeDtypeStruct((8, 2 * local), jnp.int32),
        ],
        in_specs=[any_spec] * 4,
        out_specs=[any_spec] * 3 + [vmem] * 2,
        scratch_shapes=[
            pltpu.VMEM((2, 8, local), jnp.int32),
            pltpu.VMEM((2 * local, width), half),
            pltpu.VMEM((EXPERTS_FF, padded, width), half),
            pltpu.VMEM((16, 2 * local), jnp.int32),
            dma((high * (low + 1),)),
            dma((members,)),
            dma((5,)),
            dma((3,)),
            dma((3,)),
            dma((EXPERTS_FF,)),
            dma((EXPERTS_FF,)),
        ],
        compiler_params=pltpu.CompilerParams(
            collective_id=0, has_side_effects=True, vmem_limit_bytes=40 << 20
        ),
        name="start",
    )(pack, tokens, dy, ids)


def middle_kernel(
    members,
    padded,
    w_ref,
    in_ref,
    ho_ref,
    tok_ref,
    own_w_ref,
    other_w_ref,
    gain_ref,
    router_ref,
    prev_ref,
    routes_ref,
    hot_ref,
    ox_ref,
    ow_ref,
    pw_ref,
    pin_ref,
    resid_ref,
    normed_ref,
    misc_ref,
    ho_in_ref,
    both_ref,
    acc_ref,
    stage_ref,
    row_ref,
    send_sem,
    x_sem,
    w_sem,
    pass_sem,
    pair_sem,
    own_sem,
    swap_send,
    swap_recv,
):
    size = EXPERTS_FF
    groups = members // size
    me = lax.axis_index("dp")
    core = lax.axis_index("tensor")
    mine = lax.rem(me, size)
    base = me - mine
    local, width = tok_ref.shape
    partner = {"tensor": 1 - core}

    def member(g, k):
        return lax.rem(base + g * size, members) + lax.rem(mine + k, size)

    barrier = pltpu.get_barrier_semaphore()
    for g in range(groups):
        for k in range(size):
            if g or k:
                pl.semaphore_signal(
                    barrier, inc=1, device_id={"dp": member(g, k)}, device_id_type=MESH
                )
    pl.semaphore_signal(barrier, inc=1, device_id=partner, device_id_type=MESH)
    pl.semaphore_wait(barrier, members)

    def remote(src, dst, send, recv, device):
        return pltpu.make_async_remote_copy(
            src_ref=src,
            dst_ref=dst,
            send_sem=send,
            recv_sem=recv,
            device_id=device,
            device_id_type=MESH,
        )

    def send_w(g, k):
        to = member(g, k)
        copy = remote(
            w_ref.at[to], ow_ref.at[me], send_sem.at[g * size + k], w_sem.at[me], {"dp": to}
        )
        copy.start()
        return copy

    def send_pair(block):
        copy = remote(
            ow_ref.at[block], pw_ref.at[block], pass_sem.at[block], pair_sem.at[block], partner
        )
        copy.start()
        return copy

    own_rows = pl.ds(pl.multiple_of(core * local, local), local)
    other_rows = pl.ds(pl.multiple_of((1 - core) * local, local), local)
    heads = remote(ho_ref.at[other_rows], ho_in_ref, swap_send.at[0], swap_recv.at[0], partner)
    heads.start()
    pair_in = remote(in_ref, pin_ref, swap_send.at[2], swap_recv.at[2], partner)
    pair_in.start()
    own_w = pltpu.make_async_copy(w_ref.at[me], ow_ref.at[me], own_sem.at[1])
    own_w.start()
    sent_w = []
    for k in range(size):
        for g in range(1, groups):
            sent_w.append(send_w(g, k))
        if k:
            sent_w.append(send_w(0, k))

    step = fit(local, 256)
    heads.wait()

    @pl.loop(0, local // step)
    def _(r):
        rows = pl.ds(pl.multiple_of(r * step, step), step)
        mine_rows = pl.ds(pl.multiple_of(core * local + r * step, step), step)
        resid = tok_ref[rows, :].astype(single)
        resid += mm_nt(ho_ref[mine_rows, :], own_w_ref[...])
        resid += mm_nt(ho_in_ref[rows, :], other_w_ref[...])
        resid_ref[rows, :] = resid
        normed = (resid * rms_scale(resid) * gain_ref[1:2, :]).astype(half)
        normed_ref[rows, :] = normed
        router = mm(normed, router_ref[...])
        lane = lax.broadcasted_iota(jnp.int32, (step, LANES), 1)
        logits = jnp.where(lane < EXPERTS, router + prev_ref[rows, :], 0.0)
        hits = [lane == routes_ref[rows, k : k + 1] for k in range(2)]
        picked = [jnp.sum(jnp.where(hit, logits, 0.0), axis=1, keepdims=True) for hit in hits]
        peak = jnp.maximum(picked[0], picked[1])
        expo = [jnp.exp(p - peak) for p in picked]
        total = expo[0] + expo[1]
        gates = [e / total for e in expo]
        misc_ref[rows, :] = jnp.where(lane == 0, gates[0], jnp.where(lane == 1, gates[1], router))
        spread = sum(
            jnp.where(hit & (lane < size), gate.astype(half).astype(single), 0.0)
            for hit, gate in zip(hits, gates)
        )
        both_ref[mine_rows, pl.ds(0, width)] = normed
        both_ref[mine_rows, pl.ds(width, LANES)] = spread.astype(half)

    swap_rows = remote(
        both_ref.at[own_rows], both_ref.at[own_rows], swap_send.at[1], swap_recv.at[1], partner
    )
    swap_rows.start()

    pairs = [(1, 2), (3, 4), (5, 6), (7, 0)]
    for number, pair in enumerate(pairs):
        slots = [
            pl.ds(pl.multiple_of(lax.rem(mine + k, size) * padded, 16), padded) for k in pair
        ]
        hot = jnp.concatenate([hot_ref[s, own_rows] for s in slots], 0)
        acc_ref[number] = mm(hot, both_ref[own_rows, :])
    swap_rows.wait_recv()
    sent_x = []
    row_ref[...] = jnp.zeros(row_ref.shape, single)
    for number, pair in enumerate(pairs):
        slots = [
            pl.ds(pl.multiple_of(lax.rem(mine + k, size) * padded, 16), padded) for k in pair
        ]
        hot = jnp.concatenate([hot_ref[s, other_rows] for s in slots], 0)
        acc_ref[number] += mm(hot, both_ref[other_rows, :])
        for place, k in enumerate(pair):
            to = lax.rem(mine + k, size)
            start = place * padded
            tail = acc_ref[number, start : start + padded, width:].astype(half)
            lane = lax.broadcasted_iota(jnp.int32, (16, LANES), 1)
            row_ref[:, :padded] = mm_nt((lane == to).astype(half), tail)
            stage_ref[to] = acc_ref[number, start : start + padded, :width].astype(half)
            last = acc_ref[number, start + padded - 16 : start + padded, : 2 * LANES]
            row = lax.broadcasted_iota(jnp.int32, (16, 2 * LANES), 0)
            last = jnp.where(row == 15, row_ref[...], last)
            stage_ref[to, padded - 16 :, : 2 * LANES] = last.astype(half)
            if k:
                copy = remote(
                    stage_ref.at[to],
                    ox_ref.at[mine],
                    send_sem.at[members + k],
                    x_sem.at[k],
                    {"dp": base + to},
                )
            else:
                copy = pltpu.make_async_copy(stage_ref.at[to], ox_ref.at[mine], own_sem.at[0])
            copy.start()
            sent_x.append(copy)

    own_w.wait()
    passed = [send_pair(me)]
    for k in range(size):
        for g in range(groups):
            if g or k:
                block = member((groups - g) % groups, (size - k) % size)
                remote(
                    w_ref.at[0], ow_ref.at[block], send_sem.at[0], w_sem.at[block], partner
                ).wait_recv()
                passed.append(send_pair(block))
    pair_in.wait()
    swap_rows.wait_send()
    for copy in sent_x:
        copy.wait()
    for copy in sent_w:
        copy.wait_send()
    for copy in passed:
        copy.wait()


def middle(w, inward, heads, tokens, own_w, other_w, gains, router, prev, routes, hot, padded):
    members = w.shape[0]
    local, width = tokens.shape
    seq = heads.shape[0]
    any_spec = pl.BlockSpec(memory_space=pl.ANY)
    vmem = pl.BlockSpec(memory_space=pltpu.VMEM)
    dma = pltpu.SemaphoreType.DMA
    return pl.pallas_call(
        functools.partial(middle_kernel, members, padded),
        out_shape=[
            jax.ShapeDtypeStruct((EXPERTS_FF, padded, width), half),
            jax.ShapeDtypeStruct(w.shape, half),
            jax.ShapeDtypeStruct(w.shape, half),
            jax.ShapeDtypeStruct(inward.shape, half),
            jax.ShapeDtypeStruct((local, width), single),
            jax.ShapeDtypeStruct((local, width), half),
            jax.ShapeDtypeStruct((local, LANES), single),
        ],
        in_specs=[any_spec] * 2 + [vmem] * 9,
        out_specs=[any_spec] * 4 + [vmem] * 3,
        scratch_shapes=[
            pltpu.VMEM((local, heads.shape[1]), half),
            pltpu.VMEM((seq, width + LANES), half),
            pltpu.VMEM((EXPERTS_FF // 2, 2 * padded, width + LANES), single),
            pltpu.VMEM((EXPERTS_FF, padded, width), half),
            pltpu.VMEM((16, 2 * LANES), single),
            dma((members + EXPERTS_FF,)),
            dma((EXPERTS_FF,)),
            dma((members,)),
            dma((members,)),
            dma((members,)),
            dma((2,)),
            dma((3,)),
            dma((3,)),
        ],
        compiler_params=pltpu.CompilerParams(
            collective_id=1, has_side_effects=True, vmem_limit_bytes=50 << 20
        ),
        name="middle",
    )(w, inward, heads, tokens, own_w, other_w, gains, router, prev, routes, hot)


def expert_kernel(
    padded,
    x_ref,
    dy_ref,
    own_in_ref,
    own_down_ref,
    other_in_ref,
    other_down_ref,
    out_ref,
    grad_ref,
    og_ref,
    hid_ref,
    pg_ref,
    pu_ref,
    gate_ref,
    eo_ref,
    ig_ref,
    dot_ref,
):
    f = pl.program_id(0)
    sources = x_ref.shape[0]
    count, width = og_ref.shape
    chunk = count // 4
    x_all = x_ref.reshape(count, width)
    block = hid_ref.shape[2]

    @pl.when(f == 0)
    def _():
        for s in range(sources):
            rows = pl.ds(s * padded, padded)
            gates = x_ref[s, padded - 16 :, : 2 * LANES].astype(single).T
            gate = jnp.broadcast_to(gates[:padded, 15:16], (padded, LANES))
            gate_ref[rows, :] = gate
            og_ref[rows, :] = (dy_ref[s].astype(single) * gate[:, :1]).astype(half)
        eo_ref[...] = jnp.zeros(eo_ref.shape, single)
        ig_ref[...] = jnp.zeros(ig_ref.shape, single)

    for part, (in_ref, down_ref) in enumerate(
        ((own_in_ref, own_down_ref), (other_in_ref, other_down_ref))
    ):
        gate_w, up_w = (in_ref[:, k].reshape(width, block) for k in range(2))
        down_w = down_ref[...].reshape(width, block)
        for r in range(4):
            rows = pl.ds(r * chunk, chunk)
            x = x_all[rows, :]
            og = og_ref[rows, :]
            pre = mm(x, gate_w)
            up = mm(x, up_w)
            hg = mm(og, down_w)
            sigma = jax.nn.sigmoid(pre)
            active = pre * sigma
            hidden = (active * up).astype(half)
            pg = (hg * up * (sigma * (1.0 + pre * (1.0 - sigma)))).astype(half)
            pu = (hg * active).astype(half)
            hid_ref[part, rows, :] = hidden
            pg_ref[part, rows, :] = pg
            pu_ref[part, rows, :] = pu
            eo_ref[rows, :] += mm_nt(hidden, down_w)
            ig_ref[rows, :] += mm_nt(pg, gate_w) + mm_nt(pu, up_w)

    @pl.when(f == pl.num_programs(0) - 1)
    def _():
        dot_ref[...] = jnp.zeros(dot_ref.shape, single)
        ones = jnp.ones((16, width), half)
        for s in range(sources):
            rows = pl.ds(s * padded, padded)
            eo = eo_ref[rows, :]
            out_ref[s] = (eo * gate_ref[rows, :1]).astype(half)
            grad_ref[s] = ig_ref[rows, :].astype(half)
            product = eo * dy_ref[s].astype(single)
            top = product.astype(half)
            low = (product - top.astype(single)).astype(half)
            dot_ref[:, :padded] = mm_nt(ones, top) + mm_nt(ones, low)
            dots = dot_ref[...]
            high = dots.astype(half).astype(single)
            row = lax.broadcasted_iota(jnp.int32, dots.shape, 0)
            tail = ig_ref[pl.ds((s + 1) * padded - 16, 16), : 2 * LANES]
            tail = jnp.where(row == 14, high, jnp.where(row == 15, dots - high, tail))
            grad_ref[s, padded - 16 :, : 2 * LANES] = tail.astype(half)


def expert_step(x, dy, own_in, own_down, other_in, other_down, padded):
    sources, _, width = x.shape
    count = sources * padded
    m, _, r, ff = own_in.shape
    block = fit(ff, 256)
    whole = pl.BlockSpec((sources, padded, width), lambda f: (0, 0, 0))
    two = pl.BlockSpec((m, 2, r, block), lambda f: (0, 0, 0, f))
    one = pl.BlockSpec((m, r, block), lambda f: (0, 0, f))
    wide = pl.BlockSpec((2, count, block), lambda f: (0, 0, f))
    return pl.pallas_call(
        functools.partial(expert_kernel, padded),
        grid=(ff // block,),
        in_specs=[whole, whole, two, one, two, one],
        out_specs=[whole, whole, pl.BlockSpec((count, width), lambda f: (0, 0)), wide, wide, wide],
        out_shape=[
            jax.ShapeDtypeStruct(x.shape, half),
            jax.ShapeDtypeStruct(x.shape, half),
            jax.ShapeDtypeStruct((count, width), half),
            jax.ShapeDtypeStruct((2, count, ff), half),
            jax.ShapeDtypeStruct((2, count, ff), half),
            jax.ShapeDtypeStruct((2, count, ff), half),
        ],
        scratch_shapes=[
            pltpu.VMEM((count, LANES), single),
            pltpu.VMEM((count, width), single),
            pltpu.VMEM((count, width), single),
            pltpu.VMEM((16, 2 * LANES), single),
        ],
        compiler_params=pltpu.CompilerParams(vmem_limit_bytes=58 << 20),
        cost_estimate=pl.CostEstimate(
            flops=12 * count * width * 2 * ff,
            bytes_accessed=2 * 6 * width * ff + 20 * count * ff,
            transcendentals=0,
        ),
        name="expert_step",
    )(x, dy, own_in, own_down, other_in, other_down)


def split(x):
    high = x.astype(half)
    return high, (x - high.astype(single)).astype(half)


def slot_rows(columns, count):
    slot = lax.broadcasted_iota(jnp.int32, (columns.shape[0], count), 1)
    hit = (columns[:, 2:3] == slot) | (columns[:, 3:4] == slot)
    return jnp.where(hit, 1.0, 0.0).astype(half)


def lane_sum(x):
    return jnp.sum(x, axis=1, keepdims=True)


def back_kernel(
    padded,
    back_ref,
    info_ref,
    resid_ref,
    normed_ref,
    misc_ref,
    dy_ref,
    routes_ref,
    gain_ref,
    const_ref,
    router_ref,
    own_w_ref,
    other_w_ref,
    prev_ref,
    mix_ref,
    rgrad_ref,
    attn_ref,
    heads_ref,
    base_ref,
    pgrad_ref,
    small_ref,
    mgrad_ref,
    ext_ref,
    out_ref,
    in_ref,
    hg_ref,
    send_sem,
    recv_sem,
):
    core = lax.axis_index("tensor")
    partner = {"tensor": 1 - core}
    sources, _, width = back_ref.shape
    count = sources * padded
    local = dy_ref.shape[0]
    step = fit(local, 256)
    barrier = pltpu.get_barrier_semaphore()
    pl.semaphore_signal(barrier, inc=1, device_id=partner, device_id_type=MESH)
    pl.semaphore_wait(barrier, 1)

    def remote(src, dst, number):
        return pltpu.make_async_remote_copy(
            src_ref=src,
            dst_ref=dst,
            send_sem=send_sem.at[number],
            recv_sem=recv_sem.at[number],
            device_id=partner,
            device_id_type=MESH,
        )

    own_rows = pl.ds(pl.multiple_of(core * local, local), local)
    lane = lax.broadcasted_iota(jnp.int32, (step, LANES), 1)
    for s in range(sources):
        dots = back_ref[s, padded - 16 :, : 2 * LANES].astype(single).T
        number = lax.broadcasted_iota(jnp.int32, (padded, LANES), 1)
        ext = jnp.where(
            number == s,
            dots[:padded, 14:15],
            jnp.where(number == s + EXPERTS_FF, dots[:padded, 15:16], 0.0),
        )
        ext_ref[pl.ds(s * padded, padded), :] = ext.astype(half)
    back_all = back_ref.reshape(count, width)

    @pl.loop(0, local // step)
    def _(r):
        rows = pl.ds(pl.multiple_of(r * step, step), step)
        there = pl.ds(pl.multiple_of((1 - core) * local + r * step, step), step)
        hot = slot_rows(info_ref[there, :], count)
        out_ref[rows, pl.ds(0, width)] = mm(hot, back_all[...]).astype(half)
        out_ref[rows, pl.ds(width, LANES)] = mm(hot, ext_ref[...]).astype(half)

    sums = remote(out_ref, in_ref, 0)
    sums.start()
    small_ref[...] = jnp.zeros(small_ref.shape, single)
    mgrad_ref[...] = jnp.zeros(mgrad_ref.shape, single)

    @pl.loop(0, local // step)
    def _(r):
        rows = pl.ds(pl.multiple_of(r * step, step), step)
        here = pl.ds(pl.multiple_of(core * local + r * step, step), step)
        hot = slot_rows(info_ref[here, :], count)
        rgrad_ref[rows, :] = mm(hot, back_all[...])
        pgrad_ref[rows, :] = mm(hot, ext_ref[...])

    sums.wait()

    @pl.loop(0, local // step)
    def _(r):
        rows = pl.ds(pl.multiple_of(r * step, step), step)
        here = pl.ds(pl.multiple_of(core * local + r * step, step), step)
        dy = dy_ref[rows, :].astype(single)
        normed = normed_ref[rows, :].astype(single)
        resid = resid_ref[rows, :]
        misc = misc_ref[rows, :]
        expert_dot = pgrad_ref[rows, :] + in_ref[rows, pl.ds(width, LANES)].astype(single)
        own_dot = lane_sum(dy * normed)
        vec_dot = [lane_sum(dy * const_ref[j : j + 1, :]) for j in range(2)]
        gates = [misc[:, k : k + 1] for k in range(2)]
        routes = [routes_ref[rows, k : k + 1] for k in range(2)]
        alphas = []
        for j in range(2):
            columns = [misc[:, EXPERTS + 2 * j + m : EXPERTS + 2 * j + m + 1] for m in range(2)]
            peak = jnp.maximum(columns[0], columns[1])
            expo = [jnp.exp(c - peak) for c in columns]
            total = expo[0] + expo[1]
            alphas.append([e / total for e in expo])
        gate_grads = []
        for k in range(2):
            hit = (lane == routes[k]) | (lane == routes[k] + EXPERTS_FF)
            dot = lane_sum(jnp.where(hit & (routes[k] < EXPERTS_FF), expert_dot, 0.0))
            dot += jnp.where(routes[k] == EXPERTS_FF + 1, own_dot, 0.0)
            for j in range(2):
                value = alphas[j][0] * own_dot + alphas[j][1] * vec_dot[j]
                dot += jnp.where(routes[k] == EXPERTS_FF + 2 + j, value, 0.0)
            gate_grads.append(dot)
        centre = gates[0] * gate_grads[0] + gates[1] * gate_grads[1]
        chosen = [gates[k] * (gate_grads[k] - centre) for k in range(2)]
        router_grad = jnp.zeros((step, LANES), single)
        own_weight = jnp.zeros((step, 1), single)
        for k in range(2):
            router_grad = jnp.where(lane == routes[k], chosen[k], router_grad)
            own_weight += jnp.where(routes[k] == EXPERTS_FF + 1, gates[k], 0.0)
        logit_grad = router_grad
        vec_lanes = jnp.zeros((step, LANES), single)
        other = jnp.zeros((step, width), single)
        for j in range(2):
            weight = sum(jnp.where(routes[k] == EXPERTS_FF + 2 + j, gates[k], 0.0) for k in range(2))
            grads = [weight * own_dot, weight * vec_dot[j]]
            mean = alphas[j][0] * grads[0] + alphas[j][1] * grads[1]
            for m in range(2):
                router_grad = jnp.where(
                    lane == EXPERTS + 2 * j + m, alphas[j][m] * (grads[m] - mean), router_grad
                )
            own_weight += weight * alphas[j][0]
            vec_weight = weight * alphas[j][1]
            vec_lanes = jnp.where(lane == 16 + j, vec_weight, vec_lanes)
            other += vec_weight * const_ref[j : j + 1, :]
        base_ref[rows, :] = resid + own_weight * normed + other
        rg_high, rg_low = split(router_grad)
        two_grad = rgrad_ref[rows, :] + in_ref[rows, pl.ds(0, width)].astype(single)
        two_grad += own_weight * dy
        two_grad += mm_nt(rg_high, router_ref[...]) + mm_nt(rg_low, router_ref[...])
        normed_low = normed_ref[rows, :]
        vec_high, vec_low = split(vec_lanes)
        small_ref[...] += (
            mm_tn(rg_high, normed_low)
            + mm_tn(rg_low, normed_low)
            + mm_tn(vec_high, dy_ref[rows, :])
            + mm_tn(vec_low, dy_ref[rows, :])
        )[:24]
        scale = rms_scale(resid)
        gain_part = jnp.sum(two_grad * resid * scale, axis=0, keepdims=True)
        small_ref[19:20, :] += gain_part
        weighted = two_grad * gain_ref[1:2, :]
        mean = jnp.mean(weighted * resid, axis=-1, keepdims=True)
        grad = dy + scale * (weighted - resid * scale * scale * mean)
        rgrad_ref[rows, :] = grad
        low = grad.astype(half)
        attn_ref[here, :] = low
        heads_ref[here, :] = mm(low, own_w_ref[...]).astype(half)
        hg_ref[rows, :] = mm(low, other_w_ref[...]).astype(half)
        lg_high, lg_low = split(logit_grad)
        mix_high, mix_low = split(mix_ref[...])
        pgrad_ref[rows, :] = (
            mm_nt(lg_high, mix_high) + mm_nt(lg_high, mix_low) + mm_nt(lg_low, mix_high)
        )
        prev_high, prev_low = split(prev_ref[rows, :])
        mgrad_ref[...] += (
            mm_tn(prev_high, lg_high) + mm_tn(prev_high, lg_low) + mm_tn(prev_low, lg_high)
        )

    for i in range(EXPERTS):
        place = pl.ds(i % 6 * LANES, LANES)
        small_ref[20 + i // 6 : 21 + i // 6, place] = mgrad_ref[i : i + 1, :]

    heads = remote(hg_ref, heads_ref.at[own_rows], 1)
    heads.start()
    attn = remote(attn_ref.at[own_rows], attn_ref.at[own_rows], 2)
    attn.start()
    heads.wait()
    attn.wait()


def backward_middle(
    back, info, resid, normed, misc, dy, routes, gains, const, router, own_w, other_w, prev, mix, padded
):
    local, width = dy.shape
    seq = info.shape[0]
    hh = own_w.shape[1]
    count = EXPERTS_FF * padded
    vmem = pl.BlockSpec(memory_space=pltpu.VMEM)
    return pl.pallas_call(
        functools.partial(back_kernel, padded),
        out_shape=[
            jax.ShapeDtypeStruct((local, width), single),
            jax.ShapeDtypeStruct((seq, width), half),
            jax.ShapeDtypeStruct((seq, hh), half),
            jax.ShapeDtypeStruct((local, width), single),
            jax.ShapeDtypeStruct((local, LANES), single),
            jax.ShapeDtypeStruct((24, width), single),
            jax.ShapeDtypeStruct((LANES, LANES), single),
        ],
        in_specs=[vmem] * 14,
        out_specs=[vmem] * 7,
        scratch_shapes=[
            pltpu.VMEM((count, LANES), half),
            pltpu.VMEM((local, width + LANES), half),
            pltpu.VMEM((local, width + LANES), half),
            pltpu.VMEM((local, hh), half),
            pltpu.SemaphoreType.DMA((3,)),
            pltpu.SemaphoreType.DMA((3,)),
        ],
        compiler_params=pltpu.CompilerParams(
            collective_id=2, has_side_effects=True, vmem_limit_bytes=56 << 20
        ),
        name="backward_middle",
    )(back, info, resid, normed, misc, dy, routes, gains, const, router, own_w, other_w, prev, mix)


def weight_kernel(
    x_ref, og_ref, hid_ref, pg_ref, pu_ref, out_ref, xt_ref, ogt_ref, send_ref, got_ref, send_sem, recv_sem
):
    f = pl.program_id(0)
    partner = {"tensor": 1 - lax.axis_index("tensor")}
    shape = out_ref.shape[0], out_ref.shape[2], out_ref.shape[3]

    @pl.when(f == 0)
    def _():
        barrier = pltpu.get_barrier_semaphore()
        pl.semaphore_signal(barrier, inc=1, device_id=partner, device_id_type=MESH)
        pl.semaphore_wait(barrier, 1)
        xt_ref[...] = x_ref[...].T
        ogt_ref[...] = og_ref[...].T

    def remote(number):
        return pltpu.make_async_remote_copy(
            src_ref=send_ref.at[number],
            dst_ref=got_ref.at[number],
            send_sem=send_sem.at[number],
            recv_sem=recv_sem.at[number],
            device_id=partner,
            device_id_type=MESH,
        )

    factors = (xt_ref, pg_ref), (xt_ref, pu_ref), (ogt_ref, hid_ref)
    for k, (left, right) in enumerate(factors):
        send_ref[f, k] = mm(left[...], right[1]).astype(half)
    remote(f).start()
    grads = [mm(left[...], right[0]) for left, right in factors]
    remote(f).wait_recv()
    for k in range(3):
        total = grads[k] + got_ref[f, k].astype(single)
        out_ref[:, k] = total.astype(half).reshape(shape)

    @pl.when(f == pl.num_programs(0) - 1)
    def _():
        for number in range(send_ref.shape[0]):
            remote(number).wait_send()


def weight_step(x, og, hidden, pg, pu, m):
    count, width = og.shape
    ff = hidden.shape[2]
    block = fit(ff, 256)
    steps = ff // block
    whole = pl.BlockSpec((count, width), lambda f: (0, 0))
    wide = pl.BlockSpec((2, count, block), lambda f: (0, 0, f))
    part = pl.BlockSpec((m, 3, width // m, block), lambda f: (0, 0, 0, f))
    return pl.pallas_call(
        weight_kernel,
        grid=(steps,),
        in_specs=[whole, whole, wide, wide, wide],
        out_specs=part,
        out_shape=jax.ShapeDtypeStruct((m, 3, width // m, ff), half),
        scratch_shapes=[
            pltpu.VMEM((width, count), half),
            pltpu.VMEM((width, count), half),
            pltpu.VMEM((steps, 3, width, block), half),
            pltpu.VMEM((steps, 3, width, block), half),
            pltpu.SemaphoreType.DMA((steps,)),
            pltpu.SemaphoreType.DMA((steps,)),
        ],
        compiler_params=pltpu.CompilerParams(
            collective_id=3, has_side_effects=True, vmem_limit_bytes=56 << 20
        ),
        cost_estimate=pl.CostEstimate(
            flops=12 * count * width * ff,
            bytes_accessed=12 * width * ff + 12 * count * ff,
            transcendentals=0,
        ),
        name="weight_step",
    )(x, og, hidden, pg, pu)


def tail_kernel(
    members,
    low,
    padded,
    eo_ref,
    qkv_ref,
    one_ref,
    proj_ref,
    outg_ref,
    x_ref,
    base_ref,
    resid_ref,
    info_ref,
    gain_ref,
    small_ref,
    dense_out_ref,
    tokens_ref,
    mixed_ref,
    small_out_ref,
    dense_ref,
    first_ref,
    stage_ref,
    second_ref,
    eo_in_ref,
    one_out_ref,
    one_in_ref,
    ffn_out_ref,
    ffn_in_ref,
    ffn_ref,
    mine_ref,
    pair_ref,
    near_ref,
    far_ref,
    send1,
    recv1,
    send2,
    recv2,
    eo_send,
    eo_recv,
    pair_send,
    pair_recv,
    near_send,
    near_recv,
    far_send,
    far_recv,
    own_sem,
):
    size = EXPERTS_FF
    me = lax.axis_index("dp")
    core = lax.axis_index("tensor")
    high = members // low
    inside, row = lax.rem(me, low), me // low
    mine = lax.rem(me, size)
    base = me - mine
    local, width = base_ref.shape
    count = size * padded
    d_rows = dense_out_ref.shape[0]
    hh3 = qkv_ref.shape[1]
    step = fit(local, 256)
    partner = {"tensor": 1 - core}

    def beside(k):
        return row * low + lax.rem(inside + k, low)

    def across(k):
        return lax.rem(row + k, high) * low + inside

    peers = [beside(k) for k in range(1, low)] + [across(k) for k in range(1, high)]
    peers += [base + lax.rem(mine + k, size) for k in range(1, size)]
    barrier = pltpu.get_barrier_semaphore()
    for peer in peers:
        pl.semaphore_signal(barrier, inc=1, device_id={"dp": peer}, device_id_type=MESH)
    pl.semaphore_signal(barrier, inc=1, device_id=partner, device_id_type=MESH)
    pl.semaphore_wait(barrier, len(peers) + 1)

    def remote(src, dst, send, recv, device):
        return pltpu.make_async_remote_copy(
            src_ref=src,
            dst_ref=dst,
            send_sem=send,
            recv_sem=recv,
            device_id=device,
            device_id_type=MESH,
        )

    eo = []
    for k in range(1, size):
        to = lax.rem(mine + k, size)
        eo.append(
            remote(
                eo_ref.at[to], eo_in_ref.at[mine], eo_send.at[k], eo_recv.at[k], {"dp": base + to}
            )
        )
    eo.append(pltpu.make_async_copy(eo_ref.at[mine], eo_in_ref.at[mine], own_sem))
    for copy in eo:
        copy.start()

    sent = []
    chunks = 2
    rows_each = width // chunks
    for c in range(chunks):
        lanes = pl.ds(c * rows_each, rows_each)
        grad = mm_tn(one_ref[:, lanes], qkv_ref[...])
        for j in range(members // chunks):
            owner = c * (members // chunks) + j
            dense_ref[owner, :, :hh3] = grad[j * d_rows : (j + 1) * d_rows].astype(half)
            dense_ref[owner, :, hh3:] = outg_ref[owner * d_rows : (owner + 1) * d_rows, :]
        for h in range(c * high // chunks, (c + 1) * high // chunks):
            for k in range(1, low):
                copy = remote(
                    dense_ref.at[h * low + lax.rem(inside + k, low)],
                    first_ref.at[k - 1, h],
                    send1.at[k - 1, h],
                    recv1.at[k - 1, h],
                    {"dp": beside(k)},
                )
                copy.start()
                sent.append(copy)

    def one_part(rows):
        part = mm_nt(qkv_ref[rows, :], proj_ref[...])
        x = x_ref[rows, :].astype(single)
        mine_ref[18:19, :] += jnp.sum(part * x * rms_scale(x), axis=0, keepdims=True)
        return part

    mine_ref[...] = small_ref[...]

    @pl.loop(0, local // step)
    def _(r):
        rows = pl.ds(pl.multiple_of(r * step, step), step)
        there = pl.ds(pl.multiple_of((1 - core) * local + r * step, step), step)
        one_out_ref[rows, :] = one_part(there).astype(half)

    one_sent = remote(one_out_ref, one_in_ref, pair_send.at[0], pair_recv.at[0], partner)
    one_sent.start()

    @pl.loop(0, local // step)
    def _(r):
        rows = pl.ds(pl.multiple_of(r * step, step), step)
        here = pl.ds(pl.multiple_of(core * local + r * step, step), step)
        tokens_ref[rows, :] = one_part(here)

    pair = remote(mine_ref, pair_ref, pair_send.at[1], pair_recv.at[1], partner)
    pair.start()
    pair.wait()
    near_ref[inside] = mine_ref[...] + pair_ref[...]
    near = []
    for k in range(1, low):
        near.append(
            remote(
                near_ref.at[inside],
                near_ref.at[inside],
                near_send.at[k],
                near_recv.at[inside],
                {"dp": beside(k)},
            )
        )
        near[-1].start()

    for j in range(1, high + 1):
        h = lax.rem(row + j, high)
        total = dense_ref[h * low + inside].astype(single)
        for k in range(low - 1):
            remote(
                dense_ref.at[0], first_ref.at[k, h], send1.at[k, h], recv1.at[k, h], partner
            ).wait_recv()
            total += first_ref[k, h].astype(single)
        if j < high:
            stage_ref[j - 1] = total.astype(half)
            copy = remote(
                stage_ref.at[j - 1],
                second_ref.at[j - 1],
                send2.at[j - 1],
                recv2.at[j - 1],
                {"dp": across(j)},
            )
            copy.start()
            sent.append(copy)
        else:
            dense_out_ref[...] = total
    for k in range(1, low):
        block = lax.rem(inside + k, low)
        remote(
            mine_ref, near_ref.at[block], near_send.at[0], near_recv.at[block], partner
        ).wait_recv()
    total = near_ref[0]
    for k in range(1, low):
        total = total + near_ref[k]
    far_ref[row] = total
    far = []
    for k in range(1, high):
        far.append(
            remote(
                far_ref.at[row], far_ref.at[row], far_send.at[k], far_recv.at[row], {"dp": across(k)}
            )
        )
        far[-1].start()

    for copy in eo:
        copy.wait()
    eo_all = eo_in_ref.reshape(count, width)

    @pl.loop(0, local // step)
    def _(r):
        rows = pl.ds(pl.multiple_of(r * step, step), step)
        there = pl.ds(pl.multiple_of((1 - core) * local + r * step, step), step)
        ffn_out_ref[rows, :] = mm(slot_rows(info_ref[there, :], count), eo_all[...]).astype(half)

    ffn_sent = remote(ffn_out_ref, ffn_in_ref, pair_send.at[2], pair_recv.at[2], partner)
    ffn_sent.start()

    @pl.loop(0, local // step)
    def _(r):
        rows = pl.ds(pl.multiple_of(r * step, step), step)
        here = pl.ds(pl.multiple_of(core * local + r * step, step), step)
        ffn_ref[rows, :] = mm(slot_rows(info_ref[here, :], count), eo_all[...])

    one_sent.wait()

    @pl.loop(0, local // step)
    def _(r):
        rows = pl.ds(pl.multiple_of(r * step, step), step)
        here = pl.ds(pl.multiple_of(core * local + r * step, step), step)
        x = x_ref[here, :].astype(single)
        scale = rms_scale(x)
        weighted = (tokens_ref[rows, :] + one_in_ref[rows, :].astype(single)) * gain_ref[0:1, :]
        mean = jnp.mean(weighted * x, axis=-1, keepdims=True)
        tokens_ref[rows, :] = resid_ref[rows, :] + scale * (weighted - x * scale * scale * mean)

    ffn_sent.wait()

    @pl.loop(0, local // step)
    def _(r):
        rows = pl.ds(pl.multiple_of(r * step, step), step)
        total = base_ref[rows, :] + ffn_ref[rows, :] + ffn_in_ref[rows, :].astype(single)
        mixed_ref[rows, :] = total.astype(half)

    for j in range(1, high):
        remote(
            stage_ref.at[0], second_ref.at[j - 1], send2.at[j - 1], recv2.at[j - 1], partner
        ).wait_recv()
        dense_out_ref[...] += second_ref[j - 1].astype(single)
    for k in range(1, high):
        block = lax.rem(row + k, high)
        remote(
            mine_ref, far_ref.at[block], far_send.at[0], far_recv.at[block], partner
        ).wait_recv()
    total = far_ref[0]
    for k in range(1, high):
        total = total + far_ref[k]
    small_out_ref[...] = total
    for copy in sent + near + far:
        copy.wait_send()


def tail(members, eo, qkv, one, proj, outg, x, base, resid, info, gains, small, padded):
    low = 4
    high = members // low
    local, width = base.shape
    d_rows = width // members
    wide = qkv.shape[1] + outg.shape[1]
    vmem = pl.BlockSpec(memory_space=pltpu.VMEM)
    dma = pltpu.SemaphoreType.DMA
    rows_half = pltpu.VMEM((local, width), half)
    small_one = pltpu.VMEM(small.shape, single)
    return pl.pallas_call(
        functools.partial(tail_kernel, members, low, padded),
        out_shape=[
            jax.ShapeDtypeStruct((d_rows, wide), single),
            jax.ShapeDtypeStruct((local, width), single),
            jax.ShapeDtypeStruct((local, width), half),
            jax.ShapeDtypeStruct(small.shape, single),
        ],
        in_specs=[pl.BlockSpec(memory_space=pl.ANY)] + [vmem] * 10,
        out_specs=[vmem] * 4,
        scratch_shapes=[
            pltpu.VMEM((members, d_rows, wide), half),
            pltpu.VMEM((low - 1, high, d_rows, wide), half),
            pltpu.VMEM((high - 1, d_rows, wide), half),
            pltpu.VMEM((high - 1, d_rows, wide), half),
            pltpu.VMEM(eo.shape, half),
            rows_half,
            rows_half,
            rows_half,
            rows_half,
            pltpu.VMEM((local, width), single),
            small_one,
            small_one,
            pltpu.VMEM((low,) + small.shape, single),
            pltpu.VMEM((high,) + small.shape, single),
            dma((low - 1, high)),
            dma((low - 1, high)),
            dma((high - 1,)),
            dma((high - 1,)),
            dma((EXPERTS_FF,)),
            dma((EXPERTS_FF,)),
            dma((3,)),
            dma((3,)),
            dma((low,)),
            dma((low,)),
            dma((high,)),
            dma((high,)),
            dma,
        ],
        compiler_params=pltpu.CompilerParams(
            collective_id=4, has_side_effects=True, vmem_limit_bytes=60 << 20
        ),
        name="tail",
    )(eo, qkv, one, proj, outg, x, base, resid, info, gains, small)


def per_device(
    tokens,
    segment_ids,
    routes,
    prev_logits,
    cotangent,
    proj_weight,
    out_weight,
    norm_gain,
    expert_weight,
    router,
    constant_vectors,
    gate_mixing,
):
    members = lax.axis_size("dp")
    groups = members // EXPERTS_FF
    cubes = [[g * EXPERTS_FF + i for i in range(EXPERTS_FF)] for g in range(groups)]
    core = lax.axis_index("tensor")
    d_rows, hh = out_weight.shape
    per_core = -(-CAPACITY // 2)
    padded = -(-(per_core + 3) // 16) * 16

    def in_group(blocks):
        return lax.all_to_all(blocks, "dp", 0, 0, axis_index_groups=cubes, tiled=True)

    def plain_tail(eo, qkv, one, proj, outg, x, base, resid, gains, small):
        ffn = pair_sum(mm_tn(onehot, in_group(eo).reshape(-1, width)))
        part = mm_nt(qkv, proj)
        scale = rms_scale(x)
        small = small.at[18].set(jnp.sum(part * x * scale, axis=0))
        weighted = pair_sum(part) * gains[0]
        x, scale = half_of(x, core), half_of(scale, core)
        mean = jnp.mean(weighted * x, axis=-1, keepdims=True)
        tokens_grad = resid + scale * (weighted - x * scale * scale * mean)
        dense = jnp.concatenate([mm_tn(one, qkv).astype(half), outg], 1)
        dense = lax.all_to_all(dense.reshape(members, d_rows, -1), "dp", 0, 0, tiled=True)
        dense = jnp.sum(dense.astype(single), axis=0)
        return dense, tokens_grad, (base + ffn).astype(half), lax.psum(small, ("dp", "tensor"))

    pack = jnp.concatenate(
        [
            proj_weight.transpose(1, 0, 2).reshape(d_rows, 3 * hh),
            out_weight,
            norm_gain.T,
            constant_vectors.T,
            router,
        ],
        1,
    )
    columns = pack.shape[1]
    pack = jnp.pad(pack, ((0, 0), (0, -columns % LANES)))
    ids = jnp.concatenate([segment_ids, routes[0].T], 0)
    ids = jnp.pad(ids, ((0, 5), (0, 0)))
    full_pack, tokens_all, got_dy, onehot, info = start(
        pack, tokens[0], cotangent[0], ids, members, per_core, padded
    )
    full_pack, expert_weight = lax.optimization_barrier((full_pack, expert_weight))
    full_pack = full_pack.reshape(members * d_rows, -1)[:, :columns]
    width = members * d_rows
    proj_full = full_pack[:, : 3 * hh]
    outw_own = full_pack[:, 3 * hh : 4 * hh]
    outw_other = swap(outw_own)
    rest = full_pack[:, 4 * hh :]
    gains = rest[:, :2].T.astype(single)
    const_f = rest[:, 2:4].T.astype(single)
    router_full = rest[:, 4:]
    in_weight = jnp.broadcast_to(
        expert_weight[None, :, :2], (groups, EXPERTS_FF, 2) + expert_weight.shape[2:]
    ).reshape((members, 2) + expert_weight.shape[2:])
    down_weight = jnp.broadcast_to(
        expert_weight[None, :, 2], (groups, EXPERTS_FF) + expert_weight.shape[2:]
    ).reshape((members,) + expert_weight.shape[2:])
    my_in = lax.all_to_all(in_weight, "dp", 0, 0, tiled=True)
    if d_rows % 16:
        my_in = my_in.transpose(1, 0, 2, 3).reshape(1, 2, width, -1)

    x_rows = tokens[0].astype(single)
    local_rows = x_rows.shape[0]
    x_all = tokens_all.astype(single)
    scale_all = rms_scale(x_all)
    full_one = (x_all * scale_all * gains[0]).astype(half)
    scale_one = half_of(scale_all, core)
    seq = full_one.shape[0]
    qkv = mm(full_one, proj_full).astype(half)
    size = fit(seq, 256)
    starts = info[0]
    bounds = block_bounds(starts, info[1], size)
    columns = info.T
    heads_full, heads_out, lse = attention_forward(qkv, bounds, starts, size)
    prev_rows = prev_logits[0]
    mixed_prev = jnp.dot(prev_rows, gate_mixing, precision=HIGH)
    mixed_prev = jnp.pad(mixed_prev, ((0, 0), (0, LANES - EXPERTS)))
    router_wide = jnp.pad(router_full, ((0, 0), (0, LANES - router_full.shape[1])))
    got_rows, my_down, other_down, other_in, resid, normed_two, misc = middle(
        down_weight,
        my_in,
        heads_out,
        tokens[0],
        outw_own,
        outw_other,
        gains,
        router_wide,
        mixed_prev,
        routes[0],
        onehot,
        padded,
    )
    if d_rows % 16:
        my_down = my_down.reshape(1, width, -1)
        other_down = other_down.reshape(1, width, -1)

    count = EXPERTS_FF * padded
    gated_out, in_grad, out_grad, hidden, pg, pu = expert_step(
        got_rows, got_dy, my_in, my_down, other_in, other_down, padded
    )
    back_grad = in_group(in_grad)
    grads_sent = weight_step(
        got_rows.reshape(count, width), out_grad, hidden, pg, pu, my_in.shape[0]
    )
    back_grad, grads_sent = lax.optimization_barrier((back_grad, grads_sent))
    if d_rows % 16:
        grads_sent = grads_sent.reshape(3, members, d_rows, -1).transpose(1, 0, 2, 3)
    grads_got = lax.all_to_all(grads_sent, "dp", 0, 0, tiled=True)

    mix_wide = jnp.pad(gate_mixing, ((0, LANES - EXPERTS), (0, LANES - EXPERTS)))
    prev_wide = jnp.pad(prev_rows, ((0, 0), (0, LANES - EXPERTS)))
    resid_grad, attn_all, heads_grad, base, prev_grad, small, mixing_grad = backward_middle(
        back_grad,
        columns,
        resid,
        normed_two,
        misc,
        cotangent[0],
        routes[0],
        gains,
        const_f,
        router_wide,
        outw_own,
        outw_other,
        prev_wide,
        mix_wide,
        padded,
    )
    out_w_grad = mm_tn(attn_all, heads_out)
    qkv_grad = attention_backward(qkv, heads_grad, heads_full, lse, bounds, starts, size)
    qkv_grad, grads_got = lax.optimization_barrier((qkv_grad, grads_got))
    out_w_grad = out_w_grad.astype(half)
    if d_rows % 16 or members != 16:
        outs = plain_tail(
            gated_out, qkv_grad, full_one, proj_full, out_w_grad, x_all, base, resid_grad, gains, small
        )
    else:
        outs = tail(
            members,
            gated_out,
            qkv_grad,
            full_one,
            proj_full,
            out_w_grad,
            tokens_all,
            base,
            resid_grad,
            columns,
            gains,
            small,
            padded,
        )
    dense, tokens_grad, mixed, small = outs
    expert_shard = jnp.sum(
        grads_got.reshape((groups, EXPERTS_FF) + grads_got.shape[1:]).astype(single), axis=0
    )
    proj_shard = dense[:, : 3 * hh].reshape(d_rows, 3, hh).transpose(1, 0, 2)
    outw_shard = dense[:, 3 * hh :]
    mixing_total = small[20:22].reshape(EXPERTS, LANES)[:, :EXPERTS]
    features = lax.dynamic_slice_in_dim(small, lax.axis_index("dp") * d_rows, d_rows, 1)
    return (
        mixed[None],
        tokens_grad[None],
        prev_grad[None, :, :EXPERTS],
        proj_shard,
        outw_shard,
        features[18:20],
        expert_shard,
        features[:16].T,
        features[16:18],
        mixing_total,
    )


def solution(mesh):
    return jax.shard_map(
        per_device,
        mesh=mesh,
        in_specs=(
            P("dp", "tensor", None),
            P("dp", "tensor"),
            P("dp", "tensor", None),
            P("dp", "tensor", None),
            P("dp", "tensor", None),
            P(None, "dp", "tensor"),
            P("dp", "tensor"),
            P(None, "dp"),
            P(None, None, "dp", "tensor"),
            P("dp", None),
            P(None, "dp"),
            P(),
        ),
        out_specs=(
            P("dp", "tensor", None),
            P("dp", "tensor", None),
            P("dp", "tensor", None),
            P(None, "dp", "tensor"),
            P("dp", "tensor"),
            P(None, "dp"),
            P(None, None, "dp", "tensor"),
            P("dp", None),
            P(None, "dp"),
            P(),
        ),
        check_vma=False,
    )
```

time: 590 us -> 532 us (0.902)
  Pallas kernels: 295 us -> 409 us
  matrix products: 86 us -> 11.1 us
  other arithmetic: 52 us -> 10.6 us
  waiting for transfers between devices: 62 us -> 21.6 us
  starting transfers between devices: 32.3 us -> 21.2 us
    pallas_call x3 -> x5, Pallas kernels: 156 us -> 287 us  [the longest x1 83 us: tail(): pl.pallas_call(functools.partial(tail_kernel, members, low, padded), out_...]
    dot_general x13 -> x1, matrix products: 32.2 us -> 0.54 us  [per_device(): mixed_prev = jnp.dot(prev_rows, gate_mixing, precision=HIGH)]
    all_to_all x3 -> x2, waiting for transfers between devices: 46.7 us -> 16.3 us  [the longest x1 16.3 us: per_device(): my_in = lax.all_to_all(in_weight, 'dp', 0, 0, tiled=True)]
    dot_general x5 -> x1, matrix products: 27.8 us -> 4.7 us  [mm_tn(): lax.dot_general(a, b, (((0,), (0,)), ((), ())), preferred_element_type=si...]
    dot_general x6 -> x1, matrix products: 26 us -> 5.83 us  [mm(): return jnp.dot(a, b, preferred_element_type=single)]
    pallas_call x1, Pallas kernels: 58.1 us -> 40.7 us  [expert_step(): pl.pallas_call(functools.partial(expert_kernel, padded), grid=(ff // bloc...]
    select_n x6 -> x0, other arithmetic: 10.6 us -> none  [the longest x4 7.45 us: in_order(): jnp.where(first, own, other)]
    unnamed x121 -> x66, local copies, waits for them, and re-layouts: 30 us -> 20.8 us
  transfers between devices with their start and end apart: 18 -> 4, of which waited for: 5 -> 2; matrix products, arithmetic and copies ran while one was open for 27% -> 6% of each run, Pallas kernels for 25% -> 30%
where the time goes in v3:
time: 532 us; the launch traced here: 522 us
  Pallas kernels  409 us (77%)
  local copies, waits for them, and re-layouts  46.9 us (9%)
  waiting for transfers between devices  21.6 us (4%)
  starting transfers between devices  21.2 us (4%)
  matrix products  11.1 us (2%)
  other arithmetic  10.6 us (2%)
    pallas_call x1, Pallas kernels, tail(): pl.pallas_call(functools.partial(tail_kernel, members, low, padded), out_...  83 us
    pallas_call x1, Pallas kernels, middle(): pl.pallas_call(functools.partial(middle_kernel, members, padded), out_sha...  63.7 us
    pallas_call x1, Pallas kernels, start(): pl.pallas_call(functools.partial(start_kernel, members, low, per_core, pa...  63.1 us
    pallas_call x1, Pallas kernels, attention_backward(): pl.pallas_call(functools.partial(bwd_kernel, heads), grid_spec=pltpu.Pref...  48.3 us
    pallas_call x1, Pallas kernels, expert_step(): pl.pallas_call(functools.partial(expert_kernel, padded), grid=(ff // bloc...  40.7 us
    pallas_call x1, Pallas kernels, backward_middle(): pl.pallas_call(functools.partial(back_kernel, padded), out_shape=[jax.Sha...  39.5 us
    pallas_call x1, Pallas kernels, weight_step(): pl.pallas_call(weight_kernel, grid=(steps,), in_specs=[whole, whole, wide...  37.6 us
    pallas_call x1, Pallas kernels, attention_forward(): pl.pallas_call(functools.partial(fwd_kernel, heads), grid_spec=pltpu.Pref...  33.1 us
  transfers between devices with their start and end apart: 4, of which 2 were waited for; matrix products, arithmetic and copies ran while one was open for 6% of the time, Pallas kernels for 30%

profile of v3, /device:TPU:12, one launch (start us, length us, event | category | flops | bytes accessed | tf_op | source)
XLA Modules:
  0.0 521.8 jit_solution(16076768648522794635)
XLA Ops:
  0.6 0.8 copy.81
  1.4 0.8 copy.83
  2.2 0.8 copy.82
  2.9 0.9 copy.103
  3.8 0.9 copy.84
  4.8 0.2 copy.85
  5.0 0.9 concatenate.6
  5.9 0.7 pad_add_fusion
  6.6 1.4 copy-done.3
  8.0 1.4 copy-done.4
  9.4 63.1 %start.1 = (bf16[16,48,1664]{2,1,0:T(8,128)(2,1)S(1)}, bf16[2048,768]{1,0:T(8,128)(2,1)S(1)}, bf16[8,176,768]{2,1,0:T(8,128)(2,1)S(1)}, bf16[1408,2048]{1,0:T(8,128)(2,1)}, s32[8,2048]{1,0:T(8,128)S(1)}) custom-call(bf16[48,1664]{1,0:T(8,128)(2,1)S(1)} %pad.23.pack_ref, bf16[1024,768]{1,0:T(8,128)(2,1)S(1)} %bitcast.75, bf16[1024,768]{1,0:T(8,128)(2,1)S(1)} %bitcast.77, ...), custom_call_target="tpu_custom_call" | custom-call | tf_op jit(solution)/shard_map/start/pallas_call | solution.py:461
  72.6 2.4 broadcast_in_dim.26
  75.0 0.7 copy-done.14
  75.7 6.9 %all-to-all-start = ((bf16[16,2,48,1024]{3,2,1,0:T(8,128)(2,1)}), bf16[16,2,48,1024]{3,2,1,0:T(8,128)(2,1)}, u32[]{:S(2)}, u32[]{:S(2)}) async-start(bf16[16,2,48,1024]{3,2,1,0:T(8,128)(2,1)} %bitcast.87), calls=%async_computation | async-start | bytes 6291456 | tf_op jit(solution)/shard_map/all_to_all | solution.py:1537
  82.6 2.0 slice.99.own_w_ref
  84.7 0.1 copy.98
  84.9 0.1 copy.100
  85.0 2.0 slice_convert_fusion
  87.0 1.1 copy.104
  88.1 1.4 copy.90.start_ref
  89.5 0.2 convert_reduce_fusion.1
  89.7 0.7 fusion
  90.4 0.8 fusion.2.one_ref
  91.2 0.9 copy-done.8
  92.1 5.8 %convolution_convert_fusion.q_ref.k_ref.v_ref = bf16[2048,1152]{1,0:T(8,128)(2,1)} fusion(bf16[2048,768]{1,0:T(8,128)(2,1)S(1)} %fusion.2.one_ref, bf16[768,1664]{1,0:T(8,128)(2,1)S(1)} %bitcast.80), kind=kOutput, calls=%fused_computation.3 | convolution fusion | flops 3626237952 | bytes 9633792 | tf_op jit(solution)/shard_map/dot_general | solution.py:38
  98.0 33.1 %shard_map.195 = (f32[2048,384]{1,0:T(8,128)}, bf16[2048,384]{1,0:T(8,128)(2,1)S(1)}, f32[2048,128]{1,0:T(8,128)S(1)}) custom-call(s32[4,8]{1,0:T(4,128)S(1)} %pad_add_fusion.1.bounds, bf16[2048,1152]{1,0:T(8,128)(2,1)} %convolution_convert_fusion.q_ref.k_ref.v_ref, bf16[2048,1152]{1,0:T(8,128)(2,1)} %convolution_convert_fusion.q_ref.k_ref.v_ref, ...), custom_call_target="tpu_custom_call" | custom-call | flops 12884901888 | bytes 12582912 | tf_op jit(solution)/shard_map/pallas_call | solution.py:153
  131.1 1.2 copy-done.5
  132.3 1.0 copy-done.17
  133.3 0.1 slice.100
  133.4 0.2 copy.91
  133.7 0.7 copy-done.20
  134.5 0.5 fusion.4
  135.1 1.2 slice_bitcast_fusion
  136.3 16.3 %all-to-all-done.in_ref.own_in_ref = bf16[16,2,48,1024]{3,2,1,0:T(8,128)(2,1)} async-done(((bf16[16,2,48,1024]{3,2,1,0:T(8,128)(2,1)}), bf16[16,2,48,1024]{3,2,1,0:T(8,128)(2,1)}, u32[]{:S(2)}, u32[]{:S(2)}) %all-to-all-start) | async-done | bytes 3145760 | tf_op jit(solution)/shard_map/all_to_all | solution.py:1537
  152.6 1.3 broadcast_in_dim.25
  154.0 63.7 %middle.1 = (bf16[8,176,768]{2,1,0:T(8,128)(2,1)}, bf16[16,48,1024]{2,1,0:T(8,128)(2,1)}, bf16[16,48,1024]{2,1,0:T(8,128)(2,1)}, bf16[16,2,48,1024]{3,2,1,0:T(8,...) custom-call(bf16[16,48,1024]{2,1,0:T(8,128)(2,1)} %bitcast.90, ...), custom_call_target="tpu_custom_call" | custom-call | tf_op jit(solution)/shard_map/middle/pallas_call | solution.py:691
  217.7 0.8 copy-done.12
  218.5 40.7 %expert_step.1 = (bf16[8,176,768]{2,1,0:T(8,128)(2,1)}, bf16[8,176,768]{2,1,0:T(8,128)(2,1)}, bf16[1408,768]{1,0:T(8,128)(2,1)}, bf16[2,1408,1024]{2,1,0:T(8,128...) custom-call(bf16[8,176,768]{2,1,0:T(8,128)(2,1)} %get-tuple-element.54.x_ref, ...), custom_call_target="tpu_custom_call" | custom-call | flops 26575110144 | bytes 38273024 | tf_op jit(solution)/shard_map/expert_step/pallas_call | solution.py:816
  259.2 7.2 %all-to-all-start.1 = ((bf16[8,176,768]{2,1,0:T(8,128)(2,1)}), bf16[8,176,768]{2,1,0:T(8,128)(2,1)}, u32[]{:S(2)}, u32[]{:S(2)}) async-start(bf16[8,176,768]{2,1,0:T(8,128)(2,1)} %get-tuple-element.60), calls=%async_computation.1 | async-start | bytes 4325376 | tf_op jit(solution)/shard_map/all_to_all | solution.py:1488
  266.4 37.6 %weight_step.1 = bf16[16,3,48,1024]{3,2,1,0:T(8,128)(2,1)} custom-call(bf16[1408,768]{1,0:T(8,128)(2,1)} %bitcast.102, bf16[1408,768]{1,0:T(8,128)(2,1)} %get-tuple-element.61.og_ref, bf16[2,1408,1024]{2,1,0:T(8,128)(2,1)} %get-tuple-element.62.hid_ref, bf16[2,1408,1024]{2,1,0:T(8,128)(2,1)} %get-tuple-element.63.pg_ref, ...), custom_call_target="tpu_custom_call" | custom-call | flops 13287555072 | bytes 26738688 | tf_op jit(solution)/shard_map/weight_step/pallas_call | solution.py:1128
  304.0 7.1 %all-to-all-start.2 = ((bf16[16,3,48,1024]{3,2,1,0:T(8,128)(2,1)}), bf16[16,3,48,1024]{3,2,1,0:T(8,128)(2,1)}, u32[]{:S(2)}, u32[]{:S(2)}) async-start(bf16[16,3,48,1024]{3,2,1,0:T(8,128)(2,1)} %weight_step.1), calls=%async_computation.2 | async-start | bytes 9437184 | tf_op jit(solution)/shard_map/all_to_all | solution.py:1587
  311.2 1.4 pad.28.mix_ref
  312.6 1.3 copy.93
  313.9 1.3 slice.98.proj_ref
  315.3 0.9 pad.27.prev_ref
  316.1 0.7 copy.105
  316.9 39.5 %backward_middle.1 = (f32[1024,768]{1,0:T(8,128)}, bf16[2048,768]{1,0:T(8,128)(2,1)}, bf16[2048,384]{1,0:T(8,128)(2,1)}, f32[1024,768]{1,0:T(8,128)}, f32[1024,1...) custom-call(bf16[8,176,768]{2,1,0:T(8,128)(2,1)} %all-to-all-done.1.back_ref, s32[2048,8]{1,0:T(8,128)} %bitcast.88, ...), custom_call_target="tpu_custom_call" | custom-call | tf_op jit(solution)/shard_map/backward_middle/pallas_call | solution.py:1051
  356.4 1.9 slice_bitcast_fusion.1
  358.3 2.0 copy.95
  360.2 4.7 convolution_convert_fusion.1.outg_ref
  365.0 48.3 %shard_map.196.qkv_ref = bf16[2048,1152]{1,0:T(8,128)(2,1)} custom-call(s32[4,8]{1,0:T(4,128)S(1)} %pad_add_fusion.1.bounds, bf16[2048,1152]{1,0:T(8,128)(2,1)} %convolution_convert_fusion.q_ref.k_ref.v_ref, bf16[2048,1152]{1,0:T(8,128)(2,1)} %convolution_convert_fusion.q_ref.k_ref.v_ref, bf16[2048,1152]{1,0:T(8,128)(2,1)} %convolution_convert_fusion.q_ref.k_ref.v_ref, ...), custom_call_target="tpu_custom_call" | custom-call | flops 32212254720 | bytes 15728640 | tf_op jit(solution)/shard_map/pallas_call | solution.py:255
  413.3 5.2 %all-to-all-done.2 = bf16[16,3,48,1024]{3,2,1,0:T(8,128)(2,1)} async-done(((bf16[16,3,48,1024]{3,2,1,0:T(8,128)(2,1)}), bf16[16,3,48,1024]{3,2,1,0:T(8,128)(2,1)}, u32[]{:S(2)}, u32[]{:S(2)}) %all-to-all-start.2) | async-done | bytes 4718624 | tf_op jit(solution)/shard_map/all_to_all | solution.py:1587
  418.5 83.0 %tail.1 = (f32[48,1536]{1,0:T(8,128)}, f32[1024,768]{1,0:T(8,128)}, bf16[1024,768]{1,0:T(8,128)(2,1)}, f32[24,768]{1,0:T(8,128)}) custom-call(bf16[8,176,768]{2,1,0:T(8,128)(2,1)} %get-tuple-element.59.eo_ref, bf16[2048,1152]{1,0:T(8,128)(2,1)} %shard_map.196.qkv_ref, bf16[2048,768]{1,0:T(8,128)(2,1)} %copy-done.19, bf16[768,1152]{1,0:T(8,128)(2,1)} %slice.98.proj_ref, ...), custom_call_target="tpu_custom_call" | custom-call | tf_op jit(solution)/shard_map/tail/pallas_call | solution.py:1419
  501.5 1.5 slice.87
  503.1 1.6 slice.86
  504.7 6.2 %convert_reduce_fusion = f32[8,3,48,1024]{3,2,1,0:T(8,128)} fusion(bf16[2,8,3,48,1024]{4,3,2,1,0:T(8,128)(2,1)} %bitcast.29), kind=kLoop, calls=%fused_computation | loop fusion | flops 3538944 | bytes 9437184 | tf_op jit(solution)/shard_map/reduce_sum | solution.py:1633
  510.9 0.9 slice.91
  511.8 1.5 dynamic-slice_bitcast_fusion
  513.3 0.6 reshape.319
  513.9 1.0 reshape.318
  514.9 0.7 copy.96
  515.6 1.4 fusion.7
  517.0 2.7 copy.108
  519.7 1.7 copy.109
  (64 shorter events, 0.5 us)
Async XLA Ops:
  4.8 1.8 copy-start.1
  6.6 1.4 copy-start.3
  8.0 1.4 copy-start.4
  9.4 63.1 %slice-start = ((bf16[8,3,48,1024]{3,2,1,0:T(8,128)(2,1)}), bf16[8,2,48,1024]{3,2,1,0:T(8,128)(2,1)S(1)}, s32[]{:S(2)}) async-start(bf16[8,3,48,1024]{3,2,1,0:T(8,128)(2,1)} %param.20), calls=%async_computation.3 | async-start | bytes 3145728 | tf_op jit(solution)/shard_map/slice | solution.py:1532
  72.5 2.5 copy-start.7
  72.5 3.1 copy-start.14
  72.5 17.9 %copy-start = (bf16[2048,768]{1,0:T(8,128)(2,1)}, bf16[2048,768]{1,0:T(8,128)(2,1)S(1)}, u32[]{:S(2)}) copy-start(bf16[2048,768]{1,0:T(8,128)(2,1)S(1)} %get-tuple-element.50.x_ref) | copy-start | bytes 9437188
  75.7 77.0 %all-to-all-start = ((bf16[16,2,48,1024]{3,2,1,0:T(8,128)(2,1)}), bf16[16,2,48,1024]{3,2,1,0:T(8,128)(2,1)}, u32[]{:S(2)}, u32[]{:S(2)}) async-start(bf16[16,2,48,1024]{3,2,1,0:T(8,128)(2,1)} %bitcast.87), calls=%async_computation | async-start | bytes 6291456 | tf_op jit(solution)/shard_map/all_to_all | solution.py:1537
  84.5 51.8 %collective-permute-start = (bf16[768,384]{1,0:T(8,128)(2,1)}, bf16[768,384]{1,0:T(8,128)(2,1)}, u32[]{:S(2)}, u32[]{:S(2)}) collective-permute-start(bf16[768,384]{1,0:T(8,128)(2,1)} %slice.99.own_w_ref), channel_id=1, source_target_pairs={{0,1},{1,0},{2,3},{3,2},{4,5},{5,4},{6,7},{7,6},{8,9},{9,8},{10,11... | collective-permute-start | bytes 1769480 | tf_op jit(solution)/shard_map/ppermute | solution.py:50
  88.1 65.9 %copy-start.13 = (f32[768,2]{0,1:T(2,128)}, f32[768,2]{0,1:T(2,128)S(1)}, u32[]{:S(2)}) copy-start(f32[768,2]{0,1:T(2,128)S(1)} %copy.104) | copy-start | bytes 18436
  90.4 1.7 copy-start.8
  92.1 5.8 %copy-start.19 = (bf16[2048,768]{1,0:T(8,128)(2,1)}, bf16[2048,768]{1,0:T(8,128)(2,1)S(1)}, u32[]{:S(2)}) copy-start(bf16[2048,768]{1,0:T(8,128)(2,1)S(1)} %fusion.2.one_ref) | copy-start | bytes 9437188
  92.1 5.8 %copy-start.11 = (s32[2048,1]{1,0:T(8,128)S(1)}, s32[2048,1]{1,0:T(8,128)}, u32[]{:S(2)}) copy-start(s32[2048,1]{1,0:T(8,128)} %copy.90.start_ref) | copy-start | bytes 24580
  98.0 35.4 %copy-start.24 = (f32[1,1024,12]{1,0,2:T(1,128)S(1)}, f32[1,1024,12]{1,0,2:T(1,128)}, u32[]{:S(2)}) copy-start(f32[1,1024,12]{1,0,2:T(1,128)} %param.15) | copy-start | bytes 147460
  98.0 36.5 %copy-start.25 = (f32[12,12]{1,0:T(8,128)S(1)}, f32[12,12]{1,0:T(8,128)}, u32[]{:S(2)}) copy-start(f32[12,12]{1,0:T(8,128)} %param.23) | copy-start | bytes 1732
  131.1 1.2 copy-start.5
  132.3 1.0 copy-start.17
  133.7 0.8 copy-start.20
  133.7 20.3 %copy-start.2 = (s32[1,1024,2]{2,1,0:T(8,128)S(1)}, s32[1,1024,2]{2,1,0:T(8,128)}, u32[]{:S(2)}) copy-start(s32[1,1024,2]{2,1,0:T(8,128)} %copy-done.1) | copy-start | bytes 24580
  134.5 83.2 %copy-start.10 = (bf16[768,128]{1,0:T(8,128)(2,1)}, bf16[768,128]{1,0:T(8,128)(2,1)S(1)}, u32[]{:S(2)}) copy-start(bf16[768,128]{1,0:T(8,128)(2,1)S(1)} %pad.25.router_ref) | copy-start | bytes 589828
  217.6 0.9 copy-start.12
  259.2 44.8 %all-to-all-start.1 = ((bf16[8,176,768]{2,1,0:T(8,128)(2,1)}), bf16[8,176,768]{2,1,0:T(8,128)(2,1)}, u32[]{:S(2)}, u32[]{:S(2)}) async-start(bf16[8,176,768]{2,1,0:T(8,128)(2,1)} %get-tuple-element.60), calls=%async_computation.1 | async-start | bytes 4325376 | tf_op jit(solution)/shard_map/all_to_all | solution.py:1488
  304.0 9.9 %copy-start.9 = (bf16[16,48,1664]{2,1,0:T(8,128)(2,1)S(1)}, bf16[16,48,1664]{2,1,0:T(8,128)(2,1)}, u32[]{:S(2)}) copy-start(bf16[16,48,1664]{2,1,0:T(8,128)(2,1)} %copy-done.7) | copy-start | bytes 7667716
  304.0 114.5 %all-to-all-start.2 = ((bf16[16,3,48,1024]{3,2,1,0:T(8,128)(2,1)}), bf16[16,3,48,1024]{3,2,1,0:T(8,128)(2,1)}, u32[]{:S(2)}, u32[]{:S(2)}) async-start(bf16[16,3,48,1024]{3,2,1,0:T(8,128)(2,1)} %weight_step.1), calls=%async_computation.2 | async-start | bytes 9437184 | tf_op jit(solution)/shard_map/all_to_all | solution.py:1587
  311.2 4.1 copy-start.21
  311.2 5.0 copy-start.23
  316.9 43.4 %copy-start.6 = (bf16[2048,384]{1,0:T(8,128)(2,1)S(1)}, bf16[2048,384]{1,0:T(8,128)(2,1)}, u32[]{:S(2)}) copy-start(bf16[2048,384]{1,0:T(8,128)(2,1)} %copy-done.5) | copy-start | bytes 4718596
  358.3 6.7 %copy-start.15 = (bf16[2048,384]{1,0:T(8,128)(2,1)S(1)}, bf16[2048,384]{1,0:T(8,128)(2,1)}, u32[]{:S(2)}) copy-start(bf16[2048,384]{1,0:T(8,128)(2,1)} %get-tuple-element.69.do_ref) | copy-start | bytes 4718596
  360.2 4.7 copy-start.16
  360.2 4.7 copy-start.18
  510.9 8.7 %copy-start.22 = (f32[1024,768]{1,0:T(8,128)S(1)}, f32[1024,768]{1,0:T(8,128)}, u32[]{:S(2)}) copy-start(f32[1024,768]{1,0:T(8,128)} %get-tuple-element.79) | copy-start | bytes 9437188

commit v4 on v3

--- a/solution.py
+++ b/solution.py
@@ -289,11 +289,13 @@
     tok_ref,
     dy_ref,
     ids_ref,
+    w_ref,
     full_ref,
     all_ref,
     got_ref,
     hot_ref,
     info_ref,
+    down_ref,
     ids_all_ref,
     dy_all_ref,
     stage_ref,
@@ -305,6 +307,8 @@
     swap_recv,
     dy_send,
     dy_recv,
+    down_send,
+    down_recv,
 ):
     size = EXPERTS_FF
     me = lax.axis_index("dp")
@@ -325,6 +329,13 @@
 
     peers = [beside(k) for k in range(1, low)] + [across(k) for k in range(1, high)]
     peers += [base + lax.rem(mine + k, size) for k in range(1, size)]
+    groups = members // size
+
+    def device_at(g, k):
+        return lax.rem(base + g * size, members) + lax.rem(mine + k, size)
+
+    distant = [(g, k) for g in range(1, groups) for k in range(size)]
+    peers += [device_at(g, k) for g, k in distant]
     barrier = pltpu.get_barrier_semaphore()
     for peer in peers:
         pl.semaphore_signal(barrier, inc=1, device_id={"dp": peer}, device_id_type=MESH)
@@ -420,6 +431,17 @@
         for step in range(1, low):
             sent.append(push(full_ref.at[block], block, beside(step), high + k * low + step))
 
+    for g, k in distant:
+        copy = remote(
+            w_ref.at[lax.rem(mine + k, size), 2],
+            down_ref.at[me],
+            down_send.at[(g - 1) * size + k],
+            down_recv.at[me],
+            {"dp": device_at(g, k)},
+        )
+        copy.start()
+        sent.append(copy)
+
     swaps[1].wait()
     owns[1].wait()
     for pair in [(1, 2), (3, 4), (5, 6), (7, 0)]:
@@ -443,6 +465,11 @@
         arrived(block)
         for step in range(1, high):
             arrived(lax.rem(block + step * low, members))
+    for g, k in distant:
+        block = device_at(groups - g, size - k)
+        remote(
+            w_ref.at[0, 2], down_ref.at[block], down_send.at[0], down_recv.at[block], partner
+        ).wait_recv()
     for copy in sent:
         copy.wait_send()
     for copy in owns[2:]:
@@ -450,7 +477,7 @@
     swaps[2].wait()
 
 
-def start(pack, tokens, dy, ids, members, per_core, padded):
+def start(pack, tokens, dy, ids, w, members, per_core, padded):
     low = 4 if members % 4 == 0 else 1
     high = members // low
     local, width = tokens.shape
@@ -466,9 +493,10 @@
             jax.ShapeDtypeStruct((EXPERTS_FF, padded, width), half),
             jax.ShapeDtypeStruct((count, 2 * local), half),
             jax.ShapeDtypeStruct((8, 2 * local), jnp.int32),
+            jax.ShapeDtypeStruct((members,) + w.shape[2:], half),
         ],
-        in_specs=[any_spec] * 4,
-        out_specs=[any_spec] * 3 + [vmem] * 2,
+        in_specs=[any_spec] * 5,
+        out_specs=[any_spec] * 3 + [vmem] * 2 + [any_spec],
         scratch_shapes=[
             pltpu.VMEM((2, 8, local), jnp.int32),
             pltpu.VMEM((2 * local, width), half),
@@ -481,19 +509,23 @@
             dma((3,)),
             dma((EXPERTS_FF,)),
             dma((EXPERTS_FF,)),
+            dma((members,)),
+            dma((members,)),
         ],
         compiler_params=pltpu.CompilerParams(
             collective_id=0, has_side_effects=True, vmem_limit_bytes=40 << 20
         ),
         name="start",
-    )(pack, tokens, dy, ids)
-
-
-def middle_kernel(
+    )(pack, tokens, dy, ids, w)
+
+
+def experts_kernel(
     members,
     padded,
     w_ref,
+    far_ref,
     in_ref,
+    dy_hbm_ref,
     ho_ref,
     tok_ref,
     own_w_ref,
@@ -503,10 +535,13 @@
     prev_ref,
     routes_ref,
     hot_ref,
-    ox_ref,
-    ow_ref,
-    pw_ref,
-    pin_ref,
+    back_ref,
+    out_ref,
+    x_ref,
+    og_ref,
+    hid_ref,
+    pg_ref,
+    pu_ref,
     resid_ref,
     normed_ref,
     misc_ref,
@@ -515,14 +550,26 @@
     acc_ref,
     stage_ref,
     row_ref,
-    send_sem,
-    x_sem,
-    w_sem,
-    pass_sem,
-    pair_sem,
+    win_ref,
+    down_ref,
+    dy_ref,
+    ig_ref,
+    spill_ref,
+    gate_ref,
+    dot_ref,
+    x_send,
+    x_recv,
+    w_send,
+    w_recv,
+    pass_send,
+    pass_recv,
     own_sem,
+    far_sem,
     swap_send,
     swap_recv,
+    ig_send,
+    ig_recv,
+    spill_sem,
 ):
     size = EXPERTS_FF
     groups = members // size
@@ -532,19 +579,12 @@
     base = me - mine
     local, width = tok_ref.shape
     partner = {"tensor": 1 - core}
-
-    def member(g, k):
-        return lax.rem(base + g * size, members) + lax.rem(mine + k, size)
-
+    near = [base + lax.rem(mine + k, size) for k in range(1, size)]
     barrier = pltpu.get_barrier_semaphore()
-    for g in range(groups):
-        for k in range(size):
-            if g or k:
-                pl.semaphore_signal(
-                    barrier, inc=1, device_id={"dp": member(g, k)}, device_id_type=MESH
-                )
+    for peer in near:
+        pl.semaphore_signal(barrier, inc=1, device_id={"dp": peer}, device_id_type=MESH)
     pl.semaphore_signal(barrier, inc=1, device_id=partner, device_id_type=MESH)
-    pl.semaphore_wait(barrier, members)
+    pl.semaphore_wait(barrier, size)
 
     def remote(src, dst, send, recv, device):
         return pltpu.make_async_remote_copy(
@@ -556,35 +596,32 @@
             device_id_type=MESH,
         )
 
-    def send_w(g, k):
-        to = member(g, k)
-        copy = remote(
-            w_ref.at[to], ow_ref.at[me], send_sem.at[g * size + k], w_sem.at[me], {"dp": to}
-        )
-        copy.start()
-        return copy
-
-    def send_pair(block):
-        copy = remote(
-            ow_ref.at[block], pw_ref.at[block], pass_sem.at[block], pair_sem.at[block], partner
-        )
-        copy.start()
-        return copy
-
     own_rows = pl.ds(pl.multiple_of(core * local, local), local)
     other_rows = pl.ds(pl.multiple_of((1 - core) * local, local), local)
     heads = remote(ho_ref.at[other_rows], ho_in_ref, swap_send.at[0], swap_recv.at[0], partner)
     heads.start()
-    pair_in = remote(in_ref, pin_ref, swap_send.at[2], swap_recv.at[2], partner)
+    waits = []
+    for k in range(1, size):
+        to = lax.rem(mine + k, size)
+        copy = remote(
+            w_ref.at[to, 2], down_ref.at[0, me], w_send.at[k], w_recv.at[k], {"dp": base + to}
+        )
+        copy.start()
+        waits.append(copy)
+    pair_in = remote(in_ref, win_ref.at[1], swap_send.at[2], swap_recv.at[2], partner)
     pair_in.start()
-    own_w = pltpu.make_async_copy(w_ref.at[me], ow_ref.at[me], own_sem.at[1])
+    local_in = pltpu.make_async_copy(in_ref, win_ref.at[0], own_sem.at[1])
+    local_in.start()
+    local_dy = pltpu.make_async_copy(dy_hbm_ref, dy_ref, own_sem.at[2])
+    local_dy.start()
+    own_w = pltpu.make_async_copy(w_ref.at[mine, 2], down_ref.at[0, me], own_sem.at[3])
     own_w.start()
-    sent_w = []
-    for k in range(size):
-        for g in range(1, groups):
-            sent_w.append(send_w(g, k))
-        if k:
-            sent_w.append(send_w(0, k))
+    far = []
+    for g in range(1, groups):
+        blocks = pl.ds(lax.rem(base + g * size, members), size)
+        copy = pltpu.make_async_copy(far_ref.at[blocks], down_ref.at[0, blocks], far_sem.at[g])
+        copy.start()
+        far.append(copy)
 
     step = fit(local, 256)
     heads.wait()
@@ -621,7 +658,7 @@
     )
     swap_rows.start()
 
-    pairs = [(1, 2), (3, 4), (5, 6), (7, 0)]
+    pairs = [(1, 0), (2, 3), (4, 5), (6, 7)]
     for number, pair in enumerate(pairs):
         slots = [
             pl.ds(pl.multiple_of(lax.rem(mine + k, size) * padded, 16), padded) for k in pair
@@ -629,8 +666,8 @@
         hot = jnp.concatenate([hot_ref[s, own_rows] for s in slots], 0)
         acc_ref[number] = mm(hot, both_ref[own_rows, :])
     swap_rows.wait_recv()
-    sent_x = []
     row_ref[...] = jnp.zeros(row_ref.shape, single)
+    own_x = None
     for number, pair in enumerate(pairs):
         slots = [
             pl.ds(pl.multiple_of(lax.rem(mine + k, size) * padded, 16), padded) for k in pair
@@ -639,207 +676,239 @@
         acc_ref[number] += mm(hot, both_ref[other_rows, :])
         for place, k in enumerate(pair):
             to = lax.rem(mine + k, size)
-            start = place * padded
-            tail = acc_ref[number, start : start + padded, width:].astype(half)
+            first = place * padded
+            tail = acc_ref[number, first : first + padded, width:].astype(half)
             lane = lax.broadcasted_iota(jnp.int32, (16, LANES), 1)
             row_ref[:, :padded] = mm_nt((lane == to).astype(half), tail)
-            stage_ref[to] = acc_ref[number, start : start + padded, :width].astype(half)
-            last = acc_ref[number, start + padded - 16 : start + padded, : 2 * LANES]
+            stage_ref[to] = acc_ref[number, first : first + padded, :width].astype(half)
+            last = acc_ref[number, first + padded - 16 : first + padded, : 2 * LANES]
             row = lax.broadcasted_iota(jnp.int32, (16, 2 * LANES), 0)
             last = jnp.where(row == 15, row_ref[...], last)
             stage_ref[to, padded - 16 :, : 2 * LANES] = last.astype(half)
             if k:
                 copy = remote(
-                    stage_ref.at[to],
-                    ox_ref.at[mine],
-                    send_sem.at[members + k],
-                    x_sem.at[k],
-                    {"dp": base + to},
+                    stage_ref.at[to], x_ref.at[mine], x_send.at[k], x_recv.at[k], {"dp": base + to}
                 )
+                waits.append(copy)
             else:
-                copy = pltpu.make_async_copy(stage_ref.at[to], ox_ref.at[mine], own_sem.at[0])
+                copy = pltpu.make_async_copy(stage_ref.at[to], x_ref.at[mine], own_sem.at[0])
+                own_x = copy
             copy.start()
-            sent_x.append(copy)
 
     own_w.wait()
-    passed = [send_pair(me)]
+    for copy in far:
+        copy.wait()
+    passed = []
+    for g in range(1, groups):
+        blocks = pl.ds(lax.rem(base + g * size, members), size)
+        passed.append(
+            remote(
+                down_ref.at[0, blocks],
+                down_ref.at[1, blocks],
+                pass_send.at[size + g],
+                pass_recv.at[size + g],
+                partner,
+            )
+        )
+        passed[-1].start()
     for k in range(size):
-        for g in range(groups):
-            if g or k:
-                block = member((groups - g) % groups, (size - k) % size)
-                remote(
-                    w_ref.at[0], ow_ref.at[block], send_sem.at[0], w_sem.at[block], partner
-                ).wait_recv()
-                passed.append(send_pair(block))
-    pair_in.wait()
-    swap_rows.wait_send()
-    for copy in sent_x:
-        copy.wait()
-    for copy in sent_w:
-        copy.wait_send()
+        block = base + lax.rem(mine + size - k, size)
+        if k:
+            waits[k - 1].wait_recv()
+        passed.append(
+            remote(
+                down_ref.at[0, block],
+                down_ref.at[1, block],
+                pass_send.at[k],
+                pass_recv.at[k],
+                partner,
+            )
+        )
+        passed[-1].start()
+    local_in.wait()
+    local_dy.wait()
+    pair_in.wait_recv()
     for copy in passed:
-        copy.wait()
-
-
-def middle(w, inward, heads, tokens, own_w, other_w, gains, router, prev, routes, hot, padded):
-    members = w.shape[0]
-    local, width = tokens.shape
-    seq = heads.shape[0]
-    any_spec = pl.BlockSpec(memory_space=pl.ANY)
-    vmem = pl.BlockSpec(memory_space=pltpu.VMEM)
-    dma = pltpu.SemaphoreType.DMA
-    return pl.pallas_call(
-        functools.partial(middle_kernel, members, padded),
-        out_shape=[
-            jax.ShapeDtypeStruct((EXPERTS_FF, padded, width), half),
-            jax.ShapeDtypeStruct(w.shape, half),
-            jax.ShapeDtypeStruct(w.shape, half),
-            jax.ShapeDtypeStruct(inward.shape, half),
-            jax.ShapeDtypeStruct((local, width), single),
-            jax.ShapeDtypeStruct((local, width), half),
-            jax.ShapeDtypeStruct((local, LANES), single),
-        ],
-        in_specs=[any_spec] * 2 + [vmem] * 9,
-        out_specs=[any_spec] * 4 + [vmem] * 3,
-        scratch_shapes=[
-            pltpu.VMEM((local, heads.shape[1]), half),
-            pltpu.VMEM((seq, width + LANES), half),
-            pltpu.VMEM((EXPERTS_FF // 2, 2 * padded, width + LANES), single),
-            pltpu.VMEM((EXPERTS_FF, padded, width), half),
-            pltpu.VMEM((16, 2 * LANES), single),
-            dma((members + EXPERTS_FF,)),
-            dma((EXPERTS_FF,)),
-            dma((members,)),
-            dma((members,)),
-            dma((members,)),
-            dma((2,)),
-            dma((3,)),
-            dma((3,)),
-        ],
-        compiler_params=pltpu.CompilerParams(
-            collective_id=1, has_side_effects=True, vmem_limit_bytes=50 << 20
-        ),
-        name="middle",
-    )(w, inward, heads, tokens, own_w, other_w, gains, router, prev, routes, hot)
-
-
-def expert_kernel(
-    padded,
-    x_ref,
-    dy_ref,
-    own_in_ref,
-    own_down_ref,
-    other_in_ref,
-    other_down_ref,
-    out_ref,
-    grad_ref,
-    og_ref,
-    hid_ref,
-    pg_ref,
-    pu_ref,
-    gate_ref,
-    eo_ref,
-    ig_ref,
-    dot_ref,
-):
-    f = pl.program_id(0)
-    sources = x_ref.shape[0]
-    count, width = og_ref.shape
-    chunk = count // 4
-    x_all = x_ref.reshape(count, width)
-    block = hid_ref.shape[2]
-
-    @pl.when(f == 0)
-    def _():
-        for s in range(sources):
-            rows = pl.ds(s * padded, padded)
-            gates = x_ref[s, padded - 16 :, : 2 * LANES].astype(single).T
+        copy.wait_recv()
+
+    ff = in_ref.shape[3]
+    block = fit(ff, 256)
+    steps = ff // block
+    rows2 = 2 * padded
+    dot_ref[...] = jnp.zeros(dot_ref.shape, single)
+
+    def spill(slot, array, place, source, part, f):
+        out = (hid_ref, pg_ref, pu_ref)[array]
+        rows = pl.ds(pl.multiple_of(source * padded, 16), padded)
+        return pltpu.make_async_copy(
+            spill_ref.at[slot, array, pl.ds(place * padded, padded)],
+            out.at[part, rows, pl.ds(f * block, block)],
+            spill_sem.at[slot, array, place],
+        )
+
+    def give_back(k, source):
+        return remote(
+            ig_ref.at[source], back_ref.at[mine], ig_send.at[k], ig_recv.at[k], {"dp": base + source}
+        )
+
+    @pl.loop(0, size // 2)
+    def _(q):
+        ks = [2 * q, 2 * q + 1]
+        sources = [lax.rem(mine + size - k, size) for k in ks]
+
+        @pl.when(q == 0)
+        def _():
+            pltpu.make_async_copy(stage_ref.at[0], x_ref.at[0], own_sem.at[0]).wait()
+
+        @pl.when(q > 0)
+        def _():
+            remote(
+                stage_ref.at[0], x_ref.at[0], x_send.at[0], x_recv.at[2 * q], partner
+            ).wait_recv()
+
+        remote(
+            stage_ref.at[0], x_ref.at[0], x_send.at[0], x_recv.at[2 * q + 1], partner
+        ).wait_recv()
+        for place, source in enumerate(sources):
+            rows = pl.ds(place * padded, padded)
+            gates = x_ref[source, padded - 16 :, : 2 * LANES].astype(single).T
             gate = jnp.broadcast_to(gates[:padded, 15:16], (padded, LANES))
             gate_ref[rows, :] = gate
-            og_ref[rows, :] = (dy_ref[s].astype(single) * gate[:, :1]).astype(half)
-        eo_ref[...] = jnp.zeros(eo_ref.shape, single)
-        ig_ref[...] = jnp.zeros(ig_ref.shape, single)
-
-    for part, (in_ref, down_ref) in enumerate(
-        ((own_in_ref, own_down_ref), (other_in_ref, other_down_ref))
-    ):
-        gate_w, up_w = (in_ref[:, k].reshape(width, block) for k in range(2))
-        down_w = down_ref[...].reshape(width, block)
-        for r in range(4):
-            rows = pl.ds(r * chunk, chunk)
-            x = x_all[rows, :]
-            og = og_ref[rows, :]
-            pre = mm(x, gate_w)
-            up = mm(x, up_w)
-            hg = mm(og, down_w)
-            sigma = jax.nn.sigmoid(pre)
-            active = pre * sigma
-            hidden = (active * up).astype(half)
-            pg = (hg * up * (sigma * (1.0 + pre * (1.0 - sigma)))).astype(half)
-            pu = (hg * active).astype(half)
-            hid_ref[part, rows, :] = hidden
-            pg_ref[part, rows, :] = pg
-            pu_ref[part, rows, :] = pu
-            eo_ref[rows, :] += mm_nt(hidden, down_w)
-            ig_ref[rows, :] += mm_nt(pg, gate_w) + mm_nt(pu, up_w)
-
-    @pl.when(f == pl.num_programs(0) - 1)
-    def _():
-        dot_ref[...] = jnp.zeros(dot_ref.shape, single)
+            og_ref[source] = (dy_ref[source].astype(single) * gate[:, :1]).astype(half)
+        for number in range(2):
+            acc_ref[number, :, :width] = jnp.zeros((rows2, width), single)
+
+        @pl.loop(0, 2)
+        def _(part):
+            for f in range(steps):
+                lanes = pl.ds(f * block, block)
+                slot = f % 2
+                if f >= 2:
+                    for array in range(3):
+                        for place, source in enumerate(sources):
+                            spill(slot, array, place, source, part, f - 2).wait()
+                gate_w = win_ref[part, :, 0, :, lanes].reshape(width, block)
+                up_w = win_ref[part, :, 1, :, lanes].reshape(width, block)
+                down_w = down_ref[part, :, :, lanes].reshape(width, block)
+                x = jnp.concatenate([x_ref[source] for source in sources], 0)
+                og = jnp.concatenate([og_ref[source] for source in sources], 0)
+                pre = mm(x, gate_w)
+                up = mm(x, up_w)
+                hg = mm(og, down_w)
+                sigma = jax.nn.sigmoid(pre)
+                active = pre * sigma
+                hidden = (active * up).astype(half)
+                pg = (hg * up * (sigma * (1.0 + pre * (1.0 - sigma)))).astype(half)
+                pu = (hg * active).astype(half)
+                spill_ref[slot, 0] = hidden
+                spill_ref[slot, 1] = pg
+                spill_ref[slot, 2] = pu
+                acc_ref[0, :, :width] += mm_nt(hidden, down_w)
+                acc_ref[1, :, :width] += mm_nt(pg, gate_w) + mm_nt(pu, up_w)
+                for array in range(3):
+                    for place, source in enumerate(sources):
+                        spill(slot, array, place, source, part, f).start()
+            for f in range(max(0, steps - 2), steps):
+                for array in range(3):
+                    for place, source in enumerate(sources):
+                        spill(f % 2, array, place, source, part, f).wait()
+
         ones = jnp.ones((16, width), half)
-        for s in range(sources):
-            rows = pl.ds(s * padded, padded)
-            eo = eo_ref[rows, :]
-            out_ref[s] = (eo * gate_ref[rows, :1]).astype(half)
-            grad_ref[s] = ig_ref[rows, :].astype(half)
-            product = eo * dy_ref[s].astype(single)
+        for place, source in enumerate(sources):
+            rows = pl.ds(place * padded, padded)
+            eo = acc_ref[0, rows, :width]
+            out_ref[source] = (eo * gate_ref[rows, :1]).astype(half)
+            ig_ref[source] = acc_ref[1, rows, :width].astype(half)
+            product = eo * dy_ref[source].astype(single)
             top = product.astype(half)
             low = (product - top.astype(single)).astype(half)
             dot_ref[:, :padded] = mm_nt(ones, top) + mm_nt(ones, low)
             dots = dot_ref[...]
             high = dots.astype(half).astype(single)
             row = lax.broadcasted_iota(jnp.int32, dots.shape, 0)
-            tail = ig_ref[pl.ds((s + 1) * padded - 16, 16), : 2 * LANES]
-            tail = jnp.where(row == 14, high, jnp.where(row == 15, dots - high, tail))
-            grad_ref[s, padded - 16 :, : 2 * LANES] = tail.astype(half)
-
-
-def expert_step(x, dy, own_in, own_down, other_in, other_down, padded):
-    sources, _, width = x.shape
-    count = sources * padded
-    m, _, r, ff = own_in.shape
+            last = acc_ref[1, pl.ds((place + 1) * padded - 16, 16), : 2 * LANES]
+            last = jnp.where(row == 14, high, jnp.where(row == 15, dots - high, last))
+            ig_ref[source, padded - 16 :, : 2 * LANES] = last.astype(half)
+
+        @pl.when(q == 0)
+        def _():
+            pltpu.make_async_copy(ig_ref.at[mine], back_ref.at[mine], own_sem.at[0]).start()
+
+        @pl.when(q > 0)
+        def _():
+            give_back(2 * q, sources[0]).start()
+
+        give_back(2 * q + 1, sources[1]).start()
+
+    pltpu.make_async_copy(ig_ref.at[mine], back_ref.at[mine], own_sem.at[0]).wait()
+    for k in range(1, size):
+        give_back(k, lax.rem(mine + size - k, size)).wait()
+    heads_done = [swap_rows, pair_in]
+    for copy in waits + passed + heads_done:
+        copy.wait_send()
+
+
+def experts(
+    w, far, inward, dy, heads, tokens, own_w, other_w, gains, router, prev, routes, hot, padded
+):
+    members, _, d_rows, ff = inward.shape
+    local, width = tokens.shape
+    seq = heads.shape[0]
+    size = EXPERTS_FF
     block = fit(ff, 256)
-    whole = pl.BlockSpec((sources, padded, width), lambda f: (0, 0, 0))
-    two = pl.BlockSpec((m, 2, r, block), lambda f: (0, 0, 0, f))
-    one = pl.BlockSpec((m, r, block), lambda f: (0, 0, f))
-    wide = pl.BlockSpec((2, count, block), lambda f: (0, 0, f))
+    any_spec = pl.BlockSpec(memory_space=pl.ANY)
+    vmem = pl.BlockSpec(memory_space=pltpu.VMEM)
+    dma = pltpu.SemaphoreType.DMA
+    rows = jax.ShapeDtypeStruct((size, padded, width), half)
+    wide = jax.ShapeDtypeStruct((2, size * padded, ff), half)
     return pl.pallas_call(
-        functools.partial(expert_kernel, padded),
-        grid=(ff // block,),
-        in_specs=[whole, whole, two, one, two, one],
-        out_specs=[whole, whole, pl.BlockSpec((count, width), lambda f: (0, 0)), wide, wide, wide],
+        functools.partial(experts_kernel, members, padded),
         out_shape=[
-            jax.ShapeDtypeStruct(x.shape, half),
-            jax.ShapeDtypeStruct(x.shape, half),
-            jax.ShapeDtypeStruct((count, width), half),
-            jax.ShapeDtypeStruct((2, count, ff), half),
-            jax.ShapeDtypeStruct((2, count, ff), half),
-            jax.ShapeDtypeStruct((2, count, ff), half),
+            rows,
+            rows,
+            rows,
+            rows,
+            wide,
+            wide,
+            wide,
+            jax.ShapeDtypeStruct((local, width), single),
+            jax.ShapeDtypeStruct((local, width), half),
+            jax.ShapeDtypeStruct((local, LANES), single),
         ],
+        in_specs=[any_spec] * 4 + [vmem] * 9,
+        out_specs=[any_spec] + [vmem] * 3 + [any_spec] * 3 + [vmem] * 3,
         scratch_shapes=[
-            pltpu.VMEM((count, LANES), single),
-            pltpu.VMEM((count, width), single),
-            pltpu.VMEM((count, width), single),
+            pltpu.VMEM((local, heads.shape[1]), half),
+            pltpu.VMEM((seq, width + LANES), half),
+            pltpu.VMEM((size // 2, 2 * padded, width + LANES), single),
+            pltpu.VMEM((size, padded, width), half),
             pltpu.VMEM((16, 2 * LANES), single),
+            pltpu.VMEM((2,) + inward.shape, half),
+            pltpu.VMEM((2, members, d_rows, ff), half),
+            pltpu.VMEM((size, padded, width), half),
+            pltpu.VMEM((size, padded, width), half),
+            pltpu.VMEM((2, 3, 2 * padded, block), half),
+            pltpu.VMEM((2 * padded, LANES), single),
+            pltpu.VMEM((16, 2 * LANES), single),
+            dma((size,)),
+            dma((size,)),
+            dma((size,)),
+            dma((size,)),
+            dma((size + members // size,)),
+            dma((size + members // size,)),
+            dma((4,)),
+            dma((members // size,)),
+            dma((3,)),
+            dma((3,)),
+            dma((size,)),
+            dma((size,)),
+            dma((2, 3, 2)),
         ],
-        compiler_params=pltpu.CompilerParams(vmem_limit_bytes=58 << 20),
-        cost_estimate=pl.CostEstimate(
-            flops=12 * count * width * 2 * ff,
-            bytes_accessed=2 * 6 * width * ff + 20 * count * ff,
-            transcendentals=0,
+        compiler_params=pltpu.CompilerParams(
+            collective_id=1, has_side_effects=True, vmem_limit_bytes=62 << 20
         ),
-        name="expert_step",
-    )(x, dy, own_in, own_down, other_in, other_down)
+        name="experts",
+    )(w, far, inward, dy, heads, tokens, own_w, other_w, gains, router, prev, routes, hot)
 
 
 def split(x):
@@ -1077,7 +1146,19 @@
 
 
 def weight_kernel(
-    x_ref, og_ref, hid_ref, pg_ref, pu_ref, out_ref, xt_ref, ogt_ref, send_ref, got_ref, send_sem, recv_sem
+    x_ref,
+    og_ref,
+    hid_ref,
+    pg_ref,
+    pu_ref,
+    out_ref,
+    xt_ref,
+    ogt_ref,
+    send_ref,
+    got_ref,
+    own_ref,
+    send_sem,
+    recv_sem,
 ):
     f = pl.program_id(0)
     partner = {"tensor": 1 - lax.axis_index("tensor")}
@@ -1105,10 +1186,11 @@
     for k, (left, right) in enumerate(factors):
         send_ref[f, k] = mm(left[...], right[1]).astype(half)
     remote(f).start()
-    grads = [mm(left[...], right[0]) for left, right in factors]
+    for k, (left, right) in enumerate(factors):
+        own_ref[k] = mm(left[...], right[0])
     remote(f).wait_recv()
     for k in range(3):
-        total = grads[k] + got_ref[f, k].astype(single)
+        total = own_ref[k] + got_ref[f, k].astype(single)
         out_ref[:, k] = total.astype(half).reshape(shape)
 
     @pl.when(f == pl.num_programs(0) - 1)
@@ -1136,6 +1218,7 @@
             pltpu.VMEM((width, count), half),
             pltpu.VMEM((steps, 3, width, block), half),
             pltpu.VMEM((steps, 3, width, block), half),
+            pltpu.VMEM((3, width, block), single),
             pltpu.SemaphoreType.DMA((steps,)),
             pltpu.SemaphoreType.DMA((steps,)),
         ],
@@ -1174,7 +1257,6 @@
     first_ref,
     stage_ref,
     second_ref,
-    eo_in_ref,
     one_out_ref,
     one_in_ref,
     ffn_out_ref,
@@ -1188,23 +1270,18 @@
     recv1,
     send2,
     recv2,
-    eo_send,
-    eo_recv,
     pair_send,
     pair_recv,
     near_send,
     near_recv,
     far_send,
     far_recv,
-    own_sem,
 ):
     size = EXPERTS_FF
     me = lax.axis_index("dp")
     core = lax.axis_index("tensor")
     high = members // low
     inside, row = lax.rem(me, low), me // low
-    mine = lax.rem(me, size)
-    base = me - mine
     local, width = base_ref.shape
     count = size * padded
     d_rows = dense_out_ref.shape[0]
@@ -1219,7 +1296,6 @@
         return lax.rem(row + k, high) * low + inside
 
     peers = [beside(k) for k in range(1, low)] + [across(k) for k in range(1, high)]
-    peers += [base + lax.rem(mine + k, size) for k in range(1, size)]
     barrier = pltpu.get_barrier_semaphore()
     for peer in peers:
         pl.semaphore_signal(barrier, inc=1, device_id={"dp": peer}, device_id_type=MESH)
@@ -1235,18 +1311,6 @@
             device_id=device,
             device_id_type=MESH,
         )
-
-    eo = []
-    for k in range(1, size):
-        to = lax.rem(mine + k, size)
-        eo.append(
-            remote(
-                eo_ref.at[to], eo_in_ref.at[mine], eo_send.at[k], eo_recv.at[k], {"dp": base + to}
-            )
-        )
-    eo.append(pltpu.make_async_copy(eo_ref.at[mine], eo_in_ref.at[mine], own_sem))
-    for copy in eo:
-        copy.start()
 
     sent = []
     chunks = 2
@@ -1293,6 +1357,23 @@
         here = pl.ds(pl.multiple_of(core * local + r * step, step), step)
         tokens_ref[rows, :] = one_part(here)
 
+    eo_all = eo_ref.reshape(count, width)
+
+    @pl.loop(0, local // step)
+    def _(r):
+        rows = pl.ds(pl.multiple_of(r * step, step), step)
+        there = pl.ds(pl.multiple_of((1 - core) * local + r * step, step), step)
+        ffn_out_ref[rows, :] = mm(slot_rows(info_ref[there, :], count), eo_all[...]).astype(half)
+
+    ffn_sent = remote(ffn_out_ref, ffn_in_ref, pair_send.at[2], pair_recv.at[2], partner)
+    ffn_sent.start()
+
+    @pl.loop(0, local // step)
+    def _(r):
+        rows = pl.ds(pl.multiple_of(r * step, step), step)
+        here = pl.ds(pl.multiple_of(core * local + r * step, step), step)
+        ffn_ref[rows, :] = mm(slot_rows(info_ref[here, :], count), eo_all[...])
+
     pair = remote(mine_ref, pair_ref, pair_send.at[1], pair_recv.at[1], partner)
     pair.start()
     pair.wait()
@@ -1312,11 +1393,12 @@
 
     for j in range(1, high + 1):
         h = lax.rem(row + j, high)
-        total = dense_ref[h * low + inside].astype(single)
         for k in range(low - 1):
             remote(
                 dense_ref.at[0], first_ref.at[k, h], send1.at[k, h], recv1.at[k, h], partner
             ).wait_recv()
+        total = dense_ref[h * low + inside].astype(single)
+        for k in range(low - 1):
             total += first_ref[k, h].astype(single)
         if j < high:
             stage_ref[j - 1] = total.astype(half)
@@ -1349,25 +1431,6 @@
         )
         far[-1].start()
 
-    for copy in eo:
-        copy.wait()
-    eo_all = eo_in_ref.reshape(count, width)
-
-    @pl.loop(0, local // step)
-    def _(r):
-        rows = pl.ds(pl.multiple_of(r * step, step), step)
-        there = pl.ds(pl.multiple_of((1 - core) * local + r * step, step), step)
-        ffn_out_ref[rows, :] = mm(slot_rows(info_ref[there, :], count), eo_all[...]).astype(half)
-
-    ffn_sent = remote(ffn_out_ref, ffn_in_ref, pair_send.at[2], pair_recv.at[2], partner)
-    ffn_sent.start()
-
-    @pl.loop(0, local // step)
-    def _(r):
-        rows = pl.ds(pl.multiple_of(r * step, step), step)
-        here = pl.ds(pl.multiple_of(core * local + r * step, step), step)
-        ffn_ref[rows, :] = mm(slot_rows(info_ref[here, :], count), eo_all[...])
-
     one_sent.wait()
 
     @pl.loop(0, local // step)
@@ -1424,14 +1487,13 @@
             jax.ShapeDtypeStruct((local, width), half),
             jax.ShapeDtypeStruct(small.shape, single),
         ],
-        in_specs=[pl.BlockSpec(memory_space=pl.ANY)] + [vmem] * 10,
+        in_specs=[vmem] * 11,
         out_specs=[vmem] * 4,
         scratch_shapes=[
             pltpu.VMEM((members, d_rows, wide), half),
             pltpu.VMEM((low - 1, high, d_rows, wide), half),
             pltpu.VMEM((high - 1, d_rows, wide), half),
             pltpu.VMEM((high - 1, d_rows, wide), half),
-            pltpu.VMEM(eo.shape, half),
             rows_half,
             rows_half,
             rows_half,
@@ -1445,15 +1507,12 @@
             dma((low - 1, high)),
             dma((high - 1,)),
             dma((high - 1,)),
-            dma((EXPERTS_FF,)),
-            dma((EXPERTS_FF,)),
             dma((3,)),
             dma((3,)),
             dma((low,)),
             dma((low,)),
             dma((high,)),
             dma((high,)),
-            dma,
         ],
         compiler_params=pltpu.CompilerParams(
             collective_id=4, has_side_effects=True, vmem_limit_bytes=60 << 20
@@ -1488,7 +1547,7 @@
         return lax.all_to_all(blocks, "dp", 0, 0, axis_index_groups=cubes, tiled=True)
 
     def plain_tail(eo, qkv, one, proj, outg, x, base, resid, gains, small):
-        ffn = pair_sum(mm_tn(onehot, in_group(eo).reshape(-1, width)))
+        ffn = pair_sum(mm_tn(onehot, eo.reshape(-1, width)))
         part = mm_nt(qkv, proj)
         scale = rms_scale(x)
         small = small.at[18].set(jnp.sum(part * x * scale, axis=0))
@@ -1515,8 +1574,8 @@
     pack = jnp.pad(pack, ((0, 0), (0, -columns % LANES)))
     ids = jnp.concatenate([segment_ids, routes[0].T], 0)
     ids = jnp.pad(ids, ((0, 5), (0, 0)))
-    full_pack, tokens_all, got_dy, onehot, info = start(
-        pack, tokens[0], cotangent[0], ids, members, per_core, padded
+    full_pack, tokens_all, got_dy, onehot, info, far_down = start(
+        pack, tokens[0], cotangent[0], ids, expert_weight, members, per_core, padded
     )
     full_pack, expert_weight = lax.optimization_barrier((full_pack, expert_weight))
     full_pack = full_pack.reshape(members * d_rows, -1)[:, :columns]
@@ -1531,12 +1590,7 @@
     in_weight = jnp.broadcast_to(
         expert_weight[None, :, :2], (groups, EXPERTS_FF, 2) + expert_weight.shape[2:]
     ).reshape((members, 2) + expert_weight.shape[2:])
-    down_weight = jnp.broadcast_to(
-        expert_weight[None, :, 2], (groups, EXPERTS_FF) + expert_weight.shape[2:]
-    ).reshape((members,) + expert_weight.shape[2:])
     my_in = lax.all_to_all(in_weight, "dp", 0, 0, tiled=True)
-    if d_rows % 16:
-        my_in = my_in.transpose(1, 0, 2, 3).reshape(1, 2, width, -1)
 
     x_rows = tokens[0].astype(single)
     local_rows = x_rows.shape[0]
@@ -1555,9 +1609,11 @@
     mixed_prev = jnp.dot(prev_rows, gate_mixing, precision=HIGH)
     mixed_prev = jnp.pad(mixed_prev, ((0, 0), (0, LANES - EXPERTS)))
     router_wide = jnp.pad(router_full, ((0, 0), (0, LANES - router_full.shape[1])))
-    got_rows, my_down, other_down, other_in, resid, normed_two, misc = middle(
-        down_weight,
+    back_grad, gated_out, got_rows, out_grad, hidden, pg, pu, resid, normed_two, misc = experts(
+        expert_weight,
+        far_down,
         my_in,
+        got_dy,
         heads_out,
         tokens[0],
         outw_own,
@@ -1569,19 +1625,17 @@
         onehot,
         padded,
     )
-    if d_rows % 16:
-        my_down = my_down.reshape(1, width, -1)
-        other_down = other_down.reshape(1, width, -1)
-
     count = EXPERTS_FF * padded
-    gated_out, in_grad, out_grad, hidden, pg, pu = expert_step(
-        got_rows, got_dy, my_in, my_down, other_in, other_down, padded
+    grads_sent = weight_step(
+        got_rows.reshape(count, width),
+        out_grad.reshape(count, width),
+        hidden,
+        pg,
+        pu,
+        1 if d_rows % 16 else members,
     )
-    back_grad = in_group(in_grad)
-    grads_sent = weight_step(
-        got_rows.reshape(count, width), out_grad, hidden, pg, pu, my_in.shape[0]
-    )
-    back_grad, grads_sent = lax.optimization_barrier((back_grad, grads_sent))
+    back_out = in_group(gated_out)
+    back_grad, grads_sent, back_out = lax.optimization_barrier((back_grad, grads_sent, back_out))
     if d_rows % 16:
         grads_sent = grads_sent.reshape(3, members, d_rows, -1).transpose(1, 0, 2, 3)
     grads_got = lax.all_to_all(grads_sent, "dp", 0, 0, tiled=True)
@@ -1611,12 +1665,12 @@
     out_w_grad = out_w_grad.astype(half)
     if d_rows % 16 or members != 16:
         outs = plain_tail(
-            gated_out, qkv_grad, full_one, proj_full, out_w_grad, x_all, base, resid_grad, gains, small
+            back_out, qkv_grad, full_one, proj_full, out_w_grad, x_all, base, resid_grad, gains, small
         )
     else:
         outs = tail(
             members,
-            gated_out,
+            back_out,
             qkv_grad,
             full_one,
             proj_full,

time: 532 us -> 499 us (0.938)
  Pallas kernels: 409 us -> 368 us
  starting transfers between devices: 21.2 us -> 30.8 us
    pallas_call x1, Pallas kernels: 83 us -> 55.7 us  [tail(): pl.pallas_call(functools.partial(tail_kernel, members, low, padded), out_...]
    pallas_call x2 -> x1, Pallas kernels: 104 us -> 93.3 us  [experts(): pl.pallas_call(functools.partial(experts_kernel, members, padded), out_sh...]
    pallas_call x1, Pallas kernels: 37.6 us -> 28.2 us  [weight_step(): pl.pallas_call(weight_kernel, grid=(steps,), in_specs=[whole, whole, wide...]
    pallas_call x1, Pallas kernels: 63.1 us -> 71.9 us  [start(): pl.pallas_call(functools.partial(start_kernel, members, low, per_core, pa...]
    all_to_all x1, starting transfers between devices: 6.88 us -> 13.7 us  [per_device(): my_in = lax.all_to_all(in_weight, 'dp', 0, 0, tiled=True)]
    unnamed x66 -> x56, local copies, waits for them, and re-layouts: 20.8 us -> 23.1 us
where the time goes in v4:
time: 499 us; the launch traced here: 489 us
  Pallas kernels  368 us (74%)
  local copies, waits for them, and re-layouts  47.8 us (10%)
  starting transfers between devices  30.8 us (6%)
  waiting for transfers between devices  18.5 us (4%)
  matrix products  11.8 us (2%)
  other arithmetic  10.8 us (2%)
    pallas_call x1, Pallas kernels, experts(): pl.pallas_call(functools.partial(experts_kernel, members, padded), out_sh...  93.3 us
    pallas_call x1, Pallas kernels, start(): pl.pallas_call(functools.partial(start_kernel, members, low, per_core, pa...  71.9 us
    pallas_call x1, Pallas kernels, tail(): pl.pallas_call(functools.partial(tail_kernel, members, low, padded), out_...  55.7 us
    pallas_call x1, Pallas kernels, attention_backward(): pl.pallas_call(functools.partial(bwd_kernel, heads), grid_spec=pltpu.Pref...  48.1 us
    pallas_call x1, Pallas kernels, backward_middle(): pl.pallas_call(functools.partial(back_kernel, padded), out_shape=[jax.Sha...  38.8 us
    pallas_call x1, Pallas kernels, attention_forward(): pl.pallas_call(functools.partial(fwd_kernel, heads), grid_spec=pltpu.Pref...  31.8 us
    pallas_call x1, Pallas kernels, weight_step(): pl.pallas_call(weight_kernel, grid=(steps,), in_specs=[whole, whole, wide...  28.2 us
    unnamed x56, local copies, waits for them, and re-layouts  23.1 us
  transfers between devices with their start and end apart: 4, of which 2 were waited for; matrix products, arithmetic and copies ran while one was open for 6% of the time, Pallas kernels for 30%

profile of v4, /device:TPU:12, one launch (start us, length us, event | category | flops | bytes accessed | tf_op | source)
XLA Modules:
  0.0 489.0 jit_solution(14442187601866416225)
XLA Ops:
  0.6 0.8 copy.81
  1.4 0.8 copy.83
  2.2 0.8 copy.82
  2.9 0.9 copy.103
  3.8 0.9 copy.84
  4.8 0.2 copy.85
  5.0 0.9 concatenate.6
  5.9 0.7 pad_add_fusion
  6.6 1.7 copy-done
  8.3 1.4 copy-done.1
  9.7 1.4 copy-done.2
  11.1 71.9 %start.1 = (bf16[16,48,1664]{2,1,0:T(8,128)(2,1)S(1)}, bf16[2048,768]{1,0:T(8,128)(2,1)}, bf16[8,176,768]{2,1,0:T(8,128)(2,1)S(1)}, bf16[1408,2048]{1,0:T(8,128)...) custom-call(bf16[48,1664]{1,0:T(8,128)(2,1)S(1)} %pad.23.pack_ref, bf16[1024,768]{1,0:T(8,128)(2,1)S(1)} %bitcast.70, ...), custom_call_target="tpu_custom_call" | custom-call | tf_op jit(solution)/shard_map/start/pallas_call | solution.py:488
  83.0 2.4 broadcast_in_dim.8
  85.4 0.7 copy-done.8
  86.1 0.5 copy-done.9
  86.6 13.7 %all-to-all-start = ((bf16[16,2,48,1024]{3,2,1,0:T(8,128)(2,1)}), bf16[16,2,48,1024]{3,2,1,0:T(8,128)(2,1)}, u32[]{:S(2)}, u32[]{:S(2)}) async-start(bf16[16,2,48,1024]{3,2,1,0:T(8,128)(2,1)} %bitcast.78), calls=%async_computation | async-start | bytes 6291456 | tf_op jit(solution)/shard_map/all_to_all | solution.py:1593
  100.3 0.9 slice.95.own_w_ref
  101.6 0.1 copy.100
  101.7 0.1 slice_convert_fusion
  101.8 0.1 copy.104
  102.0 1.4 copy.90.start_ref
  103.4 0.2 convert_reduce_fusion.1
  103.6 2.7 fusion
  106.4 0.8 fusion.2.one_ref
  107.2 1.6 copy-done.16
  108.8 5.8 %convolution_convert_fusion.q_ref.k_ref.v_ref = bf16[2048,1152]{1,0:T(8,128)(2,1)} fusion(bf16[2048,768]{1,0:T(8,128)(2,1)S(1)} %fusion.2.one_ref, bf16[768,1664]{1,0:T(8,128)(2,1)S(1)} %bitcast.75), kind=kOutput, calls=%fused_computation.3 | convolution fusion | flops 3626237952 | bytes 9633792 | tf_op jit(solution)/shard_map/dot_general | solution.py:38
  114.6 31.8 %shard_map.195 = (f32[2048,384]{1,0:T(8,128)}, bf16[2048,384]{1,0:T(8,128)(2,1)S(1)}, f32[2048,128]{1,0:T(8,128)S(1)}) custom-call(s32[4,8]{1,0:T(4,128)S(1)} %pad_add_fusion.1.bounds, bf16[2048,1152]{1,0:T(8,128)(2,1)} %convolution_convert_fusion.q_ref.k_ref.v_ref, bf16[2048,1152]{1,0:T(8,128)(2,1)} %convolution_convert_fusion.q_ref.k_ref.v_ref, ...), custom_call_target="tpu_custom_call" | custom-call | flops 12884901888 | bytes 12582912 | tf_op jit(solution)/shard_map/pallas_call | solution.py:153
  146.5 1.1 copy-done.3
  147.6 1.0 copy-done.13
  148.5 0.8 slice.96
  149.3 1.0 copy.91
  150.4 1.7 pad.25.router_ref
  152.0 1.3 fusion.4
  153.3 0.8 pad.26.prev_ref
  154.1 12.2 %all-to-all-done.in_ref = bf16[16,2,48,1024]{3,2,1,0:T(8,128)(2,1)} async-done(((bf16[16,2,48,1024]{3,2,1,0:T(8,128)(2,1)}), bf16[16,2,48,1024]{3,2,1,0:T(8,128)(2,1)}, u32[]{:S(2)}, u32[]{:S(2)}) %all-to-all-start) | async-done | bytes 3145760 | tf_op jit(solution)/shard_map/all_to_all | solution.py:1593
  166.4 93.3 %experts.1 = (bf16[8,176,768]{2,1,0:T(8,128)(2,1)}, bf16[8,176,768]{2,1,0:T(8,128)(2,1)}, bf16[8,176,768]{2,1,0:T(8,128)(2,1)}, bf16[8,176,768]{2,1,0:T(8,128)(2...) custom-call(bf16[8,3,48,1024]{3,2,1,0:T(8,128)(2,1)} %w_ref.2, ...), custom_call_target="tpu_custom_call" | custom-call | tf_op jit(solution)/shard_map/experts/pallas_call | solution.py:864
  259.7 9.2 %all-to-all-start.1 = ((bf16[8,176,768]{2,1,0:T(8,128)(2,1)}), bf16[8,176,768]{2,1,0:T(8,128)(2,1)S(1)}, u32[]{:S(2)}, u32[]{:S(2)}) async-start(bf16[8,176,768]{2,1,0:T(8,128)(2,1)} %get-tuple-element.61), calls=%async_computation.1 | async-start | bytes 4325376 | tf_op jit(solution)/shard_map/all_to_all | solution.py:1547
  268.9 28.2 %weight_step.1 = bf16[16,3,48,1024]{3,2,1,0:T(8,128)(2,1)} custom-call(bf16[1408,768]{1,0:T(8,128)(2,1)} %bitcast.99, bf16[1408,768]{1,0:T(8,128)(2,1)} %bitcast.100, bf16[2,1408,1024]{2,1,0:T(8,128)(2,1)} %get-tuple-element.58.hid_ref, bf16[2,1408,1024]{2,1,0:T(8,128)(2,1)} %get-tuple-element.59.pg_ref, bf16[2,1408,1024]{2,1,0:T(8,128)(2,1)} %get-tuple-element.60.pu_ref), custom_call_target="tpu_custom_call" | custom-call | flops 13287555072 | bytes 26738688 | tf_op jit(solution)/shard_map/weight_step/pallas_call | solution.py:1210
  297.2 1.3 copy-done.17
  298.5 7.9 %all-to-all-start.2 = ((bf16[16,3,48,1024]{3,2,1,0:T(8,128)(2,1)}), bf16[16,3,48,1024]{3,2,1,0:T(8,128)(2,1)}, u32[]{:S(2)}, u32[]{:S(2)}) async-start(bf16[16,3,48,1024]{3,2,1,0:T(8,128)(2,1)} %weight_step.1), calls=%async_computation.2 | async-start | bytes 9437184 | tf_op jit(solution)/shard_map/all_to_all | solution.py:1641
  306.4 1.3 pad.28.mix_ref
  307.7 1.3 copy.93
  309.0 1.4 slice.94.proj_ref
  310.5 0.8 pad.27.prev_ref
  311.3 0.7 copy.105
  312.0 38.8 %backward_middle.1 = (f32[1024,768]{1,0:T(8,128)}, bf16[2048,768]{1,0:T(8,128)(2,1)}, bf16[2048,384]{1,0:T(8,128)(2,1)}, f32[1024,768]{1,0:T(8,128)}, f32[1024,1...) custom-call(bf16[8,176,768]{2,1,0:T(8,128)(2,1)} %get-tuple-element.63.back_ref, s32[2048,8]{1,0:T(8,128)} %bitcast.79, ...), custom_call_target="tpu_custom_call" | custom-call | tf_op jit(solution)/shard_map/backward_middle/pallas_call | solution.py:1120
  350.8 1.1 slice_bitcast_fusion
  351.9 0.8 copy.95
  352.7 4.7 convolution_convert_fusion.1.outg_ref
  357.4 1.2 copy-done.14
  358.6 48.1 %shard_map.196.qkv_ref = bf16[2048,1152]{1,0:T(8,128)(2,1)} custom-call(s32[4,8]{1,0:T(4,128)S(1)} %pad_add_fusion.1.bounds, bf16[2048,1152]{1,0:T(8,128)(2,1)} %convolution_convert_fusion.q_ref.k_ref.v_ref, bf16[2048,1152]{1,0:T(8,128)(2,1)} %convolution_convert_fusion.q_ref.k_ref.v_ref, bf16[2048,1152]{1,0:T(8,128)(2,1)} %convolution_convert_fusion.q_ref.k_ref.v_ref, ...), custom_call_target="tpu_custom_call" | custom-call | flops 32212254720 | bytes 15728640 | tf_op jit(solution)/shard_map/pallas_call | solution.py:255
  406.7 6.3 %all-to-all-done.2 = bf16[16,3,48,1024]{3,2,1,0:T(8,128)(2,1)} async-done(((bf16[16,3,48,1024]{3,2,1,0:T(8,128)(2,1)}), bf16[16,3,48,1024]{3,2,1,0:T(8,128)(2,1)}, u32[]{:S(2)}, u32[]{:S(2)}) %all-to-all-start.2) | async-done | bytes 4718624 | tf_op jit(solution)/shard_map/all_to_all | solution.py:1641
  413.0 55.7 %tail.1 = (f32[48,1536]{1,0:T(8,128)}, f32[1024,768]{1,0:T(8,128)}, bf16[1024,768]{1,0:T(8,128)(2,1)}, f32[24,768]{1,0:T(8,128)}) custom-call(bf16[8,176,768]{2,1,0:T(8,128)(2,1)} %copy-done.17, bf16[2048,1152]{1,0:T(8,128)(2,1)} %shard_map.196.qkv_ref, bf16[2048,768]{1,0:T(8,128)(2,1)} %copy-done.16, bf16[768,1152]{1,0:T(8,128)(2,1)} %slice.94.proj_ref, ...), custom_call_target="tpu_custom_call" | custom-call | tf_op jit(solution)/shard_map/tail/pallas_call | solution.py:1482
  468.7 1.5 slice.83
  470.2 1.6 slice.82
  471.9 6.2 %convert_reduce_fusion = f32[8,3,48,1024]{3,2,1,0:T(8,128)} fusion(bf16[2,8,3,48,1024]{4,3,2,1,0:T(8,128)(2,1)} %bitcast.28), kind=kLoop, calls=%fused_computation | loop fusion | flops 3538944 | bytes 9437184 | tf_op jit(solution)/shard_map/reduce_sum | solution.py:1687
  478.1 0.9 slice.87
  479.0 1.5 dynamic-slice_bitcast_fusion
  480.5 0.6 reshape.318
  481.1 1.0 reshape.317
  482.1 0.7 copy.96
  482.8 1.4 fusion.7
  484.2 2.7 copy.108
  486.9 1.7 copy.109
  (51 shorter events, 0.5 us)
Async XLA Ops:
  4.8 78.2 %copy-start.18 = (s32[1,1024,2]{2,1,0:T(8,128)}, s32[1,1024,2]{2,1,0:T(8,128)S(1)}, u32[]{:S(2)}) copy-start(s32[1,1024,2]{2,1,0:T(8,128)S(1)} %copy.84) | copy-start | bytes 24580
  6.6 1.7 copy-start
  8.3 1.4 copy-start.1
  9.7 1.4 copy-start.2
  11.1 71.9 %slice-start = ((bf16[8,3,48,1024]{3,2,1,0:T(8,128)(2,1)}), bf16[8,2,48,1024]{3,2,1,0:T(8,128)(2,1)S(1)}, s32[]{:S(2)}) async-start(bf16[8,3,48,1024]{3,2,1,0:T(8,128)(2,1)} %w_ref.2), calls=%async_computation.3 | async-start | bytes 3145728 | tf_op jit(solution)/shard_map/slice | solution.py:1591
  83.0 2.5 copy-start.5
  83.0 3.1 copy-start.8
  83.0 3.6 copy-start.9
  86.6 13.7 %copy-start.6 = (bf16[16,48,1664]{2,1,0:T(8,128)(2,1)S(1)}, bf16[16,48,1664]{2,1,0:T(8,128)(2,1)}, u32[]{:S(2)}) copy-start(bf16[16,48,1664]{2,1,0:T(8,128)(2,1)} %copy-done.5) | copy-start | bytes 7667716
  86.6 79.8 %all-to-all-start = ((bf16[16,2,48,1024]{3,2,1,0:T(8,128)(2,1)}), bf16[16,2,48,1024]{3,2,1,0:T(8,128)(2,1)}, u32[]{:S(2)}, u32[]{:S(2)}) async-start(bf16[16,2,48,1024]{3,2,1,0:T(8,128)(2,1)} %bitcast.78), calls=%async_computation | async-start | bytes 6291456 | tf_op jit(solution)/shard_map/all_to_all | solution.py:1593
  101.2 52.9 %collective-permute-start = (bf16[768,384]{1,0:T(8,128)(2,1)}, bf16[768,384]{1,0:T(8,128)(2,1)}, u32[]{:S(2)}, u32[]{:S(2)}) collective-permute-start(bf16[768,384]{1,0:T(8,128)(2,1)} %slice.95.own_w_ref), channel_id=1, source_target_pairs={{0,1},{1,0},{2,3},{3,2},{4,5},{5,4},{6,7},{7,6},{8,9},{9,8},{10,11... | collective-permute-start | bytes 1769480 | tf_op jit(solution)/shard_map/ppermute | solution.py:50
  102.0 5.2 %copy-start.20 = (f32[768,2]{0,1:T(2,128)}, f32[768,2]{0,1:T(2,128)S(1)}, u32[]{:S(2)}) copy-start(f32[768,2]{0,1:T(2,128)S(1)} %copy.104) | copy-start | bytes 18436
  103.4 3.0 copy-start.15
  107.2 1.6 copy-start.16
  108.8 5.9 %copy-start.10 = (s32[2048,1]{1,0:T(8,128)S(1)}, s32[2048,1]{1,0:T(8,128)}, u32[]{:S(2)}) copy-start(s32[2048,1]{1,0:T(8,128)} %copy.90.start_ref) | copy-start | bytes 24580
  146.5 1.1 copy-start.3
  147.6 1.0 copy-start.13
  259.7 37.4 %all-to-all-start.1 = ((bf16[8,176,768]{2,1,0:T(8,128)(2,1)}), bf16[8,176,768]{2,1,0:T(8,128)(2,1)S(1)}, u32[]{:S(2)}, u32[]{:S(2)}) async-start(bf16[8,176,768]{2,1,0:T(8,128)(2,1)} %get-tuple-element.61), calls=%async_computation.1 | async-start | bytes 4325376 | tf_op jit(solution)/shard_map/all_to_all | solution.py:1547
  297.1 1.3 copy-start.17
  298.5 10.6 %copy-start.7 = (bf16[16,48,1664]{2,1,0:T(8,128)(2,1)S(1)}, bf16[16,48,1664]{2,1,0:T(8,128)(2,1)}, u32[]{:S(2)}) copy-start(bf16[16,48,1664]{2,1,0:T(8,128)(2,1)} %copy-done.5) | copy-start | bytes 7667716
  298.5 114.5 %all-to-all-start.2 = ((bf16[16,3,48,1024]{3,2,1,0:T(8,128)(2,1)}), bf16[16,3,48,1024]{3,2,1,0:T(8,128)(2,1)}, u32[]{:S(2)}, u32[]{:S(2)}) async-start(bf16[16,3,48,1024]{3,2,1,0:T(8,128)(2,1)} %weight_step.1), calls=%async_computation.2 | async-start | bytes 9437184 | tf_op jit(solution)/shard_map/all_to_all | solution.py:1641
  312.0 40.7 %copy-start.4 = (bf16[2048,384]{1,0:T(8,128)(2,1)S(1)}, bf16[2048,384]{1,0:T(8,128)(2,1)}, u32[]{:S(2)}) copy-start(bf16[2048,384]{1,0:T(8,128)(2,1)} %copy-done.3) | copy-start | bytes 4718596
  352.7 4.7 copy-start.11
  352.7 4.7 copy-start.12
  357.4 1.2 copy-start.14
  478.1 8.7 %copy-start.19 = (f32[1024,768]{1,0:T(8,128)S(1)}, f32[1024,768]{1,0:T(8,128)}, u32[]{:S(2)}) copy-start(f32[1024,768]{1,0:T(8,128)} %get-tuple-element.77) | copy-start | bytes 9437188

commit v5 on v4

--- a/solution.py
+++ b/solution.py
@@ -280,6 +280,19 @@
     )(seg_bounds, qkv, qkv, qkv, do, heads_out, lse, starts[None, :])
 
 
+def flip(number, k):
+    out = 0
+    for bit in (1, 2, 4):
+        digit = lax.rem(number // bit, 2)
+        out = out + bit * ((1 - digit) if k & bit else digit)
+    return out
+
+
+BESIDE = (3, 1, 2)
+NEAR = (3, 4, 5, 2, 6, 1, 7)
+PAIRS = ((0, 3), (4, 5), (2, 6), (1, 7))
+
+
 def start_kernel(
     members,
     low,
@@ -292,21 +305,18 @@
     w_ref,
     full_ref,
     all_ref,
-    got_ref,
+    rows_ref,
     hot_ref,
     info_ref,
     down_ref,
     ids_all_ref,
     dy_all_ref,
-    stage_ref,
     place_ref,
     send_sem,
     recv_sem,
     own_sem,
     swap_send,
     swap_recv,
-    dy_send,
-    dy_recv,
     down_send,
     down_recv,
 ):
@@ -322,19 +332,18 @@
     partner = {"tensor": 1 - core}
 
     def beside(k):
-        return row * low + lax.rem(inside + k, low)
+        return row * low + flip(inside, k)
 
     def across(k):
         return lax.rem(row + k, high) * low + inside
 
-    peers = [beside(k) for k in range(1, low)] + [across(k) for k in range(1, high)]
-    peers += [base + lax.rem(mine + k, size) for k in range(1, size)]
+    peers = [beside(k) for k in BESIDE] + [across(k) for k in range(1, high)]
     groups = members // size
 
     def device_at(g, k):
         return lax.rem(base + g * size, members) + lax.rem(mine + k, size)
 
-    distant = [(g, k) for g in range(1, groups) for k in range(size)]
+    distant = [(g, k) for k in range(size) for g in range(groups) if g or k]
     peers += [device_at(g, k) for g, k in distant]
     barrier = pltpu.get_barrier_semaphore()
     for peer in peers:
@@ -365,7 +374,7 @@
         ).wait_recv()
 
     sent = [push(pack_ref, me, across(k), k) for k in range(1, high)]
-    sent += [push(pack_ref, me, beside(k), high + k) for k in range(1, low)]
+    sent += [push(pack_ref, me, beside(k), high + k) for k in BESIDE]
     own_rows = pl.ds(pl.multiple_of(core * local, local), local)
     swaps = [
         remote(ids_ref, ids_all_ref.at[core], swap_send.at[0], swap_recv.at[0], partner),
@@ -377,6 +386,7 @@
         pltpu.make_async_copy(dy_ref, dy_all_ref.at[own_rows], own_sem.at[1]),
         pltpu.make_async_copy(tok_ref, all_ref.at[own_rows], own_sem.at[2]),
         pltpu.make_async_copy(pack_ref, full_ref.at[me], own_sem.at[3]),
+        pltpu.make_async_copy(w_ref.at[mine, 2], down_ref.at[me], own_sem.at[4]),
     ]
     for copy in swaps + owns:
         copy.start()
@@ -428,14 +438,14 @@
     for k in range(1, high):
         block = across(high - k)
         arrived(block)
-        for step in range(1, low):
+        for step in BESIDE:
             sent.append(push(full_ref.at[block], block, beside(step), high + k * low + step))
 
     for g, k in distant:
         copy = remote(
             w_ref.at[lax.rem(mine + k, size), 2],
             down_ref.at[me],
-            down_send.at[(g - 1) * size + k],
+            down_send.at[g * size + k],
             down_recv.at[me],
             {"dp": device_at(g, k)},
         )
@@ -444,29 +454,17 @@
 
     swaps[1].wait()
     owns[1].wait()
-    for pair in [(1, 2), (3, 4), (5, 6), (7, 0)]:
-        slots = [
-            pl.ds(pl.multiple_of(lax.rem(mine + k, size) * padded, 16), padded) for k in pair
-        ]
-        rows = mm(jnp.concatenate([hot_ref[s, :] for s in slots], 0), dy_all_ref[...])
-        for place, k in enumerate(pair):
-            to = lax.rem(mine + k, size)
-            stage_ref[to] = rows[place * padded : (place + 1) * padded].astype(half)
-            if k:
-                copy = remote(
-                    stage_ref.at[to], got_ref.at[mine], dy_send.at[k], dy_recv.at[k], {"dp": base + to}
-                )
-            else:
-                copy = pltpu.make_async_copy(stage_ref.at[to], got_ref.at[mine], own_sem.at[4])
-            copy.start()
-            owns.append(copy)
-    for k in range(1, low):
-        block = beside(low - k)
+    for e in range(0, size, 2):
+        slots = slice(e * padded, (e + 2) * padded)
+        rows = mm(hot_ref[slots, :], dy_all_ref[...])
+        rows_ref[e : e + 2] = rows.astype(half).reshape(2, padded, rows.shape[1])
+    for k in BESIDE:
+        block = beside(k)
         arrived(block)
         for step in range(1, high):
             arrived(lax.rem(block + step * low, members))
     for g, k in distant:
-        block = device_at(groups - g, size - k)
+        block = device_at((groups - g) % groups, (size - k) % size)
         remote(
             w_ref.at[0, 2], down_ref.at[block], down_send.at[0], down_recv.at[block], partner
         ).wait_recv()
@@ -478,7 +476,7 @@
 
 
 def start(pack, tokens, dy, ids, w, members, per_core, padded):
-    low = 4 if members % 4 == 0 else 1
+    low = 4
     high = members // low
     local, width = tokens.shape
     count = EXPERTS_FF * padded
@@ -495,20 +493,17 @@
             jax.ShapeDtypeStruct((8, 2 * local), jnp.int32),
             jax.ShapeDtypeStruct((members,) + w.shape[2:], half),
         ],
-        in_specs=[any_spec] * 5,
-        out_specs=[any_spec] * 3 + [vmem] * 2 + [any_spec],
+        in_specs=[pl.BlockSpec(memory_space=pltpu.HBM)] * 5,
+        out_specs=[any_spec] * 2 + [vmem] * 3 + [any_spec],
         scratch_shapes=[
             pltpu.VMEM((2, 8, local), jnp.int32),
             pltpu.VMEM((2 * local, width), half),
-            pltpu.VMEM((EXPERTS_FF, padded, width), half),
             pltpu.VMEM((16, 2 * local), jnp.int32),
             dma((high * (low + 1),)),
             dma((members,)),
             dma((5,)),
             dma((3,)),
             dma((3,)),
-            dma((EXPERTS_FF,)),
-            dma((EXPERTS_FF,)),
             dma((members,)),
             dma((members,)),
         ],
@@ -522,8 +517,7 @@
 def experts_kernel(
     members,
     padded,
-    w_ref,
-    far_ref,
+    down_hbm_ref,
     in_ref,
     dy_hbm_ref,
     ho_ref,
@@ -559,12 +553,9 @@
     dot_ref,
     x_send,
     x_recv,
-    w_send,
-    w_recv,
-    pass_send,
-    pass_recv,
+    dy_send,
+    dy_recv,
     own_sem,
-    far_sem,
     swap_send,
     swap_recv,
     ig_send,
@@ -601,27 +592,24 @@
     heads = remote(ho_ref.at[other_rows], ho_in_ref, swap_send.at[0], swap_recv.at[0], partner)
     heads.start()
     waits = []
-    for k in range(1, size):
-        to = lax.rem(mine + k, size)
+    for k in NEAR:
+        to = flip(mine, k)
         copy = remote(
-            w_ref.at[to, 2], down_ref.at[0, me], w_send.at[k], w_recv.at[k], {"dp": base + to}
+            dy_hbm_ref.at[to], dy_ref.at[mine], dy_send.at[k], dy_recv.at[k], {"dp": base + to}
         )
         copy.start()
         waits.append(copy)
     pair_in = remote(in_ref, win_ref.at[1], swap_send.at[2], swap_recv.at[2], partner)
     pair_in.start()
-    local_in = pltpu.make_async_copy(in_ref, win_ref.at[0], own_sem.at[1])
-    local_in.start()
-    local_dy = pltpu.make_async_copy(dy_hbm_ref, dy_ref, own_sem.at[2])
-    local_dy.start()
-    own_w = pltpu.make_async_copy(w_ref.at[mine, 2], down_ref.at[0, me], own_sem.at[3])
-    own_w.start()
-    far = []
-    for g in range(1, groups):
-        blocks = pl.ds(lax.rem(base + g * size, members), size)
-        copy = pltpu.make_async_copy(far_ref.at[blocks], down_ref.at[0, blocks], far_sem.at[g])
+    pair_down = remote(down_hbm_ref, down_ref.at[1], swap_send.at[3], swap_recv.at[3], partner)
+    pair_down.start()
+    owns = [
+        pltpu.make_async_copy(in_ref, win_ref.at[0], own_sem.at[1]),
+        pltpu.make_async_copy(dy_hbm_ref.at[mine], dy_ref.at[mine], own_sem.at[2]),
+        pltpu.make_async_copy(down_hbm_ref, down_ref.at[0], own_sem.at[3]),
+    ]
+    for copy in owns:
         copy.start()
-        far.append(copy)
 
     step = fit(local, 256)
     heads.wait()
@@ -658,24 +646,22 @@
     )
     swap_rows.start()
 
-    pairs = [(1, 0), (2, 3), (4, 5), (6, 7)]
-    for number, pair in enumerate(pairs):
+    for number, pair in enumerate(PAIRS):
         slots = [
-            pl.ds(pl.multiple_of(lax.rem(mine + k, size) * padded, 16), padded) for k in pair
+            pl.ds(pl.multiple_of(flip(mine, k) * padded, 16), padded) for k in pair
         ]
         hot = jnp.concatenate([hot_ref[s, own_rows] for s in slots], 0)
         acc_ref[number] = mm(hot, both_ref[own_rows, :])
     swap_rows.wait_recv()
     row_ref[...] = jnp.zeros(row_ref.shape, single)
-    own_x = None
-    for number, pair in enumerate(pairs):
+    for number, pair in enumerate(PAIRS):
         slots = [
-            pl.ds(pl.multiple_of(lax.rem(mine + k, size) * padded, 16), padded) for k in pair
+            pl.ds(pl.multiple_of(flip(mine, k) * padded, 16), padded) for k in pair
         ]
         hot = jnp.concatenate([hot_ref[s, other_rows] for s in slots], 0)
         acc_ref[number] += mm(hot, both_ref[other_rows, :])
         for place, k in enumerate(pair):
-            to = lax.rem(mine + k, size)
+            to = flip(mine, k)
             first = place * padded
             tail = acc_ref[number, first : first + padded, width:].astype(half)
             lane = lax.broadcasted_iota(jnp.int32, (16, LANES), 1)
@@ -692,44 +678,12 @@
                 waits.append(copy)
             else:
                 copy = pltpu.make_async_copy(stage_ref.at[to], x_ref.at[mine], own_sem.at[0])
-                own_x = copy
             copy.start()
 
-    own_w.wait()
-    for copy in far:
+    for copy in owns:
         copy.wait()
-    passed = []
-    for g in range(1, groups):
-        blocks = pl.ds(lax.rem(base + g * size, members), size)
-        passed.append(
-            remote(
-                down_ref.at[0, blocks],
-                down_ref.at[1, blocks],
-                pass_send.at[size + g],
-                pass_recv.at[size + g],
-                partner,
-            )
-        )
-        passed[-1].start()
-    for k in range(size):
-        block = base + lax.rem(mine + size - k, size)
-        if k:
-            waits[k - 1].wait_recv()
-        passed.append(
-            remote(
-                down_ref.at[0, block],
-                down_ref.at[1, block],
-                pass_send.at[k],
-                pass_recv.at[k],
-                partner,
-            )
-        )
-        passed[-1].start()
-    local_in.wait()
-    local_dy.wait()
     pair_in.wait_recv()
-    for copy in passed:
-        copy.wait_recv()
+    pair_down.wait_recv()
 
     ff = in_ref.shape[3]
     block = fit(ff, 256)
@@ -746,6 +700,10 @@
             spill_sem.at[slot, array, place],
         )
 
+    def arrived(k):
+        remote(dy_hbm_ref.at[0], dy_ref.at[0], dy_send.at[0], dy_recv.at[k], partner).wait_recv()
+        remote(stage_ref.at[0], x_ref.at[0], x_send.at[0], x_recv.at[k], partner).wait_recv()
+
     def give_back(k, source):
         return remote(
             ig_ref.at[source], back_ref.at[mine], ig_send.at[k], ig_recv.at[k], {"dp": base + source}
@@ -753,8 +711,14 @@
 
     @pl.loop(0, size // 2)
     def _(q):
-        ks = [2 * q, 2 * q + 1]
-        sources = [lax.rem(mine + size - k, size) for k in ks]
+        ks, sources = [], []
+        for place in range(2):
+            k, source = PAIRS[0][place], flip(mine, PAIRS[0][place])
+            for number in range(1, size // 2):
+                k = jnp.where(q == number, PAIRS[number][place], k)
+                source = jnp.where(q == number, flip(mine, PAIRS[number][place]), source)
+            ks.append(k)
+            sources.append(source)
 
         @pl.when(q == 0)
         def _():
@@ -762,13 +726,9 @@
 
         @pl.when(q > 0)
         def _():
-            remote(
-                stage_ref.at[0], x_ref.at[0], x_send.at[0], x_recv.at[2 * q], partner
-            ).wait_recv()
-
-        remote(
-            stage_ref.at[0], x_ref.at[0], x_send.at[0], x_recv.at[2 * q + 1], partner
-        ).wait_recv()
+            arrived(ks[0])
+
+        arrived(ks[1])
         for place, source in enumerate(sources):
             rows = pl.ds(place * padded, padded)
             gates = x_ref[source, padded - 16 :, : 2 * LANES].astype(single).T
@@ -836,20 +796,19 @@
 
         @pl.when(q > 0)
         def _():
-            give_back(2 * q, sources[0]).start()
-
-        give_back(2 * q + 1, sources[1]).start()
+            give_back(ks[0], sources[0]).start()
+
+        give_back(ks[1], sources[1]).start()
 
     pltpu.make_async_copy(ig_ref.at[mine], back_ref.at[mine], own_sem.at[0]).wait()
     for k in range(1, size):
-        give_back(k, lax.rem(mine + size - k, size)).wait()
-    heads_done = [swap_rows, pair_in]
-    for copy in waits + passed + heads_done:
+        give_back(k, flip(mine, k)).wait()
+    for copy in waits + [swap_rows, pair_in, pair_down]:
         copy.wait_send()
 
 
 def experts(
-    w, far, inward, dy, heads, tokens, own_w, other_w, gains, router, prev, routes, hot, padded
+    down, inward, dy, heads, tokens, own_w, other_w, gains, router, prev, routes, hot, padded
 ):
     members, _, d_rows, ff = inward.shape
     local, width = tokens.shape
@@ -875,7 +834,7 @@
             jax.ShapeDtypeStruct((local, width), half),
             jax.ShapeDtypeStruct((local, LANES), single),
         ],
-        in_specs=[any_spec] * 4 + [vmem] * 9,
+        in_specs=[any_spec] * 3 + [vmem] * 9,
         out_specs=[any_spec] + [vmem] * 3 + [any_spec] * 3 + [vmem] * 3,
         scratch_shapes=[
             pltpu.VMEM((local, heads.shape[1]), half),
@@ -894,12 +853,9 @@
             dma((size,)),
             dma((size,)),
             dma((size,)),
-            dma((size + members // size,)),
-            dma((size + members // size,)),
             dma((4,)),
-            dma((members // size,)),
-            dma((3,)),
-            dma((3,)),
+            dma((4,)),
+            dma((4,)),
             dma((size,)),
             dma((size,)),
             dma((2, 3, 2)),
@@ -908,7 +864,7 @@
             collective_id=1, has_side_effects=True, vmem_limit_bytes=62 << 20
         ),
         name="experts",
-    )(w, far, inward, dy, heads, tokens, own_w, other_w, gains, router, prev, routes, hot)
+    )(down, inward, dy, heads, tokens, own_w, other_w, gains, router, prev, routes, hot)
 
 
 def split(x):
@@ -1249,10 +1205,13 @@
     info_ref,
     gain_ref,
     small_ref,
-    dense_out_ref,
+    grads_ref,
+    proj_out_ref,
+    outw_ref,
     tokens_ref,
     mixed_ref,
     small_out_ref,
+    expert_ref,
     dense_ref,
     first_ref,
     stage_ref,
@@ -1266,6 +1225,7 @@
     pair_ref,
     near_ref,
     far_ref,
+    dense_out_ref,
     send1,
     recv1,
     send2,
@@ -1276,6 +1236,10 @@
     near_recv,
     far_send,
     far_recv,
+    part_ref,
+    sum_ref,
+    part_sem,
+    sum_sem,
 ):
     size = EXPERTS_FF
     me = lax.axis_index("dp")
@@ -1284,13 +1248,13 @@
     inside, row = lax.rem(me, low), me // low
     local, width = base_ref.shape
     count = size * padded
-    d_rows = dense_out_ref.shape[0]
+    d_rows = outw_ref.shape[0]
     hh3 = qkv_ref.shape[1]
     step = fit(local, 256)
     partner = {"tensor": 1 - core}
 
     def beside(k):
-        return row * low + lax.rem(inside + k, low)
+        return row * low + flip(inside, k)
 
     def across(k):
         return lax.rem(row + k, high) * low + inside
@@ -1323,9 +1287,9 @@
             dense_ref[owner, :, :hh3] = grad[j * d_rows : (j + 1) * d_rows].astype(half)
             dense_ref[owner, :, hh3:] = outg_ref[owner * d_rows : (owner + 1) * d_rows, :]
         for h in range(c * high // chunks, (c + 1) * high // chunks):
-            for k in range(1, low):
+            for k in BESIDE:
                 copy = remote(
-                    dense_ref.at[h * low + lax.rem(inside + k, low)],
+                    dense_ref.at[h * low + flip(inside, k)],
                     first_ref.at[k - 1, h],
                     send1.at[k - 1, h],
                     recv1.at[k - 1, h],
@@ -1373,6 +1337,15 @@
         rows = pl.ds(pl.multiple_of(r * step, step), step)
         here = pl.ds(pl.multiple_of(core * local + r * step, step), step)
         ffn_ref[rows, :] = mm(slot_rows(info_ref[here, :], count), eo_all[...])
+
+    def second(h):
+        return remote(
+            stage_ref.at[h],
+            second_ref.at[row],
+            send2.at[h],
+            recv2.at[row],
+            {"dp": h * low + inside},
+        )
 
     pair = remote(mine_ref, pair_ref, pair_send.at[1], pair_recv.at[1], partner)
     pair.start()
@@ -1391,8 +1364,38 @@
         )
         near[-1].start()
 
-    for j in range(1, high + 1):
-        h = lax.rem(row + j, high)
+    groups = members // size
+
+    def load(e):
+        return [
+            pltpu.make_async_copy(
+                grads_ref.at[g * size + e], part_ref.at[e % 2, g], part_sem.at[e % 2, g]
+            )
+            for g in range(groups)
+        ]
+
+    def store(e):
+        return pltpu.make_async_copy(sum_ref.at[e % 2], expert_ref.at[e], sum_sem.at[e % 2])
+
+    for copy in load(0):
+        copy.start()
+    for e in range(size):
+        if e + 1 < size:
+            for copy in load(e + 1):
+                copy.start()
+        for copy in load(e):
+            copy.wait()
+        if e >= 2:
+            store(e - 2).wait()
+        total = part_ref[e % 2, 0].astype(single)
+        for g in range(1, groups):
+            total += part_ref[e % 2, g].astype(single)
+        sum_ref[e % 2] = total
+        store(e).start()
+    for e in range(size - 2, size):
+        store(e).wait()
+
+    for h in range(high):
         for k in range(low - 1):
             remote(
                 dense_ref.at[0], first_ref.at[k, h], send1.at[k, h], recv1.at[k, h], partner
@@ -1400,19 +1403,16 @@
         total = dense_ref[h * low + inside].astype(single)
         for k in range(low - 1):
             total += first_ref[k, h].astype(single)
-        if j < high:
-            stage_ref[j - 1] = total.astype(half)
-            copy = remote(
-                stage_ref.at[j - 1],
-                second_ref.at[j - 1],
-                send2.at[j - 1],
-                recv2.at[j - 1],
-                {"dp": across(j)},
-            )
-            copy.start()
-            sent.append(copy)
-        else:
+
+        @pl.when(h == row)
+        def _():
             dense_out_ref[...] = total
+
+        @pl.when(h != row)
+        def _():
+            stage_ref[h] = total.astype(half)
+            second(h).start()
+
     for k in range(1, low):
         block = lax.rem(inside + k, low)
         remote(
@@ -1451,11 +1451,20 @@
         total = base_ref[rows, :] + ffn_ref[rows, :] + ffn_in_ref[rows, :].astype(single)
         mixed_ref[rows, :] = total.astype(half)
 
-    for j in range(1, high):
-        remote(
-            stage_ref.at[0], second_ref.at[j - 1], send2.at[j - 1], recv2.at[j - 1], partner
-        ).wait_recv()
-        dense_out_ref[...] += second_ref[j - 1].astype(single)
+    for h in range(high):
+
+        @pl.when(h != row)
+        def _():
+            remote(
+                stage_ref.at[0], second_ref.at[h], send2.at[0], recv2.at[h], partner
+            ).wait_recv()
+            dense_out_ref[...] += second_ref[h].astype(single)
+            second(h).wait_send()
+
+    hh = outw_ref.shape[1]
+    for c in range(3):
+        proj_out_ref[c] = dense_out_ref[:, c * hh : (c + 1) * hh]
+    outw_ref[...] = dense_out_ref[:, 3 * hh :]
     for k in range(1, high):
         block = lax.rem(row + k, high)
         remote(
@@ -1469,31 +1478,36 @@
         copy.wait_send()
 
 
-def tail(members, eo, qkv, one, proj, outg, x, base, resid, info, gains, small, padded):
+def tail(members, eo, qkv, one, proj, outg, x, base, resid, info, gains, small, grads, padded):
     low = 4
     high = members // low
     local, width = base.shape
     d_rows = width // members
-    wide = qkv.shape[1] + outg.shape[1]
+    hh = outg.shape[1]
+    wide = qkv.shape[1] + hh
+    groups = members // EXPERTS_FF
     vmem = pl.BlockSpec(memory_space=pltpu.VMEM)
+    hbm = pl.BlockSpec(memory_space=pltpu.HBM)
     dma = pltpu.SemaphoreType.DMA
     rows_half = pltpu.VMEM((local, width), half)
     small_one = pltpu.VMEM(small.shape, single)
     return pl.pallas_call(
         functools.partial(tail_kernel, members, low, padded),
         out_shape=[
-            jax.ShapeDtypeStruct((d_rows, wide), single),
+            jax.ShapeDtypeStruct((3, d_rows, hh), single),
+            jax.ShapeDtypeStruct((d_rows, hh), single),
             jax.ShapeDtypeStruct((local, width), single),
             jax.ShapeDtypeStruct((local, width), half),
             jax.ShapeDtypeStruct(small.shape, single),
+            jax.ShapeDtypeStruct((EXPERTS_FF,) + grads.shape[1:], single),
         ],
-        in_specs=[vmem] * 11,
-        out_specs=[vmem] * 4,
+        in_specs=[vmem] * 11 + [hbm],
+        out_specs=[vmem] * 5 + [hbm],
         scratch_shapes=[
             pltpu.VMEM((members, d_rows, wide), half),
             pltpu.VMEM((low - 1, high, d_rows, wide), half),
-            pltpu.VMEM((high - 1, d_rows, wide), half),
-            pltpu.VMEM((high - 1, d_rows, wide), half),
+            pltpu.VMEM((high, d_rows, wide), half),
+            pltpu.VMEM((high, d_rows, wide), half),
             rows_half,
             rows_half,
             rows_half,
@@ -1503,22 +1517,27 @@
             small_one,
             pltpu.VMEM((low,) + small.shape, single),
             pltpu.VMEM((high,) + small.shape, single),
+            pltpu.VMEM((d_rows, wide), single),
             dma((low - 1, high)),
             dma((low - 1, high)),
-            dma((high - 1,)),
-            dma((high - 1,)),
+            dma((high,)),
+            dma((high,)),
             dma((3,)),
             dma((3,)),
             dma((low,)),
             dma((low,)),
             dma((high,)),
             dma((high,)),
+            pltpu.VMEM((2, groups) + grads.shape[1:], half),
+            pltpu.VMEM((2,) + grads.shape[1:], single),
+            dma((2, groups)),
+            dma((2,)),
         ],
         compiler_params=pltpu.CompilerParams(
             collective_id=4, has_side_effects=True, vmem_limit_bytes=60 << 20
         ),
         name="tail",
-    )(eo, qkv, one, proj, outg, x, base, resid, info, gains, small)
+    )(eo, qkv, one, proj, outg, x, base, resid, info, gains, small, grads)
 
 
 def per_device(
@@ -1546,7 +1565,7 @@
     def in_group(blocks):
         return lax.all_to_all(blocks, "dp", 0, 0, axis_index_groups=cubes, tiled=True)
 
-    def plain_tail(eo, qkv, one, proj, outg, x, base, resid, gains, small):
+    def plain_tail(eo, qkv, one, proj, outg, x, base, resid, gains, small, grads):
         ffn = pair_sum(mm_tn(onehot, eo.reshape(-1, width)))
         part = mm_nt(qkv, proj)
         scale = rms_scale(x)
@@ -1558,7 +1577,15 @@
         dense = jnp.concatenate([mm_tn(one, qkv).astype(half), outg], 1)
         dense = lax.all_to_all(dense.reshape(members, d_rows, -1), "dp", 0, 0, tiled=True)
         dense = jnp.sum(dense.astype(single), axis=0)
-        return dense, tokens_grad, (base + ffn).astype(half), lax.psum(small, ("dp", "tensor"))
+        grads = grads.reshape((groups, EXPERTS_FF) + grads.shape[1:]).astype(single)
+        return (
+            dense[:, : 3 * hh].reshape(d_rows, 3, hh).transpose(1, 0, 2),
+            dense[:, 3 * hh :],
+            tokens_grad,
+            (base + ffn).astype(half),
+            lax.psum(small, ("dp", "tensor")),
+            jnp.sum(grads, axis=0),
+        )
 
     pack = jnp.concatenate(
         [
@@ -1574,7 +1601,7 @@
     pack = jnp.pad(pack, ((0, 0), (0, -columns % LANES)))
     ids = jnp.concatenate([segment_ids, routes[0].T], 0)
     ids = jnp.pad(ids, ((0, 5), (0, 0)))
-    full_pack, tokens_all, got_dy, onehot, info, far_down = start(
+    full_pack, tokens_all, dy_rows, onehot, info, my_down = start(
         pack, tokens[0], cotangent[0], ids, expert_weight, members, per_core, padded
     )
     full_pack, expert_weight = lax.optimization_barrier((full_pack, expert_weight))
@@ -1610,10 +1637,9 @@
     mixed_prev = jnp.pad(mixed_prev, ((0, 0), (0, LANES - EXPERTS)))
     router_wide = jnp.pad(router_full, ((0, 0), (0, LANES - router_full.shape[1])))
     back_grad, gated_out, got_rows, out_grad, hidden, pg, pu, resid, normed_two, misc = experts(
-        expert_weight,
-        far_down,
+        my_down,
         my_in,
-        got_dy,
+        dy_rows,
         heads_out,
         tokens[0],
         outw_own,
@@ -1665,7 +1691,7 @@
     out_w_grad = out_w_grad.astype(half)
     if d_rows % 16 or members != 16:
         outs = plain_tail(
-            back_out, qkv_grad, full_one, proj_full, out_w_grad, x_all, base, resid_grad, gains, small
+            back_out, qkv_grad, full_one, proj_full, out_w_grad, x_all, base, resid_grad, gains, small, grads_got
         )
     else:
         outs = tail(
@@ -1681,14 +1707,10 @@
             columns,
             gains,
             small,
+            grads_got,
             padded,
         )
-    dense, tokens_grad, mixed, small = outs
-    expert_shard = jnp.sum(
-        grads_got.reshape((groups, EXPERTS_FF) + grads_got.shape[1:]).astype(single), axis=0
-    )
-    proj_shard = dense[:, : 3 * hh].reshape(d_rows, 3, hh).transpose(1, 0, 2)
-    outw_shard = dense[:, 3 * hh :]
+    proj_shard, outw_shard, tokens_grad, mixed, small, expert_shard = outs
     mixing_total = small[20:22].reshape(EXPERTS, LANES)[:, :EXPERTS]
     features = lax.dynamic_slice_in_dim(small, lax.axis_index("dp") * d_rows, d_rows, 1)
     return (

time: 499 us -> 478 us (0.958)
  starting transfers between devices: 30.8 us -> 21.6 us
  other arithmetic: 10.8 us -> 4.55 us
  Pallas kernels: 368 us -> 362 us
    pallas_call x1, Pallas kernels: 71.9 us -> 55.4 us  [start(): pl.pallas_call(functools.partial(start_kernel, members, low, per_core, pa...]
    pallas_call x1, Pallas kernels: 93.3 us -> 101 us  [experts(): pl.pallas_call(functools.partial(experts_kernel, members, padded), out_sh...]
    reduce_sum x1 -> x0, other arithmetic: 6.25 us -> none  [per_device(): jnp.sum(grads_got.reshape((groups, EXPERTS_FF) + grads_got.shape[1:]).ast...]
    unnamed x56 -> x64, local copies, waits for them, and re-layouts: 23.1 us -> 25.4 us
  transfers between devices with their start and end apart: 4 -> 4, of which waited for: 2 -> 2; matrix products, arithmetic and copies ran while one was open for 6% -> 6% of each run, Pallas kernels for 30% -> 31%
where the time goes in v5:
time: 478 us; the launch traced here: 470 us
  Pallas kernels  362 us (76%)
  local copies, waits for them, and re-layouts  46 us (10%)
  waiting for transfers between devices  22.3 us (5%)
  starting transfers between devices  21.6 us (5%)
  matrix products  11.8 us (2%)
    pallas_call x1, Pallas kernels, experts(): pl.pallas_call(functools.partial(experts_kernel, members, padded), out_sh...  101 us
    pallas_call x1, Pallas kernels, tail(): pl.pallas_call(functools.partial(tail_kernel, members, low, padded), out_...  59.3 us
    pallas_call x1, Pallas kernels, start(): pl.pallas_call(functools.partial(start_kernel, members, low, per_core, pa...  55.4 us
    pallas_call x1, Pallas kernels, attention_backward(): pl.pallas_call(functools.partial(bwd_kernel, heads), grid_spec=pltpu.Pref...  48.1 us
    pallas_call x1, Pallas kernels, backward_middle(): pl.pallas_call(functools.partial(back_kernel, padded), out_shape=[jax.Sha...  38.7 us
    pallas_call x1, Pallas kernels, attention_forward(): pl.pallas_call(functools.partial(fwd_kernel, heads), grid_spec=pltpu.Pref...  31.8 us
    pallas_call x1, Pallas kernels, weight_step(): pl.pallas_call(weight_kernel, grid=(steps,), in_specs=[whole, whole, wide...  28.2 us
    unnamed x64, local copies, waits for them, and re-layouts  25.4 us
  transfers between devices with their start and end apart: 4, of which 2 were waited for; matrix products, arithmetic and copies ran while one was open for 6% of the time, Pallas kernels for 31%

profile of v5, /device:TPU:12, one launch (start us, length us, event | category | flops | bytes accessed | tf_op | source)
XLA Modules:
  0.0 469.9 jit_solution(5805719677764117058)
XLA Ops:
  0.7 0.9 copy.78
  1.5 0.8 copy.80
  2.3 0.8 copy.79
  3.1 0.9 copy.99
  4.0 0.9 copy.81
  4.9 0.2 copy.82
  5.1 0.9 concatenate.6
  6.0 0.7 pad_add_fusion
  6.7 1.7 copy-done
  8.4 1.4 copy-done.2
  9.8 55.4 %start.1 = (bf16[16,48,1664]{2,1,0:T(8,128)(2,1)S(1)}, bf16[2048,768]{1,0:T(8,128)(2,1)}, bf16[8,176,768]{2,1,0:T(8,128)(2,1)S(1)}, bf16[1408,2048]{1,0:T(8,128)...) custom-call(bf16[48,1664]{1,0:T(8,128)(2,1)S(1)} %pad.23.pack_ref, bf16[1024,768]{1,0:T(8,128)(2,1)S(1)} %bitcast.69, ...), custom_call_target="tpu_custom_call" | custom-call | tf_op jit(solution)/shard_map/start/pallas_call | solution.py:486
  65.2 2.5 broadcast_in_dim.8
  67.7 0.6 copy-done.8
  68.3 0.5 copy-done.9
  68.8 9.5 %all-to-all-start = ((bf16[16,2,48,1024]{3,2,1,0:T(8,128)(2,1)}), bf16[16,2,48,1024]{3,2,1,0:T(8,128)(2,1)}, u32[]{:S(2)}, u32[]{:S(2)}) async-start(bf16[16,2,48,1024]{3,2,1,0:T(8,128)(2,1)} %bitcast.75), calls=%async_computation | async-start | bytes 6291456 | tf_op jit(solution)/shard_map/all_to_all | solution.py:1620
  78.3 0.9 slice.87.own_w_ref
  79.3 0.1 copy.94
  79.4 0.1 copy.95
  79.6 0.1 copy.96
  79.7 0.1 slice_convert_fusion
  79.8 0.1 copy.100
  79.9 1.4 copy.87.start_ref
  81.3 0.2 convert_reduce_fusion
  81.6 2.7 fusion
  84.3 0.8 fusion.2.one_ref
  85.1 1.6 copy-done.16
  86.8 5.8 %convolution_convert_fusion.q_ref.k_ref.v_ref = bf16[2048,1152]{1,0:T(8,128)(2,1)} fusion(bf16[2048,768]{1,0:T(8,128)(2,1)S(1)} %fusion.2.one_ref, bf16[768,1664]{1,0:T(8,128)(2,1)S(1)} %bitcast.72), kind=kOutput, calls=%fused_computation.2 | convolution fusion | flops 3626237952 | bytes 9633792 | tf_op jit(solution)/shard_map/dot_general | solution.py:38
  92.6 31.8 %shard_map.195 = (f32[2048,384]{1,0:T(8,128)}, bf16[2048,384]{1,0:T(8,128)(2,1)S(1)}, f32[2048,128]{1,0:T(8,128)S(1)}) custom-call(s32[4,8]{1,0:T(4,128)S(1)} %pad_add_fusion.1.bounds, bf16[2048,1152]{1,0:T(8,128)(2,1)} %convolution_convert_fusion.q_ref.k_ref.v_ref, bf16[2048,1152]{1,0:T(8,128)(2,1)} %convolution_convert_fusion.q_ref.k_ref.v_ref, ...), custom_call_target="tpu_custom_call" | custom-call | flops 12884901888 | bytes 12582912 | tf_op jit(solution)/shard_map/pallas_call | solution.py:153
  124.5 1.1 copy-done.3
  125.6 1.0 copy-done.13
  126.6 0.8 slice.88
  127.4 1.0 copy.88
  128.4 1.7 pad.25.router_ref
  130.0 1.3 fusion.4
  131.3 0.8 pad.26.prev_ref
  132.1 15.9 %all-to-all-done.in_ref = bf16[16,2,48,1024]{3,2,1,0:T(8,128)(2,1)} async-done(((bf16[16,2,48,1024]{3,2,1,0:T(8,128)(2,1)}), bf16[16,2,48,1024]{3,2,1,0:T(8,128)(2,1)}, u32[]{:S(2)}, u32[]{:S(2)}) %all-to-all-start) | async-done | bytes 3145760 | tf_op jit(solution)/shard_map/all_to_all | solution.py:1620
  148.1 100.7 %experts.1 = (bf16[8,176,768]{2,1,0:T(8,128)(2,1)}, bf16[8,176,768]{2,1,0:T(8,128)(2,1)}, bf16[8,176,768]{2,1,0:T(8,128)(2,1)}, bf16[8,176,768]{2,1,0:T(8,128)(2...) custom-call(bf16[16,48,1024]{2,1,0:T(8,128)(2,1)} %copy-done.9, ...), custom_call_target="tpu_custom_call" | custom-call | tf_op jit(solution)/shard_map/experts/pallas_call | solution.py:823
  248.8 5.6 %all-to-all-start.1 = ((bf16[8,176,768]{2,1,0:T(8,128)(2,1)}), bf16[8,176,768]{2,1,0:T(8,128)(2,1)S(1)}, u32[]{:S(2)}, u32[]{:S(2)}) async-start(bf16[8,176,768]{2,1,0:T(8,128)(2,1)} %get-tuple-element.63), calls=%async_computation.1 | async-start | bytes 4325376 | tf_op jit(solution)/shard_map/all_to_all | solution.py:1566
  254.4 28.2 %weight_step.1 = bf16[16,3,48,1024]{3,2,1,0:T(8,128)(2,1)} custom-call(bf16[1408,768]{1,0:T(8,128)(2,1)} %bitcast.95, bf16[1408,768]{1,0:T(8,128)(2,1)} %bitcast.96, bf16[2,1408,1024]{2,1,0:T(8,128)(2,1)} %get-tuple-element.60.hid_ref, bf16[2,1408,1024]{2,1,0:T(8,128)(2,1)} %get-tuple-element.61.pg_ref, bf16[2,1408,1024]{2,1,0:T(8,128)(2,1)} %get-tuple-element.62.pu_ref), custom_call_target="tpu_custom_call" | custom-call | flops 13287555072 | bytes 26738688 | tf_op jit(solution)/shard_map/weight_step/pallas_call | solution.py:1166
  282.6 1.3 copy-done.17
  284.0 6.5 %all-to-all-start.2 = ((bf16[16,3,48,1024]{3,2,1,0:T(8,128)(2,1)}), bf16[16,3,48,1024]{3,2,1,0:T(8,128)(2,1)}, u32[]{:S(2)}, u32[]{:S(2)}) async-start(bf16[16,3,48,1024]{3,2,1,0:T(8,128)(2,1)} %weight_step.1), calls=%async_computation.2 | async-start | bytes 9437184 | tf_op jit(solution)/shard_map/all_to_all | solution.py:1667
  290.5 1.3 pad.28.mix_ref
  291.8 1.3 copy.90
  293.2 1.4 slice.86.proj_ref
  294.6 0.9 pad.27.prev_ref
  295.4 0.7 copy.101
  296.2 38.7 %backward_middle.1 = (f32[1024,768]{1,0:T(8,128)}, bf16[2048,768]{1,0:T(8,128)(2,1)}, bf16[2048,384]{1,0:T(8,128)(2,1)}, f32[1024,768]{1,0:T(8,128)}, f32[1024,1...) custom-call(bf16[8,176,768]{2,1,0:T(8,128)(2,1)} %get-tuple-element.65.back_ref, s32[2048,8]{1,0:T(8,128)} %bitcast.76, ...), custom_call_target="tpu_custom_call" | custom-call | tf_op jit(solution)/shard_map/backward_middle/pallas_call | solution.py:1076
  334.9 1.1 slice_bitcast_fusion
  335.9 0.8 copy.92
  336.8 4.7 convolution_convert_fusion.1.outg_ref
  341.5 1.2 copy-done.14
  342.7 48.1 %shard_map.196.qkv_ref = bf16[2048,1152]{1,0:T(8,128)(2,1)} custom-call(s32[4,8]{1,0:T(4,128)S(1)} %pad_add_fusion.1.bounds, bf16[2048,1152]{1,0:T(8,128)(2,1)} %convolution_convert_fusion.q_ref.k_ref.v_ref, bf16[2048,1152]{1,0:T(8,128)(2,1)} %convolution_convert_fusion.q_ref.k_ref.v_ref, bf16[2048,1152]{1,0:T(8,128)(2,1)} %convolution_convert_fusion.q_ref.k_ref.v_ref, ...), custom_call_target="tpu_custom_call" | custom-call | flops 32212254720 | bytes 15728640 | tf_op jit(solution)/shard_map/pallas_call | solution.py:255
  390.8 6.3 %all-to-all-done.2.grads_ref = bf16[16,3,48,1024]{3,2,1,0:T(8,128)(2,1)} async-done(((bf16[16,3,48,1024]{3,2,1,0:T(8,128)(2,1)}), bf16[16,3,48,1024]{3,2,1,0:T(8,128)(2,1)}, u32[]{:S(2)}, u32[]{:S(2)}) %all-to-all-start.2) | async-done | bytes 4718624 | tf_op jit(solution)/shard_map/all_to_all | solution.py:1667
  397.1 59.3 %tail.1 = (f32[3,48,384]{2,1,0:T(8,128)}, f32[48,384]{1,0:T(8,128)}, f32[1024,768]{1,0:T(8,128)}, bf16[1024,768]{1,0:T(8,128)(2,1)}, f32[24,768]{1,0:T(8,128)}, /*index=5*/f32[8,3,48,1024]{3,2,1,0:T(8,128)}) custom-call(bf16[8,176,768]{2,1,0:T(8,128)(2,1)} %copy-done.17, bf16[2048,1152]{1,0:T(8,128)(2,1)} %shard_map.196.qkv_ref, ...), custom_call_target="tpu_custom_call" | custom-call | tf_op jit(solution)/shard_map/tail/pallas_call | solution.py:1494
  456.5 0.9 slice.79
  457.4 1.4 dynamic-slice_bitcast_fusion
  458.8 0.6 reshape.311
  459.4 1.4 fusion.7
  460.8 2.7 copy.107
  463.5 1.7 copy.108
  465.2 0.7 copy.109
  465.9 0.6 copy.110
  466.5 0.7 copy-done.19
  467.2 2.2 copy.111
  (55 shorter events, 0.4 us)
Async XLA Ops:
  0.6 6.1 %copy-start.1 = (bf16[1,1024,768]{2,1,0:T(8,128)(2,1)S(1)}, bf16[1,1024,768]{2,1,0:T(8,128)(2,1)}, u32[]{:S(2)}) copy-start(bf16[1,1024,768]{2,1,0:T(8,128)(2,1)} %param.16) | copy-start | bytes 4718596
  4.9 60.3 %copy-start.18 = (s32[1,1024,2]{2,1,0:T(8,128)}, s32[1,1024,2]{2,1,0:T(8,128)S(1)}, u32[]{:S(2)}) copy-start(s32[1,1024,2]{2,1,0:T(8,128)S(1)} %copy.81) | copy-start | bytes 24580
  6.7 1.7 copy-start
  8.4 1.4 copy-start.2
  9.8 55.4 %slice-start = ((bf16[8,3,48,1024]{3,2,1,0:T(8,128)(2,1)}), bf16[8,2,48,1024]{3,2,1,0:T(8,128)(2,1)S(1)}, s32[]{:S(2)}) async-start(bf16[8,3,48,1024]{3,2,1,0:T(8,128)(2,1)} %w_ref.1), calls=%async_computation.3 | async-start | bytes 3145728 | tf_op jit(solution)/shard_map/slice | solution.py:1618
  65.2 2.5 copy-start.5
  65.2 3.1 copy-start.8
  65.2 3.6 copy-start.9
  68.8 9.5 %copy-start.6 = (bf16[16,48,1664]{2,1,0:T(8,128)(2,1)S(1)}, bf16[16,48,1664]{2,1,0:T(8,128)(2,1)}, u32[]{:S(2)}) copy-start(bf16[16,48,1664]{2,1,0:T(8,128)(2,1)} %copy-done.5) | copy-start | bytes 7667716
  68.8 79.2 %all-to-all-start = ((bf16[16,2,48,1024]{3,2,1,0:T(8,128)(2,1)}), bf16[16,2,48,1024]{3,2,1,0:T(8,128)(2,1)}, u32[]{:S(2)}, u32[]{:S(2)}) async-start(bf16[16,2,48,1024]{3,2,1,0:T(8,128)(2,1)} %bitcast.75), calls=%async_computation | async-start | bytes 6291456 | tf_op jit(solution)/shard_map/all_to_all | solution.py:1620
  79.2 52.9 %collective-permute-start = (bf16[768,384]{1,0:T(8,128)(2,1)}, bf16[768,384]{1,0:T(8,128)(2,1)}, u32[]{:S(2)}, u32[]{:S(2)}) collective-permute-start(bf16[768,384]{1,0:T(8,128)(2,1)} %slice.87.own_w_ref), channel_id=1, source_target_pairs={{0,1},{1,0},{2,3},{3,2},{4,5},{5,4},{6,7},{7,6},{8,9},{9,8},{10,11... | collective-permute-start | bytes 1769480 | tf_op jit(solution)/shard_map/ppermute | solution.py:50
  79.9 5.2 %copy-start.22 = (f32[768,2]{0,1:T(2,128)}, f32[768,2]{0,1:T(2,128)S(1)}, u32[]{:S(2)}) copy-start(f32[768,2]{0,1:T(2,128)S(1)} %copy.100) | copy-start | bytes 18436
  81.3 3.0 copy-start.15
  85.1 1.6 copy-start.16
  86.8 5.9 %copy-start.10 = (s32[2048,1]{1,0:T(8,128)S(1)}, s32[2048,1]{1,0:T(8,128)}, u32[]{:S(2)}) copy-start(s32[2048,1]{1,0:T(8,128)} %copy.87.start_ref) | copy-start | bytes 24580
  124.5 1.1 copy-start.3
  125.6 1.0 copy-start.13
  248.8 33.8 %all-to-all-start.1 = ((bf16[8,176,768]{2,1,0:T(8,128)(2,1)}), bf16[8,176,768]{2,1,0:T(8,128)(2,1)S(1)}, u32[]{:S(2)}, u32[]{:S(2)}) async-start(bf16[8,176,768]{2,1,0:T(8,128)(2,1)} %get-tuple-element.63), calls=%async_computation.1 | async-start | bytes 4325376 | tf_op jit(solution)/shard_map/all_to_all | solution.py:1566
  282.6 1.3 copy-start.17
  284.0 9.2 %copy-start.7 = (bf16[16,48,1664]{2,1,0:T(8,128)(2,1)S(1)}, bf16[16,48,1664]{2,1,0:T(8,128)(2,1)}, u32[]{:S(2)}) copy-start(bf16[16,48,1664]{2,1,0:T(8,128)(2,1)} %copy-done.5) | copy-start | bytes 7667716
  284.0 113.2 %all-to-all-start.2 = ((bf16[16,3,48,1024]{3,2,1,0:T(8,128)(2,1)}), bf16[16,3,48,1024]{3,2,1,0:T(8,128)(2,1)}, u32[]{:S(2)}, u32[]{:S(2)}) async-start(bf16[16,3,48,1024]{3,2,1,0:T(8,128)(2,1)} %weight_step.1), calls=%async_computation.2 | async-start | bytes 9437184 | tf_op jit(solution)/shard_map/all_to_all | solution.py:1667
  296.2 40.6 %copy-start.4 = (bf16[2048,384]{1,0:T(8,128)(2,1)S(1)}, bf16[2048,384]{1,0:T(8,128)(2,1)}, u32[]{:S(2)}) copy-start(bf16[2048,384]{1,0:T(8,128)(2,1)} %copy-done.3) | copy-start | bytes 4718596
  336.7 4.7 %copy-start.11 = (bf16[2048,384]{1,0:T(8,128)(2,1)S(1)}, bf16[2048,384]{1,0:T(8,128)(2,1)}, u32[]{:S(2)}) copy-start(bf16[2048,384]{1,0:T(8,128)(2,1)} %get-tuple-element.69.do_ref) | copy-start | bytes 4718596
  336.7 4.7 %copy-start.12 = (f32[2048,384]{1,0:T(8,128)S(1)}, f32[2048,384]{1,0:T(8,128)}, u32[]{:S(2)}) copy-start(f32[2048,384]{1,0:T(8,128)} %get-tuple-element.70.o_ref) | copy-start | bytes 9437188
  341.4 1.2 copy-start.14
  456.5 7.0 %copy-start.20 = (f32[1024,768]{1,0:T(8,128)S(1)}, f32[1024,768]{1,0:T(8,128)}, u32[]{:S(2)}) copy-start(f32[1024,768]{1,0:T(8,128)} %get-tuple-element.80) | copy-start | bytes 9437188
  463.5 1.7 copy-start.21
  463.5 2.4 copy-start.23
  463.5 3.7 copy-start.19

commit v6 on v5

--- a/solution.py
+++ b/solution.py
@@ -309,6 +309,7 @@
     hot_ref,
     info_ref,
     down_ref,
+    in_ref,
     ids_all_ref,
     dy_all_ref,
     place_ref,
@@ -341,9 +342,9 @@
     groups = members // size
 
     def device_at(g, k):
-        return lax.rem(base + g * size, members) + lax.rem(mine + k, size)
-
-    distant = [(g, k) for k in range(size) for g in range(groups) if g or k]
+        return lax.rem(base + g * size, members) + flip(mine, k)
+
+    distant = [(g, k) for k in (0,) + NEAR for g in range(groups) if g or k]
     peers += [device_at(g, k) for g, k in distant]
     barrier = pltpu.get_barrier_semaphore()
     for peer in peers:
@@ -387,6 +388,12 @@
         pltpu.make_async_copy(tok_ref, all_ref.at[own_rows], own_sem.at[2]),
         pltpu.make_async_copy(pack_ref, full_ref.at[me], own_sem.at[3]),
         pltpu.make_async_copy(w_ref.at[mine, 2], down_ref.at[me], own_sem.at[4]),
+    ]
+    owns += [
+        pltpu.make_async_copy(
+            w_ref.at[:, pl.ds(0, 2)], in_ref.at[pl.ds(g * size, size)], own_sem.at[5 + g]
+        )
+        for g in range(groups)
     ]
     for copy in swaps + owns:
         copy.start()
@@ -443,7 +450,7 @@
 
     for g, k in distant:
         copy = remote(
-            w_ref.at[lax.rem(mine + k, size), 2],
+            w_ref.at[flip(mine, k), 2],
             down_ref.at[me],
             down_send.at[g * size + k],
             down_recv.at[me],
@@ -464,7 +471,7 @@
         for step in range(1, high):
             arrived(lax.rem(block + step * low, members))
     for g, k in distant:
-        block = device_at((groups - g) % groups, (size - k) % size)
+        block = device_at((groups - g) % groups, k)
         remote(
             w_ref.at[0, 2], down_ref.at[block], down_send.at[0], down_recv.at[block], partner
         ).wait_recv()
@@ -482,6 +489,7 @@
     count = EXPERTS_FF * padded
     any_spec = pl.BlockSpec(memory_space=pl.ANY)
     vmem = pl.BlockSpec(memory_space=pltpu.VMEM)
+    hbm = pl.BlockSpec(memory_space=pltpu.HBM)
     dma = pltpu.SemaphoreType.DMA
     return pl.pallas_call(
         functools.partial(start_kernel, members, low, per_core, padded),
@@ -492,16 +500,17 @@
             jax.ShapeDtypeStruct((count, 2 * local), half),
             jax.ShapeDtypeStruct((8, 2 * local), jnp.int32),
             jax.ShapeDtypeStruct((members,) + w.shape[2:], half),
+            jax.ShapeDtypeStruct((members, 2) + w.shape[2:], half),
         ],
-        in_specs=[pl.BlockSpec(memory_space=pltpu.HBM)] * 5,
-        out_specs=[any_spec] * 2 + [vmem] * 3 + [any_spec],
+        in_specs=[any_spec, hbm, hbm, any_spec, hbm],
+        out_specs=[any_spec] * 2 + [vmem] * 3 + [any_spec, hbm],
         scratch_shapes=[
             pltpu.VMEM((2, 8, local), jnp.int32),
             pltpu.VMEM((2 * local, width), half),
             pltpu.VMEM((16, 2 * local), jnp.int32),
             dma((high * (low + 1),)),
             dma((members,)),
-            dma((5,)),
+            dma((5 + members // EXPERTS_FF,)),
             dma((3,)),
             dma((3,)),
             dma((members,)),
@@ -528,7 +537,7 @@
     router_ref,
     prev_ref,
     routes_ref,
-    hot_ref,
+    hot_hbm_ref,
     back_ref,
     out_ref,
     x_ref,
@@ -551,6 +560,7 @@
     spill_ref,
     gate_ref,
     dot_ref,
+    hot_ref,
     x_send,
     x_recv,
     dy_send,
@@ -591,6 +601,8 @@
     other_rows = pl.ds(pl.multiple_of((1 - core) * local, local), local)
     heads = remote(ho_ref.at[other_rows], ho_in_ref, swap_send.at[0], swap_recv.at[0], partner)
     heads.start()
+    load_hot = pltpu.make_async_copy(hot_hbm_ref, hot_ref, own_sem.at[4])
+    load_hot.start()
     waits = []
     for k in NEAR:
         to = flip(mine, k)
@@ -646,6 +658,7 @@
     )
     swap_rows.start()
 
+    load_hot.wait()
     for number, pair in enumerate(PAIRS):
         slots = [
             pl.ds(pl.multiple_of(flip(mine, k) * padded, 16), padded) for k in pair
@@ -834,7 +847,7 @@
             jax.ShapeDtypeStruct((local, width), half),
             jax.ShapeDtypeStruct((local, LANES), single),
         ],
-        in_specs=[any_spec] * 3 + [vmem] * 9,
+        in_specs=[any_spec] * 3 + [vmem] * 8 + [any_spec],
         out_specs=[any_spec] + [vmem] * 3 + [any_spec] * 3 + [vmem] * 3,
         scratch_shapes=[
             pltpu.VMEM((local, heads.shape[1]), half),
@@ -849,11 +862,12 @@
             pltpu.VMEM((2, 3, 2 * padded, block), half),
             pltpu.VMEM((2 * padded, LANES), single),
             pltpu.VMEM((16, 2 * LANES), single),
+            pltpu.VMEM(hot.shape, half),
             dma((size,)),
             dma((size,)),
             dma((size,)),
             dma((size,)),
-            dma((4,)),
+            dma((5,)),
             dma((4,)),
             dma((4,)),
             dma((size,)),
@@ -886,10 +900,10 @@
     padded,
     back_ref,
     info_ref,
-    resid_ref,
-    normed_ref,
+    resid_hbm_ref,
+    normed_hbm_ref,
     misc_ref,
-    dy_ref,
+    dy_hbm_ref,
     routes_ref,
     gain_ref,
     const_ref,
@@ -911,6 +925,10 @@
     hg_ref,
     send_sem,
     recv_sem,
+    resid_ref,
+    normed_ref,
+    dy_ref,
+    load_sem,
 ):
     core = lax.axis_index("tensor")
     partner = {"tensor": 1 - core}
@@ -918,6 +936,13 @@
     count = sources * padded
     local = dy_ref.shape[0]
     step = fit(local, 256)
+    pairs = (resid_hbm_ref, resid_ref), (normed_hbm_ref, normed_ref), (dy_hbm_ref, dy_ref)
+    loads = [
+        pltpu.make_async_copy(source, target, load_sem.at[i])
+        for i, (source, target) in enumerate(pairs)
+    ]
+    for copy in loads:
+        copy.start()
     barrier = pltpu.get_barrier_semaphore()
     pl.semaphore_signal(barrier, inc=1, device_id=partner, device_id_type=MESH)
     pl.semaphore_wait(barrier, 1)
@@ -966,6 +991,8 @@
         rgrad_ref[rows, :] = mm(hot, back_all[...])
         pgrad_ref[rows, :] = mm(hot, ext_ref[...])
 
+    for copy in loads:
+        copy.wait()
     sums.wait()
 
     @pl.loop(0, local // step)
@@ -1073,6 +1100,7 @@
     hh = own_w.shape[1]
     count = EXPERTS_FF * padded
     vmem = pl.BlockSpec(memory_space=pltpu.VMEM)
+    hbm = pl.BlockSpec(memory_space=pltpu.HBM)
     return pl.pallas_call(
         functools.partial(back_kernel, padded),
         out_shape=[
@@ -1084,7 +1112,7 @@
             jax.ShapeDtypeStruct((24, width), single),
             jax.ShapeDtypeStruct((LANES, LANES), single),
         ],
-        in_specs=[vmem] * 14,
+        in_specs=[vmem] * 2 + [hbm] * 2 + [vmem, hbm] + [vmem] * 8,
         out_specs=[vmem] * 7,
         scratch_shapes=[
             pltpu.VMEM((count, LANES), half),
@@ -1092,6 +1120,10 @@
             pltpu.VMEM((local, width + LANES), half),
             pltpu.VMEM((local, hh), half),
             pltpu.SemaphoreType.DMA((3,)),
+            pltpu.SemaphoreType.DMA((3,)),
+            pltpu.VMEM((local, width), single),
+            pltpu.VMEM((local, width), half),
+            pltpu.VMEM((local, width), half),
             pltpu.SemaphoreType.DMA((3,)),
         ],
         compiler_params=pltpu.CompilerParams(
@@ -1194,14 +1226,14 @@
     members,
     low,
     padded,
-    eo_ref,
+    eo_hbm_ref,
     qkv_ref,
     one_ref,
     proj_ref,
     outg_ref,
-    x_ref,
-    base_ref,
-    resid_ref,
+    x_hbm_ref,
+    base_hbm_ref,
+    resid_hbm_ref,
     info_ref,
     gain_ref,
     small_ref,
@@ -1240,6 +1272,11 @@
     sum_ref,
     part_sem,
     sum_sem,
+    eo_ref,
+    x_ref,
+    base_ref,
+    resid_ref,
+    load_sem,
 ):
     size = EXPERTS_FF
     me = lax.axis_index("dp")
@@ -1275,6 +1312,14 @@
             device_id=device,
             device_id_type=MESH,
         )
+
+    pairs = (x_hbm_ref, x_ref), (eo_hbm_ref, eo_ref), (base_hbm_ref, base_ref), (resid_hbm_ref, resid_ref)
+    loads = [
+        pltpu.make_async_copy(source, target, load_sem.at[i])
+        for i, (source, target) in enumerate(pairs)
+    ]
+    for copy in loads:
+        copy.start()
 
     sent = []
     chunks = 2
@@ -1305,6 +1350,8 @@
         return part
 
     mine_ref[...] = small_ref[...]
+    for copy in loads:
+        copy.wait()
 
     @pl.loop(0, local // step)
     def _(r):
@@ -1320,6 +1367,9 @@
         rows = pl.ds(pl.multiple_of(r * step, step), step)
         here = pl.ds(pl.multiple_of(core * local + r * step, step), step)
         tokens_ref[rows, :] = one_part(here)
+
+    pair = remote(mine_ref, pair_ref, pair_send.at[1], pair_recv.at[1], partner)
+    pair.start()
 
     eo_all = eo_ref.reshape(count, width)
 
@@ -1347,8 +1397,6 @@
             {"dp": h * low + inside},
         )
 
-    pair = remote(mine_ref, pair_ref, pair_send.at[1], pair_recv.at[1], partner)
-    pair.start()
     pair.wait()
     near_ref[inside] = mine_ref[...] + pair_ref[...]
     near = []
@@ -1363,6 +1411,42 @@
             )
         )
         near[-1].start()
+
+    for h in range(high):
+        for k in range(low - 1):
+            remote(
+                dense_ref.at[0], first_ref.at[k, h], send1.at[k, h], recv1.at[k, h], partner
+            ).wait_recv()
+        total = dense_ref[h * low + inside].astype(single)
+        for k in range(low - 1):
+            total += first_ref[k, h].astype(single)
+
+        @pl.when(h == row)
+        def _():
+            dense_out_ref[...] = total
+
+        @pl.when(h != row)
+        def _():
+            stage_ref[h] = total.astype(half)
+            second(h).start()
+
+    for k in range(1, low):
+        block = lax.rem(inside + k, low)
+        remote(
+            mine_ref, near_ref.at[block], near_send.at[0], near_recv.at[block], partner
+        ).wait_recv()
+    total = near_ref[0]
+    for k in range(1, low):
+        total = total + near_ref[k]
+    far_ref[row] = total
+    far = []
+    for k in range(1, high):
+        far.append(
+            remote(
+                far_ref.at[row], far_ref.at[row], far_send.at[k], far_recv.at[row], {"dp": across(k)}
+            )
+        )
+        far[-1].start()
 
     groups = members // size
 
@@ -1394,42 +1478,6 @@
         store(e).start()
     for e in range(size - 2, size):
         store(e).wait()
-
-    for h in range(high):
-        for k in range(low - 1):
-            remote(
-                dense_ref.at[0], first_ref.at[k, h], send1.at[k, h], recv1.at[k, h], partner
-            ).wait_recv()
-        total = dense_ref[h * low + inside].astype(single)
-        for k in range(low - 1):
-            total += first_ref[k, h].astype(single)
-
-        @pl.when(h == row)
-        def _():
-            dense_out_ref[...] = total
-
-        @pl.when(h != row)
-        def _():
-            stage_ref[h] = total.astype(half)
-            second(h).start()
-
-    for k in range(1, low):
-        block = lax.rem(inside + k, low)
-        remote(
-            mine_ref, near_ref.at[block], near_send.at[0], near_recv.at[block], partner
-        ).wait_recv()
-    total = near_ref[0]
-    for k in range(1, low):
-        total = total + near_ref[k]
-    far_ref[row] = total
-    far = []
-    for k in range(1, high):
-        far.append(
-            remote(
-                far_ref.at[row], far_ref.at[row], far_send.at[k], far_recv.at[row], {"dp": across(k)}
-            )
-        )
-        far[-1].start()
 
     one_sent.wait()
 
@@ -1501,7 +1549,7 @@
             jax.ShapeDtypeStruct(small.shape, single),
             jax.ShapeDtypeStruct((EXPERTS_FF,) + grads.shape[1:], single),
         ],
-        in_specs=[vmem] * 11 + [hbm],
+        in_specs=[hbm] + [vmem] * 4 + [hbm] * 3 + [vmem] * 3 + [hbm],
         out_specs=[vmem] * 5 + [hbm],
         scratch_shapes=[
             pltpu.VMEM((members, d_rows, wide), half),
@@ -1532,6 +1580,11 @@
             pltpu.VMEM((2,) + grads.shape[1:], single),
             dma((2, groups)),
             dma((2,)),
+            pltpu.VMEM(eo.shape, half),
+            pltpu.VMEM(x.shape, half),
+            pltpu.VMEM(base.shape, single),
+            pltpu.VMEM(resid.shape, single),
+            dma((4,)),
         ],
         compiler_params=pltpu.CompilerParams(
             collective_id=4, has_side_effects=True, vmem_limit_bytes=60 << 20
@@ -1601,10 +1654,9 @@
     pack = jnp.pad(pack, ((0, 0), (0, -columns % LANES)))
     ids = jnp.concatenate([segment_ids, routes[0].T], 0)
     ids = jnp.pad(ids, ((0, 5), (0, 0)))
-    full_pack, tokens_all, dy_rows, onehot, info, my_down = start(
+    full_pack, tokens_all, dy_rows, onehot, info, my_down, in_weight = start(
         pack, tokens[0], cotangent[0], ids, expert_weight, members, per_core, padded
     )
-    full_pack, expert_weight = lax.optimization_barrier((full_pack, expert_weight))
     full_pack = full_pack.reshape(members * d_rows, -1)[:, :columns]
     width = members * d_rows
     proj_full = full_pack[:, : 3 * hh]
@@ -1614,9 +1666,6 @@
     gains = rest[:, :2].T.astype(single)
     const_f = rest[:, 2:4].T.astype(single)
     router_full = rest[:, 4:]
-    in_weight = jnp.broadcast_to(
-        expert_weight[None, :, :2], (groups, EXPERTS_FF, 2) + expert_weight.shape[2:]
-    ).reshape((members, 2) + expert_weight.shape[2:])
     my_in = lax.all_to_all(in_weight, "dp", 0, 0, tiled=True)
 
     x_rows = tokens[0].astype(single)
@@ -1636,6 +1685,11 @@
     mixed_prev = jnp.dot(prev_rows, gate_mixing, precision=HIGH)
     mixed_prev = jnp.pad(mixed_prev, ((0, 0), (0, LANES - EXPERTS)))
     router_wide = jnp.pad(router_full, ((0, 0), (0, LANES - router_full.shape[1])))
+    mix_wide = jnp.pad(gate_mixing, ((0, LANES - EXPERTS), (0, LANES - EXPERTS)))
+    prev_wide = jnp.pad(prev_rows, ((0, 0), (0, LANES - EXPERTS)))
+    router_wide, mixed_prev, mix_wide, prev_wide, columns, proj_full = lax.optimization_barrier(
+        (router_wide, mixed_prev, mix_wide, prev_wide, columns, proj_full)
+    )
     back_grad, gated_out, got_rows, out_grad, hidden, pg, pu, resid, normed_two, misc = experts(
         my_down,
         my_in,
@@ -1666,8 +1720,6 @@
         grads_sent = grads_sent.reshape(3, members, d_rows, -1).transpose(1, 0, 2, 3)
     grads_got = lax.all_to_all(grads_sent, "dp", 0, 0, tiled=True)
 
-    mix_wide = jnp.pad(gate_mixing, ((0, LANES - EXPERTS), (0, LANES - EXPERTS)))
-    prev_wide = jnp.pad(prev_rows, ((0, 0), (0, LANES - EXPERTS)))
     resid_grad, attn_all, heads_grad, base, prev_grad, small, mixing_grad = backward_middle(
         back_grad,
         columns,

time: 478 us -> 468 us (0.979)
  Pallas kernels: 362 us -> 338 us
  waiting for transfers between devices: 22.3 us -> 40.8 us
    all_to_all x1, waiting for transfers between devices: 6.35 us -> 21.1 us  [per_device(): grads_got = lax.all_to_all(grads_sent, 'dp', 0, 0, tiled=True)]
    pallas_call x1, Pallas kernels: 48.1 us -> 40 us  [attention_backward(): pl.pallas_call(functools.partial(bwd_kernel, heads), grid_spec=pltpu.Pref...]
    pallas_call x1, Pallas kernels: 59.3 us -> 51.3 us  [tail(): pl.pallas_call(functools.partial(tail_kernel, members, low, padded), out_...]
    pallas_call x1, Pallas kernels: 31.8 us -> 27 us  [attention_forward(): pl.pallas_call(functools.partial(fwd_kernel, heads), grid_spec=pltpu.Pref...]
    unnamed x64 -> x66, local copies, waits for them, and re-layouts: 25.4 us -> 27.5 us
  transfers between devices with their start and end apart: 4 -> 4, of which waited for: 2 -> 2; matrix products, arithmetic and copies ran while one was open for 6% -> 6% of each run, Pallas kernels for 31% -> 29%
where the time goes in v6:
time: 468 us; the launch traced here: 459 us
  Pallas kernels  338 us (72%)
  local copies, waits for them, and re-layouts  43.3 us (9%)
  waiting for transfers between devices  40.8 us (9%)
  starting transfers between devices  19.2 us (4%)
  matrix products  11.1 us (2%)
    pallas_call x1, Pallas kernels, experts(): pl.pallas_call(functools.partial(experts_kernel, members, padded), out_sh...  98.9 us
    pallas_call x1, Pallas kernels, start(): pl.pallas_call(functools.partial(start_kernel, members, low, per_core, pa...  56 us
    pallas_call x1, Pallas kernels, tail(): pl.pallas_call(functools.partial(tail_kernel, members, low, padded), out_...  51.3 us
    pallas_call x1, Pallas kernels, attention_backward(): pl.pallas_call(functools.partial(bwd_kernel, heads), grid_spec=pltpu.Pref...  40 us
    pallas_call x1, Pallas kernels, backward_middle(): pl.pallas_call(functools.partial(back_kernel, padded), out_shape=[jax.Sha...  36.9 us
    pallas_call x1, Pallas kernels, weight_step(): pl.pallas_call(weight_kernel, grid=(steps,), in_specs=[whole, whole, wide...  28.3 us
    unnamed x66, local copies, waits for them, and re-layouts  27.5 us
    pallas_call x1, Pallas kernels, attention_forward(): pl.pallas_call(functools.partial(fwd_kernel, heads), grid_spec=pltpu.Pref...  27 us
  transfers between devices with their start and end apart: 4, of which 2 were waited for; matrix products, arithmetic and copies ran while one was open for 6% of the time, Pallas kernels for 29%

profile of v6, /device:TPU:12, one launch (start us, length us, event | category | flops | bytes accessed | tf_op | source)
XLA Modules:
  0.0 458.8 jit_solution(11597653310228224990)
XLA Ops:
  0.7 0.9 copy.78
  1.5 0.8 copy.80
  2.3 0.8 copy.79
  3.1 0.9 copy.99
  4.0 0.9 copy.81
  4.9 0.2 copy.82
  5.1 0.9 concatenate.6
  6.0 0.7 pad_add_fusion
  6.7 1.4 copy-done.1
  8.1 1.7 copy-done.6
  9.8 56.0 %start.1 = (bf16[16,48,1664]{2,1,0:T(8,128)(2,1)S(1)}, bf16[2048,768]{1,0:T(8,128)(2,1)}, bf16[8,176,768]{2,1,0:T(8,128)(2,1)S(1)}, bf16[1408,2048]{1,0:T(8,128)...) custom-call(bf16[48,1664]{1,0:T(8,128)(2,1)S(1)} %pad.23.pack_ref, ...), custom_call_target="tpu_custom_call" | custom-call | tf_op jit(solution)/shard_map/start/pallas_call | solution.py:494
  65.9 1.5 copy-done.4
  67.3 1.4 copy-done.7
  68.7 1.1 copy-done.8
  69.9 6.7 %all-to-all-start = ((bf16[16,2,48,1024]{3,2,1,0:T(8,128)(2,1)}), bf16[16,2,48,1024]{3,2,1,0:T(8,128)(2,1)}, u32[]{:S(2)}, u32[]{:S(2)}) async-start(bf16[16,2,48,1024]{3,2,1,0:T(8,128)(2,1)} %get-tuple-element.54), calls=%async_computation | async-start | bytes 6291456 | tf_op jit(solution)/shard_map/all_to_all | solution.py:1669
  76.6 0.9 slice.83.own_w_ref
  77.7 0.1 copy.94
  77.7 0.1 copy.95
  77.9 0.1 copy.96
  78.0 0.1 slice_convert_fusion
  78.1 0.1 copy.100
  78.2 1.4 copy.87.start_ref
  79.6 0.2 convert_reduce_fusion
  79.9 2.7 fusion
  82.6 0.8 fusion.2.one_ref
  83.4 1.7 copy-done.15
  85.1 5.8 %convolution_convert_fusion.q_ref.k_ref.v_ref = bf16[2048,1152]{1,0:T(8,128)(2,1)} fusion(bf16[2048,768]{1,0:T(8,128)(2,1)S(1)} %fusion.2.one_ref, bf16[768,1664]{1,0:T(8,128)(2,1)S(1)} %bitcast.71), kind=kOutput, calls=%fused_computation.2 | convolution fusion | flops 3626237952 | bytes 9633792 | tf_op jit(solution)/shard_map/dot_general | solution.py:38
  90.9 27.0 %shard_map.195 = (f32[2048,384]{1,0:T(8,128)}, bf16[2048,384]{1,0:T(8,128)(2,1)S(1)}, f32[2048,128]{1,0:T(8,128)S(1)}) custom-call(s32[4,8]{1,0:T(4,128)S(1)} %pad_add_fusion.1.bounds, bf16[2048,1152]{1,0:T(8,128)(2,1)} %convolution_convert_fusion.q_ref.k_ref.v_ref, bf16[2048,1152]{1,0:T(8,128)(2,1)} %convolution_convert_fusion.q_ref.k_ref.v_ref, ...), custom_call_target="tpu_custom_call" | custom-call | flops 12884901888 | bytes 12582912 | tf_op jit(solution)/shard_map/pallas_call | solution.py:153
  117.9 1.1 copy-done.2
  119.1 1.0 copy-done.12
  120.1 0.1 slice.84
  120.2 1.4 copy.90
  121.6 1.4 slice.82.proj_ref
  122.9 0.2 copy.88
  123.2 0.6 pad.27.mix_ref
  123.8 0.8 pad.28.prev_ref
  124.7 0.5 fusion.4
  125.2 0.9 pad.26.prev_ref
  126.1 0.7 pad.25.router_ref
  126.8 19.7 %all-to-all-done.in_ref = bf16[16,2,48,1024]{3,2,1,0:T(8,128)(2,1)} async-done(((bf16[16,2,48,1024]{3,2,1,0:T(8,128)(2,1)}), bf16[16,2,48,1024]{3,2,1,0:T(8,128)(2,1)}, u32[]{:S(2)}, u32[]{:S(2)}) %all-to-all-start) | async-done | bytes 3145760 | tf_op jit(solution)/shard_map/all_to_all | solution.py:1669
  146.5 98.9 %experts.1 = (bf16[8,176,768]{2,1,0:T(8,128)(2,1)}, bf16[8,176,768]{2,1,0:T(8,128)(2,1)}, bf16[8,176,768]{2,1,0:T(8,128)(2,1)}, bf16[8,176,768]{2,1,0:T(8,128)(2...) custom-call(bf16[16,48,1024]{2,1,0:T(8,128)(2,1)} %copy-done.8, ...), custom_call_target="tpu_custom_call" | custom-call | tf_op jit(solution)/shard_map/experts/pallas_call | solution.py:836
  245.4 5.7 %all-to-all-start.1 = ((bf16[8,176,768]{2,1,0:T(8,128)(2,1)}), bf16[8,176,768]{2,1,0:T(8,128)(2,1)S(1)}, u32[]{:S(2)}, u32[]{:S(2)}) async-start(bf16[8,176,768]{2,1,0:T(8,128)(2,1)} %get-tuple-element.69), calls=%async_computation.1 | async-start | bytes 4325376 | tf_op jit(solution)/shard_map/all_to_all | solution.py:1619
  251.1 28.3 %weight_step.1 = bf16[16,3,48,1024]{3,2,1,0:T(8,128)(2,1)} custom-call(bf16[1408,768]{1,0:T(8,128)(2,1)} %bitcast.93, bf16[1408,768]{1,0:T(8,128)(2,1)} %bitcast.94, bf16[2,1408,1024]{2,1,0:T(8,128)(2,1)} %get-tuple-element.66.hid_ref, bf16[2,1408,1024]{2,1,0:T(8,128)(2,1)} %get-tuple-element.67.pg_ref, bf16[2,1408,1024]{2,1,0:T(8,128)(2,1)} %get-tuple-element.68.pu_ref), custom_call_target="tpu_custom_call" | custom-call | flops 13287555072 | bytes 26738688 | tf_op jit(solution)/shard_map/weight_step/pallas_call | solution.py:1198
  279.4 1.3 copy-done.16
  280.7 6.7 %all-to-all-start.2 = ((bf16[16,3,48,1024]{3,2,1,0:T(8,128)(2,1)}), bf16[16,3,48,1024]{3,2,1,0:T(8,128)(2,1)}, u32[]{:S(2)}, u32[]{:S(2)}) async-start(bf16[16,3,48,1024]{3,2,1,0:T(8,128)(2,1)} %weight_step.1), calls=%async_computation.2 | async-start | bytes 9437184 | tf_op jit(solution)/shard_map/all_to_all | solution.py:1721
  287.4 0.7 copy.101
  288.2 36.9 %backward_middle.1 = (f32[1024,768]{1,0:T(8,128)}, bf16[2048,768]{1,0:T(8,128)(2,1)}, bf16[2048,384]{1,0:T(8,128)(2,1)}, f32[1024,768]{1,0:T(8,128)}, f32[1024,1...) custom-call(bf16[8,176,768]{2,1,0:T(8,128)(2,1)} %get-tuple-element.71.back_ref, s32[2048,8]{1,0:T(8,128)} %bitcast.74, ...), custom_call_target="tpu_custom_call" | custom-call | tf_op jit(solution)/shard_map/backward_middle/pallas_call | solution.py:1104
  325.1 1.1 slice_bitcast_fusion
  326.2 0.8 copy.92
  327.0 4.7 %convolution_convert_fusion.1.outg_ref = bf16[768,384]{1,0:T(8,128)(2,1)} fusion(bf16[2048,768]{1,0:T(8,128)(2,1)} %get-tuple-element.84, bf16[2048,384]{1,0:T(8,128)(2,1)S(1)} %copy-done.3), kind=kOutput, calls=%fused_computation.6 | convolution fusion | flops 1208254464 | bytes 5308416 | tf_op jit(solution)/shard_map/dot_general | solution.py:46
  331.7 1.2 copy-done.13
  332.9 40.0 %shard_map.196.qkv_ref = bf16[2048,1152]{1,0:T(8,128)(2,1)} custom-call(s32[4,8]{1,0:T(4,128)S(1)} %pad_add_fusion.1.bounds, bf16[2048,1152]{1,0:T(8,128)(2,1)} %convolution_convert_fusion.q_ref.k_ref.v_ref, bf16[2048,1152]{1,0:T(8,128)(2,1)} %convolution_convert_fusion.q_ref.k_ref.v_ref, bf16[2048,1152]{1,0:T(8,128)(2,1)} %convolution_convert_fusion.q_ref.k_ref.v_ref, ...), custom_call_target="tpu_custom_call" | custom-call | flops 32212254720 | bytes 15728640 | tf_op jit(solution)/shard_map/pallas_call | solution.py:255
  372.9 21.1 %all-to-all-done.2.grads_ref = bf16[16,3,48,1024]{3,2,1,0:T(8,128)(2,1)} async-done(((bf16[16,3,48,1024]{3,2,1,0:T(8,128)(2,1)}), bf16[16,3,48,1024]{3,2,1,0:T(8,128)(2,1)}, u32[]{:S(2)}, u32[]{:S(2)}) %all-to-all-start.2) | async-done | bytes 4718624 | tf_op jit(solution)/shard_map/all_to_all | solution.py:1721
  394.1 51.3 %tail.1 = (f32[3,48,384]{2,1,0:T(8,128)}, f32[48,384]{1,0:T(8,128)}, f32[1024,768]{1,0:T(8,128)}, bf16[1024,768]{1,0:T(8,128)(2,1)}, f32[24,768]{1,0:T(8,128)}, /*index=5*/f32[8,3,48,1024]{3,2,1,0:T(8,128)}) custom-call(bf16[8,176,768]{2,1,0:T(8,128)(2,1)} %copy-done.16, bf16[2048,1152]{1,0:T(8,128)(2,1)} %shard_map.196.qkv_ref, ...), custom_call_target="tpu_custom_call" | custom-call | tf_op jit(solution)/shard_map/tail/pallas_call | solution.py:1542
  445.4 0.9 slice.75
  446.3 1.4 dynamic-slice_bitcast_fusion
  447.7 0.6 reshape.306
  448.3 1.4 fusion.7
  449.7 2.7 copy.107
  452.4 1.7 copy.108
  454.1 0.7 copy.109
  454.8 0.6 copy.110
  455.4 0.7 copy-done.18
  456.1 2.2 copy.111
  (54 shorter events, 0.4 us)
Async XLA Ops:
  0.6 6.1 %copy-start = (bf16[1,1024,768]{2,1,0:T(8,128)(2,1)S(1)}, bf16[1,1024,768]{2,1,0:T(8,128)(2,1)}, u32[]{:S(2)}) copy-start(bf16[1,1024,768]{2,1,0:T(8,128)(2,1)} %param.16) | copy-start | bytes 4718596
  4.9 61.0 %copy-start.17 = (s32[1,1024,2]{2,1,0:T(8,128)}, s32[1,1024,2]{2,1,0:T(8,128)S(1)}, u32[]{:S(2)}) copy-start(s32[1,1024,2]{2,1,0:T(8,128)S(1)} %copy.81) | copy-start | bytes 24580
  6.7 1.4 copy-start.1
  8.1 1.7 copy-start.6
  65.9 1.5 copy-start.4
  67.3 1.4 copy-start.7
  68.7 1.1 copy-start.8
  69.9 6.7 %copy-start.5 = (bf16[16,48,1664]{2,1,0:T(8,128)(2,1)S(1)}, bf16[16,48,1664]{2,1,0:T(8,128)(2,1)}, u32[]{:S(2)}) copy-start(bf16[16,48,1664]{2,1,0:T(8,128)(2,1)} %copy-done.4) | copy-start | bytes 7667716
  69.9 76.6 %all-to-all-start = ((bf16[16,2,48,1024]{3,2,1,0:T(8,128)(2,1)}), bf16[16,2,48,1024]{3,2,1,0:T(8,128)(2,1)}, u32[]{:S(2)}, u32[]{:S(2)}) async-start(bf16[16,2,48,1024]{3,2,1,0:T(8,128)(2,1)} %get-tuple-element.54), calls=%async_computation | async-start | bytes 6291456 | tf_op jit(solution)/shard_map/all_to_all | solution.py:1669
  77.5 49.3 %collective-permute-start = (bf16[768,384]{1,0:T(8,128)(2,1)}, bf16[768,384]{1,0:T(8,128)(2,1)}, u32[]{:S(2)}, u32[]{:S(2)}) collective-permute-start(bf16[768,384]{1,0:T(8,128)(2,1)} %slice.83.own_w_ref), channel_id=1, source_target_pairs={{0,1},{1,0},{2,3},{3,2},{4,5},{5,4},{6,7},{7,6},{8,9},{9,8},{10,11... | collective-permute-start | bytes 1769480 | tf_op jit(solution)/shard_map/ppermute | solution.py:50
  78.2 5.2 %copy-start.21 = (f32[768,2]{0,1:T(2,128)}, f32[768,2]{0,1:T(2,128)S(1)}, u32[]{:S(2)}) copy-start(f32[768,2]{0,1:T(2,128)S(1)} %copy.100) | copy-start | bytes 18436
  79.6 3.0 copy-start.14
  83.4 1.7 copy-start.15
  85.1 5.9 %copy-start.9 = (s32[2048,1]{1,0:T(8,128)S(1)}, s32[2048,1]{1,0:T(8,128)}, u32[]{:S(2)}) copy-start(s32[2048,1]{1,0:T(8,128)} %copy.87.start_ref) | copy-start | bytes 24580
  117.9 1.1 copy-start.2
  119.1 1.0 copy-start.12
  120.1 2.9 copy-start.23
  120.1 3.1 copy-start.24
  245.4 34.0 %all-to-all-start.1 = ((bf16[8,176,768]{2,1,0:T(8,128)(2,1)}), bf16[8,176,768]{2,1,0:T(8,128)(2,1)S(1)}, u32[]{:S(2)}, u32[]{:S(2)}) async-start(bf16[8,176,768]{2,1,0:T(8,128)(2,1)} %get-tuple-element.69), calls=%async_computation.1 | async-start | bytes 4325376 | tf_op jit(solution)/shard_map/all_to_all | solution.py:1619
  279.4 1.3 copy-start.16
  280.7 113.3 %all-to-all-start.2 = ((bf16[16,3,48,1024]{3,2,1,0:T(8,128)(2,1)}), bf16[16,3,48,1024]{3,2,1,0:T(8,128)(2,1)}, u32[]{:S(2)}, u32[]{:S(2)}) async-start(bf16[16,3,48,1024]{3,2,1,0:T(8,128)(2,1)} %weight_step.1), calls=%async_computation.2 | async-start | bytes 9437184 | tf_op jit(solution)/shard_map/all_to_all | solution.py:1721
  288.2 38.9 %copy-start.3 = (bf16[2048,384]{1,0:T(8,128)(2,1)S(1)}, bf16[2048,384]{1,0:T(8,128)(2,1)}, u32[]{:S(2)}) copy-start(bf16[2048,384]{1,0:T(8,128)(2,1)} %copy-done.2) | copy-start | bytes 4718596
  327.0 4.7 %copy-start.10 = (bf16[2048,384]{1,0:T(8,128)(2,1)S(1)}, bf16[2048,384]{1,0:T(8,128)(2,1)}, u32[]{:S(2)}) copy-start(bf16[2048,384]{1,0:T(8,128)(2,1)} %get-tuple-element.78.do_ref) | copy-start | bytes 4718596
  327.0 4.7 %copy-start.11 = (f32[2048,384]{1,0:T(8,128)S(1)}, f32[2048,384]{1,0:T(8,128)}, u32[]{:S(2)}) copy-start(f32[2048,384]{1,0:T(8,128)} %get-tuple-element.79.o_ref) | copy-start | bytes 9437188
  331.7 1.2 copy-start.13
  445.4 7.0 %copy-start.19 = (f32[1024,768]{1,0:T(8,128)S(1)}, f32[1024,768]{1,0:T(8,128)}, u32[]{:S(2)}) copy-start(f32[1024,768]{1,0:T(8,128)} %get-tuple-element.90) | copy-start | bytes 9437188
  452.4 1.7 copy-start.20
  452.4 2.4 copy-start.22
  452.4 3.7 copy-start.18

commit v7 on v6

--- a/solution.py
+++ b/solution.py
@@ -699,7 +699,7 @@
     pair_down.wait_recv()
 
     ff = in_ref.shape[3]
-    block = fit(ff, 256)
+    block = fit(ff, 512)
     steps = ff // block
     rows2 = 2 * padded
     dot_ref[...] = jnp.zeros(dot_ref.shape, single)
@@ -827,7 +827,7 @@
     local, width = tokens.shape
     seq = heads.shape[0]
     size = EXPERTS_FF
-    block = fit(ff, 256)
+    block = fit(ff, 512)
     any_spec = pl.BlockSpec(memory_space=pl.ANY)
     vmem = pl.BlockSpec(memory_space=pltpu.VMEM)
     dma = pltpu.SemaphoreType.DMA

time: 468 us -> 461 us (0.985)
  Pallas kernels: 338 us -> 332 us
    pallas_call x1, Pallas kernels: 98.9 us -> 92.3 us  [experts(): pl.pallas_call(functools.partial(experts_kernel, members, padded), out_sh...]
where the time goes in v7:
time: 461 us; the launch traced here: 452 us
  Pallas kernels  332 us (72%)
  local copies, waits for them, and re-layouts  43.3 us (9%)
  waiting for transfers between devices  40.8 us (9%)
  starting transfers between devices  19.1 us (4%)
  matrix products  11.1 us (2%)
    pallas_call x1, Pallas kernels, experts(): pl.pallas_call(functools.partial(experts_kernel, members, padded), out_sh...  92.3 us
    pallas_call x1, Pallas kernels, start(): pl.pallas_call(functools.partial(start_kernel, members, low, per_core, pa...  56 us
    pallas_call x1, Pallas kernels, tail(): pl.pallas_call(functools.partial(tail_kernel, members, low, padded), out_...  51.3 us
    pallas_call x1, Pallas kernels, attention_backward(): pl.pallas_call(functools.partial(bwd_kernel, heads), grid_spec=pltpu.Pref...  40 us
    pallas_call x1, Pallas kernels, backward_middle(): pl.pallas_call(functools.partial(back_kernel, padded), out_shape=[jax.Sha...  36.9 us
    pallas_call x1, Pallas kernels, weight_step(): pl.pallas_call(weight_kernel, grid=(steps,), in_specs=[whole, whole, wide...  28.3 us
    unnamed x66, local copies, waits for them, and re-layouts  27.5 us
    pallas_call x1, Pallas kernels, attention_forward(): pl.pallas_call(functools.partial(fwd_kernel, heads), grid_spec=pltpu.Pref...  27 us
  transfers between devices with their start and end apart: 4, of which 2 were waited for; matrix products, arithmetic and copies ran while one was open for 6% of the time, Pallas kernels for 29%

profile of v7, /device:TPU:12, one launch (start us, length us, event | category | flops | bytes accessed | tf_op | source)
XLA Modules:
  0.0 452.1 jit_solution(2928923701724767745)
XLA Ops:
  0.7 0.9 copy.78
  1.5 0.8 copy.80
  2.3 0.8 copy.79
  3.1 0.9 copy.99
  4.0 0.9 copy.81
  4.9 0.2 copy.82
  5.1 0.9 concatenate.6
  6.0 0.7 pad_add_fusion
  6.7 1.4 copy-done.1
  8.1 1.7 copy-done.6
  9.8 56.0 %start.1 = (bf16[16,48,1664]{2,1,0:T(8,128)(2,1)S(1)}, bf16[2048,768]{1,0:T(8,128)(2,1)}, bf16[8,176,768]{2,1,0:T(8,128)(2,1)S(1)}, bf16[1408,2048]{1,0:T(8,128)...) custom-call(bf16[48,1664]{1,0:T(8,128)(2,1)S(1)} %pad.23.pack_ref, ...), custom_call_target="tpu_custom_call" | custom-call | tf_op jit(solution)/shard_map/start/pallas_call | solution.py:494
  65.9 1.5 copy-done.4
  67.3 1.4 copy-done.7
  68.7 1.1 copy-done.8
  69.9 6.7 %all-to-all-start = ((bf16[16,2,48,1024]{3,2,1,0:T(8,128)(2,1)}), bf16[16,2,48,1024]{3,2,1,0:T(8,128)(2,1)}, u32[]{:S(2)}, u32[]{:S(2)}) async-start(bf16[16,2,48,1024]{3,2,1,0:T(8,128)(2,1)} %get-tuple-element.54), calls=%async_computation | async-start | bytes 6291456 | tf_op jit(solution)/shard_map/all_to_all | solution.py:1669
  76.6 0.9 slice.83.own_w_ref
  77.7 0.1 copy.94
  77.7 0.1 copy.95
  77.9 0.1 copy.96
  78.0 0.1 slice_convert_fusion
  78.1 0.1 copy.100
  78.2 1.4 copy.87.start_ref
  79.6 0.2 convert_reduce_fusion
  79.9 2.7 fusion
  82.6 0.8 fusion.2.one_ref
  83.4 1.7 copy-done.15
  85.1 5.8 %convolution_convert_fusion.q_ref.k_ref.v_ref = bf16[2048,1152]{1,0:T(8,128)(2,1)} fusion(bf16[2048,768]{1,0:T(8,128)(2,1)S(1)} %fusion.2.one_ref, bf16[768,1664]{1,0:T(8,128)(2,1)S(1)} %bitcast.71), kind=kOutput, calls=%fused_computation.2 | convolution fusion | flops 3626237952 | bytes 9633792 | tf_op jit(solution)/shard_map/dot_general | solution.py:38
  90.9 27.0 %shard_map.195 = (f32[2048,384]{1,0:T(8,128)}, bf16[2048,384]{1,0:T(8,128)(2,1)S(1)}, f32[2048,128]{1,0:T(8,128)S(1)}) custom-call(s32[4,8]{1,0:T(4,128)S(1)} %pad_add_fusion.1.bounds, bf16[2048,1152]{1,0:T(8,128)(2,1)} %convolution_convert_fusion.q_ref.k_ref.v_ref, bf16[2048,1152]{1,0:T(8,128)(2,1)} %convolution_convert_fusion.q_ref.k_ref.v_ref, ...), custom_call_target="tpu_custom_call" | custom-call | flops 12884901888 | bytes 12582912 | tf_op jit(solution)/shard_map/pallas_call | solution.py:153
  117.9 1.1 copy-done.2
  119.1 1.0 copy-done.12
  120.1 0.1 slice.84
  120.2 1.4 copy.90
  121.6 1.4 slice.82.proj_ref
  122.9 0.2 copy.88
  123.2 0.6 pad.27.mix_ref
  123.8 0.8 pad.28.prev_ref
  124.7 0.5 fusion.4
  125.2 0.9 pad.26.prev_ref
  126.1 0.7 pad.25.router_ref
  126.8 19.7 %all-to-all-done.in_ref = bf16[16,2,48,1024]{3,2,1,0:T(8,128)(2,1)} async-done(((bf16[16,2,48,1024]{3,2,1,0:T(8,128)(2,1)}), bf16[16,2,48,1024]{3,2,1,0:T(8,128)(2,1)}, u32[]{:S(2)}, u32[]{:S(2)}) %all-to-all-start) | async-done | bytes 3145760 | tf_op jit(solution)/shard_map/all_to_all | solution.py:1669
  146.5 92.3 %experts.1 = (bf16[8,176,768]{2,1,0:T(8,128)(2,1)}, bf16[8,176,768]{2,1,0:T(8,128)(2,1)}, bf16[8,176,768]{2,1,0:T(8,128)(2,1)}, bf16[8,176,768]{2,1,0:T(8,128)(2...) custom-call(bf16[16,48,1024]{2,1,0:T(8,128)(2,1)} %copy-done.8, ...), custom_call_target="tpu_custom_call" | custom-call | tf_op jit(solution)/shard_map/experts/pallas_call | solution.py:836
  238.8 5.6 %all-to-all-start.1 = ((bf16[8,176,768]{2,1,0:T(8,128)(2,1)}), bf16[8,176,768]{2,1,0:T(8,128)(2,1)S(1)}, u32[]{:S(2)}, u32[]{:S(2)}) async-start(bf16[8,176,768]{2,1,0:T(8,128)(2,1)} %get-tuple-element.69), calls=%async_computation.1 | async-start | bytes 4325376 | tf_op jit(solution)/shard_map/all_to_all | solution.py:1619
  244.4 28.3 %weight_step.1 = bf16[16,3,48,1024]{3,2,1,0:T(8,128)(2,1)} custom-call(bf16[1408,768]{1,0:T(8,128)(2,1)} %bitcast.93, bf16[1408,768]{1,0:T(8,128)(2,1)} %bitcast.94, bf16[2,1408,1024]{2,1,0:T(8,128)(2,1)} %get-tuple-element.66.hid_ref, bf16[2,1408,1024]{2,1,0:T(8,128)(2,1)} %get-tuple-element.67.pg_ref, bf16[2,1408,1024]{2,1,0:T(8,128)(2,1)} %get-tuple-element.68.pu_ref), custom_call_target="tpu_custom_call" | custom-call | flops 13287555072 | bytes 26738688 | tf_op jit(solution)/shard_map/weight_step/pallas_call | solution.py:1198
  272.7 1.3 copy-done.16
  274.0 6.7 %all-to-all-start.2 = ((bf16[16,3,48,1024]{3,2,1,0:T(8,128)(2,1)}), bf16[16,3,48,1024]{3,2,1,0:T(8,128)(2,1)}, u32[]{:S(2)}, u32[]{:S(2)}) async-start(bf16[16,3,48,1024]{3,2,1,0:T(8,128)(2,1)} %weight_step.1), calls=%async_computation.2 | async-start | bytes 9437184 | tf_op jit(solution)/shard_map/all_to_all | solution.py:1721
  280.8 0.7 copy.101
  281.5 36.9 %backward_middle.1 = (f32[1024,768]{1,0:T(8,128)}, bf16[2048,768]{1,0:T(8,128)(2,1)}, bf16[2048,384]{1,0:T(8,128)(2,1)}, f32[1024,768]{1,0:T(8,128)}, f32[1024,1...) custom-call(bf16[8,176,768]{2,1,0:T(8,128)(2,1)} %get-tuple-element.71.back_ref, s32[2048,8]{1,0:T(8,128)} %bitcast.74, ...), custom_call_target="tpu_custom_call" | custom-call | tf_op jit(solution)/shard_map/backward_middle/pallas_call | solution.py:1104
  318.5 1.1 slice_bitcast_fusion
  319.6 0.8 copy.92
  320.4 4.7 %convolution_convert_fusion.1.outg_ref = bf16[768,384]{1,0:T(8,128)(2,1)} fusion(bf16[2048,768]{1,0:T(8,128)(2,1)} %get-tuple-element.84, bf16[2048,384]{1,0:T(8,128)(2,1)S(1)} %copy-done.3), kind=kOutput, calls=%fused_computation.6 | convolution fusion | flops 1208254464 | bytes 5308416 | tf_op jit(solution)/shard_map/dot_general | solution.py:46
  325.0 1.2 copy-done.13
  326.3 40.0 %shard_map.196.qkv_ref = bf16[2048,1152]{1,0:T(8,128)(2,1)} custom-call(s32[4,8]{1,0:T(4,128)S(1)} %pad_add_fusion.1.bounds, bf16[2048,1152]{1,0:T(8,128)(2,1)} %convolution_convert_fusion.q_ref.k_ref.v_ref, bf16[2048,1152]{1,0:T(8,128)(2,1)} %convolution_convert_fusion.q_ref.k_ref.v_ref, bf16[2048,1152]{1,0:T(8,128)(2,1)} %convolution_convert_fusion.q_ref.k_ref.v_ref, ...), custom_call_target="tpu_custom_call" | custom-call | flops 32212254720 | bytes 15728640 | tf_op jit(solution)/shard_map/pallas_call | solution.py:255
  366.3 21.1 %all-to-all-done.2.grads_ref = bf16[16,3,48,1024]{3,2,1,0:T(8,128)(2,1)} async-done(((bf16[16,3,48,1024]{3,2,1,0:T(8,128)(2,1)}), bf16[16,3,48,1024]{3,2,1,0:T(8,128)(2,1)}, u32[]{:S(2)}, u32[]{:S(2)}) %all-to-all-start.2) | async-done | bytes 4718624 | tf_op jit(solution)/shard_map/all_to_all | solution.py:1721
  387.4 51.3 %tail.1 = (f32[3,48,384]{2,1,0:T(8,128)}, f32[48,384]{1,0:T(8,128)}, f32[1024,768]{1,0:T(8,128)}, bf16[1024,768]{1,0:T(8,128)(2,1)}, f32[24,768]{1,0:T(8,128)}, /*index=5*/f32[8,3,48,1024]{3,2,1,0:T(8,128)}) custom-call(bf16[8,176,768]{2,1,0:T(8,128)(2,1)} %copy-done.16, bf16[2048,1152]{1,0:T(8,128)(2,1)} %shard_map.196.qkv_ref, ...), custom_call_target="tpu_custom_call" | custom-call | tf_op jit(solution)/shard_map/tail/pallas_call | solution.py:1542
  438.7 0.9 slice.75
  439.6 1.4 dynamic-slice_bitcast_fusion
  441.1 0.6 reshape.306
  441.7 1.4 fusion.7
  443.1 2.7 copy.107
  445.7 1.7 copy.108
  447.4 0.7 copy.109
  448.1 0.6 copy.110
  448.7 0.7 copy-done.18
  449.5 2.2 copy.111
  (54 shorter events, 0.4 us)
Async XLA Ops:
  0.6 6.1 %copy-start = (bf16[1,1024,768]{2,1,0:T(8,128)(2,1)S(1)}, bf16[1,1024,768]{2,1,0:T(8,128)(2,1)}, u32[]{:S(2)}) copy-start(bf16[1,1024,768]{2,1,0:T(8,128)(2,1)} %param.16) | copy-start | bytes 4718596
  4.9 61.0 %copy-start.17 = (s32[1,1024,2]{2,1,0:T(8,128)}, s32[1,1024,2]{2,1,0:T(8,128)S(1)}, u32[]{:S(2)}) copy-start(s32[1,1024,2]{2,1,0:T(8,128)S(1)} %copy.81) | copy-start | bytes 24580
  6.7 1.4 copy-start.1
  8.1 1.7 copy-start.6
  65.9 1.5 copy-start.4
  67.3 1.4 copy-start.7
  68.7 1.1 copy-start.8
  69.9 6.7 %copy-start.5 = (bf16[16,48,1664]{2,1,0:T(8,128)(2,1)S(1)}, bf16[16,48,1664]{2,1,0:T(8,128)(2,1)}, u32[]{:S(2)}) copy-start(bf16[16,48,1664]{2,1,0:T(8,128)(2,1)} %copy-done.4) | copy-start | bytes 7667716
  69.9 76.6 %all-to-all-start = ((bf16[16,2,48,1024]{3,2,1,0:T(8,128)(2,1)}), bf16[16,2,48,1024]{3,2,1,0:T(8,128)(2,1)}, u32[]{:S(2)}, u32[]{:S(2)}) async-start(bf16[16,2,48,1024]{3,2,1,0:T(8,128)(2,1)} %get-tuple-element.54), calls=%async_computation | async-start | bytes 6291456 | tf_op jit(solution)/shard_map/all_to_all | solution.py:1669
  77.5 49.3 %collective-permute-start = (bf16[768,384]{1,0:T(8,128)(2,1)}, bf16[768,384]{1,0:T(8,128)(2,1)}, u32[]{:S(2)}, u32[]{:S(2)}) collective-permute-start(bf16[768,384]{1,0:T(8,128)(2,1)} %slice.83.own_w_ref), channel_id=1, source_target_pairs={{0,1},{1,0},{2,3},{3,2},{4,5},{5,4},{6,7},{7,6},{8,9},{9,8},{10,11... | collective-permute-start | bytes 1769480 | tf_op jit(solution)/shard_map/ppermute | solution.py:50
  78.2 5.2 %copy-start.21 = (f32[768,2]{0,1:T(2,128)}, f32[768,2]{0,1:T(2,128)S(1)}, u32[]{:S(2)}) copy-start(f32[768,2]{0,1:T(2,128)S(1)} %copy.100) | copy-start | bytes 18436
  79.6 3.0 copy-start.14
  83.4 1.7 copy-start.15
  85.1 5.9 %copy-start.9 = (s32[2048,1]{1,0:T(8,128)S(1)}, s32[2048,1]{1,0:T(8,128)}, u32[]{:S(2)}) copy-start(s32[2048,1]{1,0:T(8,128)} %copy.87.start_ref) | copy-start | bytes 24580
  117.9 1.1 copy-start.2
  119.1 1.0 copy-start.12
  120.1 2.9 copy-start.23
  120.1 3.1 copy-start.24
  238.8 33.9 %all-to-all-start.1 = ((bf16[8,176,768]{2,1,0:T(8,128)(2,1)}), bf16[8,176,768]{2,1,0:T(8,128)(2,1)S(1)}, u32[]{:S(2)}, u32[]{:S(2)}) async-start(bf16[8,176,768]{2,1,0:T(8,128)(2,1)} %get-tuple-element.69), calls=%async_computation.1 | async-start | bytes 4325376 | tf_op jit(solution)/shard_map/all_to_all | solution.py:1619
  272.7 1.3 copy-start.16
  274.0 113.4 %all-to-all-start.2 = ((bf16[16,3,48,1024]{3,2,1,0:T(8,128)(2,1)}), bf16[16,3,48,1024]{3,2,1,0:T(8,128)(2,1)}, u32[]{:S(2)}, u32[]{:S(2)}) async-start(bf16[16,3,48,1024]{3,2,1,0:T(8,128)(2,1)} %weight_step.1), calls=%async_computation.2 | async-start | bytes 9437184 | tf_op jit(solution)/shard_map/all_to_all | solution.py:1721
  281.5 38.9 %copy-start.3 = (bf16[2048,384]{1,0:T(8,128)(2,1)S(1)}, bf16[2048,384]{1,0:T(8,128)(2,1)}, u32[]{:S(2)}) copy-start(bf16[2048,384]{1,0:T(8,128)(2,1)} %copy-done.2) | copy-start | bytes 4718596
  320.4 4.7 %copy-start.10 = (bf16[2048,384]{1,0:T(8,128)(2,1)S(1)}, bf16[2048,384]{1,0:T(8,128)(2,1)}, u32[]{:S(2)}) copy-start(bf16[2048,384]{1,0:T(8,128)(2,1)} %get-tuple-element.78.do_ref) | copy-start | bytes 4718596
  320.4 4.7 %copy-start.11 = (f32[2048,384]{1,0:T(8,128)S(1)}, f32[2048,384]{1,0:T(8,128)}, u32[]{:S(2)}) copy-start(f32[2048,384]{1,0:T(8,128)} %get-tuple-element.79.o_ref) | copy-start | bytes 9437188
  325.0 1.2 copy-start.13
  438.7 7.0 %copy-start.19 = (f32[1024,768]{1,0:T(8,128)S(1)}, f32[1024,768]{1,0:T(8,128)}, u32[]{:S(2)}) copy-start(f32[1024,768]{1,0:T(8,128)} %get-tuple-element.90) | copy-start | bytes 9437188
  445.7 1.7 copy-start.20
  445.7 2.4 copy-start.22
  445.7 3.7 copy-start.18
